TPU v7x, 512 devices: a whole 4x4x16 slice. The times are simulated.
512 devices in a mesh: pos: 64 (over z, x), tm: 8 (over y, core).
Axes of the slice: x: 4, y: 4, z: 16, core: 2. Of those that a mesh axis runs over, the one named last changes fastest.
Arguments:
- frames_in: bfloat16 [64, 512, 3072], P('pos'), may hold values from -24 to 24
- qkv_weight: bfloat16 [3072, 3, 3072], P('pos', None, 'tm'), may hold values from -0.109375 to 0.109375
- span_mask: int32 [8, 8], replicated, may hold values from 0 to 1, as said below
Outputs:
- attended: bfloat16 [64, 512, 3072], P('pos', None, 'tm')
Inputs may be any that keep to these rules, and one draw needn't show every extreme that they name: span_mask has ones on the diagonal and zeros above it.
All inputs are finite; a program needn't handle non-finite values.
Results may differ from a plain program's by a relative error of at most 0.0078.
Values may be sent and summed in bfloat16 or wider, within the bound.
No kernel may reach another device: no remote copies, remote signals or barrier semaphores. Data moves between devices by JAX's collectives and lax.ppermute only.
A program may use at most 64 MiB of HBM per device.

v0:
```python
import jax
import jax.numpy as jnp
from jax import lax
from jax.sharding import PartitionSpec as P

HD = 128
FRAMES = 64
SPANS = 8


def span_onehot(count):
    span_len = FRAMES // SPANS
    frame_ids = jnp.arange(count, dtype=jnp.int32)
    span_ids = frame_ids // span_len
    return (span_ids[:, None] == jnp.arange(SPANS, dtype=jnp.int32)[None, :]).astype(jnp.float32)


def attend_all(query, keys, values, mask_table):
    scale = 1.0 / jnp.sqrt(jnp.float32(HD))
    scores = jnp.einsum("fphd,gphd->phfg", query, keys, preferred_element_type=jnp.float32) * scale
    onehot = span_onehot(query.shape[0])
    allowed = jnp.dot(jnp.dot(onehot, mask_table), onehot.T) > 0.5
    scores = jnp.where(allowed[None, None], scores, jnp.float32(-1e30))
    row_max = jnp.max(scores, axis=-1)
    weights = jnp.where(allowed[None, None], jnp.exp(scores - row_max[..., None]), jnp.float32(0.0))
    total = jnp.sum(weights, axis=-1)
    summed = jnp.einsum(
        "phfg,gphd->phfd", weights.astype(jnp.bfloat16), values, preferred_element_type=jnp.float32
    )
    result = (summed / total[..., None]).astype(jnp.bfloat16)
    places, heads, frames, size = result.shape
    return jnp.transpose(result, (2, 0, 1, 3)).reshape(frames, places, heads * size)


def split_parts(columns):
    all_frames, places, three, part_width = columns.shape
    heads = part_width // HD
    query = columns[:, :, 0].reshape(all_frames, places, heads, HD)
    keys = columns[:, :, 1].reshape(all_frames, places, heads, HD)
    values = columns[:, :, 2].reshape(all_frames, places, heads, HD)
    return (query, keys, values)


def per_device(frames_in, qkv_weight, span_mask):
    local_frames, places_all, width = frames_in.shape
    local_width = qkv_weight.shape[2]
    flat_rows = frames_in.reshape(local_frames * places_all, width)
    piece = lax.all_gather(qkv_weight, "pos", axis=0, tiled=True)
    projected = jnp.dot(
        flat_rows,
        piece.reshape(piece.shape[0], 3 * local_width),
        preferred_element_type=jnp.float32,
    )
    packed = projected.astype(jnp.bfloat16).reshape(local_frames, places_all, 3, local_width)
    mask_table = span_mask.astype(jnp.float32)
    columns = lax.all_to_all(packed, "pos", split_axis=1, concat_axis=0, tiled=True)
    query, keys, values = split_parts(columns)
    output = attend_all(query, keys, values, mask_table)
    return lax.all_to_all(output, "pos", split_axis=0, concat_axis=1, tiled=True)


def solution(mesh):
    in_specs = (P("pos", None, None), P("pos", None, "tm"), P())
    out_specs = P("pos", None, "tm")
    return jax.shard_map(
        per_device, mesh=mesh, in_specs=in_specs, out_specs=out_specs, check_vma=False
    )
```

profile of v0, /device:TPU:16, one launch (start us, length us, event | category | flops | bytes accessed | tf_op | source)
XLA Modules:
  0.0 316.5 jit_solution(9183060549769326393)
XLA Ops:
  6.5 0.0 copy-start
  6.5 0.0 all-gather.2.cloned.1.call-start
  6.5 0.7 all-gather.2.cloned.1.call-update
  7.3 161.6 %all-gather.2.cloned.1.call-done = bf16[3072,3,384]{2,0,1:T(8,128)(2,1)} async-done(((bf16[48,3,384]{2,0,1:T(8,128)(2,1)}), bf16[3072,3,384]{2,0,1:T(8,128)(2,1)}) %all-gather.2.cloned.1.call-update) | async-done | bytes 7077904 | tf_op jit(solution)/shard_map/all_gather | solution.py:48
  168.9 10.3 %copy.27 = bf16[3072,3,384]{0,2,1:T(8,128)(2,1)} copy(bf16[3072,3,384]{2,0,1:T(8,128)(2,1)} %all-gather.2.cloned.1.call-done) | data formatting | bytes 14155776 | tf_op jit(solution)/shard_map/all_gather | solution.py:48
  179.1 0.0 copy-done
  179.1 8.3 %fusion.3 = bf16[512,1152]{1,0:T(8,128)(2,1)} fusion(bf16[3072,1152]{0,1:T(8,128)(2,1)} %bitcast.30, bf16[1,512,3072]{2,1,0:T(8,128)(2,1)S(1)} %copy-done), kind=kOutput, calls=%fused_computation.3 | convolution fusion | flops 3624468480 | bytes 11403264 | tf_op jit(solution)/shard_map/dot_general | solution.py:49
  187.4 2.4 copy.28
  189.9 0.0 copy-start.1
  189.9 3.6 %copy.29 = bf16[1,512,3,384]{3,2,0,1:T(4,128)(2,1)} copy(bf16[1,512,3,384]{1,3,2,0:T(8,128)(2,1)} %bitcast.32) | data formatting | bytes 2359296 | tf_op jit(solution)/shard_map/reshape | solution.py:54
  193.5 9.4 %all-to-all-start = ((bf16[1,512,3,384]{3,2,0,1:T(4,128)(2,1)}), bf16[1,512,3,384]{3,2,0,1:T(4,128)(2,1)}, u32[]{:S(2)}, u32[]{:S(2)}) async-start(bf16[1,512,3,384]{3,2,0,1:T(4,128)(2,1)} %copy.29), calls=%async_computation | async-start | bytes 3145728 | tf_op jit(solution)/shard_map/all_to_all | solution.py:56
  202.9 0.0 copy-done.1
  202.9 0.4 convolution_compare_fusion
  203.3 0.1 copy.26
  203.4 69.8 %all-to-all-done = bf16[1,512,3,384]{3,2,0,1:T(4,128)(2,1)} async-done(((bf16[1,512,3,384]{3,2,0,1:T(4,128)(2,1)}), bf16[1,512,3,384]{3,2,0,1:T(4,128)(2,1)}, u32[]{:S(2)}, u32[]{:S(2)}) %all-to-all-start) | async-done | bytes 1179680 | tf_op jit(solution)/shard_map/all_to_all | solution.py:56
  273.1 1.6 copy.45
  274.7 0.2 slice_bitcast_fusion.2
  274.9 0.3 fusion.10
  275.2 0.0 copy-start.2
  275.3 0.9 copy-done.2
  276.1 0.8 fusion.24
  277.0 2.6 fusion.11
  279.6 1.3 copy.46
  280.8 28.1 %all_to_all.24 = bf16[64,8,384]{2,1,0:T(8,128)(2,1)S(1)} all-to-all(bf16[64,8,384]{2,1,0:T(8,128)(2,1)S(1)} %bitcast.33), channel_id=1, replica_groups=mesh['pos'=64,'tm'=8] {'pos'}, dimensions={0} | all-to-all | bytes 786432 | tf_op jit(solution)/shard_map/all_to_all | solution.py:59
  308.9 0.7 copy.48
  (1 shorter events, 0.0 us)
Async XLA Ops:
  6.5 172.6 %copy-start = (bf16[1,512,3072]{2,1,0:T(8,128)(2,1)S(1)}, bf16[1,512,3072]{2,1,0:T(8,128)(2,1)}, u32[]{:S(2)}) copy-start(bf16[1,512,3072]{2,1,0:T(8,128)(2,1)} %param.3) | copy-start | bytes 9437188
  6.5 162.3 %all-gather.2.cloned.1.call-start = ((), (), s32[]{:S(2)}) async-start(), calls=%async_computation.2 | async-start | bytes 7188480 | tf_op jit(solution)/shard_map/all_gather | solution.py:48
  189.9 13.0 %copy-start.1 = (s32[8,8]{1,0:T(8,128)S(1)}, s32[8,8]{1,0:T(8,128)}, u32[]{:S(2)}) copy-start(s32[8,8]{1,0:T(8,128)} %param.5) | copy-start | bytes 772
  193.5 79.6 %all-to-all-start = ((bf16[1,512,3,384]{3,2,0,1:T(4,128)(2,1)}), bf16[1,512,3,384]{3,2,0,1:T(4,128)(2,1)}, u32[]{:S(2)}, u32[]{:S(2)}) async-start(bf16[1,512,3,384]{3,2,0,1:T(4,128)(2,1)} %copy.29), calls=%async_computation | async-start | bytes 3145728 | tf_op jit(solution)/shard_map/all_to_all | solution.py:56
  275.2 0.9 copy-start.2
Sparse Core Ops, SparseCore 0:
  10.4 158.3 all-gather.1
where the time goes:
time: 317 us
  waiting for transfers between devices  232 us (73%)
  blocking collectives  28.1 us (9%)
  local copies, waits for them, and re-layouts  21.1 us (7%)
  between operations  13.5 us (4%)
  matrix products  11.6 us (4%)
  starting transfers between devices  9.35 us (3%)
    all_gather x1, waiting for transfers between devices, per_device(): piece = lax.all_gather(qkv_weight, 'pos', axis=0, tiled=True)  162 us
    all_to_all x1, waiting for transfers between devices, per_device(): lax.all_to_all(packed, 'pos', split_axis=1, concat_axis=0, tiled=True)  69.8 us
    all_to_all x1, blocking collectives, per_device(): lax.all_to_all(output, 'pos', split_axis=0, concat_axis=1, tiled=True)  28.1 us
    all_gather x1, local copies, waits for them, and re-layouts, per_device(): piece = lax.all_gather(qkv_weight, 'pos', axis=0, tiled=True)  10.3 us
    all_to_all x1, starting transfers between devices, per_device(): lax.all_to_all(packed, 'pos', split_axis=1, concat_axis=0, tiled=True)  9.35 us
    dot_general x1, matrix products, per_device(): jnp.dot(flat_rows, piece.reshape(piece.shape[0], 3 * local_width), prefer...  8.28 us
  transfers between devices with their start and end apart: 2, of which 2 were waited for; matrix products, arithmetic and copies ran while one was open for 0% of the time, Pallas kernels for 0%

commit v1 on v0

v1 whole, which is shorter than its diff:
```python
import jax
import jax.numpy as jnp
from jax import lax
from jax.experimental import pallas as pl
from jax.experimental.pallas import tpu as pltpu
from jax.sharding import Mesh
from jax.sharding import PartitionSpec as P

D = 3072
HD = 128
FRAMES = 64
SPANS = 8
GROUP = 384
NZ, NX, NY, NC = 16, 4, 4, 2
AXES = ("z", "x", "y", "c")
SLICE = D // (NZ * NX)
ROWS = NX * SLICE
TOKENS = FRAMES * 8


def permute(array, where_to):
    pairs = []
    for z in range(NZ):
        for x in range(NX):
            for y in range(NY):
                for c in range(NC):
                    a, b, d, e = where_to(z, x, y, c)
                    source = ((z * NX + x) * NY + y) * NC + c
                    pairs.append((source, (((a % NZ) * NX + b % NX) * NY + d % NY) * NC + e))
    return lax.ppermute(array, AXES, pairs)


def home(z, x, y, c):
    return (z, x, y, c) if c == x // 2 else (z, 3 - x, y, 1 - c)


def second(z, x, y, c):
    near = x ^ 1
    return (z, near if x // 2 == c else 3 - near, y, x // 2)


def swap(z, x, y, c):
    return (z, x, y, 1 - c)


def ring(z, x, y, c):
    return (z + (1 if c == 0 else -1), x, y, c)


def attend_kernel(place, mask, *refs):
    own, mine, theirs = refs[0], refs[1:9], refs[9:17]
    pieces = refs[17:21]
    out = refs[21]
    weights, tokens, qkv, bias, w_sems, x_sems = refs[22:]
    z, y, c = place[0], place[1], place[2]
    sign = 1 - 2 * c

    copies = []
    for i, (piece, shift) in enumerate(zip(pieces, (0, 1, 3, 2))):
        source = lax.rem(y + shift, NY)
        for half in range(2):
            at = pl.multiple_of((2 * source + half) * GROUP, GROUP)
            copies.append(
                pltpu.make_async_copy(piece.at[half], tokens.at[:, pl.ds(at, GROUP)], x_sems.at[2 * i + half])
            )
    by_part = []
    for j in range(3):
        part = []

        def add(ref, row):
            rows = ref.shape[1]
            at = pl.multiple_of(row, 32)
            part.append(
                pltpu.make_async_copy(ref.at[j], weights.at[j, pl.ds(at, rows)], w_sems.at[j, len(part)])
            )

        add(own, z * ROWS)
        for t in range(1, 8):
            add(mine[t - 1], lax.rem(z - sign * t + NZ, NZ) * ROWS)
            add(theirs[t - 1], lax.rem(z + sign * t + NZ, NZ) * ROWS)
        far = lax.rem(z + 8, NZ) * ROWS
        add(mine[7], far + c * (ROWS // 2))
        add(theirs[7], far + (1 - c) * (ROWS // 2))
        by_part.append(part)
    for copy in copies:
        copy.start()
    for part in by_part:
        for copy in part:
            copy.start()

    span_rows = TOKENS // SPANS
    column = lax.broadcasted_iota(jnp.int32, (1, TOKENS), 1)
    same = (
        lax.broadcasted_iota(jnp.int32, (span_rows, TOKENS), 0) & 7
    ) == (lax.broadcasted_iota(jnp.int32, (span_rows, TOKENS), 1) & 7)
    for i in range(SPANS):
        row = jnp.zeros((1, TOKENS), jnp.int32)
        for j in range(SPANS):
            row = jnp.where((column // span_rows) == j, mask[i, j], row)
        ok = same & (jnp.broadcast_to(row, (span_rows, TOKENS)) > 0)
        bias[pl.ds(i * span_rows, span_rows), :] = jnp.where(ok, 0.0, -1e30)

    for copy in copies:
        copy.wait()
    for j in range(3):
        for copy in by_part[j]:
            copy.wait()
        for r in range(2):
            rows = pl.ds(r * (TOKENS // 2), TOKENS // 2)
            qkv[j, rows, :] = jnp.dot(
                tokens[rows, :], weights[j], preferred_element_type=jnp.float32
            ).astype(jnp.bfloat16)

    scale = 1.0 / jnp.sqrt(jnp.float32(HD))
    for h in range(GROUP // HD):
        lanes = pl.ds(h * HD, HD)
        for i in range(4):
            rows = pl.ds(i * 128, 128)
            width = (i + 1) * 128
            scores = lax.dot_general(
                qkv[0, rows, lanes],
                qkv[1, pl.ds(0, width), lanes],
                (((1,), (1,)), ((), ())),
                preferred_element_type=jnp.float32,
            )
            scores = scores * scale + bias[rows, pl.ds(0, width)]
            shares = jnp.exp(scores - jnp.max(scores, axis=-1, keepdims=True))
            total = jnp.sum(shares, axis=-1, keepdims=True)
            summed = jnp.dot(
                shares.astype(jnp.bfloat16),
                qkv[2, pl.ds(0, width), lanes],
                preferred_element_type=jnp.float32,
            )
            out[rows, lanes] = (summed / total).astype(jnp.bfloat16)


def project_and_attend(place, span_mask, own, mine, theirs, pieces):
    arrays = [own, *mine, *theirs, *pieces]
    return pl.pallas_call(
        attend_kernel,
        out_shape=jax.ShapeDtypeStruct((TOKENS, GROUP), jnp.bfloat16),
        in_specs=[pl.BlockSpec(memory_space=pltpu.SMEM)] * 2
        + [pl.BlockSpec(memory_space=pl.ANY)] * len(arrays),
        out_specs=pl.BlockSpec(memory_space=pltpu.VMEM),
        scratch_shapes=[
            pltpu.VMEM((3, D, GROUP), jnp.bfloat16),
            pltpu.VMEM((TOKENS, D), jnp.bfloat16),
            pltpu.VMEM((3, TOKENS, GROUP), jnp.bfloat16),
            pltpu.VMEM((TOKENS, TOKENS), jnp.float32),
            pltpu.SemaphoreType.DMA((3, 17)),
            pltpu.SemaphoreType.DMA((8,)),
        ],
        compiler_params=pltpu.CompilerParams(vmem_limit_bytes=40 * 1024 * 1024),
    )(place, span_mask, *arrays)


def per_device(frames_in, qkv_weight, span_mask):
    z, x, y, c = (lax.axis_index(name) for name in AXES)
    group = x // 2

    piece = jnp.transpose(qkv_weight, (1, 0, 2))
    first = permute(piece, home)
    other = permute(piece, second)
    slot = jnp.where(c == group, x, 3 - x)
    half = jnp.where(
        slot % 2 == 0,
        jnp.concatenate([first, other], axis=1),
        jnp.concatenate([other, first], axis=1),
    )
    half_other = permute(half, swap)
    own = jnp.where(
        c == 0,
        jnp.concatenate([half, half_other], axis=1),
        jnp.concatenate([half_other, half], axis=1),
    )

    places = frames_in.reshape(NZ, NX, 8, D)
    places = lax.dynamic_slice(places, (0, 2 * c, 0, 2 * GROUP * y), (NZ, 2, 8, 2 * GROUP))
    low, high = places[..., :GROUP], places[..., GROUP:]
    low = jnp.where(c == 0, low, low[:, ::-1])
    high = jnp.where(c == 0, high[:, ::-1], high)
    packed = jnp.concatenate([low, high], axis=1).reshape(NZ * NX, 8, GROUP)
    spread = lax.all_to_all(packed, ("z", "x"), split_axis=0, concat_axis=0, tiled=True)
    spread = spread.reshape(1, TOKENS, GROUP)
    partner = permute(spread, lambda z, x, y, c: (z, 3 - x, y, c))
    both = jnp.where(
        group == 0,
        jnp.concatenate([spread, partner], axis=0),
        jnp.concatenate([partner, spread], axis=0),
    )
    pieces = [both] + [
        permute(both, lambda z, x, y, c, k=k: (z, x, y + k, c)) for k in (-1, 1, 2)
    ]

    mine, theirs = [], []
    block = own
    for t in range(1, 9):
        if t == 8:
            block = lax.dynamic_slice(block, (0, c * (ROWS // 2), 0), (3, ROWS // 2, GROUP))
        block = permute(block, ring)
        mine.append(block)
        theirs.append(permute(block, swap))

    place = jnp.stack([z, y, c]).astype(jnp.int32)
    output = project_and_attend(place, span_mask, own, mine, theirs, pieces)
    output = permute(output.reshape(FRAMES, 8, GROUP), home)
    output = lax.all_to_all(output, ("z", "x"), split_axis=0, concat_axis=0, tiled=True)
    return output.reshape(1, NZ * NX * 8, GROUP)


def solution(mesh):
    fine = Mesh(mesh.devices.reshape(NZ, NX, NY, NC), AXES)
    in_specs = (P(("z", "x"), None, None), P(("z", "x"), None, ("y", "c")), P())
    out_specs = P(("z", "x"), None, ("y", "c"))
    return jax.shard_map(
        per_device, mesh=fine, in_specs=in_specs, out_specs=out_specs, check_vma=False
    )
```

time: 317 us -> 226 us (0.71)
  the two profiles are of different devices: /device:TPU:16 before, /device:TPU:8 now
where the time goes in v1:
time: 226 us; the launch traced here: 225 us
  starting transfers between devices  76.1 us (34%)
  waiting for transfers between devices  73.5 us (33%)
  blocking collectives  49 us (22%)
  Pallas kernels  14.8 us (7%)
  local copies, waits for them, and re-layouts  9.99 us (4%)
    ppermute x24, waiting for transfers between devices, permute(): return lax.ppermute(array, AXES, pairs)  73.5 us
    ppermute x24, starting transfers between devices, permute(): return lax.ppermute(array, AXES, pairs)  65.5 us
    all_to_all x1, blocking collectives, per_device(): lax.all_to_all(output, ('z', 'x'), split_axis=0, concat_axis=0, tiled=True)  49 us
    pallas_call x1, Pallas kernels, project_and_attend(): pl.pallas_call(attend_kernel, out_shape=jax.ShapeDtypeStruct((TOKENS, GRO...  14.8 us
    all_to_all x1, starting transfers between devices, per_device(): lax.all_to_all(packed, ('z', 'x'), split_axis=0, concat_axis=0, tiled=True)  10.7 us
    unnamed x23, local copies, waits for them, and re-layouts  8.88 us
  transfers between devices with their start and end apart: 25, of which 11 were waited for; matrix products, arithmetic and copies ran while one was open for 1% of the time, Pallas kernels for 0%

profile of v1, /device:TPU:8, one launch (start us, length us, event | category | flops | bytes accessed | tf_op | source)
XLA Modules:
  0.0 225.3 jit_solution(10090506588395532392)
XLA Ops:
  0.0 3.4 %collective-permute-start.1 = (bf16[3,48,384]{2,1,0:T(8,128)(2,1)}, bf16[3,48,384]{2,1,0:T(8,128)(2,1)S(1)}, u32[]{:S(2)}, u32[]{:S(2)}) collective-permute-start(bf16[3,48,384]{2,1,0:T(8,128)(2,1)} %bitcast.14), channel_id=1, source_target_pairs={{0,8},{1,16},{2,10},{3,18},{4,12},{5,20},{6,14},{7,22},{8,0},{9,24... | collective-permute-start | bytes 331784 | tf_op jit(solution)/shard_map/ppermute | solution.py:30
  5.0 2.1 collective-permute-done.1
  7.1 7.4 %collective-permute-start.2 = (bf16[3,96,384]{2,1,0:T(8,128)(2,1)S(1)}, bf16[3,96,384]{2,1,0:T(8,128)(2,1)S(1)}, u32[]{:S(2)}, u32[]{:S(2)}) collective-permute-start(bf16[3,96,384]{2,1,0:T(8,128)(2,1)S(1)} %maximum_select_fusion.2), channel_id=1, source_target_pairs={{0,1},{1,0},{2,3},{3,2},{4,5},{5,4},{6,7},{7,6},{8,9},{9,8},{10,11... | collective-permute-start | bytes 663560 | tf_op jit(solution)/shard_map/ppermute | solution.py:30
  15.8 3.8 %collective-permute-start.3 = (bf16[3,192,384]{2,1,0:T(8,128)(2,1)S(1)}, bf16[3,192,384]{2,1,0:T(8,128)(2,1)}, u32[]{:S(2)}, u32[]{:S(2)}) collective-permute-start(bf16[3,192,384]{2,1,0:T(8,128)(2,1)S(1)} %maximum_select_fusion.1.refs_0_), channel_id=1, source_target_pairs={{0,32},{1,481},{2,34},{3,483},{4,36},{5,485},{6,38},{7,487},{8,40}... | collective-permute-start | bytes 1327112 | tf_op jit(solution)/shard_map/ppermute | solution.py:30
  20.7 12.9 %collective-permute-done.3.refs_1_ = bf16[3,192,384]{2,1,0:T(8,128)(2,1)} collective-permute-done((bf16[3,192,384]{2,1,0:T(8,128)(2,1)S(1)}, bf16[3,192,384]{2,1,0:T(8,128)(2,1)}, u32[]{:S(2)}, u32[]{:S(2)}) %collective-permute-start.3) | collective-permute-done | bytes 442400 | tf_op jit(solution)/shard_map/ppermute | solution.py:30
  33.5 1.9 collective-permute-start.4
  36.4 10.7 %all-to-all-start = ((bf16[64,8,384]{2,1,0:T(8,128)(2,1)}), bf16[64,8,384]{2,1,0:T(8,128)(2,1)S(1)}, u32[]{:S(2)}, u32[]{:S(2)}) async-start(bf16[64,8,384]{2,1,0:T(8,128)(2,1)} %bitcast.5), calls=%async_computation | async-start | bytes 786432 | tf_op jit(solution)/shard_map/all_to_all | solution.py:183
  47.1 3.5 %collective-permute-start.5 = (bf16[3,192,384]{2,1,0:T(8,128)(2,1)}, bf16[3,192,384]{2,1,0:T(8,128)(2,1)S(1)}, u32[]{:S(2)}, u32[]{:S(2)}) collective-permute-start(bf16[3,192,384]{2,1,0:T(8,128)(2,1)} %collective-permute-done.4.refs_2_), channel_id=1, source_target_pairs={{0,32},{1,481},{2,34},{3,483},{4,36},{5,485},{6,38},{7,487},{8,40}... | collective-permute-start | bytes 1327112 | tf_op jit(solution)/shard_map/ppermute | solution.py:30
  50.6 19.7 %collective-permute-done.5.refs_3_ = bf16[3,192,384]{2,1,0:T(8,128)(2,1)S(1)} collective-permute-done((bf16[3,192,384]{2,1,0:T(8,128)(2,1)}, bf16[3,192,384]{2,1,0:T(8,128)(2,1)S(1)}, u32[]{:S(2)}, u32[]{:S(2)}) %collective-permute-start.5) | collective-permute-done | bytes 442400 | tf_op jit(solution)/shard_map/ppermute | solution.py:30
  71.0 1.9 collective-permute-start.6
  72.9 9.5 %collective-permute-done.6.refs_4_ = bf16[3,192,384]{2,1,0:T(8,128)(2,1)S(1)} collective-permute-done((bf16[3,192,384]{2,1,0:T(8,128)(2,1)S(1)}, bf16[3,192,384]{2,1,0:T(8,128)(2,1)S(1)}, u32[]{:S(2)}, u32[]{:S(2)}) %collective-permute-start.6) | collective-permute-done | bytes 442400 | tf_op jit(solution)/shard_map/ppermute | solution.py:30
  83.2 1.9 collective-permute-start.7
  85.1 9.5 %collective-permute-done.7.refs_5_ = bf16[3,192,384]{2,1,0:T(8,128)(2,1)S(1)} collective-permute-done((bf16[3,192,384]{2,1,0:T(8,128)(2,1)S(1)}, bf16[3,192,384]{2,1,0:T(8,128)(2,1)S(1)}, u32[]{:S(2)}, u32[]{:S(2)}) %collective-permute-start.7) | collective-permute-done | bytes 442400 | tf_op jit(solution)/shard_map/ppermute | solution.py:30
  94.6 1.9 collective-permute-start.8
  96.5 4.5 %collective-permute-start.19 = (bf16[1,512,384]{2,1,0:T(8,128)(2,1)S(1)}, bf16[1,512,384]{2,1,0:T(8,128)(2,1)S(1)}, u32[]{:S(2)}, u32[]{:S(2)}) collective-permute-start(bf16[1,512,384]{2,1,0:T(8,128)(2,1)S(1)} %bitcast.11), channel_id=1, source_target_pairs={{0,24},{1,25},{2,26},{3,27},{4,28},{5,29},{6,30},{7,31},{8,16},{9,... | collective-permute-start | bytes 1179656 | tf_op jit(solution)/shard_map/ppermute | solution.py:30
  101.0 1.9 collective-permute-start.11
  102.9 2.4 %collective-permute-start.12 = (bf16[3,192,384]{2,1,0:T(8,128)(2,1)}, bf16[3,192,384]{2,1,0:T(8,128)(2,1)S(1)}, u32[]{:S(2)}, u32[]{:S(2)}) collective-permute-start(bf16[3,192,384]{2,1,0:T(8,128)(2,1)} %collective-permute-done.4.refs_2_), channel_id=1, source_target_pairs={{0,1},{1,0},{2,3},{3,2},{4,5},{5,4},{6,7},{7,6},{8,9},{9,8},{10,11... | collective-permute-start | bytes 1327112 | tf_op jit(solution)/shard_map/ppermute | solution.py:30
  106.1 1.9 collective-permute-start.9
  108.5 4.2 %collective-permute-start.22 = (bf16[2,512,384]{2,1,0:T(8,128)(2,1)S(1)}, bf16[2,512,384]{2,1,0:T(8,128)(2,1)S(1)}, u32[]{:S(2)}, u32[]{:S(2)}) collective-permute-start(bf16[2,512,384]{2,1,0:T(8,128)(2,1)S(1)} %maximum_select_fusion.refs_17_), channel_id=1, source_target_pairs={{0,4},{1,5},{2,6},{3,7},{4,0},{5,1},{6,2},{7,3},{8,12},{9,13},{10,... | collective-permute-start | bytes 2359304 | tf_op jit(solution)/shard_map/ppermute | solution.py:30
  112.8 1.9 collective-permute-start.21
  115.5 3.4 %collective-permute-start.13 = (bf16[3,192,384]{2,1,0:T(8,128)(2,1)}, bf16[3,192,384]{2,1,0:T(8,128)(2,1)}, u32[]{:S(2)}, u32[]{:S(2)}) collective-permute-start(bf16[3,192,384]{2,1,0:T(8,128)(2,1)} %copy-done), channel_id=1, source_target_pairs={{0,1},{1,0},{2,3},{3,2},{4,5},{5,4},{6,7},{7,6},{8,9},{9,8},{10,11... | collective-permute-start | bytes 1327112 | tf_op jit(solution)/shard_map/ppermute | solution.py:30
  119.7 1.9 collective-permute-start.14
  121.6 3.6 %collective-permute-start.20 = (bf16[2,512,384]{2,1,0:T(8,128)(2,1)S(1)}, bf16[2,512,384]{2,1,0:T(8,128)(2,1)}, u32[]{:S(2)}, u32[]{:S(2)}) collective-permute-start(bf16[2,512,384]{2,1,0:T(8,128)(2,1)S(1)} %maximum_select_fusion.refs_17_), channel_id=1, source_target_pairs={{0,6},{1,7},{2,0},{3,1},{4,2},{5,3},{6,4},{7,5},{8,14},{9,15},{10,... | collective-permute-start | bytes 2359304 | tf_op jit(solution)/shard_map/ppermute | solution.py:30
  125.3 2.1 collective-permute-start.15
  127.5 2.2 collective-permute-start.16
  129.7 1.9 collective-permute-done.22.refs_20_
  131.6 2.6 %collective-permute-start.10 = (bf16[3,96,384]{2,1,0:T(8,128)(2,1)S(1)}, bf16[3,96,384]{2,1,0:T(8,128)(2,1)S(1)}, u32[]{:S(2)}, u32[]{:S(2)}) collective-permute-start(bf16[3,96,384]{2,1,0:T(8,128)(2,1)S(1)} %constant_dynamic-slice_fusion.2), channel_id=1, source_target_pairs={{0,32},{1,481},{2,34},{3,483},{4,36},{5,485},{6,38},{7,487},{8,40}... | collective-permute-start | bytes 663560 | tf_op jit(solution)/shard_map/ppermute | solution.py:30
  134.2 14.3 %collective-permute-done.21.refs_19_ = bf16[2,512,384]{2,1,0:T(8,128)(2,1)S(1)} collective-permute-done((bf16[2,512,384]{2,1,0:T(8,128)(2,1)S(1)}, bf16[2,512,384]{2,1,0:T(8,128)(2,1)S(1)}, u32[]{:S(2)}, u32[]{:S(2)}) %collective-permute-start.21) | collective-permute-done | bytes 786464 | tf_op jit(solution)/shard_map/ppermute | solution.py:30
  148.5 2.8 %collective-permute-start.17 = (bf16[3,192,384]{2,1,0:T(8,128)(2,1)S(1)}, bf16[3,192,384]{2,1,0:T(8,128)(2,1)}, u32[]{:S(2)}, u32[]{:S(2)}) collective-permute-start(bf16[3,192,384]{2,1,0:T(8,128)(2,1)S(1)} %collective-permute-done.9.refs_7_), channel_id=1, source_target_pairs={{0,1},{1,0},{2,3},{3,2},{4,5},{5,4},{6,7},{7,6},{8,9},{9,8},{10,11... | collective-permute-start | bytes 1327112 | tf_op jit(solution)/shard_map/ppermute | solution.py:30
  151.3 1.9 collective-permute-start.18
  159.9 14.8 %shard_map.37 = bf16[512,384]{1,0:T(8,128)(2,1)S(1)} custom-call(s32[3]{0:T(128)S(1)} %pad_add_fusion.place, s32[8,8]{1,0:T(8,128)S(1)} %copy-done.10, bf16[3,192,384]{2,1,0:T(8,128)(2,1)S(1)} %maximum_select_fusion.1.refs_0_, bf16[3,192,384]{2,1,0:T(8,128)(2,1)} %collective-permute-done.3.refs_1_, bf16[3,192,384]{2,1,0:T(8,128)(2,1)} %collective-permute-done.4.refs_2_, ...), custom_call_target="tpu_custom_call" | custom-call | tf_op jit(solution)/shard_map/pallas_call | solution.py:139
  175.5 49.0 %all_to_all.10 = bf16[64,8,384]{2,1,0:T(8,128)(2,1)S(1)} all-to-all(bf16[64,8,384]{2,1,0:T(8,128)(2,1)S(1)} %collective-permute-done.23), channel_id=1, replica_groups=mesh['z'=16,'x'=4,'y'=4,'c'=2] {'z','x'}, dimensions={0} | all-to-all | bytes 786432 | tf_op jit(solution)/shard_map/all_to_all | solution.py:207
  (51 shorter events, 17.3 us)
Async XLA Ops:
  0.0 7.0 %collective-permute-start.1 = (bf16[3,48,384]{2,1,0:T(8,128)(2,1)}, bf16[3,48,384]{2,1,0:T(8,128)(2,1)S(1)}, u32[]{:S(2)}, u32[]{:S(2)}) collective-permute-start(bf16[3,48,384]{2,1,0:T(8,128)(2,1)} %bitcast.14), channel_id=1, source_target_pairs={{0,8},{1,16},{2,10},{3,18},{4,12},{5,20},{6,14},{7,22},{8,0},{9,24... | collective-permute-start | bytes 331784 | tf_op jit(solution)/shard_map/ppermute | solution.py:30
  3.4 3.6 %collective-permute-start = (bf16[3,48,384]{2,1,0:T(8,128)(2,1)}, bf16[3,48,384]{2,1,0:T(8,128)(2,1)S(1)}, u32[]{:S(2)}, u32[]{:S(2)}) collective-permute-start(bf16[3,48,384]{2,1,0:T(8,128)(2,1)} %bitcast.15), channel_id=1, source_target_pairs={{0,0},{1,24},{2,2},{3,26},{4,4},{5,28},{6,6},{7,30},{8,8},{9,16},{... | collective-permute-start | bytes 331784 | tf_op jit(solution)/shard_map/ppermute | solution.py:30
  7.1 147.8 %copy-start.10 = (s32[8,8]{1,0:T(8,128)S(1)}, s32[8,8]{1,0:T(8,128)}, u32[]{:S(2)}) copy-start(s32[8,8]{1,0:T(8,128)} %mask.1) | copy-start | bytes 772
  7.1 8.5 %collective-permute-start.2 = (bf16[3,96,384]{2,1,0:T(8,128)(2,1)S(1)}, bf16[3,96,384]{2,1,0:T(8,128)(2,1)S(1)}, u32[]{:S(2)}, u32[]{:S(2)}) collective-permute-start(bf16[3,96,384]{2,1,0:T(8,128)(2,1)S(1)} %maximum_select_fusion.2), channel_id=1, source_target_pairs={{0,1},{1,0},{2,3},{3,2},{4,5},{5,4},{6,7},{7,6},{8,9},{9,8},{10,11... | collective-permute-start | bytes 663560 | tf_op jit(solution)/shard_map/ppermute | solution.py:30
  15.8 17.8 %collective-permute-start.3 = (bf16[3,192,384]{2,1,0:T(8,128)(2,1)S(1)}, bf16[3,192,384]{2,1,0:T(8,128)(2,1)}, u32[]{:S(2)}, u32[]{:S(2)}) collective-permute-start(bf16[3,192,384]{2,1,0:T(8,128)(2,1)S(1)} %maximum_select_fusion.1.refs_0_), channel_id=1, source_target_pairs={{0,32},{1,481},{2,34},{3,483},{4,36},{5,485},{6,38},{7,487},{8,40}... | collective-permute-start | bytes 1327112 | tf_op jit(solution)/shard_map/ppermute | solution.py:30
  33.5 13.5 %collective-permute-start.4 = (bf16[3,192,384]{2,1,0:T(8,128)(2,1)}, bf16[3,192,384]{2,1,0:T(8,128)(2,1)}, u32[]{:S(2)}, u32[]{:S(2)}) collective-permute-start(bf16[3,192,384]{2,1,0:T(8,128)(2,1)} %collective-permute-done.3.refs_1_), channel_id=1, source_target_pairs={{0,32},{1,481},{2,34},{3,483},{4,36},{5,485},{6,38},{7,487},{8,40}... | collective-permute-start | bytes 1327112 | tf_op jit(solution)/shard_map/ppermute | solution.py:30
  36.4 60.1 %all-to-all-start = ((bf16[64,8,384]{2,1,0:T(8,128)(2,1)}), bf16[64,8,384]{2,1,0:T(8,128)(2,1)S(1)}, u32[]{:S(2)}, u32[]{:S(2)}) async-start(bf16[64,8,384]{2,1,0:T(8,128)(2,1)} %bitcast.5), calls=%async_computation | async-start | bytes 786432 | tf_op jit(solution)/shard_map/all_to_all | solution.py:183
  47.1 23.2 %collective-permute-start.5 = (bf16[3,192,384]{2,1,0:T(8,128)(2,1)}, bf16[3,192,384]{2,1,0:T(8,128)(2,1)S(1)}, u32[]{:S(2)}, u32[]{:S(2)}) collective-permute-start(bf16[3,192,384]{2,1,0:T(8,128)(2,1)} %collective-permute-done.4.refs_2_), channel_id=1, source_target_pairs={{0,32},{1,481},{2,34},{3,483},{4,36},{5,485},{6,38},{7,487},{8,40}... | collective-permute-start | bytes 1327112 | tf_op jit(solution)/shard_map/ppermute | solution.py:30
  71.0 11.4 %collective-permute-start.6 = (bf16[3,192,384]{2,1,0:T(8,128)(2,1)S(1)}, bf16[3,192,384]{2,1,0:T(8,128)(2,1)S(1)}, u32[]{:S(2)}, u32[]{:S(2)}) collective-permute-start(bf16[3,192,384]{2,1,0:T(8,128)(2,1)S(1)} %collective-permute-done.5.refs_3_), channel_id=1, source_target_pairs={{0,32},{1,481},{2,34},{3,483},{4,36},{5,485},{6,38},{7,487},{8,40}... | collective-permute-start | bytes 1327112 | tf_op jit(solution)/shard_map/ppermute | solution.py:30
  83.2 11.4 %collective-permute-start.7 = (bf16[3,192,384]{2,1,0:T(8,128)(2,1)S(1)}, bf16[3,192,384]{2,1,0:T(8,128)(2,1)S(1)}, u32[]{:S(2)}, u32[]{:S(2)}) collective-permute-start(bf16[3,192,384]{2,1,0:T(8,128)(2,1)S(1)} %collective-permute-done.6.refs_4_), channel_id=1, source_target_pairs={{0,32},{1,481},{2,34},{3,483},{4,36},{5,485},{6,38},{7,487},{8,40}... | collective-permute-start | bytes 1327112 | tf_op jit(solution)/shard_map/ppermute | solution.py:30
  94.6 10.8 %copy-start.4 = (bf16[3,192,384]{2,1,0:T(8,128)(2,1)}, bf16[3,192,384]{2,1,0:T(8,128)(2,1)S(1)}, u32[]{:S(2)}) copy-start(bf16[3,192,384]{2,1,0:T(8,128)(2,1)S(1)} %collective-permute-done.7.refs_5_) | copy-start | bytes 1327108
  94.6 11.5 %collective-permute-start.8 = (bf16[3,192,384]{2,1,0:T(8,128)(2,1)S(1)}, bf16[3,192,384]{2,1,0:T(8,128)(2,1)}, u32[]{:S(2)}, u32[]{:S(2)}) collective-permute-start(bf16[3,192,384]{2,1,0:T(8,128)(2,1)S(1)} %collective-permute-done.7.refs_5_), channel_id=1, source_target_pairs={{0,32},{1,481},{2,34},{3,483},{4,36},{5,485},{6,38},{7,487},{8,40}... | collective-permute-start | bytes 1327112 | tf_op jit(solution)/shard_map/ppermute | solution.py:30
  96.5 11.9 %collective-permute-start.19 = (bf16[1,512,384]{2,1,0:T(8,128)(2,1)S(1)}, bf16[1,512,384]{2,1,0:T(8,128)(2,1)S(1)}, u32[]{:S(2)}, u32[]{:S(2)}) collective-permute-start(bf16[1,512,384]{2,1,0:T(8,128)(2,1)S(1)} %bitcast.11), channel_id=1, source_target_pairs={{0,24},{1,25},{2,26},{3,27},{4,28},{5,29},{6,30},{7,31},{8,16},{9,... | collective-permute-start | bytes 1179656 | tf_op jit(solution)/shard_map/ppermute | solution.py:30
  101.0 13.7 %collective-permute-start.11 = (bf16[3,192,384]{2,1,0:T(8,128)(2,1)}, bf16[3,192,384]{2,1,0:T(8,128)(2,1)S(1)}, u32[]{:S(2)}, u32[]{:S(2)}) collective-permute-start(bf16[3,192,384]{2,1,0:T(8,128)(2,1)} %collective-permute-done.3.refs_1_), channel_id=1, source_target_pairs={{0,1},{1,0},{2,3},{3,2},{4,5},{5,4},{6,7},{7,6},{8,9},{9,8},{10,11... | collective-permute-start | bytes 1327112 | tf_op jit(solution)/shard_map/ppermute | solution.py:30
  102.9 16.0 %collective-permute-start.12 = (bf16[3,192,384]{2,1,0:T(8,128)(2,1)}, bf16[3,192,384]{2,1,0:T(8,128)(2,1)S(1)}, u32[]{:S(2)}, u32[]{:S(2)}) collective-permute-start(bf16[3,192,384]{2,1,0:T(8,128)(2,1)} %collective-permute-done.4.refs_2_), channel_id=1, source_target_pairs={{0,1},{1,0},{2,3},{3,2},{4,5},{5,4},{6,7},{7,6},{8,9},{9,8},{10,11... | collective-permute-start | bytes 1327112 | tf_op jit(solution)/shard_map/ppermute | solution.py:30
  106.1 15.5 %collective-permute-start.9 = (bf16[3,192,384]{2,1,0:T(8,128)(2,1)}, bf16[3,192,384]{2,1,0:T(8,128)(2,1)S(1)}, u32[]{:S(2)}, u32[]{:S(2)}) collective-permute-start(bf16[3,192,384]{2,1,0:T(8,128)(2,1)} %collective-permute-done.8.refs_6_), channel_id=1, source_target_pairs={{0,32},{1,481},{2,34},{3,483},{4,36},{5,485},{6,38},{7,487},{8,40}... | collective-permute-start | bytes 1327112 | tf_op jit(solution)/shard_map/ppermute | solution.py:30
  108.5 23.1 %collective-permute-start.22 = (bf16[2,512,384]{2,1,0:T(8,128)(2,1)S(1)}, bf16[2,512,384]{2,1,0:T(8,128)(2,1)S(1)}, u32[]{:S(2)}, u32[]{:S(2)}) collective-permute-start(bf16[2,512,384]{2,1,0:T(8,128)(2,1)S(1)} %maximum_select_fusion.refs_17_), channel_id=1, source_target_pairs={{0,4},{1,5},{2,6},{3,7},{4,0},{5,1},{6,2},{7,3},{8,12},{9,13},{10,... | collective-permute-start | bytes 2359304 | tf_op jit(solution)/shard_map/ppermute | solution.py:30
  112.8 35.8 %collective-permute-start.21 = (bf16[2,512,384]{2,1,0:T(8,128)(2,1)S(1)}, bf16[2,512,384]{2,1,0:T(8,128)(2,1)S(1)}, u32[]{:S(2)}, u32[]{:S(2)}) collective-permute-start(bf16[2,512,384]{2,1,0:T(8,128)(2,1)S(1)} %maximum_select_fusion.refs_17_), channel_id=1, source_target_pairs={{0,2},{1,3},{2,4},{3,5},{4,6},{5,7},{6,0},{7,1},{8,10},{9,11},{10,... | collective-permute-start | bytes 2359304 | tf_op jit(solution)/shard_map/ppermute | solution.py:30
  115.5 9.8 %collective-permute-start.13 = (bf16[3,192,384]{2,1,0:T(8,128)(2,1)}, bf16[3,192,384]{2,1,0:T(8,128)(2,1)}, u32[]{:S(2)}, u32[]{:S(2)}) collective-permute-start(bf16[3,192,384]{2,1,0:T(8,128)(2,1)} %copy-done), channel_id=1, source_target_pairs={{0,1},{1,0},{2,3},{3,2},{4,5},{5,4},{6,7},{7,6},{8,9},{9,8},{10,11... | collective-permute-start | bytes 1327112 | tf_op jit(solution)/shard_map/ppermute | solution.py:30
  119.7 7.8 %collective-permute-start.14 = (bf16[3,192,384]{2,1,0:T(8,128)(2,1)}, bf16[3,192,384]{2,1,0:T(8,128)(2,1)}, u32[]{:S(2)}, u32[]{:S(2)}) collective-permute-start(bf16[3,192,384]{2,1,0:T(8,128)(2,1)} %copy-done.2), channel_id=1, source_target_pairs={{0,1},{1,0},{2,3},{3,2},{4,5},{5,4},{6,7},{7,6},{8,9},{9,8},{10,11... | collective-permute-start | bytes 1327112 | tf_op jit(solution)/shard_map/ppermute | solution.py:30
  121.6 31.7 %collective-permute-start.20 = (bf16[2,512,384]{2,1,0:T(8,128)(2,1)S(1)}, bf16[2,512,384]{2,1,0:T(8,128)(2,1)}, u32[]{:S(2)}, u32[]{:S(2)}) collective-permute-start(bf16[2,512,384]{2,1,0:T(8,128)(2,1)S(1)} %maximum_select_fusion.refs_17_), channel_id=1, source_target_pairs={{0,6},{1,7},{2,0},{3,1},{4,2},{5,3},{6,4},{7,5},{8,14},{9,15},{10,... | collective-permute-start | bytes 2359304 | tf_op jit(solution)/shard_map/ppermute | solution.py:30
  125.3 28.0 %collective-permute-start.15 = (bf16[3,192,384]{2,1,0:T(8,128)(2,1)}, bf16[3,192,384]{2,1,0:T(8,128)(2,1)}, u32[]{:S(2)}, u32[]{:S(2)}) collective-permute-start(bf16[3,192,384]{2,1,0:T(8,128)(2,1)} %copy-done.4), channel_id=1, source_target_pairs={{0,1},{1,0},{2,3},{3,2},{4,5},{5,4},{6,7},{7,6},{8,9},{9,8},{10,11... | collective-permute-start | bytes 1327112 | tf_op jit(solution)/shard_map/ppermute | solution.py:30
  127.5 25.9 %collective-permute-start.16 = (bf16[3,192,384]{2,1,0:T(8,128)(2,1)}, bf16[3,192,384]{2,1,0:T(8,128)(2,1)}, u32[]{:S(2)}, u32[]{:S(2)}) collective-permute-start(bf16[3,192,384]{2,1,0:T(8,128)(2,1)} %collective-permute-done.8.refs_6_), channel_id=1, source_target_pairs={{0,1},{1,0},{2,3},{3,2},{4,5},{5,4},{6,7},{7,6},{8,9},{9,8},{10,11... | collective-permute-start | bytes 1327112 | tf_op jit(solution)/shard_map/ppermute | solution.py:30
  131.6 19.7 %collective-permute-start.10 = (bf16[3,96,384]{2,1,0:T(8,128)(2,1)S(1)}, bf16[3,96,384]{2,1,0:T(8,128)(2,1)S(1)}, u32[]{:S(2)}, u32[]{:S(2)}) collective-permute-start(bf16[3,96,384]{2,1,0:T(8,128)(2,1)S(1)} %constant_dynamic-slice_fusion.2), channel_id=1, source_target_pairs={{0,32},{1,481},{2,34},{3,483},{4,36},{5,485},{6,38},{7,487},{8,40}... | collective-permute-start | bytes 663560 | tf_op jit(solution)/shard_map/ppermute | solution.py:30
  148.5 6.3 %collective-permute-start.17 = (bf16[3,192,384]{2,1,0:T(8,128)(2,1)S(1)}, bf16[3,192,384]{2,1,0:T(8,128)(2,1)}, u32[]{:S(2)}, u32[]{:S(2)}) collective-permute-start(bf16[3,192,384]{2,1,0:T(8,128)(2,1)S(1)} %collective-permute-done.9.refs_7_), channel_id=1, source_target_pairs={{0,1},{1,0},{2,3},{3,2},{4,5},{5,4},{6,7},{7,6},{8,9},{9,8},{10,11... | collective-permute-start | bytes 1327112 | tf_op jit(solution)/shard_map/ppermute | solution.py:30
  151.3 3.5 %collective-permute-start.18 = (bf16[3,96,384]{2,1,0:T(8,128)(2,1)S(1)}, bf16[3,96,384]{2,1,0:T(8,128)(2,1)}, u32[]{:S(2)}, u32[]{:S(2)}) collective-permute-start(bf16[3,96,384]{2,1,0:T(8,128)(2,1)S(1)} %collective-permute-done.10.refs_8_), channel_id=1, source_target_pairs={{0,1},{1,0},{2,3},{3,2},{4,5},{5,4},{6,7},{7,6},{8,9},{9,8},{10,11... | collective-permute-start | bytes 663560 | tf_op jit(solution)/shard_map/ppermute | solution.py:30
  154.9 1.0 copy-start.1
  155.9 1.0 copy-start.3
  156.9 1.0 copy-start.5
  157.9 1.0 copy-start.7
  158.9 1.0 copy-start.9
  174.8 0.7 collective-permute-start.23
  (4 other events, 3.1 us)

commit v2 on v1

--- a/solution.py
+++ b/solution.py
@@ -14,7 +14,6 @@
 NZ, NX, NY, NC = 16, 4, 4, 2
 AXES = ("z", "x", "y", "c")
 SLICE = D // (NZ * NX)
-ROWS = NX * SLICE
 TOKENS = FRAMES * 8
 
 
@@ -34,26 +33,50 @@
     return (z, x, y, c) if c == x // 2 else (z, 3 - x, y, 1 - c)
 
 
-def second(z, x, y, c):
-    near = x ^ 1
-    return (z, near if x // 2 == c else 3 - near, y, x // 2)
-
-
 def swap(z, x, y, c):
     return (z, x, y, 1 - c)
 
 
+def pair(z, x, y, c):
+    return (z, x ^ 1, y, c)
+
+
 def ring(z, x, y, c):
     return (z + (1 if c == 0 else -1), x, y, c)
 
 
+def one(t, near):
+    return [(t, near, None)]
+
+
+def two(t, near):
+    return [(t, near, 0), (t, near, 1)]
+
+
+def sent(near):
+    return [
+        one(0, near) + two(1, near) + two(2, near),
+        two(3, near) + two(4, near),
+        two(5, near) + two(6, near),
+        two(7, near) + one(8, near),
+    ]
+
+
+def listing():
+    s, r = sent(False), sent(True)
+    own = [two(0, False)] + s + r
+    swapped = [s[0] + r[0] + s[1], r[1] + s[2], r[2] + s[3], r[3]]
+    return [(e, False) for e in own] + [(e, True) for e in swapped]
+
+
 def attend_kernel(place, mask, *refs):
-    own, mine, theirs = refs[0], refs[1:9], refs[9:17]
-    pieces = refs[17:21]
-    out = refs[21]
-    weights, tokens, qkv, bias, w_sems, x_sems = refs[22:]
-    z, y, c = place[0], place[1], place[2]
-    sign = 1 - 2 * c
+    blocks = listing()
+    count = len(blocks)
+    pieces = refs[count : count + 4]
+    out = refs[count + 4]
+    weights, tokens, qkv, bias, w_sems, x_sems = refs[count + 5 :]
+    z, x, y, c = place[0], place[1], place[2], place[3]
+    low = jnp.minimum(x, 3 - x)
 
     copies = []
     for i, (piece, shift) in enumerate(zip(pieces, (0, 1, 3, 2))):
@@ -63,30 +86,27 @@
             copies.append(
                 pltpu.make_async_copy(piece.at[half], tokens.at[:, pl.ds(at, GROUP)], x_sems.at[2 * i + half])
             )
-    by_part = []
-    for j in range(3):
-        part = []
-
-        def add(ref, row):
-            rows = ref.shape[1]
-            at = pl.multiple_of(row, 32)
-            part.append(
-                pltpu.make_async_copy(ref.at[j], weights.at[j, pl.ds(at, rows)], w_sems.at[j, len(part)])
-            )
-
-        add(own, z * ROWS)
-        for t in range(1, 8):
-            add(mine[t - 1], lax.rem(z - sign * t + NZ, NZ) * ROWS)
-            add(theirs[t - 1], lax.rem(z + sign * t + NZ, NZ) * ROWS)
-        far = lax.rem(z + 8, NZ) * ROWS
-        add(mine[7], far + c * (ROWS // 2))
-        add(theirs[7], far + (1 - c) * (ROWS // 2))
-        by_part.append(part)
+    done = set()
+    for ref, (entries, swapped) in zip(refs[:count], blocks):
+        owner = 1 - c if swapped else c
+        sign = 1 - 2 * owner
+        for k, (t, near, slot) in enumerate(entries):
+            if t == 0 and not near and slot is None:
+                continue
+            key = (t, near, slot, swapped)
+            assert key not in done
+            done.add(key)
+            from_z = lax.rem(z - sign * t + NZ, NZ)
+            first = 1 - low if near else low
+            high = owner if slot is None else slot
+            from_x = first + high * (3 - 2 * first)
+            row = pl.multiple_of((from_z * NX + from_x) * SLICE, SLICE)
+            copies.append(
+                pltpu.make_async_copy(ref.at[k], weights.at[:, pl.ds(row, SLICE)], w_sems.at[len(done) - 1])
+            )
+    assert len(done) == NZ * NX
     for copy in copies:
         copy.start()
-    for part in by_part:
-        for copy in part:
-            copy.start()
 
     span_rows = TOKENS // SPANS
     column = lax.broadcasted_iota(jnp.int32, (1, TOKENS), 1)
@@ -103,8 +123,6 @@
     for copy in copies:
         copy.wait()
     for j in range(3):
-        for copy in by_part[j]:
-            copy.wait()
         for r in range(2):
             rows = pl.ds(r * (TOKENS // 2), TOKENS // 2)
             qkv[j, rows, :] = jnp.dot(
@@ -134,8 +152,8 @@
             out[rows, lanes] = (summed / total).astype(jnp.bfloat16)
 
 
-def project_and_attend(place, span_mask, own, mine, theirs, pieces):
-    arrays = [own, *mine, *theirs, *pieces]
+def project_and_attend(place, span_mask, blocks, pieces):
+    arrays = [*blocks, *pieces]
     return pl.pallas_call(
         attend_kernel,
         out_shape=jax.ShapeDtypeStruct((TOKENS, GROUP), jnp.bfloat16),
@@ -147,32 +165,21 @@
             pltpu.VMEM((TOKENS, D), jnp.bfloat16),
             pltpu.VMEM((3, TOKENS, GROUP), jnp.bfloat16),
             pltpu.VMEM((TOKENS, TOKENS), jnp.float32),
-            pltpu.SemaphoreType.DMA((3, 17)),
+            pltpu.SemaphoreType.DMA((NZ * NX,)),
             pltpu.SemaphoreType.DMA((8,)),
         ],
-        compiler_params=pltpu.CompilerParams(vmem_limit_bytes=40 * 1024 * 1024),
+        compiler_params=pltpu.CompilerParams(vmem_limit_bytes=20 * 1024 * 1024),
     )(place, span_mask, *arrays)
+
+
+def join(*arrays):
+    return jnp.concatenate(arrays, axis=0)
 
 
 def per_device(frames_in, qkv_weight, span_mask):
     z, x, y, c = (lax.axis_index(name) for name in AXES)
     group = x // 2
-
-    piece = jnp.transpose(qkv_weight, (1, 0, 2))
-    first = permute(piece, home)
-    other = permute(piece, second)
-    slot = jnp.where(c == group, x, 3 - x)
-    half = jnp.where(
-        slot % 2 == 0,
-        jnp.concatenate([first, other], axis=1),
-        jnp.concatenate([other, first], axis=1),
-    )
-    half_other = permute(half, swap)
-    own = jnp.where(
-        c == 0,
-        jnp.concatenate([half, half_other], axis=1),
-        jnp.concatenate([half_other, half], axis=1),
-    )
+    hold = lax.optimization_barrier
 
     places = frames_in.reshape(NZ, NX, 8, D)
     places = lax.dynamic_slice(places, (0, 2 * c, 0, 2 * GROUP * y), (NZ, 2, 8, 2 * GROUP))
@@ -180,29 +187,60 @@
     low = jnp.where(c == 0, low, low[:, ::-1])
     high = jnp.where(c == 0, high[:, ::-1], high)
     packed = jnp.concatenate([low, high], axis=1).reshape(NZ * NX, 8, GROUP)
+    piece = jnp.transpose(qkv_weight, (1, 0, 2))[None]
+    packed, piece = hold((packed, piece))
     spread = lax.all_to_all(packed, ("z", "x"), split_axis=0, concat_axis=0, tiled=True)
+
+    first = permute(piece, home)
+    first_other = permute(first, swap)
+    own = jnp.where(c == 0, join(first, first_other), join(first_other, first))
+
+    steps = [None]
+    block = own
+    batches, returned = [], []
+
+    def step():
+        nonlocal block
+        if len(steps) == 8:
+            block = lax.dynamic_slice(block, (c, 0, 0, 0), (1, 3, SLICE, GROUP))
+        block = permute(block, ring)
+        steps.append(block)
+
+    def send(*parts):
+        batch = join(*parts)
+        batches.append(batch)
+        returned.append(permute(batch, pair))
+
+    step()
+    step()
+    block, spread = hold((block, spread))
     spread = spread.reshape(1, TOKENS, GROUP)
     partner = permute(spread, lambda z, x, y, c: (z, 3 - x, y, c))
-    both = jnp.where(
-        group == 0,
-        jnp.concatenate([spread, partner], axis=0),
-        jnp.concatenate([partner, spread], axis=0),
-    )
+    step()
+    send(first, steps[1], steps[2])
+    block, partner = hold((block, partner))
+    both = jnp.where(group == 0, join(spread, partner), join(partner, spread))
     pieces = [both] + [
         permute(both, lambda z, x, y, c, k=k: (z, x, y + k, c)) for k in (-1, 1, 2)
     ]
-
-    mine, theirs = [], []
-    block = own
-    for t in range(1, 9):
-        if t == 8:
-            block = lax.dynamic_slice(block, (0, c * (ROWS // 2), 0), (3, ROWS // 2, GROUP))
-        block = permute(block, ring)
-        mine.append(block)
-        theirs.append(permute(block, swap))
-
-    place = jnp.stack([z, y, c]).astype(jnp.int32)
-    output = project_and_attend(place, span_mask, own, mine, theirs, pieces)
+    step()
+    step()
+    send(steps[3], steps[4])
+    step()
+    step()
+    send(steps[5], steps[6])
+    step()
+    send(steps[7], steps[8])
+    swapped = [
+        join(batches[0], returned[0], batches[1]),
+        join(returned[1], batches[2]),
+        join(returned[2], batches[3]),
+        returned[3],
+    ]
+    swapped = [permute(array, swap) for array in swapped]
+
+    place = jnp.stack([z, x, y, c]).astype(jnp.int32)
+    output = project_and_attend(place, span_mask, [own, *batches, *returned, *swapped], pieces)
     output = permute(output.reshape(FRAMES, 8, GROUP), home)
     output = lax.all_to_all(output, ("z", "x"), split_axis=0, concat_axis=0, tiled=True)
     return output.reshape(1, NZ * NX * 8, GROUP)

time: 226 us -> 207 us (0.916)
  waiting for transfers between devices: 73.5 us -> 47.2 us
  starting transfers between devices: 76.1 us -> 81.2 us
  other arithmetic: 1.36 us -> 5.29 us
    ppermute x24 -> x23, waiting for transfers between devices: 73.5 us -> 47.2 us  [permute(): return lax.ppermute(array, AXES, pairs)]
    all_to_all x1, starting transfers between devices: 10.7 us -> 18.6 us  [per_device(): lax.all_to_all(packed, ('z', 'x'), split_axis=0, concat_axis=0, tiled=True)]
    concatenate x0 -> x2, other arithmetic: none -> 4.11 us  [join(): return jnp.concatenate(arrays, axis=0)]
    ppermute x24 -> x23, starting transfers between devices: 65.5 us -> 62.7 us  [permute(): return lax.ppermute(array, AXES, pairs)]
    unnamed x23 -> x24, local copies, waits for them, and re-layouts: 8.88 us -> 8.11 us
  transfers between devices with their start and end apart: 25 -> 24, of which waited for: 11 -> 10; matrix products, arithmetic and copies ran while one was open for 1% -> 5% of each run, Pallas kernels for 0% -> 0%
where the time goes in v2:
time: 207 us; the launch traced here: 206 us
  starting transfers between devices  81.2 us (39%)
  blocking collectives  47.9 us (23%)
  waiting for transfers between devices  47.2 us (23%)
  Pallas kernels  12.9 us (6%)
  local copies, waits for them, and re-layouts  11 us (5%)
  other arithmetic  5.29 us (3%)
    ppermute x23, starting transfers between devices, permute(): return lax.ppermute(array, AXES, pairs)  62.7 us
    all_to_all x1, blocking collectives, per_device(): lax.all_to_all(output, ('z', 'x'), split_axis=0, concat_axis=0, tiled=True)  47.9 us
    ppermute x23, waiting for transfers between devices, permute(): return lax.ppermute(array, AXES, pairs)  47.2 us
    all_to_all x1, starting transfers between devices, per_device(): lax.all_to_all(packed, ('z', 'x'), split_axis=0, concat_axis=0, tiled=True)  18.6 us
    pallas_call x1, Pallas kernels, project_and_attend(): pl.pallas_call(attend_kernel, out_shape=jax.ShapeDtypeStruct((TOKENS, GRO...  12.9 us
    unnamed x24, local copies, waits for them, and re-layouts  8.11 us
  transfers between devices with their start and end apart: 24, of which 10 were waited for; matrix products, arithmetic and copies ran while one was open for 5% of the time, Pallas kernels for 0%

profile of v2, /device:TPU:8, one launch (start us, length us, event | category | flops | bytes accessed | tf_op | source)
XLA Modules:
  0.0 206.0 jit_solution(6760933869594595875)
XLA Ops:
  2.0 18.6 %all-to-all-start = ((bf16[64,8,384]{2,1,0:T(8,128)(2,1)}), bf16[64,8,384]{2,1,0:T(8,128)(2,1)S(1)}, u32[]{:S(2)}, u32[]{:S(2)}) async-start(bf16[64,8,384]{2,1,0:T(8,128)(2,1)} %bitcast.5), calls=%async_computation | async-start | bytes 786432 | tf_op jit(solution)/shard_map/all_to_all | solution.py:192
  21.3 8.9 %collective-permute-start.1 = (bf16[1,3,48,384]{3,2,1,0:T(8,128)(2,1)S(1)}, bf16[1,3,48,384]{3,2,1,0:T(8,128)(2,1)S(1)}, u32[]{:S(2)}, u32[]{:S(2)}) collective-permute-start(bf16[1,3,48,384]{3,2,1,0:T(8,128)(2,1)S(1)} %collective-permute-done), channel_id=1, source_target_pairs={{0,1},{1,0},{2,3},{3,2},{4,5},{5,4},{6,7},{7,6},{8,9},{9,8},{10,11... | collective-permute-start | bytes 331784 | tf_op jit(solution)/shard_map/ppermute | solution.py:29
  31.2 3.5 %collective-permute-start.2 = (bf16[2,3,48,384]{3,2,1,0:T(8,128)(2,1)S(1)}, bf16[2,3,48,384]{3,2,1,0:T(8,128)(2,1)S(1)}, u32[]{:S(2)}, u32[]{:S(2)}) collective-permute-start(bf16[2,3,48,384]{3,2,1,0:T(8,128)(2,1)S(1)} %maximum_select_fusion.1.refs_0_), channel_id=1, source_target_pairs={{0,32},{1,481},{2,34},{3,483},{4,36},{5,485},{6,38},{7,487},{8,40}... | collective-permute-start | bytes 663560 | tf_op jit(solution)/shard_map/ppermute | solution.py:29
  34.7 7.8 %collective-permute-done.2 = bf16[2,3,48,384]{3,2,1,0:T(8,128)(2,1)S(1)} collective-permute-done((bf16[2,3,48,384]{3,2,1,0:T(8,128)(2,1)S(1)}, bf16[2,3,48,384]{3,2,1,0:T(8,128)(2,1)S(1)}, u32[]{:S(2)}, u32[]{:S(2)}) %collective-permute-start.2) | collective-permute-done | bytes 221216 | tf_op jit(solution)/shard_map/ppermute | solution.py:29
  42.5 2.6 %collective-permute-start.3 = (bf16[2,3,48,384]{3,2,1,0:T(8,128)(2,1)S(1)}, bf16[2,3,48,384]{3,2,1,0:T(8,128)(2,1)S(1)}, u32[]{:S(2)}, u32[]{:S(2)}) collective-permute-start(bf16[2,3,48,384]{3,2,1,0:T(8,128)(2,1)S(1)} %collective-permute-done.2), channel_id=1, source_target_pairs={{0,32},{1,481},{2,34},{3,483},{4,36},{5,485},{6,38},{7,487},{8,40}... | collective-permute-start | bytes 663560 | tf_op jit(solution)/shard_map/ppermute | solution.py:29
  46.4 5.1 %collective-permute-done.3 = bf16[2,3,48,384]{3,2,1,0:T(8,128)(2,1)S(1)} collective-permute-done((bf16[2,3,48,384]{3,2,1,0:T(8,128)(2,1)S(1)}, bf16[2,3,48,384]{3,2,1,0:T(8,128)(2,1)S(1)}, u32[]{:S(2)}, u32[]{:S(2)}) %collective-permute-start.3) | collective-permute-done | bytes 221216 | tf_op jit(solution)/shard_map/ppermute | solution.py:29
  52.2 3.2 %collective-permute-start.11 = (bf16[5,3,48,384]{3,2,1,0:T(8,128)(2,1)S(1)}, bf16[5,3,48,384]{3,2,1,0:T(8,128)(2,1)S(1)}, u32[]{:S(2)}, u32[]{:S(2)}) collective-permute-start(bf16[5,3,48,384]{3,2,1,0:T(8,128)(2,1)S(1)} %get-tuple-element.24.refs_1_), channel_id=1, source_target_pairs={{0,8},{1,9},{2,10},{3,11},{4,12},{5,13},{6,14},{7,15},{8,0},{9,1},... | collective-permute-start | bytes 1658888 | tf_op jit(solution)/shard_map/ppermute | solution.py:29
  55.4 4.0 %collective-permute-start.5 = (bf16[1,512,384]{2,1,0:T(8,128)(2,1)S(1)}, bf16[1,512,384]{2,1,0:T(8,128)(2,1)S(1)}, u32[]{:S(2)}, u32[]{:S(2)}) collective-permute-start(bf16[1,512,384]{2,1,0:T(8,128)(2,1)S(1)} %bitcast.14), channel_id=1, source_target_pairs={{0,24},{1,25},{2,26},{3,27},{4,28},{5,29},{6,30},{7,31},{8,16},{9,... | collective-permute-start | bytes 1179656 | tf_op jit(solution)/shard_map/ppermute | solution.py:29
  59.5 1.9 collective-permute-start.4
  61.4 7.1 %collective-permute-done.4 = bf16[2,3,48,384]{3,2,1,0:T(8,128)(2,1)S(1)} collective-permute-done((bf16[2,3,48,384]{3,2,1,0:T(8,128)(2,1)S(1)}, bf16[2,3,48,384]{3,2,1,0:T(8,128)(2,1)S(1)}, u32[]{:S(2)}, u32[]{:S(2)}) %collective-permute-start.4) | collective-permute-done | bytes 221216 | tf_op jit(solution)/shard_map/ppermute | solution.py:29
  68.5 1.9 collective-permute-start.6
  71.3 6.2 %collective-permute-done.6 = bf16[2,3,48,384]{3,2,1,0:T(8,128)(2,1)S(1)} collective-permute-done((bf16[2,3,48,384]{3,2,1,0:T(8,128)(2,1)S(1)}, bf16[2,3,48,384]{3,2,1,0:T(8,128)(2,1)S(1)}, u32[]{:S(2)}, u32[]{:S(2)}) %collective-permute-start.6) | collective-permute-done | bytes 221216 | tf_op jit(solution)/shard_map/ppermute | solution.py:29
  80.9 2.3 %collective-permute-start.12 = (bf16[4,3,48,384]{3,2,1,0:T(8,128)(2,1)S(1)}, bf16[4,3,48,384]{3,2,1,0:T(8,128)(2,1)S(1)}, u32[]{:S(2)}, u32[]{:S(2)}) collective-permute-start(bf16[4,3,48,384]{3,2,1,0:T(8,128)(2,1)S(1)} %get-tuple-element.20.refs_2_), channel_id=1, source_target_pairs={{0,8},{1,9},{2,10},{3,11},{4,12},{5,13},{6,14},{7,15},{8,0},{9,1},... | collective-permute-start | bytes 1327112 | tf_op jit(solution)/shard_map/ppermute | solution.py:29
  83.3 3.3 %collective-permute-done.7 = bf16[2,3,48,384]{3,2,1,0:T(8,128)(2,1)S(1)} collective-permute-done((bf16[2,3,48,384]{3,2,1,0:T(8,128)(2,1)S(1)}, bf16[2,3,48,384]{3,2,1,0:T(8,128)(2,1)S(1)}, u32[]{:S(2)}, u32[]{:S(2)}) %collective-permute-start.7) | collective-permute-done | bytes 221216 | tf_op jit(solution)/shard_map/ppermute | solution.py:29
  86.6 1.9 collective-permute-start.8
  88.7 2.4 %collective-permute-start.19 = (bf16[2,512,384]{2,1,0:T(8,128)(2,1)S(1)}, bf16[2,512,384]{2,1,0:T(8,128)(2,1)}, u32[]{:S(2)}, u32[]{:S(2)}) collective-permute-start(bf16[2,512,384]{2,1,0:T(8,128)(2,1)S(1)} %maximum_select_fusion.refs_13_), channel_id=1, source_target_pairs={{0,6},{1,7},{2,0},{3,1},{4,2},{5,3},{6,4},{7,5},{8,14},{9,15},{10,... | collective-permute-start | bytes 2359304 | tf_op jit(solution)/shard_map/ppermute | solution.py:29
  91.0 3.5 %collective-permute-start.20 = (bf16[2,512,384]{2,1,0:T(8,128)(2,1)S(1)}, bf16[2,512,384]{2,1,0:T(8,128)(2,1)}, u32[]{:S(2)}, u32[]{:S(2)}) collective-permute-start(bf16[2,512,384]{2,1,0:T(8,128)(2,1)S(1)} %maximum_select_fusion.refs_13_), channel_id=1, source_target_pairs={{0,2},{1,3},{2,4},{3,5},{4,6},{5,7},{6,0},{7,1},{8,10},{9,11},{10,... | collective-permute-start | bytes 2359304 | tf_op jit(solution)/shard_map/ppermute | solution.py:29
  94.5 1.9 collective-permute-start.15
  96.5 1.9 collective-permute-start.9
  99.4 2.5 %collective-permute-start.13 = (bf16[4,3,48,384]{3,2,1,0:T(8,128)(2,1)S(1)}, bf16[4,3,48,384]{3,2,1,0:T(8,128)(2,1)S(1)}, u32[]{:S(2)}, u32[]{:S(2)}) collective-permute-start(bf16[4,3,48,384]{3,2,1,0:T(8,128)(2,1)S(1)} %constant_dynamic-update-slice_fusion.5.refs_3_), channel_id=1, source_target_pairs={{0,8},{1,9},{2,10},{3,11},{4,12},{5,13},{6,14},{7,15},{8,0},{9,1},... | collective-permute-start | bytes 1327112 | tf_op jit(solution)/shard_map/ppermute | solution.py:29
  101.9 2.1 %pad_maximum_fusion = bf16[8,3,48,384]{3,2,1,0:T(8,128)(2,1)} fusion(bf16[2,3,48,384]{3,2,1,0:T(8,128)(2,1)} %collective-permute-done.8, bf16[2,3,48,384]{3,2,1,0:T(8,128)(2,1)} %copy-done.6, bf16[4,3,48,384]{3,2,1,0:T(8,128)(2,1)S(1)} %collective-permute-done.12.refs_6_), kind=kLoop, calls=%fused_computation | loop fusion | flops 884736 | bytes 1769472 | tf_op jit(solution)/shard_map/concatenate | solution.py:176
  106.4 3.1 %collective-permute-start.10 = (bf16[1,3,48,384]{3,2,1,0:T(8,128)(2,1)S(1)}, bf16[1,3,48,384]{3,2,1,0:T(8,128)(2,1)S(1)}, u32[]{:S(2)}, u32[]{:S(2)}) collective-permute-start(bf16[1,3,48,384]{3,2,1,0:T(8,128)(2,1)S(1)} %constant_dynamic-slice_fusion.1), channel_id=1, source_target_pairs={{0,32},{1,481},{2,34},{3,483},{4,36},{5,485},{6,38},{7,487},{8,40}... | collective-permute-start | bytes 331784 | tf_op jit(solution)/shard_map/ppermute | solution.py:29
  110.5 3.8 %collective-permute-done.10 = bf16[1,3,48,384]{3,2,1,0:T(8,128)(2,1)S(1)} collective-permute-done((bf16[1,3,48,384]{3,2,1,0:T(8,128)(2,1)S(1)}, bf16[1,3,48,384]{3,2,1,0:T(8,128)(2,1)S(1)}, u32[]{:S(2)}, u32[]{:S(2)}) %collective-permute-start.10) | collective-permute-done | bytes 110624 | tf_op jit(solution)/shard_map/ppermute | solution.py:29
  114.3 5.4 %collective-permute-start.21 = (bf16[2,512,384]{2,1,0:T(8,128)(2,1)S(1)}, bf16[2,512,384]{2,1,0:T(8,128)(2,1)}, u32[]{:S(2)}, u32[]{:S(2)}) collective-permute-start(bf16[2,512,384]{2,1,0:T(8,128)(2,1)S(1)} %maximum_select_fusion.refs_13_), channel_id=1, source_target_pairs={{0,4},{1,5},{2,6},{3,7},{4,0},{5,1},{6,2},{7,3},{8,12},{9,13},{10,... | collective-permute-start | bytes 2359304 | tf_op jit(solution)/shard_map/ppermute | solution.py:29
  119.7 1.9 collective-permute-start.16
  121.6 2.0 pad_maximum_fusion.1
  123.6 2.4 %collective-permute-start.17 = (bf16[7,3,48,384]{3,2,1,0:T(8,128)(2,1)}, bf16[7,3,48,384]{3,2,1,0:T(8,128)(2,1)}, u32[]{:S(2)}, u32[]{:S(2)}) collective-permute-start(bf16[7,3,48,384]{3,2,1,0:T(8,128)(2,1)} %pad_maximum_fusion.1), channel_id=1, source_target_pairs={{0,1},{1,0},{2,3},{3,2},{4,5},{5,4},{6,7},{7,6},{8,9},{9,8},{10,11... | collective-permute-start | bytes 2322440 | tf_op jit(solution)/shard_map/ppermute | solution.py:29
  126.1 2.3 %collective-permute-start.14 = (bf16[3,3,48,384]{3,2,1,0:T(8,128)(2,1)S(1)}, bf16[3,3,48,384]{3,2,1,0:T(8,128)(2,1)}, u32[]{:S(2)}, u32[]{:S(2)}) collective-permute-start(bf16[3,3,48,384]{3,2,1,0:T(8,128)(2,1)S(1)} %constant_dynamic-update-slice_fusion.7.refs_4_), channel_id=1, source_target_pairs={{0,8},{1,9},{2,10},{3,11},{4,12},{5,13},{6,14},{7,15},{8,0},{9,1},... | collective-permute-start | bytes 995336 | tf_op jit(solution)/shard_map/ppermute | solution.py:29
  128.4 9.4 %collective-permute-done.14.refs_8_ = bf16[3,3,48,384]{3,2,1,0:T(8,128)(2,1)} collective-permute-done((bf16[3,3,48,384]{3,2,1,0:T(8,128)(2,1)S(1)}, bf16[3,3,48,384]{3,2,1,0:T(8,128)(2,1)}, u32[]{:S(2)}, u32[]{:S(2)}) %collective-permute-start.14) | collective-permute-done | bytes 331808 | tf_op jit(solution)/shard_map/ppermute | solution.py:29
  137.8 1.9 collective-permute-start.18
  143.6 12.9 %shard_map.37 = bf16[512,384]{1,0:T(8,128)(2,1)S(1)} custom-call(s32[4]{0:T(128)S(1)} %pad_add_fusion.place, s32[8,8]{1,0:T(8,128)S(1)} %copy-done.4, bf16[2,3,48,384]{3,2,1,0:T(8,128)(2,1)S(1)} %copy-done.1, bf16[5,3,48,384]{3,2,1,0:T(8,128)(2,1)S(1)} %copy-done.3, bf16[4,3,48,384]{3,2,1,0:T(8,128)(2,1)S(1)} %get-tuple-element.20.refs_2_, ...), custom_call_target="tpu_custom_call" | custom-call | tf_op jit(solution)/shard_map/pallas_call | solution.py:157
  157.3 47.9 %all_to_all.10 = bf16[64,8,384]{2,1,0:T(8,128)(2,1)S(1)} all-to-all(bf16[64,8,384]{2,1,0:T(8,128)(2,1)S(1)} %collective-permute-done.22), channel_id=1, replica_groups=mesh['z'=16,'x'=4,'y'=4,'c'=2] {'z','x'}, dimensions={0} | all-to-all | bytes 786432 | tf_op jit(solution)/shard_map/all_to_all | solution.py:245
  (54 shorter events, 20.0 us)
Async XLA Ops:
  0.0 20.6 %copy-start.7 = (bf16[48,3,384]{2,0,1:T(8,128)(2,1)S(1)}, bf16[48,3,384]{2,0,1:T(8,128)(2,1)}, u32[]{:S(2)}) copy-start(bf16[48,3,384]{2,0,1:T(8,128)(2,1)} %param.4) | copy-start | bytes 331780
  2.0 53.4 %all-to-all-start = ((bf16[64,8,384]{2,1,0:T(8,128)(2,1)}), bf16[64,8,384]{2,1,0:T(8,128)(2,1)S(1)}, u32[]{:S(2)}, u32[]{:S(2)}) async-start(bf16[64,8,384]{2,1,0:T(8,128)(2,1)} %bitcast.5), calls=%async_computation | async-start | bytes 786432 | tf_op jit(solution)/shard_map/all_to_all | solution.py:192
  20.6 0.7 collective-permute-start
  21.3 9.9 %collective-permute-start.1 = (bf16[1,3,48,384]{3,2,1,0:T(8,128)(2,1)S(1)}, bf16[1,3,48,384]{3,2,1,0:T(8,128)(2,1)S(1)}, u32[]{:S(2)}, u32[]{:S(2)}) collective-permute-start(bf16[1,3,48,384]{3,2,1,0:T(8,128)(2,1)S(1)} %collective-permute-done), channel_id=1, source_target_pairs={{0,1},{1,0},{2,3},{3,2},{4,5},{5,4},{6,7},{7,6},{8,9},{9,8},{10,11... | collective-permute-start | bytes 331784 | tf_op jit(solution)/shard_map/ppermute | solution.py:29
  31.2 21.0 %copy-start = (bf16[2,3,48,384]{3,2,1,0:T(8,128)(2,1)}, bf16[2,3,48,384]{3,2,1,0:T(8,128)(2,1)S(1)}, u32[]{:S(2)}) copy-start(bf16[2,3,48,384]{3,2,1,0:T(8,128)(2,1)S(1)} %maximum_select_fusion.1.refs_0_) | copy-start | bytes 663556
  31.2 11.3 %collective-permute-start.2 = (bf16[2,3,48,384]{3,2,1,0:T(8,128)(2,1)S(1)}, bf16[2,3,48,384]{3,2,1,0:T(8,128)(2,1)S(1)}, u32[]{:S(2)}, u32[]{:S(2)}) collective-permute-start(bf16[2,3,48,384]{3,2,1,0:T(8,128)(2,1)S(1)} %maximum_select_fusion.1.refs_0_), channel_id=1, source_target_pairs={{0,32},{1,481},{2,34},{3,483},{4,36},{5,485},{6,38},{7,487},{8,40}... | collective-permute-start | bytes 663560 | tf_op jit(solution)/shard_map/ppermute | solution.py:29
  42.5 9.0 %collective-permute-start.3 = (bf16[2,3,48,384]{3,2,1,0:T(8,128)(2,1)S(1)}, bf16[2,3,48,384]{3,2,1,0:T(8,128)(2,1)S(1)}, u32[]{:S(2)}, u32[]{:S(2)}) collective-permute-start(bf16[2,3,48,384]{3,2,1,0:T(8,128)(2,1)S(1)} %collective-permute-done.2), channel_id=1, source_target_pairs={{0,32},{1,481},{2,34},{3,483},{4,36},{5,485},{6,38},{7,487},{8,40}... | collective-permute-start | bytes 663560 | tf_op jit(solution)/shard_map/ppermute | solution.py:29
  52.2 34.3 %copy-start.2 = (bf16[5,3,48,384]{3,2,1,0:T(8,128)(2,1)}, bf16[5,3,48,384]{3,2,1,0:T(8,128)(2,1)S(1)}, u32[]{:S(2)}) copy-start(bf16[5,3,48,384]{3,2,1,0:T(8,128)(2,1)S(1)} %get-tuple-element.24.refs_1_) | copy-start | bytes 1658884
  52.2 18.2 %collective-permute-start.11 = (bf16[5,3,48,384]{3,2,1,0:T(8,128)(2,1)S(1)}, bf16[5,3,48,384]{3,2,1,0:T(8,128)(2,1)S(1)}, u32[]{:S(2)}, u32[]{:S(2)}) collective-permute-start(bf16[5,3,48,384]{3,2,1,0:T(8,128)(2,1)S(1)} %get-tuple-element.24.refs_1_), channel_id=1, source_target_pairs={{0,8},{1,9},{2,10},{3,11},{4,12},{5,13},{6,14},{7,15},{8,0},{9,1},... | collective-permute-start | bytes 1658888 | tf_op jit(solution)/shard_map/ppermute | solution.py:29
  55.4 13.1 %collective-permute-start.5 = (bf16[1,512,384]{2,1,0:T(8,128)(2,1)S(1)}, bf16[1,512,384]{2,1,0:T(8,128)(2,1)S(1)}, u32[]{:S(2)}, u32[]{:S(2)}) collective-permute-start(bf16[1,512,384]{2,1,0:T(8,128)(2,1)S(1)} %bitcast.14), channel_id=1, source_target_pairs={{0,24},{1,25},{2,26},{3,27},{4,28},{5,29},{6,30},{7,31},{8,16},{9,... | collective-permute-start | bytes 1179656 | tf_op jit(solution)/shard_map/ppermute | solution.py:29
  59.5 9.0 %collective-permute-start.4 = (bf16[2,3,48,384]{3,2,1,0:T(8,128)(2,1)S(1)}, bf16[2,3,48,384]{3,2,1,0:T(8,128)(2,1)S(1)}, u32[]{:S(2)}, u32[]{:S(2)}) collective-permute-start(bf16[2,3,48,384]{3,2,1,0:T(8,128)(2,1)S(1)} %collective-permute-done.3), channel_id=1, source_target_pairs={{0,32},{1,481},{2,34},{3,483},{4,36},{5,485},{6,38},{7,487},{8,40}... | collective-permute-start | bytes 663560 | tf_op jit(solution)/shard_map/ppermute | solution.py:29
  68.5 9.0 %collective-permute-start.6 = (bf16[2,3,48,384]{3,2,1,0:T(8,128)(2,1)S(1)}, bf16[2,3,48,384]{3,2,1,0:T(8,128)(2,1)S(1)}, u32[]{:S(2)}, u32[]{:S(2)}) collective-permute-start(bf16[2,3,48,384]{3,2,1,0:T(8,128)(2,1)S(1)} %collective-permute-done.4), channel_id=1, source_target_pairs={{0,32},{1,481},{2,34},{3,483},{4,36},{5,485},{6,38},{7,487},{8,40}... | collective-permute-start | bytes 663560 | tf_op jit(solution)/shard_map/ppermute | solution.py:29
  77.6 9.0 %collective-permute-start.7 = (bf16[2,3,48,384]{3,2,1,0:T(8,128)(2,1)S(1)}, bf16[2,3,48,384]{3,2,1,0:T(8,128)(2,1)S(1)}, u32[]{:S(2)}, u32[]{:S(2)}) collective-permute-start(bf16[2,3,48,384]{3,2,1,0:T(8,128)(2,1)S(1)} %collective-permute-done.6), channel_id=1, source_target_pairs={{0,32},{1,481},{2,34},{3,483},{4,36},{5,485},{6,38},{7,487},{8,40}... | collective-permute-start | bytes 663560 | tf_op jit(solution)/shard_map/ppermute | solution.py:29
  80.9 18.5 %collective-permute-start.12 = (bf16[4,3,48,384]{3,2,1,0:T(8,128)(2,1)S(1)}, bf16[4,3,48,384]{3,2,1,0:T(8,128)(2,1)S(1)}, u32[]{:S(2)}, u32[]{:S(2)}) collective-permute-start(bf16[4,3,48,384]{3,2,1,0:T(8,128)(2,1)S(1)} %get-tuple-element.20.refs_2_), channel_id=1, source_target_pairs={{0,8},{1,9},{2,10},{3,11},{4,12},{5,13},{6,14},{7,15},{8,0},{9,1},... | collective-permute-start | bytes 1327112 | tf_op jit(solution)/shard_map/ppermute | solution.py:29
  86.6 12.8 %copy-start.6 = (bf16[2,3,48,384]{3,2,1,0:T(8,128)(2,1)}, bf16[2,3,48,384]{3,2,1,0:T(8,128)(2,1)S(1)}, u32[]{:S(2)}) copy-start(bf16[2,3,48,384]{3,2,1,0:T(8,128)(2,1)S(1)} %collective-permute-done.7) | copy-start | bytes 663556
  86.6 9.9 %collective-permute-start.8 = (bf16[2,3,48,384]{3,2,1,0:T(8,128)(2,1)S(1)}, bf16[2,3,48,384]{3,2,1,0:T(8,128)(2,1)}, u32[]{:S(2)}, u32[]{:S(2)}) collective-permute-start(bf16[2,3,48,384]{3,2,1,0:T(8,128)(2,1)S(1)} %collective-permute-done.7), channel_id=1, source_target_pairs={{0,32},{1,481},{2,34},{3,483},{4,36},{5,485},{6,38},{7,487},{8,40}... | collective-permute-start | bytes 663560 | tf_op jit(solution)/shard_map/ppermute | solution.py:29
  88.7 35.0 %collective-permute-start.19 = (bf16[2,512,384]{2,1,0:T(8,128)(2,1)S(1)}, bf16[2,512,384]{2,1,0:T(8,128)(2,1)}, u32[]{:S(2)}, u32[]{:S(2)}) collective-permute-start(bf16[2,512,384]{2,1,0:T(8,128)(2,1)S(1)} %maximum_select_fusion.refs_13_), channel_id=1, source_target_pairs={{0,6},{1,7},{2,0},{3,1},{4,2},{5,3},{6,4},{7,5},{8,14},{9,15},{10,... | collective-permute-start | bytes 2359304 | tf_op jit(solution)/shard_map/ppermute | solution.py:29
  91.0 35.0 %collective-permute-start.20 = (bf16[2,512,384]{2,1,0:T(8,128)(2,1)S(1)}, bf16[2,512,384]{2,1,0:T(8,128)(2,1)}, u32[]{:S(2)}, u32[]{:S(2)}) collective-permute-start(bf16[2,512,384]{2,1,0:T(8,128)(2,1)S(1)} %maximum_select_fusion.refs_13_), channel_id=1, source_target_pairs={{0,2},{1,3},{2,4},{3,5},{4,6},{5,7},{6,0},{7,1},{8,10},{9,11},{10,... | collective-permute-start | bytes 2359304 | tf_op jit(solution)/shard_map/ppermute | solution.py:29
  94.5 47.1 %collective-permute-start.15 = (bf16[14,3,48,384]{3,2,1,0:T(8,128)(2,1)}, bf16[14,3,48,384]{3,2,1,0:T(8,128)(2,1)}, u32[]{:S(2)}, u32[]{:S(2)}) collective-permute-start(bf16[14,3,48,384]{3,2,1,0:T(8,128)(2,1)} %get-tuple-element.19), channel_id=1, source_target_pairs={{0,1},{1,0},{2,3},{3,2},{4,5},{5,4},{6,7},{7,6},{8,9},{9,8},{10,11... | collective-permute-start | bytes 4644872 | tf_op jit(solution)/shard_map/ppermute | solution.py:29
  96.5 9.2 %collective-permute-start.9 = (bf16[2,3,48,384]{3,2,1,0:T(8,128)(2,1)}, bf16[2,3,48,384]{3,2,1,0:T(8,128)(2,1)S(1)}, u32[]{:S(2)}, u32[]{:S(2)}) collective-permute-start(bf16[2,3,48,384]{3,2,1,0:T(8,128)(2,1)} %collective-permute-done.8), channel_id=1, source_target_pairs={{0,32},{1,481},{2,34},{3,483},{4,36},{5,485},{6,38},{7,487},{8,40}... | collective-permute-start | bytes 663560 | tf_op jit(solution)/shard_map/ppermute | solution.py:29
  99.4 20.3 %collective-permute-start.13 = (bf16[4,3,48,384]{3,2,1,0:T(8,128)(2,1)S(1)}, bf16[4,3,48,384]{3,2,1,0:T(8,128)(2,1)S(1)}, u32[]{:S(2)}, u32[]{:S(2)}) collective-permute-start(bf16[4,3,48,384]{3,2,1,0:T(8,128)(2,1)S(1)} %constant_dynamic-update-slice_fusion.5.refs_3_), channel_id=1, source_target_pairs={{0,8},{1,9},{2,10},{3,11},{4,12},{5,13},{6,14},{7,15},{8,0},{9,1},... | collective-permute-start | bytes 1327112 | tf_op jit(solution)/shard_map/ppermute | solution.py:29
  104.0 37.7 %copy-start.4 = (s32[8,8]{1,0:T(8,128)S(1)}, s32[8,8]{1,0:T(8,128)}, u32[]{:S(2)}) copy-start(s32[8,8]{1,0:T(8,128)} %mask.1) | copy-start | bytes 772
  105.7 0.7 copy-start.5
  106.4 7.8 %collective-permute-start.10 = (bf16[1,3,48,384]{3,2,1,0:T(8,128)(2,1)S(1)}, bf16[1,3,48,384]{3,2,1,0:T(8,128)(2,1)S(1)}, u32[]{:S(2)}, u32[]{:S(2)}) collective-permute-start(bf16[1,3,48,384]{3,2,1,0:T(8,128)(2,1)S(1)} %constant_dynamic-slice_fusion.1), channel_id=1, source_target_pairs={{0,32},{1,481},{2,34},{3,483},{4,36},{5,485},{6,38},{7,487},{8,40}... | collective-permute-start | bytes 331784 | tf_op jit(solution)/shard_map/ppermute | solution.py:29
  114.3 25.5 %collective-permute-start.21 = (bf16[2,512,384]{2,1,0:T(8,128)(2,1)S(1)}, bf16[2,512,384]{2,1,0:T(8,128)(2,1)}, u32[]{:S(2)}, u32[]{:S(2)}) collective-permute-start(bf16[2,512,384]{2,1,0:T(8,128)(2,1)S(1)} %maximum_select_fusion.refs_13_), channel_id=1, source_target_pairs={{0,4},{1,5},{2,6},{3,7},{4,0},{5,1},{6,2},{7,3},{8,12},{9,13},{10,... | collective-permute-start | bytes 2359304 | tf_op jit(solution)/shard_map/ppermute | solution.py:29
  119.7 20.1 %collective-permute-start.16 = (bf16[8,3,48,384]{3,2,1,0:T(8,128)(2,1)}, bf16[8,3,48,384]{3,2,1,0:T(8,128)(2,1)}, u32[]{:S(2)}, u32[]{:S(2)}) collective-permute-start(bf16[8,3,48,384]{3,2,1,0:T(8,128)(2,1)} %pad_maximum_fusion), channel_id=1, source_target_pairs={{0,1},{1,0},{2,3},{3,2},{4,5},{5,4},{6,7},{7,6},{8,9},{9,8},{10,11... | collective-permute-start | bytes 2654216 | tf_op jit(solution)/shard_map/ppermute | solution.py:29
  123.6 18.0 %collective-permute-start.17 = (bf16[7,3,48,384]{3,2,1,0:T(8,128)(2,1)}, bf16[7,3,48,384]{3,2,1,0:T(8,128)(2,1)}, u32[]{:S(2)}, u32[]{:S(2)}) collective-permute-start(bf16[7,3,48,384]{3,2,1,0:T(8,128)(2,1)} %pad_maximum_fusion.1), channel_id=1, source_target_pairs={{0,1},{1,0},{2,3},{3,2},{4,5},{5,4},{6,7},{7,6},{8,9},{9,8},{10,11... | collective-permute-start | bytes 2322440 | tf_op jit(solution)/shard_map/ppermute | solution.py:29
  126.1 11.7 %collective-permute-start.14 = (bf16[3,3,48,384]{3,2,1,0:T(8,128)(2,1)S(1)}, bf16[3,3,48,384]{3,2,1,0:T(8,128)(2,1)}, u32[]{:S(2)}, u32[]{:S(2)}) collective-permute-start(bf16[3,3,48,384]{3,2,1,0:T(8,128)(2,1)S(1)} %constant_dynamic-update-slice_fusion.7.refs_4_), channel_id=1, source_target_pairs={{0,8},{1,9},{2,10},{3,11},{4,12},{5,13},{6,14},{7,15},{8,0},{9,1},... | collective-permute-start | bytes 995336 | tf_op jit(solution)/shard_map/ppermute | solution.py:29
  137.8 3.9 %collective-permute-start.18 = (bf16[3,3,48,384]{3,2,1,0:T(8,128)(2,1)}, bf16[3,3,48,384]{3,2,1,0:T(8,128)(2,1)}, u32[]{:S(2)}, u32[]{:S(2)}) collective-permute-start(bf16[3,3,48,384]{3,2,1,0:T(8,128)(2,1)} %collective-permute-done.14.refs_8_), channel_id=1, source_target_pairs={{0,1},{1,0},{2,3},{3,2},{4,5},{5,4},{6,7},{7,6},{8,9},{9,8},{10,11... | collective-permute-start | bytes 995336 | tf_op jit(solution)/shard_map/ppermute | solution.py:29
  141.7 0.9 copy-start.1
  142.6 1.1 copy-start.3
  156.6 0.7 collective-permute-start.22

commit v3 on v2

--- a/solution.py
+++ b/solution.py
@@ -41,37 +41,16 @@
     return (z, x ^ 1, y, c)
 
 
-def ring(z, x, y, c):
-    return (z + (1 if c == 0 else -1), x, y, c)
+def along_z(k):
+    return lambda z, x, y, c: (z + k, x, y, c)
 
 
-def one(t, near):
-    return [(t, near, None)]
-
-
-def two(t, near):
-    return [(t, near, 0), (t, near, 1)]
-
-
-def sent(near):
-    return [
-        one(0, near) + two(1, near) + two(2, near),
-        two(3, near) + two(4, near),
-        two(5, near) + two(6, near),
-        two(7, near) + one(8, near),
-    ]
-
-
-def listing():
-    s, r = sent(False), sent(True)
-    own = [two(0, False)] + s + r
-    swapped = [s[0] + r[0] + s[1], r[1] + s[2], r[2] + s[3], r[3]]
-    return [(e, False) for e in own] + [(e, True) for e in swapped]
+FAR = (0, 4, -4, 8)
+NEAR = (0, 1, -1, 2)
 
 
 def attend_kernel(place, mask, *refs):
-    blocks = listing()
-    count = len(blocks)
+    count = 4 * len(NEAR)
     pieces = refs[count : count + 4]
     out = refs[count + 4]
     weights, tokens, qkv, bias, w_sems, x_sems = refs[count + 5 :]
@@ -86,25 +65,17 @@
             copies.append(
                 pltpu.make_async_copy(piece.at[half], tokens.at[:, pl.ds(at, GROUP)], x_sems.at[2 * i + half])
             )
-    done = set()
-    for ref, (entries, swapped) in zip(refs[:count], blocks):
-        owner = 1 - c if swapped else c
-        sign = 1 - 2 * owner
-        for k, (t, near, slot) in enumerate(entries):
-            if t == 0 and not near and slot is None:
-                continue
-            key = (t, near, slot, swapped)
-            assert key not in done
-            done.add(key)
-            from_z = lax.rem(z - sign * t + NZ, NZ)
-            first = 1 - low if near else low
-            high = owner if slot is None else slot
-            from_x = first + high * (3 - 2 * first)
+    for i, ref in enumerate(refs[:count]):
+        shift = NEAR[i % 4]
+        owner = 1 - c if i >= 8 else c
+        first = 1 - low if i % 8 >= 4 else low
+        from_x = first + owner * (3 - 2 * first)
+        for k, far in enumerate(FAR):
+            from_z = lax.rem(z - shift - far + 2 * NZ, NZ)
             row = pl.multiple_of((from_z * NX + from_x) * SLICE, SLICE)
             copies.append(
-                pltpu.make_async_copy(ref.at[k], weights.at[:, pl.ds(row, SLICE)], w_sems.at[len(done) - 1])
+                pltpu.make_async_copy(ref.at[k], weights.at[:, pl.ds(row, SLICE)], w_sems.at[4 * i + k])
             )
-    assert len(done) == NZ * NX
     for copy in copies:
         copy.start()
 
@@ -188,59 +159,26 @@
     high = jnp.where(c == 0, high[:, ::-1], high)
     packed = jnp.concatenate([low, high], axis=1).reshape(NZ * NX, 8, GROUP)
     piece = jnp.transpose(qkv_weight, (1, 0, 2))[None]
-    packed, piece = hold((packed, piece))
-    spread = lax.all_to_all(packed, ("z", "x"), split_axis=0, concat_axis=0, tiled=True)
 
     first = permute(piece, home)
-    first_other = permute(first, swap)
-    own = jnp.where(c == 0, join(first, first_other), join(first_other, first))
-
-    steps = [None]
-    block = own
-    batches, returned = [], []
-
-    def step():
-        nonlocal block
-        if len(steps) == 8:
-            block = lax.dynamic_slice(block, (c, 0, 0, 0), (1, 3, SLICE, GROUP))
-        block = permute(block, ring)
-        steps.append(block)
-
-    def send(*parts):
-        batch = join(*parts)
-        batches.append(batch)
-        returned.append(permute(batch, pair))
-
-    step()
-    step()
-    block, spread = hold((block, spread))
+    first, packed = hold((first, packed))
+    far = join(first, *[permute(first, along_z(k)) for k in FAR[1:]])
+    spread = lax.all_to_all(packed, ("z", "x"), split_axis=0, concat_axis=0, tiled=True)
+    far_pair = permute(far, pair)
+    near = [permute(far, along_z(k)) for k in NEAR[1:]]
     spread = spread.reshape(1, TOKENS, GROUP)
     partner = permute(spread, lambda z, x, y, c: (z, 3 - x, y, c))
-    step()
-    send(first, steps[1], steps[2])
-    block, partner = hold((block, partner))
+    near[2], partner = hold((near[2], partner))
     both = jnp.where(group == 0, join(spread, partner), join(partner, spread))
     pieces = [both] + [
         permute(both, lambda z, x, y, c, k=k: (z, x, y + k, c)) for k in (-1, 1, 2)
     ]
-    step()
-    step()
-    send(steps[3], steps[4])
-    step()
-    step()
-    send(steps[5], steps[6])
-    step()
-    send(steps[7], steps[8])
-    swapped = [
-        join(batches[0], returned[0], batches[1]),
-        join(returned[1], batches[2]),
-        join(returned[2], batches[3]),
-        returned[3],
-    ]
-    swapped = [permute(array, swap) for array in swapped]
+    mine = [far, *near, far_pair] + [permute(block, pair) for block in near]
+    mine[6], mine[7], *pieces[1:] = hold((mine[6], mine[7], *pieces[1:]))
+    theirs = [permute(block, swap) for block in mine]
 
     place = jnp.stack([z, x, y, c]).astype(jnp.int32)
-    output = project_and_attend(place, span_mask, [own, *batches, *returned, *swapped], pieces)
+    output = project_and_attend(place, span_mask, [*mine, *theirs], pieces)
     output = permute(output.reshape(FRAMES, 8, GROUP), home)
     output = lax.all_to_all(output, ("z", "x"), split_axis=0, concat_axis=0, tiled=True)
     return output.reshape(1, NZ * NX * 8, GROUP)

time: 207 us -> 214 us (1.034)
  starting transfers between devices: 81.2 us -> 104 us
  waiting for transfers between devices: 47.2 us -> 30.8 us
  blocking collectives: 47.9 us -> 52.4 us
  other arithmetic: 5.29 us -> 1.15 us
    ppermute x23 -> x24, starting transfers between devices: 62.7 us -> 81.9 us  [permute(): return lax.ppermute(array, AXES, pairs)]
    ppermute x23 -> x24, waiting for transfers between devices: 47.2 us -> 30.8 us  [permute(): return lax.ppermute(array, AXES, pairs)]
    all_to_all x1, blocking collectives: 47.9 us -> 52.4 us  [per_device(): lax.all_to_all(output, ('z', 'x'), split_axis=0, concat_axis=0, tiled=True)]
    concatenate x2 -> x0, other arithmetic: 4.11 us -> none  [join(): return jnp.concatenate(arrays, axis=0)]
    all_to_all x1, starting transfers between devices: 18.6 us -> 22.2 us  [per_device(): lax.all_to_all(packed, ('z', 'x'), split_axis=0, concat_axis=0, tiled=True)]
    unnamed x24 -> x30, local copies, waits for them, and re-layouts: 8.11 us -> 9.94 us
  transfers between devices with their start and end apart: 24 -> 25, of which waited for: 10 -> 7; matrix products, arithmetic and copies ran while one was open for 5% -> 1% of each run, Pallas kernels for 0% -> 0%
where the time goes in v3:
time: 214 us; the launch traced here: 212 us
  starting transfers between devices  104 us (49%)
  blocking collectives  52.4 us (24%)
  waiting for transfers between devices  30.8 us (14%)
  Pallas kernels  12.4 us (6%)
  local copies, waits for them, and re-layouts  11 us (5%)
    ppermute x24, starting transfers between devices, permute(): return lax.ppermute(array, AXES, pairs)  81.9 us
    all_to_all x1, blocking collectives, per_device(): lax.all_to_all(output, ('z', 'x'), split_axis=0, concat_axis=0, tiled=True)  52.4 us
    ppermute x24, waiting for transfers between devices, permute(): return lax.ppermute(array, AXES, pairs)  30.8 us
    all_to_all x1, starting transfers between devices, per_device(): lax.all_to_all(packed, ('z', 'x'), split_axis=0, concat_axis=0, tiled=True)  22.2 us
    pallas_call x1, Pallas kernels, project_and_attend(): pl.pallas_call(attend_kernel, out_shape=jax.ShapeDtypeStruct((TOKENS, GRO...  12.4 us
    unnamed x30, local copies, waits for them, and re-layouts  9.94 us
  transfers between devices with their start and end apart: 25, of which 7 were waited for; matrix products, arithmetic and copies ran while one was open for 1% of the time, Pallas kernels for 0%

profile of v3, /device:TPU:8, one launch (start us, length us, event | category | flops | bytes accessed | tf_op | source)
XLA Modules:
  0.0 212.3 jit_solution(2427280483448414784)
XLA Ops:
  3.7 22.2 %all-to-all-start = ((bf16[64,8,384]{2,1,0:T(8,128)(2,1)}), bf16[64,8,384]{2,1,0:T(8,128)(2,1)S(1)}, u32[]{:S(2)}, u32[]{:S(2)}) async-start(bf16[64,8,384]{2,1,0:T(8,128)(2,1)} %bitcast.7), calls=%async_computation | async-start | bytes 786432 | tf_op jit(solution)/shard_map/all_to_all | solution.py:166
  25.9 12.3 %collective-permute-start.3 = (bf16[1,3,48,384]{3,2,1,0:T(8,128)(2,1)S(1)}, bf16[1,3,48,384]{3,2,1,0:T(8,128)(2,1)S(1)}, u32[]{:S(2)}, u32[]{:S(2)}) collective-permute-start(bf16[1,3,48,384]{3,2,1,0:T(8,128)(2,1)S(1)} %collective-permute-done), channel_id=1, source_target_pairs={{0,256},{1,257},{2,258},{3,259},{4,260},{5,261},{6,262},{7,263},{8... | collective-permute-start | bytes 331784 | tf_op jit(solution)/shard_map/ppermute | solution.py:29
  38.2 2.4 %collective-permute-start.2 = (bf16[1,3,48,384]{3,2,1,0:T(8,128)(2,1)S(1)}, bf16[1,3,48,384]{3,2,1,0:T(8,128)(2,1)S(1)}, u32[]{:S(2)}, u32[]{:S(2)}) collective-permute-start(bf16[1,3,48,384]{3,2,1,0:T(8,128)(2,1)S(1)} %collective-permute-done), channel_id=1, source_target_pairs={{0,384},{1,385},{2,386},{3,387},{4,388},{5,389},{6,390},{7,391},{8... | collective-permute-start | bytes 331784 | tf_op jit(solution)/shard_map/ppermute | solution.py:29
  40.6 7.4 %collective-permute-start.1 = (bf16[1,3,48,384]{3,2,1,0:T(8,128)(2,1)S(1)}, bf16[1,3,48,384]{3,2,1,0:T(8,128)(2,1)S(1)}, u32[]{:S(2)}, u32[]{:S(2)}) collective-permute-start(bf16[1,3,48,384]{3,2,1,0:T(8,128)(2,1)S(1)} %collective-permute-done), channel_id=1, source_target_pairs={{0,128},{1,129},{2,130},{3,131},{4,132},{5,133},{6,134},{7,135},{8... | collective-permute-start | bytes 331784 | tf_op jit(solution)/shard_map/ppermute | solution.py:29
  48.0 11.8 %collective-permute-done.1 = bf16[1,3,48,384]{3,2,1,0:T(8,128)(2,1)S(1)} collective-permute-done((bf16[1,3,48,384]{3,2,1,0:T(8,128)(2,1)S(1)}, bf16[1,3,48,384]{3,2,1,0:T(8,128)(2,1)S(1)}, u32[]{:S(2)}, u32[]{:S(2)}) %collective-permute-start.1) | collective-permute-done | bytes 110624 | tf_op jit(solution)/shard_map/ppermute | solution.py:29
  59.9 1.7 collective-permute-done.3
  61.6 5.6 %collective-permute-start.5 = (bf16[4,3,48,384]{3,2,1,0:T(8,128)(2,1)S(1)}, bf16[4,3,48,384]{3,2,1,0:T(8,128)(2,1)S(1)}, u32[]{:S(2)}, u32[]{:S(2)}) collective-permute-start(bf16[4,3,48,384]{3,2,1,0:T(8,128)(2,1)S(1)} %constant_dynamic-update-slice_fusion.refs_0_), channel_id=1, source_target_pairs={{0,480},{1,481},{2,482},{3,483},{4,484},{5,485},{6,486},{7,487},{8... | collective-permute-start | bytes 1327112 | tf_op jit(solution)/shard_map/ppermute | solution.py:29
  67.2 7.2 %collective-permute-start.6 = (bf16[4,3,48,384]{3,2,1,0:T(8,128)(2,1)S(1)}, bf16[4,3,48,384]{3,2,1,0:T(8,128)(2,1)}, u32[]{:S(2)}, u32[]{:S(2)}) collective-permute-start(bf16[4,3,48,384]{3,2,1,0:T(8,128)(2,1)S(1)} %constant_dynamic-update-slice_fusion.refs_0_), channel_id=1, source_target_pairs={{0,64},{1,65},{2,66},{3,67},{4,68},{5,69},{6,70},{7,71},{8,72},{9,... | collective-permute-start | bytes 1327112 | tf_op jit(solution)/shard_map/ppermute | solution.py:29
  74.4 4.4 %collective-permute-start.7 = (bf16[1,512,384]{2,1,0:T(8,128)(2,1)S(1)}, bf16[1,512,384]{2,1,0:T(8,128)(2,1)S(1)}, u32[]{:S(2)}, u32[]{:S(2)}) collective-permute-start(bf16[1,512,384]{2,1,0:T(8,128)(2,1)S(1)} %bitcast.14), channel_id=1, source_target_pairs={{0,24},{1,25},{2,26},{3,27},{4,28},{5,29},{6,30},{7,31},{8,16},{9,... | collective-permute-start | bytes 1179656 | tf_op jit(solution)/shard_map/ppermute | solution.py:29
  78.8 2.5 %collective-permute-start.8 = (bf16[4,3,48,384]{3,2,1,0:T(8,128)(2,1)S(1)}, bf16[4,3,48,384]{3,2,1,0:T(8,128)(2,1)S(1)}, u32[]{:S(2)}, u32[]{:S(2)}) collective-permute-start(bf16[4,3,48,384]{3,2,1,0:T(8,128)(2,1)S(1)} %constant_dynamic-update-slice_fusion.refs_0_), channel_id=1, source_target_pairs={{0,8},{1,9},{2,10},{3,11},{4,12},{5,13},{6,14},{7,15},{8,0},{9,1},... | collective-permute-start | bytes 1327112 | tf_op jit(solution)/shard_map/ppermute | solution.py:29
  81.3 1.9 collective-permute-start.4
  83.2 3.4 %collective-permute-start.10 = (bf16[4,3,48,384]{3,2,1,0:T(8,128)(2,1)S(1)}, bf16[4,3,48,384]{3,2,1,0:T(8,128)(2,1)}, u32[]{:S(2)}, u32[]{:S(2)}) collective-permute-start(bf16[4,3,48,384]{3,2,1,0:T(8,128)(2,1)S(1)} %collective-permute-done.5.refs_2_), channel_id=1, source_target_pairs={{0,8},{1,9},{2,10},{3,11},{4,12},{5,13},{6,14},{7,15},{8,0},{9,1},... | collective-permute-start | bytes 1327112 | tf_op jit(solution)/shard_map/ppermute | solution.py:29
  86.6 5.2 %collective-permute-done.6.refs_3_ = bf16[4,3,48,384]{3,2,1,0:T(8,128)(2,1)} collective-permute-done((bf16[4,3,48,384]{3,2,1,0:T(8,128)(2,1)S(1)}, bf16[4,3,48,384]{3,2,1,0:T(8,128)(2,1)}, u32[]{:S(2)}, u32[]{:S(2)}) %collective-permute-start.6) | collective-permute-done | bytes 442400 | tf_op jit(solution)/shard_map/ppermute | solution.py:29
  91.9 4.2 %collective-permute-start.14 = (bf16[2,512,384]{2,1,0:T(8,128)(2,1)S(1)}, bf16[2,512,384]{2,1,0:T(8,128)(2,1)S(1)}, u32[]{:S(2)}, u32[]{:S(2)}) collective-permute-start(bf16[2,512,384]{2,1,0:T(8,128)(2,1)S(1)} %maximum_select_fusion.refs_16_), channel_id=1, source_target_pairs={{0,4},{1,5},{2,6},{3,7},{4,0},{5,1},{6,2},{7,3},{8,12},{9,13},{10,... | collective-permute-start | bytes 2359304 | tf_op jit(solution)/shard_map/ppermute | solution.py:29
  96.1 2.9 %collective-permute-done.4.refs_1_ = bf16[4,3,48,384]{3,2,1,0:T(8,128)(2,1)} collective-permute-done((bf16[4,3,48,384]{3,2,1,0:T(8,128)(2,1)S(1)}, bf16[4,3,48,384]{3,2,1,0:T(8,128)(2,1)}, u32[]{:S(2)}, u32[]{:S(2)}) %collective-permute-start.4) | collective-permute-done | bytes 442400 | tf_op jit(solution)/shard_map/ppermute | solution.py:29
  99.0 3.1 %collective-permute-start.9 = (bf16[4,3,48,384]{3,2,1,0:T(8,128)(2,1)}, bf16[4,3,48,384]{3,2,1,0:T(8,128)(2,1)}, u32[]{:S(2)}, u32[]{:S(2)}) collective-permute-start(bf16[4,3,48,384]{3,2,1,0:T(8,128)(2,1)} %collective-permute-done.4.refs_1_), channel_id=1, source_target_pairs={{0,8},{1,9},{2,10},{3,11},{4,12},{5,13},{6,14},{7,15},{8,0},{9,1},... | collective-permute-start | bytes 1327112 | tf_op jit(solution)/shard_map/ppermute | solution.py:29
  102.1 2.7 %collective-permute-start.11 = (bf16[4,3,48,384]{3,2,1,0:T(8,128)(2,1)}, bf16[4,3,48,384]{3,2,1,0:T(8,128)(2,1)}, u32[]{:S(2)}, u32[]{:S(2)}) collective-permute-start(bf16[4,3,48,384]{3,2,1,0:T(8,128)(2,1)} %collective-permute-done.6.refs_3_), channel_id=1, source_target_pairs={{0,8},{1,9},{2,10},{3,11},{4,12},{5,13},{6,14},{7,15},{8,0},{9,1},... | collective-permute-start | bytes 1327112 | tf_op jit(solution)/shard_map/ppermute | solution.py:29
  104.9 3.5 %collective-permute-start.13 = (bf16[2,512,384]{2,1,0:T(8,128)(2,1)S(1)}, bf16[2,512,384]{2,1,0:T(8,128)(2,1)S(1)}, u32[]{:S(2)}, u32[]{:S(2)}) collective-permute-start(bf16[2,512,384]{2,1,0:T(8,128)(2,1)S(1)} %maximum_select_fusion.refs_16_), channel_id=1, source_target_pairs={{0,2},{1,3},{2,4},{3,5},{4,6},{5,7},{6,0},{7,1},{8,10},{9,11},{10,... | collective-permute-start | bytes 2359304 | tf_op jit(solution)/shard_map/ppermute | solution.py:29
  108.4 2.4 %collective-permute-start.12 = (bf16[2,512,384]{2,1,0:T(8,128)(2,1)S(1)}, bf16[2,512,384]{2,1,0:T(8,128)(2,1)S(1)}, u32[]{:S(2)}, u32[]{:S(2)}) collective-permute-start(bf16[2,512,384]{2,1,0:T(8,128)(2,1)S(1)} %maximum_select_fusion.refs_16_), channel_id=1, source_target_pairs={{0,6},{1,7},{2,0},{3,1},{4,2},{5,3},{6,4},{7,5},{8,14},{9,15},{10,... | collective-permute-start | bytes 2359304 | tf_op jit(solution)/shard_map/ppermute | solution.py:29
  110.7 3.6 %collective-permute-done.9.refs_5_ = bf16[4,3,48,384]{3,2,1,0:T(8,128)(2,1)} collective-permute-done((bf16[4,3,48,384]{3,2,1,0:T(8,128)(2,1)}, bf16[4,3,48,384]{3,2,1,0:T(8,128)(2,1)}, u32[]{:S(2)}, u32[]{:S(2)}) %collective-permute-start.9) | collective-permute-done | bytes 442400 | tf_op jit(solution)/shard_map/ppermute | solution.py:29
  114.3 1.9 collective-permute-start.15
  116.2 3.7 %collective-permute-done.11.refs_7_ = bf16[4,3,48,384]{3,2,1,0:T(8,128)(2,1)} collective-permute-done((bf16[4,3,48,384]{3,2,1,0:T(8,128)(2,1)}, bf16[4,3,48,384]{3,2,1,0:T(8,128)(2,1)}, u32[]{:S(2)}, u32[]{:S(2)}) %collective-permute-start.11) | collective-permute-done | bytes 442400 | tf_op jit(solution)/shard_map/ppermute | solution.py:29
  119.9 1.9 collective-permute-start.19
  122.6 2.4 %collective-permute-start.17 = (bf16[4,3,48,384]{3,2,1,0:T(8,128)(2,1)}, bf16[4,3,48,384]{3,2,1,0:T(8,128)(2,1)S(1)}, u32[]{:S(2)}, u32[]{:S(2)}) collective-permute-start(bf16[4,3,48,384]{3,2,1,0:T(8,128)(2,1)} %copy-done.2), channel_id=1, source_target_pairs={{0,1},{1,0},{2,3},{3,2},{4,5},{5,4},{6,7},{7,6},{8,9},{9,8},{10,11... | collective-permute-start | bytes 1327112 | tf_op jit(solution)/shard_map/ppermute | solution.py:29
  125.0 1.9 collective-permute-start.16
  126.9 2.4 %collective-permute-start.20 = (bf16[4,3,48,384]{3,2,1,0:T(8,128)(2,1)}, bf16[4,3,48,384]{3,2,1,0:T(8,128)(2,1)}, u32[]{:S(2)}, u32[]{:S(2)}) collective-permute-start(bf16[4,3,48,384]{3,2,1,0:T(8,128)(2,1)} %collective-permute-done.9.refs_5_), channel_id=1, source_target_pairs={{0,1},{1,0},{2,3},{3,2},{4,5},{5,4},{6,7},{7,6},{8,9},{9,8},{10,11... | collective-permute-start | bytes 1327112 | tf_op jit(solution)/shard_map/ppermute | solution.py:29
  130.1 1.9 collective-permute-start.18
  132.8 2.4 %collective-permute-start.21 = (bf16[4,3,48,384]{3,2,1,0:T(8,128)(2,1)}, bf16[4,3,48,384]{3,2,1,0:T(8,128)(2,1)}, u32[]{:S(2)}, u32[]{:S(2)}) collective-permute-start(bf16[4,3,48,384]{3,2,1,0:T(8,128)(2,1)} %collective-permute-done.10.refs_6_), channel_id=1, source_target_pairs={{0,1},{1,0},{2,3},{3,2},{4,5},{5,4},{6,7},{7,6},{8,9},{9,8},{10,11... | collective-permute-start | bytes 1327112 | tf_op jit(solution)/shard_map/ppermute | solution.py:29
  136.0 1.9 collective-permute-start.22
  138.0 2.0 collective-permute-done.22.refs_15_
  146.1 12.4 %shard_map.37 = bf16[512,384]{1,0:T(8,128)(2,1)S(1)} custom-call(s32[4]{0:T(128)S(1)} %pad_add_fusion.place, s32[8,8]{1,0:T(8,128)S(1)} %copy-done.12, bf16[4,3,48,384]{3,2,1,0:T(8,128)(2,1)S(1)} %copy-done.1, bf16[4,3,48,384]{3,2,1,0:T(8,128)(2,1)} %collective-permute-done.4.refs_1_, bf16[4,3,48,384]{3,2,1,0:T(8,128)(2,1)S(1)} %copy-done.3, ...), custom_call_target="tpu_custom_call" | custom-call | tf_op jit(solution)/shard_map/pallas_call | solution.py:128
  159.2 52.4 %all_to_all.10 = bf16[64,8,384]{2,1,0:T(8,128)(2,1)S(1)} all-to-all(bf16[64,8,384]{2,1,0:T(8,128)(2,1)S(1)} %collective-permute-done.23), channel_id=1, replica_groups=mesh['z'=16,'x'=4,'y'=4,'c'=2] {'z','x'}, dimensions={0} | all-to-all | bytes 786432 | tf_op jit(solution)/shard_map/all_to_all | solution.py:183
  (56 shorter events, 14.6 us)
Async XLA Ops:
  0.0 140.0 %copy-start.12 = (s32[8,8]{1,0:T(8,128)S(1)}, s32[8,8]{1,0:T(8,128)}, u32[]{:S(2)}) copy-start(s32[8,8]{1,0:T(8,128)} %mask.1) | copy-start | bytes 772
  0.0 3.7 %collective-permute-start = (bf16[1,3,48,384]{3,2,1,0:T(8,128)(2,1)}, bf16[1,3,48,384]{3,2,1,0:T(8,128)(2,1)S(1)}, u32[]{:S(2)}, u32[]{:S(2)}) collective-permute-start(bf16[1,3,48,384]{3,2,1,0:T(8,128)(2,1)} %bitcast.17), channel_id=1, source_target_pairs={{0,0},{1,24},{2,2},{3,26},{4,4},{5,28},{6,6},{7,30},{8,8},{9,16},{... | collective-permute-start | bytes 331784 | tf_op jit(solution)/shard_map/ppermute | solution.py:29
  3.7 70.7 %all-to-all-start = ((bf16[64,8,384]{2,1,0:T(8,128)(2,1)}), bf16[64,8,384]{2,1,0:T(8,128)(2,1)S(1)}, u32[]{:S(2)}, u32[]{:S(2)}) async-start(bf16[64,8,384]{2,1,0:T(8,128)(2,1)} %bitcast.7), calls=%async_computation | async-start | bytes 786432 | tf_op jit(solution)/shard_map/all_to_all | solution.py:166
  25.9 35.7 %collective-permute-start.3 = (bf16[1,3,48,384]{3,2,1,0:T(8,128)(2,1)S(1)}, bf16[1,3,48,384]{3,2,1,0:T(8,128)(2,1)S(1)}, u32[]{:S(2)}, u32[]{:S(2)}) collective-permute-start(bf16[1,3,48,384]{3,2,1,0:T(8,128)(2,1)S(1)} %collective-permute-done), channel_id=1, source_target_pairs={{0,256},{1,257},{2,258},{3,259},{4,260},{5,261},{6,262},{7,263},{8... | collective-permute-start | bytes 331784 | tf_op jit(solution)/shard_map/ppermute | solution.py:29
  38.2 21.6 %collective-permute-start.2 = (bf16[1,3,48,384]{3,2,1,0:T(8,128)(2,1)S(1)}, bf16[1,3,48,384]{3,2,1,0:T(8,128)(2,1)S(1)}, u32[]{:S(2)}, u32[]{:S(2)}) collective-permute-start(bf16[1,3,48,384]{3,2,1,0:T(8,128)(2,1)S(1)} %collective-permute-done), channel_id=1, source_target_pairs={{0,384},{1,385},{2,386},{3,387},{4,388},{5,389},{6,390},{7,391},{8... | collective-permute-start | bytes 331784 | tf_op jit(solution)/shard_map/ppermute | solution.py:29
  40.6 19.2 %collective-permute-start.1 = (bf16[1,3,48,384]{3,2,1,0:T(8,128)(2,1)S(1)}, bf16[1,3,48,384]{3,2,1,0:T(8,128)(2,1)S(1)}, u32[]{:S(2)}, u32[]{:S(2)}) collective-permute-start(bf16[1,3,48,384]{3,2,1,0:T(8,128)(2,1)S(1)} %collective-permute-done), channel_id=1, source_target_pairs={{0,128},{1,129},{2,130},{3,131},{4,132},{5,133},{6,134},{7,135},{8... | collective-permute-start | bytes 331784 | tf_op jit(solution)/shard_map/ppermute | solution.py:29
  61.6 43.2 %copy-start = (bf16[4,3,48,384]{3,2,1,0:T(8,128)(2,1)}, bf16[4,3,48,384]{3,2,1,0:T(8,128)(2,1)S(1)}, u32[]{:S(2)}) copy-start(bf16[4,3,48,384]{3,2,1,0:T(8,128)(2,1)S(1)} %constant_dynamic-update-slice_fusion.refs_0_) | copy-start | bytes 1327108
  61.6 21.6 %collective-permute-start.5 = (bf16[4,3,48,384]{3,2,1,0:T(8,128)(2,1)S(1)}, bf16[4,3,48,384]{3,2,1,0:T(8,128)(2,1)S(1)}, u32[]{:S(2)}, u32[]{:S(2)}) collective-permute-start(bf16[4,3,48,384]{3,2,1,0:T(8,128)(2,1)S(1)} %constant_dynamic-update-slice_fusion.refs_0_), channel_id=1, source_target_pairs={{0,480},{1,481},{2,482},{3,483},{4,484},{5,485},{6,486},{7,487},{8... | collective-permute-start | bytes 1327112 | tf_op jit(solution)/shard_map/ppermute | solution.py:29
  67.2 24.5 %collective-permute-start.6 = (bf16[4,3,48,384]{3,2,1,0:T(8,128)(2,1)S(1)}, bf16[4,3,48,384]{3,2,1,0:T(8,128)(2,1)}, u32[]{:S(2)}, u32[]{:S(2)}) collective-permute-start(bf16[4,3,48,384]{3,2,1,0:T(8,128)(2,1)S(1)} %constant_dynamic-update-slice_fusion.refs_0_), channel_id=1, source_target_pairs={{0,64},{1,65},{2,66},{3,67},{4,68},{5,69},{6,70},{7,71},{8,72},{9,... | collective-permute-start | bytes 1327112 | tf_op jit(solution)/shard_map/ppermute | solution.py:29
  74.4 17.4 %collective-permute-start.7 = (bf16[1,512,384]{2,1,0:T(8,128)(2,1)S(1)}, bf16[1,512,384]{2,1,0:T(8,128)(2,1)S(1)}, u32[]{:S(2)}, u32[]{:S(2)}) collective-permute-start(bf16[1,512,384]{2,1,0:T(8,128)(2,1)S(1)} %bitcast.14), channel_id=1, source_target_pairs={{0,24},{1,25},{2,26},{3,27},{4,28},{5,29},{6,30},{7,31},{8,16},{9,... | collective-permute-start | bytes 1179656 | tf_op jit(solution)/shard_map/ppermute | solution.py:29
  78.8 26.0 %collective-permute-start.8 = (bf16[4,3,48,384]{3,2,1,0:T(8,128)(2,1)S(1)}, bf16[4,3,48,384]{3,2,1,0:T(8,128)(2,1)S(1)}, u32[]{:S(2)}, u32[]{:S(2)}) collective-permute-start(bf16[4,3,48,384]{3,2,1,0:T(8,128)(2,1)S(1)} %constant_dynamic-update-slice_fusion.refs_0_), channel_id=1, source_target_pairs={{0,8},{1,9},{2,10},{3,11},{4,12},{5,13},{6,14},{7,15},{8,0},{9,1},... | collective-permute-start | bytes 1327112 | tf_op jit(solution)/shard_map/ppermute | solution.py:29
  81.3 17.7 %collective-permute-start.4 = (bf16[4,3,48,384]{3,2,1,0:T(8,128)(2,1)S(1)}, bf16[4,3,48,384]{3,2,1,0:T(8,128)(2,1)}, u32[]{:S(2)}, u32[]{:S(2)}) collective-permute-start(bf16[4,3,48,384]{3,2,1,0:T(8,128)(2,1)S(1)} %constant_dynamic-update-slice_fusion.refs_0_), channel_id=1, source_target_pairs={{0,32},{1,33},{2,34},{3,35},{4,36},{5,37},{6,38},{7,39},{8,40},{9,... | collective-permute-start | bytes 1327112 | tf_op jit(solution)/shard_map/ppermute | solution.py:29
  83.2 25.1 %copy-start.2 = (bf16[4,3,48,384]{3,2,1,0:T(8,128)(2,1)}, bf16[4,3,48,384]{3,2,1,0:T(8,128)(2,1)S(1)}, u32[]{:S(2)}) copy-start(bf16[4,3,48,384]{3,2,1,0:T(8,128)(2,1)S(1)} %collective-permute-done.5.refs_2_) | copy-start | bytes 1327108
  83.2 25.1 %collective-permute-start.10 = (bf16[4,3,48,384]{3,2,1,0:T(8,128)(2,1)S(1)}, bf16[4,3,48,384]{3,2,1,0:T(8,128)(2,1)}, u32[]{:S(2)}, u32[]{:S(2)}) collective-permute-start(bf16[4,3,48,384]{3,2,1,0:T(8,128)(2,1)S(1)} %collective-permute-done.5.refs_2_), channel_id=1, source_target_pairs={{0,8},{1,9},{2,10},{3,11},{4,12},{5,13},{6,14},{7,15},{8,0},{9,1},... | collective-permute-start | bytes 1327112 | tf_op jit(solution)/shard_map/ppermute | solution.py:29
  91.9 30.6 %collective-permute-start.14 = (bf16[2,512,384]{2,1,0:T(8,128)(2,1)S(1)}, bf16[2,512,384]{2,1,0:T(8,128)(2,1)S(1)}, u32[]{:S(2)}, u32[]{:S(2)}) collective-permute-start(bf16[2,512,384]{2,1,0:T(8,128)(2,1)S(1)} %maximum_select_fusion.refs_16_), channel_id=1, source_target_pairs={{0,4},{1,5},{2,6},{3,7},{4,0},{5,1},{6,2},{7,3},{8,12},{9,13},{10,... | collective-permute-start | bytes 2359304 | tf_op jit(solution)/shard_map/ppermute | solution.py:29
  99.0 15.3 %collective-permute-start.9 = (bf16[4,3,48,384]{3,2,1,0:T(8,128)(2,1)}, bf16[4,3,48,384]{3,2,1,0:T(8,128)(2,1)}, u32[]{:S(2)}, u32[]{:S(2)}) collective-permute-start(bf16[4,3,48,384]{3,2,1,0:T(8,128)(2,1)} %collective-permute-done.4.refs_1_), channel_id=1, source_target_pairs={{0,8},{1,9},{2,10},{3,11},{4,12},{5,13},{6,14},{7,15},{8,0},{9,1},... | collective-permute-start | bytes 1327112 | tf_op jit(solution)/shard_map/ppermute | solution.py:29
  102.1 17.8 %collective-permute-start.11 = (bf16[4,3,48,384]{3,2,1,0:T(8,128)(2,1)}, bf16[4,3,48,384]{3,2,1,0:T(8,128)(2,1)}, u32[]{:S(2)}, u32[]{:S(2)}) collective-permute-start(bf16[4,3,48,384]{3,2,1,0:T(8,128)(2,1)} %collective-permute-done.6.refs_3_), channel_id=1, source_target_pairs={{0,8},{1,9},{2,10},{3,11},{4,12},{5,13},{6,14},{7,15},{8,0},{9,1},... | collective-permute-start | bytes 1327112 | tf_op jit(solution)/shard_map/ppermute | solution.py:29
  104.9 20.1 %collective-permute-start.13 = (bf16[2,512,384]{2,1,0:T(8,128)(2,1)S(1)}, bf16[2,512,384]{2,1,0:T(8,128)(2,1)S(1)}, u32[]{:S(2)}, u32[]{:S(2)}) collective-permute-start(bf16[2,512,384]{2,1,0:T(8,128)(2,1)S(1)} %maximum_select_fusion.refs_16_), channel_id=1, source_target_pairs={{0,2},{1,3},{2,4},{3,5},{4,6},{5,7},{6,0},{7,1},{8,10},{9,11},{10,... | collective-permute-start | bytes 2359304 | tf_op jit(solution)/shard_map/ppermute | solution.py:29
  108.4 18.5 %collective-permute-start.12 = (bf16[2,512,384]{2,1,0:T(8,128)(2,1)S(1)}, bf16[2,512,384]{2,1,0:T(8,128)(2,1)S(1)}, u32[]{:S(2)}, u32[]{:S(2)}) collective-permute-start(bf16[2,512,384]{2,1,0:T(8,128)(2,1)S(1)} %maximum_select_fusion.refs_16_), channel_id=1, source_target_pairs={{0,6},{1,7},{2,0},{3,1},{4,2},{5,3},{6,4},{7,5},{8,14},{9,15},{10,... | collective-permute-start | bytes 2359304 | tf_op jit(solution)/shard_map/ppermute | solution.py:29
  114.3 15.0 %collective-permute-start.15 = (bf16[4,3,48,384]{3,2,1,0:T(8,128)(2,1)}, bf16[4,3,48,384]{3,2,1,0:T(8,128)(2,1)S(1)}, u32[]{:S(2)}, u32[]{:S(2)}) collective-permute-start(bf16[4,3,48,384]{3,2,1,0:T(8,128)(2,1)} %copy-done), channel_id=1, source_target_pairs={{0,1},{1,0},{2,3},{3,2},{4,5},{5,4},{6,7},{7,6},{8,9},{9,8},{10,11... | collective-permute-start | bytes 1327112 | tf_op jit(solution)/shard_map/ppermute | solution.py:29
  119.9 12.2 %collective-permute-start.19 = (bf16[4,3,48,384]{3,2,1,0:T(8,128)(2,1)S(1)}, bf16[4,3,48,384]{3,2,1,0:T(8,128)(2,1)S(1)}, u32[]{:S(2)}, u32[]{:S(2)}) collective-permute-start(bf16[4,3,48,384]{3,2,1,0:T(8,128)(2,1)S(1)} %collective-permute-done.8.refs_4_), channel_id=1, source_target_pairs={{0,1},{1,0},{2,3},{3,2},{4,5},{5,4},{6,7},{7,6},{8,9},{9,8},{10,11... | collective-permute-start | bytes 1327112 | tf_op jit(solution)/shard_map/ppermute | solution.py:29
  122.6 12.7 %collective-permute-start.17 = (bf16[4,3,48,384]{3,2,1,0:T(8,128)(2,1)}, bf16[4,3,48,384]{3,2,1,0:T(8,128)(2,1)S(1)}, u32[]{:S(2)}, u32[]{:S(2)}) collective-permute-start(bf16[4,3,48,384]{3,2,1,0:T(8,128)(2,1)} %copy-done.2), channel_id=1, source_target_pairs={{0,1},{1,0},{2,3},{3,2},{4,5},{5,4},{6,7},{7,6},{8,9},{9,8},{10,11... | collective-permute-start | bytes 1327112 | tf_op jit(solution)/shard_map/ppermute | solution.py:29
  125.0 13.0 %collective-permute-start.16 = (bf16[4,3,48,384]{3,2,1,0:T(8,128)(2,1)}, bf16[4,3,48,384]{3,2,1,0:T(8,128)(2,1)}, u32[]{:S(2)}, u32[]{:S(2)}) collective-permute-start(bf16[4,3,48,384]{3,2,1,0:T(8,128)(2,1)} %collective-permute-done.4.refs_1_), channel_id=1, source_target_pairs={{0,1},{1,0},{2,3},{3,2},{4,5},{5,4},{6,7},{7,6},{8,9},{9,8},{10,11... | collective-permute-start | bytes 1327112 | tf_op jit(solution)/shard_map/ppermute | solution.py:29
  126.9 11.1 %collective-permute-start.20 = (bf16[4,3,48,384]{3,2,1,0:T(8,128)(2,1)}, bf16[4,3,48,384]{3,2,1,0:T(8,128)(2,1)}, u32[]{:S(2)}, u32[]{:S(2)}) collective-permute-start(bf16[4,3,48,384]{3,2,1,0:T(8,128)(2,1)} %collective-permute-done.9.refs_5_), channel_id=1, source_target_pairs={{0,1},{1,0},{2,3},{3,2},{4,5},{5,4},{6,7},{7,6},{8,9},{9,8},{10,11... | collective-permute-start | bytes 1327112 | tf_op jit(solution)/shard_map/ppermute | solution.py:29
  130.1 7.9 %collective-permute-start.18 = (bf16[4,3,48,384]{3,2,1,0:T(8,128)(2,1)}, bf16[4,3,48,384]{3,2,1,0:T(8,128)(2,1)}, u32[]{:S(2)}, u32[]{:S(2)}) collective-permute-start(bf16[4,3,48,384]{3,2,1,0:T(8,128)(2,1)} %collective-permute-done.6.refs_3_), channel_id=1, source_target_pairs={{0,1},{1,0},{2,3},{3,2},{4,5},{5,4},{6,7},{7,6},{8,9},{9,8},{10,11... | collective-permute-start | bytes 1327112 | tf_op jit(solution)/shard_map/ppermute | solution.py:29
  132.8 5.2 %collective-permute-start.21 = (bf16[4,3,48,384]{3,2,1,0:T(8,128)(2,1)}, bf16[4,3,48,384]{3,2,1,0:T(8,128)(2,1)}, u32[]{:S(2)}, u32[]{:S(2)}) collective-permute-start(bf16[4,3,48,384]{3,2,1,0:T(8,128)(2,1)} %collective-permute-done.10.refs_6_), channel_id=1, source_target_pairs={{0,1},{1,0},{2,3},{3,2},{4,5},{5,4},{6,7},{7,6},{8,9},{9,8},{10,11... | collective-permute-start | bytes 1327112 | tf_op jit(solution)/shard_map/ppermute | solution.py:29
  136.0 4.0 %collective-permute-start.22 = (bf16[4,3,48,384]{3,2,1,0:T(8,128)(2,1)}, bf16[4,3,48,384]{3,2,1,0:T(8,128)(2,1)}, u32[]{:S(2)}, u32[]{:S(2)}) collective-permute-start(bf16[4,3,48,384]{3,2,1,0:T(8,128)(2,1)} %collective-permute-done.11.refs_7_), channel_id=1, source_target_pairs={{0,1},{1,0},{2,3},{3,2},{4,5},{5,4},{6,7},{7,6},{8,9},{9,8},{10,11... | collective-permute-start | bytes 1327112 | tf_op jit(solution)/shard_map/ppermute | solution.py:29
  140.0 1.0 copy-start.1
  141.0 1.0 copy-start.3
  142.1 1.0 copy-start.5
  143.1 1.0 copy-start.7
  158.5 0.7 collective-permute-start.23
  (6 other events, 5.1 us)

commit v4 on v3

--- a/solution.py
+++ b/solution.py
@@ -14,6 +14,7 @@
 NZ, NX, NY, NC = 16, 4, 4, 2
 AXES = ("z", "x", "y", "c")
 SLICE = D // (NZ * NX)
+PART = 2 * SLICE
 TOKENS = FRAMES * 8
 
 
@@ -33,29 +34,15 @@
     return (z, x, y, c) if c == x // 2 else (z, 3 - x, y, 1 - c)
 
 
-def swap(z, x, y, c):
-    return (z, x, y, 1 - c)
+def second(z, x, y, c):
+    near = x ^ 1
+    return (z, near if x // 2 == c else 3 - near, y, x // 2)
 
 
-def pair(z, x, y, c):
-    return (z, x ^ 1, y, c)
-
-
-def along_z(k):
-    return lambda z, x, y, c: (z + k, x, y, c)
-
-
-FAR = (0, 4, -4, 8)
-NEAR = (0, 1, -1, 2)
-
-
-def attend_kernel(place, mask, *refs):
-    count = 4 * len(NEAR)
-    pieces = refs[count : count + 4]
-    out = refs[count + 4]
-    weights, tokens, qkv, bias, w_sems, x_sems = refs[count + 5 :]
-    z, x, y, c = place[0], place[1], place[2], place[3]
-    low = jnp.minimum(x, 3 - x)
+def attend_kernel(place, mask, gathered, *refs):
+    pieces, out = refs[:4], refs[4]
+    weights, tokens, qkv, bias, w_sems, x_sems = refs[5:]
+    y = place[0]
 
     copies = []
     for i, (piece, shift) in enumerate(zip(pieces, (0, 1, 3, 2))):
@@ -65,17 +52,9 @@
             copies.append(
                 pltpu.make_async_copy(piece.at[half], tokens.at[:, pl.ds(at, GROUP)], x_sems.at[2 * i + half])
             )
-    for i, ref in enumerate(refs[:count]):
-        shift = NEAR[i % 4]
-        owner = 1 - c if i >= 8 else c
-        first = 1 - low if i % 8 >= 4 else low
-        from_x = first + owner * (3 - 2 * first)
-        for k, far in enumerate(FAR):
-            from_z = lax.rem(z - shift - far + 2 * NZ, NZ)
-            row = pl.multiple_of((from_z * NX + from_x) * SLICE, SLICE)
-            copies.append(
-                pltpu.make_async_copy(ref.at[k], weights.at[:, pl.ds(row, SLICE)], w_sems.at[4 * i + k])
-            )
+    for i in range(D // PART):
+        rows = pl.ds(i * PART, PART)
+        copies.append(pltpu.make_async_copy(gathered.at[i], weights.at[:, rows], w_sems.at[i]))
     for copy in copies:
         copy.start()
 
@@ -123,8 +102,8 @@
             out[rows, lanes] = (summed / total).astype(jnp.bfloat16)
 
 
-def project_and_attend(place, span_mask, blocks, pieces):
-    arrays = [*blocks, *pieces]
+def project_and_attend(place, span_mask, gathered, pieces):
+    arrays = [gathered, *pieces]
     return pl.pallas_call(
         attend_kernel,
         out_shape=jax.ShapeDtypeStruct((TOKENS, GROUP), jnp.bfloat16),
@@ -136,7 +115,7 @@
             pltpu.VMEM((TOKENS, D), jnp.bfloat16),
             pltpu.VMEM((3, TOKENS, GROUP), jnp.bfloat16),
             pltpu.VMEM((TOKENS, TOKENS), jnp.float32),
-            pltpu.SemaphoreType.DMA((NZ * NX,)),
+            pltpu.SemaphoreType.DMA((D // PART,)),
             pltpu.SemaphoreType.DMA((8,)),
         ],
         compiler_params=pltpu.CompilerParams(vmem_limit_bytes=20 * 1024 * 1024),
@@ -158,27 +137,27 @@
     low = jnp.where(c == 0, low, low[:, ::-1])
     high = jnp.where(c == 0, high[:, ::-1], high)
     packed = jnp.concatenate([low, high], axis=1).reshape(NZ * NX, 8, GROUP)
-    piece = jnp.transpose(qkv_weight, (1, 0, 2))[None]
 
+    piece = jnp.transpose(qkv_weight, (1, 0, 2))
     first = permute(piece, home)
-    first, packed = hold((first, packed))
-    far = join(first, *[permute(first, along_z(k)) for k in FAR[1:]])
+    other = permute(piece, second)
+    slot = jnp.where(c == group, x, 3 - x)
+    half = jnp.where(
+        slot % 2 == 0,
+        jnp.concatenate([first, other], axis=1),
+        jnp.concatenate([other, first], axis=1),
+    )
+    half, packed = hold((half, packed))
+    gathered = lax.all_gather(half[None], ("z", "c"), axis=0, tiled=True)
     spread = lax.all_to_all(packed, ("z", "x"), split_axis=0, concat_axis=0, tiled=True)
-    far_pair = permute(far, pair)
-    near = [permute(far, along_z(k)) for k in NEAR[1:]]
     spread = spread.reshape(1, TOKENS, GROUP)
     partner = permute(spread, lambda z, x, y, c: (z, 3 - x, y, c))
-    near[2], partner = hold((near[2], partner))
     both = jnp.where(group == 0, join(spread, partner), join(partner, spread))
     pieces = [both] + [
         permute(both, lambda z, x, y, c, k=k: (z, x, y + k, c)) for k in (-1, 1, 2)
     ]
-    mine = [far, *near, far_pair] + [permute(block, pair) for block in near]
-    mine[6], mine[7], *pieces[1:] = hold((mine[6], mine[7], *pieces[1:]))
-    theirs = [permute(block, swap) for block in mine]
-
-    place = jnp.stack([z, x, y, c]).astype(jnp.int32)
-    output = project_and_attend(place, span_mask, [*mine, *theirs], pieces)
+    place = jnp.stack([y]).astype(jnp.int32)
+    output = project_and_attend(place, span_mask, gathered, pieces)
     output = permute(output.reshape(FRAMES, 8, GROUP), home)
     output = lax.all_to_all(output, ("z", "x"), split_axis=0, concat_axis=0, tiled=True)
     return output.reshape(1, NZ * NX * 8, GROUP)

time: 214 us -> 183 us (0.86)
  the two profiles are of different devices: /device:TPU:8 before, /device:TPU:24 now
where the time goes in v4:
time: 183 us
  blocking collectives  94.7 us (52%)
  waiting for transfers between devices  37.1 us (20%)
  starting transfers between devices  19.2 us (10%)
  between operations  13.5 us (7%)
  Pallas kernels  12.2 us (7%)
  local copies, waits for them, and re-layouts  4.83 us (3%)
    all_to_all x1, blocking collectives, per_device(): lax.all_to_all(packed, ('z', 'x'), split_axis=0, concat_axis=0, tiled=True)  52.5 us
    all_to_all x1, blocking collectives, per_device(): lax.all_to_all(output, ('z', 'x'), split_axis=0, concat_axis=0, tiled=True)  42.1 us
    ppermute x7, waiting for transfers between devices, permute(): return lax.ppermute(array, AXES, pairs)  37.1 us
    ppermute x7, starting transfers between devices, permute(): return lax.ppermute(array, AXES, pairs)  19.2 us
    pallas_call x1, Pallas kernels, project_and_attend(): pl.pallas_call(attend_kernel, out_shape=jax.ShapeDtypeStruct((TOKENS, GRO...  12.2 us
    unnamed x5, local copies, waits for them, and re-layouts  3.76 us
  transfers between devices with their start and end apart: 8, of which 5 were waited for; matrix products, arithmetic and copies ran while one was open for 1% of the time, Pallas kernels for 0%

profile of v4, /device:TPU:24, one launch (start us, length us, event | category | flops | bytes accessed | tf_op | source)
XLA Modules:
  0.0 182.6 jit_solution(3707645306618361376)
XLA Ops:
  6.5 0.0 copy-start.1
  6.5 0.0 all-gather.3.cloned.1.call-start
  6.5 3.5 %collective-permute-start.1 = (bf16[3,48,384]{2,1,0:T(8,128)(2,1)}, bf16[3,48,384]{2,1,0:T(8,128)(2,1)S(1)}, u32[]{:S(2)}, u32[]{:S(2)}) collective-permute-start(bf16[3,48,384]{2,1,0:T(8,128)(2,1)} %bitcast.15), channel_id=1, source_target_pairs={{0,8},{1,16},{2,10},{3,18},{4,12},{5,20},{6,14},{7,22},{8,0},{9,24... | collective-permute-start | bytes 331784 | tf_op jit(solution)/shard_map/ppermute | solution.py:30
  10.1 1.6 collective-permute-start
  11.6 1.1 constant_dynamic-slice_fusion
  12.7 0.1 reverse_select_fusion
  12.9 0.8 collective-permute-done.1
  13.7 0.0 collective-permute-done
  13.7 0.7 maximum_select_fusion.1
  14.4 0.0 all-gather.3.cloned.1.call-update
  14.4 52.5 %all_to_all.10 = bf16[64,8,384]{2,1,0:T(8,128)(2,1)S(1)} all-to-all(bf16[64,8,384]{2,1,0:T(8,128)(2,1)S(1)} %bitcast.10), channel_id=1, replica_groups=mesh['z'=16,'x'=4,'y'=4,'c'=2] {'z','x'}, dimensions={0} | all-to-all | bytes 786432 | tf_op jit(solution)/shard_map/all_to_all | solution.py:152
  67.0 4.5 %collective-permute-start.2 = (bf16[1,512,384]{2,1,0:T(8,128)(2,1)S(1)}, bf16[1,512,384]{2,1,0:T(8,128)(2,1)S(1)}, u32[]{:S(2)}, u32[]{:S(2)}) collective-permute-start(bf16[1,512,384]{2,1,0:T(8,128)(2,1)S(1)} %bitcast.12), channel_id=1, source_target_pairs={{0,24},{1,25},{2,26},{3,27},{4,28},{5,29},{6,30},{7,31},{8,16},{9,... | collective-permute-start | bytes 1179656 | tf_op jit(solution)/shard_map/ppermute | solution.py:30
  71.5 8.0 %collective-permute-done.2 = bf16[1,512,384]{2,1,0:T(8,128)(2,1)S(1)} collective-permute-done((bf16[1,512,384]{2,1,0:T(8,128)(2,1)S(1)}, bf16[1,512,384]{2,1,0:T(8,128)(2,1)S(1)}, u32[]{:S(2)}, u32[]{:S(2)}) %collective-permute-start.2) | collective-permute-done | bytes 393248 | tf_op jit(solution)/shard_map/ppermute | solution.py:30
  79.5 0.1 maximum_select_fusion.refs_0_
  79.7 2.8 %collective-permute-start.5 = (bf16[2,512,384]{2,1,0:T(8,128)(2,1)S(1)}, bf16[2,512,384]{2,1,0:T(8,128)(2,1)S(1)}, u32[]{:S(2)}, u32[]{:S(2)}) collective-permute-start(bf16[2,512,384]{2,1,0:T(8,128)(2,1)S(1)} %maximum_select_fusion.refs_0_), channel_id=1, source_target_pairs={{0,4},{1,5},{2,6},{3,7},{4,0},{5,1},{6,2},{7,3},{8,12},{9,13},{10,... | collective-permute-start | bytes 2359304 | tf_op jit(solution)/shard_map/ppermute | solution.py:30
  82.5 4.2 %collective-permute-start.4 = (bf16[2,512,384]{2,1,0:T(8,128)(2,1)S(1)}, bf16[2,512,384]{2,1,0:T(8,128)(2,1)S(1)}, u32[]{:S(2)}, u32[]{:S(2)}) collective-permute-start(bf16[2,512,384]{2,1,0:T(8,128)(2,1)S(1)} %maximum_select_fusion.refs_0_), channel_id=1, source_target_pairs={{0,2},{1,3},{2,4},{3,5},{4,6},{5,7},{6,0},{7,1},{8,10},{9,11},{10,... | collective-permute-start | bytes 2359304 | tf_op jit(solution)/shard_map/ppermute | solution.py:30
  86.7 1.9 %collective-permute-start.3 = (bf16[2,512,384]{2,1,0:T(8,128)(2,1)S(1)}, bf16[2,512,384]{2,1,0:T(8,128)(2,1)S(1)}, u32[]{:S(2)}, u32[]{:S(2)}) collective-permute-start(bf16[2,512,384]{2,1,0:T(8,128)(2,1)S(1)} %maximum_select_fusion.refs_0_), channel_id=1, source_target_pairs={{0,6},{1,7},{2,0},{3,1},{4,2},{5,3},{6,4},{7,5},{8,14},{9,15},{10,... | collective-permute-start | bytes 2359304 | tf_op jit(solution)/shard_map/ppermute | solution.py:30
  88.7 14.9 %collective-permute-done.5.refs_3_ = bf16[2,512,384]{2,1,0:T(8,128)(2,1)S(1)} collective-permute-done((bf16[2,512,384]{2,1,0:T(8,128)(2,1)S(1)}, bf16[2,512,384]{2,1,0:T(8,128)(2,1)S(1)}, u32[]{:S(2)}, u32[]{:S(2)}) %collective-permute-start.5) | collective-permute-done | bytes 786464 | tf_op jit(solution)/shard_map/ppermute | solution.py:30
  103.6 10.7 %collective-permute-done.4.refs_2_ = bf16[2,512,384]{2,1,0:T(8,128)(2,1)S(1)} collective-permute-done((bf16[2,512,384]{2,1,0:T(8,128)(2,1)S(1)}, bf16[2,512,384]{2,1,0:T(8,128)(2,1)S(1)}, u32[]{:S(2)}, u32[]{:S(2)}) %collective-permute-start.4) | collective-permute-done | bytes 786464 | tf_op jit(solution)/shard_map/ppermute | solution.py:30
  114.3 2.6 %collective-permute-done.3.refs_1_ = bf16[2,512,384]{2,1,0:T(8,128)(2,1)S(1)} collective-permute-done((bf16[2,512,384]{2,1,0:T(8,128)(2,1)S(1)}, bf16[2,512,384]{2,1,0:T(8,128)(2,1)S(1)}, u32[]{:S(2)}, u32[]{:S(2)}) %collective-permute-start.3) | collective-permute-done | bytes 786464 | tf_op jit(solution)/shard_map/ppermute | solution.py:30
  116.9 0.0 all-gather.3.cloned.1.call-done
  116.9 0.0 copy-done.1
  116.9 0.0 copy-start
  116.9 3.0 %copy-done = bf16[96,96,384]{2,1,0:T(8,128)(2,1)S(1)} copy-done((bf16[96,96,384]{2,1,0:T(8,128)(2,1)S(1)}, bf16[96,96,384]{2,1,0:T(8,128)(2,1)}, u32[]{:S(2)}) %copy-start) | copy-done | bytes 7077912
  119.9 12.2 %shard_map.37 = bf16[512,384]{1,0:T(8,128)(2,1)S(1)} custom-call(s32[1]{0:T(128)} %bitcast.place, s32[8,8]{1,0:T(8,128)S(1)} %copy-done.1, bf16[32,3,96,384]{3,2,1,0:T(8,128)(2,1)S(1)} %bitcast.8, bf16[2,512,384]{2,1,0:T(8,128)(2,1)S(1)} %maximum_select_fusion.refs_0_, bf16[2,512,384]{2,1,0:T(8,128)(2,1)S(1)} %collective-permute-done.3.refs_1_, ...), custom_call_target="tpu_custom_call" | custom-call | tf_op jit(solution)/shard_map/pallas_call | solution.py:107
  132.2 0.7 collective-permute-start.6
  132.8 0.0 collective-permute-done.6
  132.9 42.1 %all_to_all.11 = bf16[64,8,384]{2,1,0:T(8,128)(2,1)S(1)} all-to-all(bf16[64,8,384]{2,1,0:T(8,128)(2,1)S(1)} %collective-permute-done.6), channel_id=1, replica_groups=mesh['z'=16,'x'=4,'y'=4,'c'=2] {'z','x'}, dimensions={0} | all-to-all | bytes 786432 | tf_op jit(solution)/shard_map/all_to_all | solution.py:162
  175.0 0.7 copy.5
  (1 shorter events, 0.0 us)
Async XLA Ops:
  6.5 110.4 %copy-start.1 = (s32[8,8]{1,0:T(8,128)S(1)}, s32[8,8]{1,0:T(8,128)}, u32[]{:S(2)}) copy-start(s32[8,8]{1,0:T(8,128)} %mask.1) | copy-start | bytes 772
  6.5 110.4 %all-gather.3.cloned.1.call-start = ((), (), s32[]{:S(2)}) async-start(), calls=%async_computation.2 | async-start | bytes 7299072 | tf_op jit(solution)/shard_map/all_gather | solution.py:151
  6.5 7.1 %collective-permute-start.1 = (bf16[3,48,384]{2,1,0:T(8,128)(2,1)}, bf16[3,48,384]{2,1,0:T(8,128)(2,1)S(1)}, u32[]{:S(2)}, u32[]{:S(2)}) collective-permute-start(bf16[3,48,384]{2,1,0:T(8,128)(2,1)} %bitcast.15), channel_id=1, source_target_pairs={{0,8},{1,16},{2,10},{3,18},{4,12},{5,20},{6,14},{7,22},{8,0},{9,24... | collective-permute-start | bytes 331784 | tf_op jit(solution)/shard_map/ppermute | solution.py:30
  10.1 3.6 %collective-permute-start = (bf16[3,48,384]{2,1,0:T(8,128)(2,1)}, bf16[3,48,384]{2,1,0:T(8,128)(2,1)S(1)}, u32[]{:S(2)}, u32[]{:S(2)}) collective-permute-start(bf16[3,48,384]{2,1,0:T(8,128)(2,1)} %bitcast.16), channel_id=1, source_target_pairs={{0,0},{1,24},{2,2},{3,26},{4,4},{5,28},{6,6},{7,30},{8,8},{9,16},{... | collective-permute-start | bytes 331784 | tf_op jit(solution)/shard_map/ppermute | solution.py:30
  67.0 12.6 %collective-permute-start.2 = (bf16[1,512,384]{2,1,0:T(8,128)(2,1)S(1)}, bf16[1,512,384]{2,1,0:T(8,128)(2,1)S(1)}, u32[]{:S(2)}, u32[]{:S(2)}) collective-permute-start(bf16[1,512,384]{2,1,0:T(8,128)(2,1)S(1)} %bitcast.12), channel_id=1, source_target_pairs={{0,24},{1,25},{2,26},{3,27},{4,28},{5,29},{6,30},{7,31},{8,16},{9,... | collective-permute-start | bytes 1179656 | tf_op jit(solution)/shard_map/ppermute | solution.py:30
  79.7 23.9 %collective-permute-start.5 = (bf16[2,512,384]{2,1,0:T(8,128)(2,1)S(1)}, bf16[2,512,384]{2,1,0:T(8,128)(2,1)S(1)}, u32[]{:S(2)}, u32[]{:S(2)}) collective-permute-start(bf16[2,512,384]{2,1,0:T(8,128)(2,1)S(1)} %maximum_select_fusion.refs_0_), channel_id=1, source_target_pairs={{0,4},{1,5},{2,6},{3,7},{4,0},{5,1},{6,2},{7,3},{8,12},{9,13},{10,... | collective-permute-start | bytes 2359304 | tf_op jit(solution)/shard_map/ppermute | solution.py:30
  82.5 31.7 %collective-permute-start.4 = (bf16[2,512,384]{2,1,0:T(8,128)(2,1)S(1)}, bf16[2,512,384]{2,1,0:T(8,128)(2,1)S(1)}, u32[]{:S(2)}, u32[]{:S(2)}) collective-permute-start(bf16[2,512,384]{2,1,0:T(8,128)(2,1)S(1)} %maximum_select_fusion.refs_0_), channel_id=1, source_target_pairs={{0,2},{1,3},{2,4},{3,5},{4,6},{5,7},{6,0},{7,1},{8,10},{9,11},{10,... | collective-permute-start | bytes 2359304 | tf_op jit(solution)/shard_map/ppermute | solution.py:30
  86.7 30.2 %collective-permute-start.3 = (bf16[2,512,384]{2,1,0:T(8,128)(2,1)S(1)}, bf16[2,512,384]{2,1,0:T(8,128)(2,1)S(1)}, u32[]{:S(2)}, u32[]{:S(2)}) collective-permute-start(bf16[2,512,384]{2,1,0:T(8,128)(2,1)S(1)} %maximum_select_fusion.refs_0_), channel_id=1, source_target_pairs={{0,6},{1,7},{2,0},{3,1},{4,2},{5,3},{6,4},{7,5},{8,14},{9,15},{10,... | collective-permute-start | bytes 2359304 | tf_op jit(solution)/shard_map/ppermute | solution.py:30
  116.9 3.0 %copy-start = (bf16[96,96,384]{2,1,0:T(8,128)(2,1)S(1)}, bf16[96,96,384]{2,1,0:T(8,128)(2,1)}, u32[]{:S(2)}) copy-start(bf16[96,96,384]{2,1,0:T(8,128)(2,1)} %all-gather.3.cloned.1.call-done) | copy-start | bytes 21233668
  132.2 0.7 collective-permute-start.6
Sparse Core Ops, SparseCore 0:
  14.6 97.3 all-gather.2

commit v5 on v4

--- a/solution.py
+++ b/solution.py
@@ -15,6 +15,8 @@
 AXES = ("z", "x", "y", "c")
 SLICE = D // (NZ * NX)
 PART = 2 * SLICE
+CHUNK = D // 4
+SHIFTS = (0, 1, 3, 2)
 TOKENS = FRAMES * 8
 
 
@@ -40,22 +42,21 @@
 
 
 def attend_kernel(place, mask, gathered, *refs):
-    pieces, out = refs[:4], refs[4]
-    weights, tokens, qkv, bias, w_sems, x_sems = refs[5:]
-    y = place[0]
+    pieces, out = refs[:8], refs[8]
+    weights, tokens, sums, qkv, bias, w_sems, x_sems = refs[9:]
+    y, group = place[0], place[1]
 
-    copies = []
-    for i, (piece, shift) in enumerate(zip(pieces, (0, 1, 3, 2))):
-        source = lax.rem(y + shift, NY)
-        for half in range(2):
-            at = pl.multiple_of((2 * source + half) * GROUP, GROUP)
-            copies.append(
-                pltpu.make_async_copy(piece.at[half], tokens.at[:, pl.ds(at, GROUP)], x_sems.at[2 * i + half])
-            )
+    token_copies = []
+    for i, piece in enumerate(pieces):
+        source = lax.rem(y + SHIFTS[i // 2], NY)
+        half = group if i % 2 == 0 else 1 - group
+        at = pl.multiple_of((2 * source + half) * GROUP, GROUP)
+        token_copies.append(pltpu.make_async_copy(piece, tokens.at[:, pl.ds(at, GROUP)], x_sems.at[i]))
+    weight_copies = []
     for i in range(D // PART):
         rows = pl.ds(i * PART, PART)
-        copies.append(pltpu.make_async_copy(gathered.at[i], weights.at[:, rows], w_sems.at[i]))
-    for copy in copies:
+        weight_copies.append(pltpu.make_async_copy(gathered.at[i], weights.at[:, rows], w_sems.at[i]))
+    for copy in token_copies + weight_copies:
         copy.start()
 
     span_rows = TOKENS // SPANS
@@ -70,14 +71,23 @@
         ok = same & (jnp.broadcast_to(row, (span_rows, TOKENS)) > 0)
         bias[pl.ds(i * span_rows, span_rows), :] = jnp.where(ok, 0.0, -1e30)
 
-    for copy in copies:
+    for copy in token_copies:
         copy.wait()
-    for j in range(3):
-        for r in range(2):
-            rows = pl.ds(r * (TOKENS // 2), TOKENS // 2)
-            qkv[j, rows, :] = jnp.dot(
-                tokens[rows, :], weights[j], preferred_element_type=jnp.float32
-            ).astype(jnp.bfloat16)
+    per_chunk = CHUNK // PART
+    for chunk in range(D // CHUNK):
+        for copy in weight_copies[chunk * per_chunk : (chunk + 1) * per_chunk]:
+            copy.wait()
+        features = pl.ds(chunk * CHUNK, CHUNK)
+        for j in range(3):
+            product = jnp.dot(
+                tokens[:, features], weights[j, features, :], preferred_element_type=jnp.float32
+            )
+            if chunk:
+                product = sums[j] + product
+            if chunk < D // CHUNK - 1:
+                sums[j] = product
+            else:
+                qkv[j] = product.astype(jnp.bfloat16)
 
     scale = 1.0 / jnp.sqrt(jnp.float32(HD))
     for h in range(GROUP // HD):
@@ -113,17 +123,14 @@
         scratch_shapes=[
             pltpu.VMEM((3, D, GROUP), jnp.bfloat16),
             pltpu.VMEM((TOKENS, D), jnp.bfloat16),
+            pltpu.VMEM((3, TOKENS, GROUP), jnp.float32),
             pltpu.VMEM((3, TOKENS, GROUP), jnp.bfloat16),
             pltpu.VMEM((TOKENS, TOKENS), jnp.float32),
             pltpu.SemaphoreType.DMA((D // PART,)),
             pltpu.SemaphoreType.DMA((8,)),
         ],
-        compiler_params=pltpu.CompilerParams(vmem_limit_bytes=20 * 1024 * 1024),
+        compiler_params=pltpu.CompilerParams(vmem_limit_bytes=44 * 1024 * 1024),
     )(place, span_mask, *arrays)
-
-
-def join(*arrays):
-    return jnp.concatenate(arrays, axis=0)
 
 
 def per_device(frames_in, qkv_weight, span_mask):
@@ -150,13 +157,14 @@
     half, packed = hold((half, packed))
     gathered = lax.all_gather(half[None], ("z", "c"), axis=0, tiled=True)
     spread = lax.all_to_all(packed, ("z", "x"), split_axis=0, concat_axis=0, tiled=True)
-    spread = spread.reshape(1, TOKENS, GROUP)
+    spread = spread.reshape(TOKENS, GROUP)
     partner = permute(spread, lambda z, x, y, c: (z, 3 - x, y, c))
-    both = jnp.where(group == 0, join(spread, partner), join(partner, spread))
-    pieces = [both] + [
-        permute(both, lambda z, x, y, c, k=k: (z, x, y + k, c)) for k in (-1, 1, 2)
-    ]
-    place = jnp.stack([y]).astype(jnp.int32)
+    pieces = [spread, partner]
+    for shift in SHIFTS[1:]:
+        for block in (spread, partner):
+            pieces.append(permute(block, lambda z, x, y, c, k=shift: (z, x, y - k, c)))
+
+    place = jnp.stack([y, group]).astype(jnp.int32)
     output = project_and_attend(place, span_mask, gathered, pieces)
     output = permute(output.reshape(FRAMES, 8, GROUP), home)
     output = lax.all_to_all(output, ("z", "x"), split_axis=0, concat_axis=0, tiled=True)

time: 183 us -> 177 us (0.967)
  the two profiles are of different devices: /device:TPU:24 before, /device:TPU:8 now
where the time goes in v5:
time: 177 us
  blocking collectives  97.8 us (55%)
  starting transfers between devices  30.1 us (17%)
  waiting for transfers between devices  21.6 us (12%)
  between operations  13.5 us (8%)
  Pallas kernels  10.9 us (6%)
  local copies, waits for them, and re-layouts  1.82 us (1%)
    all_to_all x1, blocking collectives, per_device(): lax.all_to_all(packed, ('z', 'x'), split_axis=0, concat_axis=0, tiled=True)  52.5 us
    all_to_all x1, blocking collectives, per_device(): lax.all_to_all(output, ('z', 'x'), split_axis=0, concat_axis=0, tiled=True)  45.3 us
    ppermute x10, starting transfers between devices, permute(): return lax.ppermute(array, AXES, pairs)  30.1 us
    ppermute x10, waiting for transfers between devices, permute(): return lax.ppermute(array, AXES, pairs)  19.1 us
    pallas_call x1, Pallas kernels, project_and_attend(): pl.pallas_call(attend_kernel, out_shape=jax.ShapeDtypeStruct((TOKENS, GRO...  10.9 us
  transfers between devices with their start and end apart: 11, of which 6 were waited for; matrix products, arithmetic and copies ran while one was open for 1% of the time, Pallas kernels for 0%

profile of v5, /device:TPU:8, one launch (start us, length us, event | category | flops | bytes accessed | tf_op | source)
XLA Modules:
  0.0 176.7 jit_solution(9031965649821154241)
XLA Ops:
  6.5 0.0 all-gather.3.cloned.1.call-start
  6.5 3.5 %collective-permute-start.1 = (bf16[3,48,384]{2,1,0:T(8,128)(2,1)}, bf16[3,48,384]{2,1,0:T(8,128)(2,1)S(1)}, u32[]{:S(2)}, u32[]{:S(2)}) collective-permute-start(bf16[3,48,384]{2,1,0:T(8,128)(2,1)} %bitcast.19), channel_id=1, source_target_pairs={{0,8},{1,16},{2,10},{3,18},{4,12},{5,20},{6,14},{7,22},{8,0},{9,24... | collective-permute-start | bytes 331784 | tf_op jit(solution)/shard_map/ppermute | solution.py:32
  10.1 1.6 collective-permute-start
  11.6 1.1 constant_dynamic-slice_fusion
  12.7 0.1 reverse_select_fusion
  12.9 0.8 collective-permute-done.1
  13.7 0.0 collective-permute-done
  13.7 0.7 maximum_select_fusion
  14.4 0.0 all-gather.3.cloned.1.call-update
  14.4 52.5 %all_to_all.10 = bf16[64,8,384]{2,1,0:T(8,128)(2,1)S(1)} all-to-all(bf16[64,8,384]{2,1,0:T(8,128)(2,1)S(1)} %bitcast.16), channel_id=1, replica_groups=mesh['z'=16,'x'=4,'y'=4,'c'=2] {'z','x'}, dimensions={0} | all-to-all | bytes 786432 | tf_op jit(solution)/shard_map/all_to_all | solution.py:159
  66.9 4.5 %collective-permute-start.2 = (bf16[512,384]{1,0:T(8,128)(2,1)S(1)}, bf16[512,384]{1,0:T(8,128)(2,1)S(1)}, u32[]{:S(2)}, u32[]{:S(2)}) collective-permute-start(bf16[512,384]{1,0:T(8,128)(2,1)S(1)} %bitcast.9), channel_id=1, source_target_pairs={{0,24},{1,25},{2,26},{3,27},{4,28},{5,29},{6,30},{7,31},{8,16},{9,... | collective-permute-start | bytes 1179656 | tf_op jit(solution)/shard_map/ppermute | solution.py:32
  71.4 4.3 %collective-permute-start.7 = (bf16[512,384]{1,0:T(8,128)(2,1)S(1)}, bf16[512,384]{1,0:T(8,128)(2,1)S(1)}, u32[]{:S(2)}, u32[]{:S(2)}) collective-permute-start(bf16[512,384]{1,0:T(8,128)(2,1)S(1)} %bitcast.10), channel_id=1, source_target_pairs={{0,4},{1,5},{2,6},{3,7},{4,0},{5,1},{6,2},{7,3},{8,12},{9,13},{10,... | collective-permute-start | bytes 1179656 | tf_op jit(solution)/shard_map/ppermute | solution.py:32
  75.7 1.9 %collective-permute-start.5 = (bf16[512,384]{1,0:T(8,128)(2,1)S(1)}, bf16[512,384]{1,0:T(8,128)(2,1)S(1)}, u32[]{:S(2)}, u32[]{:S(2)}) collective-permute-start(bf16[512,384]{1,0:T(8,128)(2,1)S(1)} %bitcast.11), channel_id=1, source_target_pairs={{0,2},{1,3},{2,4},{3,5},{4,6},{5,7},{6,0},{7,1},{8,10},{9,11},{10,... | collective-permute-start | bytes 1179656 | tf_op jit(solution)/shard_map/ppermute | solution.py:32
  77.7 3.9 %collective-permute-start.3 = (bf16[512,384]{1,0:T(8,128)(2,1)S(1)}, bf16[512,384]{1,0:T(8,128)(2,1)S(1)}, u32[]{:S(2)}, u32[]{:S(2)}) collective-permute-start(bf16[512,384]{1,0:T(8,128)(2,1)S(1)} %bitcast.12), channel_id=1, source_target_pairs={{0,6},{1,7},{2,0},{3,1},{4,2},{5,3},{6,4},{7,5},{8,14},{9,15},{10,... | collective-permute-start | bytes 1179656 | tf_op jit(solution)/shard_map/ppermute | solution.py:32
  81.6 0.0 collective-permute-done.2.refs_1_
  81.6 3.3 %collective-permute-start.8 = (bf16[512,384]{1,0:T(8,128)(2,1)S(1)}, bf16[512,384]{1,0:T(8,128)(2,1)S(1)}, u32[]{:S(2)}, u32[]{:S(2)}) collective-permute-start(bf16[512,384]{1,0:T(8,128)(2,1)S(1)} %collective-permute-done.2.refs_1_), channel_id=1, source_target_pairs={{0,4},{1,5},{2,6},{3,7},{4,0},{5,1},{6,2},{7,3},{8,12},{9,13},{10,... | collective-permute-start | bytes 1179656 | tf_op jit(solution)/shard_map/ppermute | solution.py:32
  84.9 4.5 %collective-permute-start.6 = (bf16[512,384]{1,0:T(8,128)(2,1)S(1)}, bf16[512,384]{1,0:T(8,128)(2,1)S(1)}, u32[]{:S(2)}, u32[]{:S(2)}) collective-permute-start(bf16[512,384]{1,0:T(8,128)(2,1)S(1)} %collective-permute-done.2.refs_1_), channel_id=1, source_target_pairs={{0,2},{1,3},{2,4},{3,5},{4,6},{5,7},{6,0},{7,1},{8,10},{9,11},{10,... | collective-permute-start | bytes 1179656 | tf_op jit(solution)/shard_map/ppermute | solution.py:32
  89.4 0.0 collective-permute-done.7.refs_6_
  89.4 1.9 %collective-permute-start.4 = (bf16[512,384]{1,0:T(8,128)(2,1)S(1)}, bf16[512,384]{1,0:T(8,128)(2,1)S(1)}, u32[]{:S(2)}, u32[]{:S(2)}) collective-permute-start(bf16[512,384]{1,0:T(8,128)(2,1)S(1)} %collective-permute-done.2.refs_1_), channel_id=1, source_target_pairs={{0,6},{1,7},{2,0},{3,1},{4,2},{5,3},{6,4},{7,5},{8,14},{9,15},{10,... | collective-permute-start | bytes 1179656 | tf_op jit(solution)/shard_map/ppermute | solution.py:32
  91.3 0.1 pad_add_fusion.place
  91.4 4.1 %collective-permute-done.5.refs_4_ = bf16[512,384]{1,0:T(8,128)(2,1)S(1)} collective-permute-done((bf16[512,384]{1,0:T(8,128)(2,1)S(1)}, bf16[512,384]{1,0:T(8,128)(2,1)S(1)}, u32[]{:S(2)}, u32[]{:S(2)}) %collective-permute-start.5) | collective-permute-done | bytes 393248 | tf_op jit(solution)/shard_map/ppermute | solution.py:32
  95.5 4.5 %collective-permute-done.3.refs_2_ = bf16[512,384]{1,0:T(8,128)(2,1)S(1)} collective-permute-done((bf16[512,384]{1,0:T(8,128)(2,1)S(1)}, bf16[512,384]{1,0:T(8,128)(2,1)S(1)}, u32[]{:S(2)}, u32[]{:S(2)}) %collective-permute-start.3) | collective-permute-done | bytes 393248 | tf_op jit(solution)/shard_map/ppermute | solution.py:32
  100.0 3.5 %collective-permute-done.8.refs_7_ = bf16[512,384]{1,0:T(8,128)(2,1)S(1)} collective-permute-done((bf16[512,384]{1,0:T(8,128)(2,1)S(1)}, bf16[512,384]{1,0:T(8,128)(2,1)S(1)}, u32[]{:S(2)}, u32[]{:S(2)}) %collective-permute-start.8) | collective-permute-done | bytes 393248 | tf_op jit(solution)/shard_map/ppermute | solution.py:32
  103.5 6.2 %collective-permute-done.6.refs_5_ = bf16[512,384]{1,0:T(8,128)(2,1)S(1)} collective-permute-done((bf16[512,384]{1,0:T(8,128)(2,1)S(1)}, bf16[512,384]{1,0:T(8,128)(2,1)S(1)}, u32[]{:S(2)}, u32[]{:S(2)}) %collective-permute-start.6) | collective-permute-done | bytes 393248 | tf_op jit(solution)/shard_map/ppermute | solution.py:32
  109.7 0.0 collective-permute-done.4.refs_3_
  109.7 2.5 %all-gather.3.cloned.1.call-done = bf16[96,96,384]{2,1,0:T(8,128)(2,1)} async-done(((bf16[3,96,384]{2,1,0:T(8,128)(2,1)}), bf16[96,96,384]{2,1,0:T(8,128)(2,1)}) %all-gather.3.cloned.1.call-update) | async-done | bytes 7077904 | tf_op jit(solution)/shard_map/all_gather | solution.py:158
  112.2 0.0 copy-done
  112.2 10.9 %shard_map.37 = bf16[512,384]{1,0:T(8,128)(2,1)S(1)} custom-call(s32[2]{0:T(128)S(1)} %pad_add_fusion.place, s32[8,8]{1,0:T(8,128)S(1)} %copy-done, bf16[32,3,96,384]{3,2,1,0:T(8,128)(2,1)} %bitcast.15, bf16[512,384]{1,0:T(8,128)(2,1)S(1)} %bitcast.13, bf16[512,384]{1,0:T(8,128)(2,1)S(1)} %collective-permute-done.2.refs_1_, ...), custom_call_target="tpu_custom_call" | custom-call | tf_op jit(solution)/shard_map/pallas_call | solution.py:117
  123.1 0.7 collective-permute-start.9
  123.8 0.0 collective-permute-done.9
  123.8 45.3 %all_to_all.11 = bf16[64,8,384]{2,1,0:T(8,128)(2,1)S(1)} all-to-all(bf16[64,8,384]{2,1,0:T(8,128)(2,1)S(1)} %collective-permute-done.9), channel_id=1, replica_groups=mesh['z'=16,'x'=4,'y'=4,'c'=2] {'z','x'}, dimensions={0} | all-to-all | bytes 786432 | tf_op jit(solution)/shard_map/all_to_all | solution.py:170
  169.1 0.7 copy.5
  (2 shorter events, 0.1 us)
Async XLA Ops:
  6.5 105.7 %copy-start = (s32[8,8]{1,0:T(8,128)S(1)}, s32[8,8]{1,0:T(8,128)}, u32[]{:S(2)}) copy-start(s32[8,8]{1,0:T(8,128)} %mask.1) | copy-start | bytes 772
  6.5 105.7 %all-gather.3.cloned.1.call-start = ((), (), s32[]{:S(2)}) async-start(), calls=%async_computation.2 | async-start | bytes 7299072 | tf_op jit(solution)/shard_map/all_gather | solution.py:158
  6.5 7.1 %collective-permute-start.1 = (bf16[3,48,384]{2,1,0:T(8,128)(2,1)}, bf16[3,48,384]{2,1,0:T(8,128)(2,1)S(1)}, u32[]{:S(2)}, u32[]{:S(2)}) collective-permute-start(bf16[3,48,384]{2,1,0:T(8,128)(2,1)} %bitcast.19), channel_id=1, source_target_pairs={{0,8},{1,16},{2,10},{3,18},{4,12},{5,20},{6,14},{7,22},{8,0},{9,24... | collective-permute-start | bytes 331784 | tf_op jit(solution)/shard_map/ppermute | solution.py:32
  10.1 3.6 %collective-permute-start = (bf16[3,48,384]{2,1,0:T(8,128)(2,1)}, bf16[3,48,384]{2,1,0:T(8,128)(2,1)S(1)}, u32[]{:S(2)}, u32[]{:S(2)}) collective-permute-start(bf16[3,48,384]{2,1,0:T(8,128)(2,1)} %bitcast.20), channel_id=1, source_target_pairs={{0,0},{1,24},{2,2},{3,26},{4,4},{5,28},{6,6},{7,30},{8,8},{9,16},{... | collective-permute-start | bytes 331784 | tf_op jit(solution)/shard_map/ppermute | solution.py:32
  66.9 14.7 %collective-permute-start.2 = (bf16[512,384]{1,0:T(8,128)(2,1)S(1)}, bf16[512,384]{1,0:T(8,128)(2,1)S(1)}, u32[]{:S(2)}, u32[]{:S(2)}) collective-permute-start(bf16[512,384]{1,0:T(8,128)(2,1)S(1)} %bitcast.9), channel_id=1, source_target_pairs={{0,24},{1,25},{2,26},{3,27},{4,28},{5,29},{6,30},{7,31},{8,16},{9,... | collective-permute-start | bytes 1179656 | tf_op jit(solution)/shard_map/ppermute | solution.py:32
  71.4 18.0 %collective-permute-start.7 = (bf16[512,384]{1,0:T(8,128)(2,1)S(1)}, bf16[512,384]{1,0:T(8,128)(2,1)S(1)}, u32[]{:S(2)}, u32[]{:S(2)}) collective-permute-start(bf16[512,384]{1,0:T(8,128)(2,1)S(1)} %bitcast.10), channel_id=1, source_target_pairs={{0,4},{1,5},{2,6},{3,7},{4,0},{5,1},{6,2},{7,3},{8,12},{9,13},{10,... | collective-permute-start | bytes 1179656 | tf_op jit(solution)/shard_map/ppermute | solution.py:32
  75.7 19.8 %collective-permute-start.5 = (bf16[512,384]{1,0:T(8,128)(2,1)S(1)}, bf16[512,384]{1,0:T(8,128)(2,1)S(1)}, u32[]{:S(2)}, u32[]{:S(2)}) collective-permute-start(bf16[512,384]{1,0:T(8,128)(2,1)S(1)} %bitcast.11), channel_id=1, source_target_pairs={{0,2},{1,3},{2,4},{3,5},{4,6},{5,7},{6,0},{7,1},{8,10},{9,11},{10,... | collective-permute-start | bytes 1179656 | tf_op jit(solution)/shard_map/ppermute | solution.py:32
  77.7 22.4 %collective-permute-start.3 = (bf16[512,384]{1,0:T(8,128)(2,1)S(1)}, bf16[512,384]{1,0:T(8,128)(2,1)S(1)}, u32[]{:S(2)}, u32[]{:S(2)}) collective-permute-start(bf16[512,384]{1,0:T(8,128)(2,1)S(1)} %bitcast.12), channel_id=1, source_target_pairs={{0,6},{1,7},{2,0},{3,1},{4,2},{5,3},{6,4},{7,5},{8,14},{9,15},{10,... | collective-permute-start | bytes 1179656 | tf_op jit(solution)/shard_map/ppermute | solution.py:32
  81.6 21.9 %collective-permute-start.8 = (bf16[512,384]{1,0:T(8,128)(2,1)S(1)}, bf16[512,384]{1,0:T(8,128)(2,1)S(1)}, u32[]{:S(2)}, u32[]{:S(2)}) collective-permute-start(bf16[512,384]{1,0:T(8,128)(2,1)S(1)} %collective-permute-done.2.refs_1_), channel_id=1, source_target_pairs={{0,4},{1,5},{2,6},{3,7},{4,0},{5,1},{6,2},{7,3},{8,12},{9,13},{10,... | collective-permute-start | bytes 1179656 | tf_op jit(solution)/shard_map/ppermute | solution.py:32
  84.9 24.8 %collective-permute-start.6 = (bf16[512,384]{1,0:T(8,128)(2,1)S(1)}, bf16[512,384]{1,0:T(8,128)(2,1)S(1)}, u32[]{:S(2)}, u32[]{:S(2)}) collective-permute-start(bf16[512,384]{1,0:T(8,128)(2,1)S(1)} %collective-permute-done.2.refs_1_), channel_id=1, source_target_pairs={{0,2},{1,3},{2,4},{3,5},{4,6},{5,7},{6,0},{7,1},{8,10},{9,11},{10,... | collective-permute-start | bytes 1179656 | tf_op jit(solution)/shard_map/ppermute | solution.py:32
  89.4 20.3 %collective-permute-start.4 = (bf16[512,384]{1,0:T(8,128)(2,1)S(1)}, bf16[512,384]{1,0:T(8,128)(2,1)S(1)}, u32[]{:S(2)}, u32[]{:S(2)}) collective-permute-start(bf16[512,384]{1,0:T(8,128)(2,1)S(1)} %collective-permute-done.2.refs_1_), channel_id=1, source_target_pairs={{0,6},{1,7},{2,0},{3,1},{4,2},{5,3},{6,4},{7,5},{8,14},{9,15},{10,... | collective-permute-start | bytes 1179656 | tf_op jit(solution)/shard_map/ppermute | solution.py:32
  123.1 0.7 collective-permute-start.9
Sparse Core Ops, SparseCore 0:
  14.6 97.5 all-gather.2

commit v6 on v5

--- a/solution.py
+++ b/solution.py
@@ -1,3 +1,5 @@
+import functools
+
 import jax
 import jax.numpy as jnp
 from jax import lax
@@ -32,8 +34,8 @@
     return lax.ppermute(array, AXES, pairs)
 
 
-def home(z, x, y, c):
-    return (z, x, y, c) if c == x // 2 else (z, 3 - x, y, 1 - c)
+def home(z, x, y, c, k=0):
+    return (z, (x if c == x // 2 else 3 - x) ^ k, y, x // 2)
 
 
 def second(z, x, y, c):
@@ -42,9 +44,9 @@
 
 
 def attend_kernel(place, mask, gathered, *refs):
-    pieces, out = refs[:8], refs[8]
-    weights, tokens, sums, qkv, bias, w_sems, x_sems = refs[9:]
-    y, group = place[0], place[1]
+    pieces, outs = refs[:8], refs[8:12]
+    weights, tokens, sums, qkv, bias, result, w_sems, x_sems = refs[12:]
+    y, group, place_x = place[0], place[1], place[2]
 
     token_copies = []
     for i, piece in enumerate(pieces):
@@ -109,23 +111,29 @@
                 qkv[2, pl.ds(0, width), lanes],
                 preferred_element_type=jnp.float32,
             )
-            out[rows, lanes] = (summed / total).astype(jnp.bfloat16)
+            attended = (summed / total).reshape(4, NX, 8, HD)
+            for to_x in range(NX):
+                part = attended[:, to_x].reshape(32, HD)
+                result[to_x, pl.ds(i * 32, 32), lanes] = part.astype(jnp.bfloat16)
+    for k, out in enumerate(outs):
+        out[...] = result[place_x ^ k]
 
 
 def project_and_attend(place, span_mask, gathered, pieces):
     arrays = [gathered, *pieces]
     return pl.pallas_call(
         attend_kernel,
-        out_shape=jax.ShapeDtypeStruct((TOKENS, GROUP), jnp.bfloat16),
+        out_shape=[jax.ShapeDtypeStruct((TOKENS // NX, GROUP), jnp.bfloat16)] * NX,
         in_specs=[pl.BlockSpec(memory_space=pltpu.SMEM)] * 2
         + [pl.BlockSpec(memory_space=pl.ANY)] * len(arrays),
-        out_specs=pl.BlockSpec(memory_space=pltpu.VMEM),
+        out_specs=[pl.BlockSpec(memory_space=pltpu.VMEM)] * NX,
         scratch_shapes=[
             pltpu.VMEM((3, D, GROUP), jnp.bfloat16),
             pltpu.VMEM((TOKENS, D), jnp.bfloat16),
             pltpu.VMEM((3, TOKENS, GROUP), jnp.float32),
             pltpu.VMEM((3, TOKENS, GROUP), jnp.bfloat16),
             pltpu.VMEM((TOKENS, TOKENS), jnp.float32),
+            pltpu.VMEM((NX, TOKENS // NX, GROUP), jnp.bfloat16),
             pltpu.SemaphoreType.DMA((D // PART,)),
             pltpu.SemaphoreType.DMA((8,)),
         ],
@@ -164,10 +172,12 @@
         for block in (spread, partner):
             pieces.append(permute(block, lambda z, x, y, c, k=shift: (z, x, y - k, c)))
 
-    place = jnp.stack([y, group]).astype(jnp.int32)
-    output = project_and_attend(place, span_mask, gathered, pieces)
-    output = permute(output.reshape(FRAMES, 8, GROUP), home)
-    output = lax.all_to_all(output, ("z", "x"), split_axis=0, concat_axis=0, tiled=True)
+    place = jnp.stack([y, group, slot]).astype(jnp.int32)
+    parts = project_and_attend(place, span_mask, gathered, pieces)
+    parts = [permute(part, functools.partial(home, k=k)) for k, part in enumerate(parts)]
+    parts = [lax.select_n(x, *[parts[k ^ at] for k in range(NX)]) for at in range(NX)]
+    output = jnp.stack([part.reshape(NZ, 8, GROUP) for part in parts], axis=1)
+    output = lax.all_to_all(output, "z", split_axis=0, concat_axis=0, tiled=True)
     return output.reshape(1, NZ * NX * 8, GROUP)
 
 

time: 177 us -> 175 us (0.989)
  the two profiles are of different devices: /device:TPU:8 before, /device:TPU:1 now
where the time goes in v6:
time: 175 us
  blocking collectives  70.9 us (41%)
  starting transfers between devices  46.3 us (26%)
  waiting for transfers between devices  30.2 us (17%)
  between operations  13.6 us (8%)
  Pallas kernels  10.9 us (6%)
  local copies, waits for them, and re-layouts  1.83 us (1%)
    ppermute x13, starting transfers between devices, permute(): return lax.ppermute(array, AXES, pairs)  46.3 us
    all_to_all x1, blocking collectives, per_device(): lax.all_to_all(packed, ('z', 'x'), split_axis=0, concat_axis=0, tiled=True)  45.1 us
    ppermute x13, waiting for transfers between devices, permute(): return lax.ppermute(array, AXES, pairs)  28.7 us
    all_to_all x1, blocking collectives, per_device(): lax.all_to_all(output, 'z', split_axis=0, concat_axis=0, tiled=True)  25.8 us
    pallas_call x1, Pallas kernels, project_and_attend(): pl.pallas_call(attend_kernel, out_shape=[jax.ShapeDtypeStruct((TOKENS //...  10.9 us
  transfers between devices with their start and end apart: 14, of which 8 were waited for; matrix products, arithmetic and copies ran while one was open for 1% of the time, Pallas kernels for 0%

profile of v6, /device:TPU:1, one launch (start us, length us, event | category | flops | bytes accessed | tf_op | source)
XLA Modules:
  0.0 174.9 jit_solution(13908590409869342789)
XLA Ops:
  6.5 5.9 %collective-permute-start = (bf16[3,48,384]{2,1,0:T(8,128)(2,1)}, bf16[3,48,384]{2,1,0:T(8,128)(2,1)S(1)}, u32[]{:S(2)}, u32[]{:S(2)}) collective-permute-start(bf16[3,48,384]{2,1,0:T(8,128)(2,1)} %bitcast.34), channel_id=1, source_target_pairs={{0,0},{1,24},{2,2},{3,26},{4,4},{5,28},{6,6},{7,30},{8,8},{9,16},{... | collective-permute-start | bytes 331784 | tf_op jit(solution)/shard_map/ppermute | solution.py:34
  12.4 2.2 %collective-permute-start.1 = (bf16[3,48,384]{2,1,0:T(8,128)(2,1)}, bf16[3,48,384]{2,1,0:T(8,128)(2,1)S(1)}, u32[]{:S(2)}, u32[]{:S(2)}) collective-permute-start(bf16[3,48,384]{2,1,0:T(8,128)(2,1)} %bitcast.35), channel_id=1, source_target_pairs={{0,8},{1,16},{2,10},{3,18},{4,12},{5,20},{6,14},{7,22},{8,0},{9,24... | collective-permute-start | bytes 331784 | tf_op jit(solution)/shard_map/ppermute | solution.py:34
  14.7 1.1 constant_dynamic-slice_fusion
  15.8 0.1 reverse_select_fusion
  16.0 4.3 %collective-permute-done.1 = bf16[3,48,384]{2,1,0:T(8,128)(2,1)S(1)} collective-permute-done((bf16[3,48,384]{2,1,0:T(8,128)(2,1)}, bf16[3,48,384]{2,1,0:T(8,128)(2,1)S(1)}, u32[]{:S(2)}, u32[]{:S(2)}) %collective-permute-start.1) | collective-permute-done | bytes 110624 | tf_op jit(solution)/shard_map/ppermute | solution.py:34
  20.2 0.7 maximum_select_fusion
  21.0 0.0 all-gather.3.cloned.1.call-update
  21.0 45.1 %all_to_all.10 = bf16[64,8,384]{2,1,0:T(8,128)(2,1)S(1)} all-to-all(bf16[64,8,384]{2,1,0:T(8,128)(2,1)S(1)} %bitcast.31), channel_id=1, replica_groups=mesh['z'=16,'x'=4,'y'=4,'c'=2] {'z','x'}, dimensions={0} | all-to-all | bytes 786432 | tf_op jit(solution)/shard_map/all_to_all | solution.py:167
  66.1 5.2 %collective-permute-start.2 = (bf16[512,384]{1,0:T(8,128)(2,1)S(1)}, bf16[512,384]{1,0:T(8,128)(2,1)S(1)}, u32[]{:S(2)}, u32[]{:S(2)}) collective-permute-start(bf16[512,384]{1,0:T(8,128)(2,1)S(1)} %bitcast.25), channel_id=1, source_target_pairs={{0,24},{1,25},{2,26},{3,27},{4,28},{5,29},{6,30},{7,31},{8,16},{9,... | collective-permute-start | bytes 1179656 | tf_op jit(solution)/shard_map/ppermute | solution.py:34
  71.3 4.6 %collective-permute-start.3 = (bf16[512,384]{1,0:T(8,128)(2,1)S(1)}, bf16[512,384]{1,0:T(8,128)(2,1)S(1)}, u32[]{:S(2)}, u32[]{:S(2)}) collective-permute-start(bf16[512,384]{1,0:T(8,128)(2,1)S(1)} %bitcast.26), channel_id=1, source_target_pairs={{0,6},{1,7},{2,0},{3,1},{4,2},{5,3},{6,4},{7,5},{8,14},{9,15},{10,... | collective-permute-start | bytes 1179656 | tf_op jit(solution)/shard_map/ppermute | solution.py:34
  76.0 1.9 %collective-permute-start.5 = (bf16[512,384]{1,0:T(8,128)(2,1)S(1)}, bf16[512,384]{1,0:T(8,128)(2,1)S(1)}, u32[]{:S(2)}, u32[]{:S(2)}) collective-permute-start(bf16[512,384]{1,0:T(8,128)(2,1)S(1)} %bitcast.27), channel_id=1, source_target_pairs={{0,2},{1,3},{2,4},{3,5},{4,6},{5,7},{6,0},{7,1},{8,10},{9,11},{10,... | collective-permute-start | bytes 1179656 | tf_op jit(solution)/shard_map/ppermute | solution.py:34
  77.9 3.6 %collective-permute-start.7 = (bf16[512,384]{1,0:T(8,128)(2,1)S(1)}, bf16[512,384]{1,0:T(8,128)(2,1)S(1)}, u32[]{:S(2)}, u32[]{:S(2)}) collective-permute-start(bf16[512,384]{1,0:T(8,128)(2,1)S(1)} %bitcast.28), channel_id=1, source_target_pairs={{0,4},{1,5},{2,6},{3,7},{4,0},{5,1},{6,2},{7,3},{8,12},{9,13},{10,... | collective-permute-start | bytes 1179656 | tf_op jit(solution)/shard_map/ppermute | solution.py:34
  81.5 2.9 %collective-permute-start.4 = (bf16[512,384]{1,0:T(8,128)(2,1)S(1)}, bf16[512,384]{1,0:T(8,128)(2,1)S(1)}, u32[]{:S(2)}, u32[]{:S(2)}) collective-permute-start(bf16[512,384]{1,0:T(8,128)(2,1)S(1)} %collective-permute-done.2.refs_1_), channel_id=1, source_target_pairs={{0,6},{1,7},{2,0},{3,1},{4,2},{5,3},{6,4},{7,5},{8,14},{9,15},{10,... | collective-permute-start | bytes 1179656 | tf_op jit(solution)/shard_map/ppermute | solution.py:34
  84.4 2.5 %collective-permute-start.6 = (bf16[512,384]{1,0:T(8,128)(2,1)S(1)}, bf16[512,384]{1,0:T(8,128)(2,1)S(1)}, u32[]{:S(2)}, u32[]{:S(2)}) collective-permute-start(bf16[512,384]{1,0:T(8,128)(2,1)S(1)} %collective-permute-done.2.refs_1_), channel_id=1, source_target_pairs={{0,2},{1,3},{2,4},{3,5},{4,6},{5,7},{6,0},{7,1},{8,10},{9,11},{10,... | collective-permute-start | bytes 1179656 | tf_op jit(solution)/shard_map/ppermute | solution.py:34
  86.9 3.7 %collective-permute-start.8 = (bf16[512,384]{1,0:T(8,128)(2,1)S(1)}, bf16[512,384]{1,0:T(8,128)(2,1)S(1)}, u32[]{:S(2)}, u32[]{:S(2)}) collective-permute-start(bf16[512,384]{1,0:T(8,128)(2,1)S(1)} %collective-permute-done.2.refs_1_), channel_id=1, source_target_pairs={{0,4},{1,5},{2,6},{3,7},{4,0},{5,1},{6,2},{7,3},{8,12},{9,13},{10,... | collective-permute-start | bytes 1179656 | tf_op jit(solution)/shard_map/ppermute | solution.py:34
  90.6 0.1 pad_add_fusion.place
  90.7 4.3 %collective-permute-done.7.refs_6_ = bf16[512,384]{1,0:T(8,128)(2,1)S(1)} collective-permute-done((bf16[512,384]{1,0:T(8,128)(2,1)S(1)}, bf16[512,384]{1,0:T(8,128)(2,1)S(1)}, u32[]{:S(2)}, u32[]{:S(2)}) %collective-permute-start.7) | collective-permute-done | bytes 393248 | tf_op jit(solution)/shard_map/ppermute | solution.py:34
  95.0 7.8 %collective-permute-done.4.refs_3_ = bf16[512,384]{1,0:T(8,128)(2,1)S(1)} collective-permute-done((bf16[512,384]{1,0:T(8,128)(2,1)S(1)}, bf16[512,384]{1,0:T(8,128)(2,1)S(1)}, u32[]{:S(2)}, u32[]{:S(2)}) %collective-permute-start.4) | collective-permute-done | bytes 393248 | tf_op jit(solution)/shard_map/ppermute | solution.py:34
  102.8 4.4 %collective-permute-done.6.refs_5_ = bf16[512,384]{1,0:T(8,128)(2,1)S(1)} collective-permute-done((bf16[512,384]{1,0:T(8,128)(2,1)S(1)}, bf16[512,384]{1,0:T(8,128)(2,1)S(1)}, u32[]{:S(2)}, u32[]{:S(2)}) %collective-permute-start.6) | collective-permute-done | bytes 393248 | tf_op jit(solution)/shard_map/ppermute | solution.py:34
  107.1 4.8 %collective-permute-done.8.refs_7_ = bf16[512,384]{1,0:T(8,128)(2,1)S(1)} collective-permute-done((bf16[512,384]{1,0:T(8,128)(2,1)S(1)}, bf16[512,384]{1,0:T(8,128)(2,1)S(1)}, u32[]{:S(2)}, u32[]{:S(2)}) %collective-permute-start.8) | collective-permute-done | bytes 393248 | tf_op jit(solution)/shard_map/ppermute | solution.py:34
  111.9 1.5 all-gather.3.cloned.1.call-done
  113.4 10.9 %shard_map.37 = (bf16[128,384]{1,0:T(8,128)(2,1)S(1)}, bf16[128,384]{1,0:T(8,128)(2,1)S(1)}, bf16[128,384]{1,0:T(8,128)(2,1)S(1)}, bf16[128,384]{1,0:T(8,128)(2,1)S(1)}) custom-call(s32[3]{0:T(128)S(1)} %pad_add_fusion.place, s32[8,8]{1,0:T(8,128)S(1)} %copy-done, bf16[32,3,96,384]{3,2,1,0:T(8,128)(2,1)} %bitcast.30, bf16[512,384]{1,0:T(8,128)(2,1)S(1)} %bitcast.29, ...), custom_call_target="tpu_custom_call" | custom-call | tf_op jit(solution)/shard_map/pallas_call | solution.py:124
  124.3 4.9 %collective-permute-start.10 = (bf16[128,384]{1,0:T(8,128)(2,1)S(1)}, bf16[128,384]{1,0:T(8,128)(2,1)S(1)}, u32[]{:S(2)}, u32[]{:S(2)}) collective-permute-start(bf16[128,384]{1,0:T(8,128)(2,1)S(1)} %get-tuple-element.14), channel_id=1, source_target_pairs={{0,8},{1,16},{2,10},{3,18},{4,12},{5,20},{6,14},{7,22},{8,0},{9,24... | collective-permute-start | bytes 294920 | tf_op jit(solution)/shard_map/ppermute | solution.py:34
  129.2 3.0 %collective-permute-start.11 = (bf16[128,384]{1,0:T(8,128)(2,1)S(1)}, bf16[128,384]{1,0:T(8,128)(2,1)S(1)}, u32[]{:S(2)}, u32[]{:S(2)}) collective-permute-start(bf16[128,384]{1,0:T(8,128)(2,1)S(1)} %get-tuple-element.15), channel_id=1, source_target_pairs={{0,16},{1,8},{2,18},{3,10},{4,20},{5,12},{6,22},{7,14},{8,24},{9,0... | collective-permute-start | bytes 294920 | tf_op jit(solution)/shard_map/ppermute | solution.py:34
  132.2 1.9 %collective-permute-start.12 = (bf16[128,384]{1,0:T(8,128)(2,1)S(1)}, bf16[128,384]{1,0:T(8,128)(2,1)S(1)}, u32[]{:S(2)}, u32[]{:S(2)}) collective-permute-start(bf16[128,384]{1,0:T(8,128)(2,1)S(1)} %get-tuple-element.16), channel_id=1, source_target_pairs={{0,24},{1,0},{2,26},{3,2},{4,28},{5,4},{6,30},{7,6},{8,16},{9,8},{... | collective-permute-start | bytes 294920 | tf_op jit(solution)/shard_map/ppermute | solution.py:34
  134.2 3.9 %collective-permute-start.9 = (bf16[128,384]{1,0:T(8,128)(2,1)S(1)}, bf16[128,384]{1,0:T(8,128)(2,1)S(1)}, u32[]{:S(2)}, u32[]{:S(2)}) collective-permute-start(bf16[128,384]{1,0:T(8,128)(2,1)S(1)} %get-tuple-element.13), channel_id=1, source_target_pairs={{0,0},{1,24},{2,2},{3,26},{4,4},{5,28},{6,6},{7,30},{8,8},{9,16},{... | collective-permute-start | bytes 294920 | tf_op jit(solution)/shard_map/ppermute | solution.py:34
  138.1 0.7 collective-permute-done.12
  138.8 2.5 %collective-permute-done.9 = bf16[128,384]{1,0:T(8,128)(2,1)S(1)} collective-permute-done((bf16[128,384]{1,0:T(8,128)(2,1)S(1)}, bf16[128,384]{1,0:T(8,128)(2,1)S(1)}, u32[]{:S(2)}, u32[]{:S(2)}) %collective-permute-start.9) | collective-permute-done | bytes 98336 | tf_op jit(solution)/shard_map/ppermute | solution.py:34
  141.3 0.1 select_bitcast_fusion.3
  141.4 0.1 pad_maximum_fusion.1
  141.5 25.8 %all_to_all.11 = bf16[16,4,8,384]{3,2,1,0:T(8,128)(2,1)S(1)} all-to-all(bf16[16,4,8,384]{3,2,1,0:T(8,128)(2,1)S(1)} %pad_maximum_fusion.1), channel_id=1, replica_groups=mesh['z'=16,'x'=4,'y'=4,'c'=2] {'z'}, dimensions={0} | all-to-all | bytes 786432 | tf_op jit(solution)/shard_map/all_to_all | solution.py:180
  167.3 0.7 copy.10
  (10 shorter events, 0.1 us)
Async XLA Ops:
  6.5 106.9 %copy-start = (s32[8,8]{1,0:T(8,128)S(1)}, s32[8,8]{1,0:T(8,128)}, u32[]{:S(2)}) copy-start(s32[8,8]{1,0:T(8,128)} %mask.1) | copy-start | bytes 772
  6.5 106.8 %all-gather.3.cloned.1.call-start = ((), (), s32[]{:S(2)}) async-start(), calls=%async_computation.2 | async-start | bytes 7299072 | tf_op jit(solution)/shard_map/all_gather | solution.py:166
  6.5 9.4 %collective-permute-start = (bf16[3,48,384]{2,1,0:T(8,128)(2,1)}, bf16[3,48,384]{2,1,0:T(8,128)(2,1)S(1)}, u32[]{:S(2)}, u32[]{:S(2)}) collective-permute-start(bf16[3,48,384]{2,1,0:T(8,128)(2,1)} %bitcast.34), channel_id=1, source_target_pairs={{0,0},{1,24},{2,2},{3,26},{4,4},{5,28},{6,6},{7,30},{8,8},{9,16},{... | collective-permute-start | bytes 331784 | tf_op jit(solution)/shard_map/ppermute | solution.py:34
  12.4 7.8 %collective-permute-start.1 = (bf16[3,48,384]{2,1,0:T(8,128)(2,1)}, bf16[3,48,384]{2,1,0:T(8,128)(2,1)S(1)}, u32[]{:S(2)}, u32[]{:S(2)}) collective-permute-start(bf16[3,48,384]{2,1,0:T(8,128)(2,1)} %bitcast.35), channel_id=1, source_target_pairs={{0,8},{1,16},{2,10},{3,18},{4,12},{5,20},{6,14},{7,22},{8,0},{9,24... | collective-permute-start | bytes 331784 | tf_op jit(solution)/shard_map/ppermute | solution.py:34
  66.1 15.4 %collective-permute-start.2 = (bf16[512,384]{1,0:T(8,128)(2,1)S(1)}, bf16[512,384]{1,0:T(8,128)(2,1)S(1)}, u32[]{:S(2)}, u32[]{:S(2)}) collective-permute-start(bf16[512,384]{1,0:T(8,128)(2,1)S(1)} %bitcast.25), channel_id=1, source_target_pairs={{0,24},{1,25},{2,26},{3,27},{4,28},{5,29},{6,30},{7,31},{8,16},{9,... | collective-permute-start | bytes 1179656 | tf_op jit(solution)/shard_map/ppermute | solution.py:34
  71.3 15.6 %collective-permute-start.3 = (bf16[512,384]{1,0:T(8,128)(2,1)S(1)}, bf16[512,384]{1,0:T(8,128)(2,1)S(1)}, u32[]{:S(2)}, u32[]{:S(2)}) collective-permute-start(bf16[512,384]{1,0:T(8,128)(2,1)S(1)} %bitcast.26), channel_id=1, source_target_pairs={{0,6},{1,7},{2,0},{3,1},{4,2},{5,3},{6,4},{7,5},{8,14},{9,15},{10,... | collective-permute-start | bytes 1179656 | tf_op jit(solution)/shard_map/ppermute | solution.py:34
  76.0 14.7 %collective-permute-start.5 = (bf16[512,384]{1,0:T(8,128)(2,1)S(1)}, bf16[512,384]{1,0:T(8,128)(2,1)S(1)}, u32[]{:S(2)}, u32[]{:S(2)}) collective-permute-start(bf16[512,384]{1,0:T(8,128)(2,1)S(1)} %bitcast.27), channel_id=1, source_target_pairs={{0,2},{1,3},{2,4},{3,5},{4,6},{5,7},{6,0},{7,1},{8,10},{9,11},{10,... | collective-permute-start | bytes 1179656 | tf_op jit(solution)/shard_map/ppermute | solution.py:34
  77.9 17.1 %collective-permute-start.7 = (bf16[512,384]{1,0:T(8,128)(2,1)S(1)}, bf16[512,384]{1,0:T(8,128)(2,1)S(1)}, u32[]{:S(2)}, u32[]{:S(2)}) collective-permute-start(bf16[512,384]{1,0:T(8,128)(2,1)S(1)} %bitcast.28), channel_id=1, source_target_pairs={{0,4},{1,5},{2,6},{3,7},{4,0},{5,1},{6,2},{7,3},{8,12},{9,13},{10,... | collective-permute-start | bytes 1179656 | tf_op jit(solution)/shard_map/ppermute | solution.py:34
  81.5 21.3 %collective-permute-start.4 = (bf16[512,384]{1,0:T(8,128)(2,1)S(1)}, bf16[512,384]{1,0:T(8,128)(2,1)S(1)}, u32[]{:S(2)}, u32[]{:S(2)}) collective-permute-start(bf16[512,384]{1,0:T(8,128)(2,1)S(1)} %collective-permute-done.2.refs_1_), channel_id=1, source_target_pairs={{0,6},{1,7},{2,0},{3,1},{4,2},{5,3},{6,4},{7,5},{8,14},{9,15},{10,... | collective-permute-start | bytes 1179656 | tf_op jit(solution)/shard_map/ppermute | solution.py:34
  84.4 22.7 %collective-permute-start.6 = (bf16[512,384]{1,0:T(8,128)(2,1)S(1)}, bf16[512,384]{1,0:T(8,128)(2,1)S(1)}, u32[]{:S(2)}, u32[]{:S(2)}) collective-permute-start(bf16[512,384]{1,0:T(8,128)(2,1)S(1)} %collective-permute-done.2.refs_1_), channel_id=1, source_target_pairs={{0,2},{1,3},{2,4},{3,5},{4,6},{5,7},{6,0},{7,1},{8,10},{9,11},{10,... | collective-permute-start | bytes 1179656 | tf_op jit(solution)/shard_map/ppermute | solution.py:34
  86.9 25.0 %collective-permute-start.8 = (bf16[512,384]{1,0:T(8,128)(2,1)S(1)}, bf16[512,384]{1,0:T(8,128)(2,1)S(1)}, u32[]{:S(2)}, u32[]{:S(2)}) collective-permute-start(bf16[512,384]{1,0:T(8,128)(2,1)S(1)} %collective-permute-done.2.refs_1_), channel_id=1, source_target_pairs={{0,4},{1,5},{2,6},{3,7},{4,0},{5,1},{6,2},{7,3},{8,12},{9,13},{10,... | collective-permute-start | bytes 1179656 | tf_op jit(solution)/shard_map/ppermute | solution.py:34
  124.3 13.8 %collective-permute-start.10 = (bf16[128,384]{1,0:T(8,128)(2,1)S(1)}, bf16[128,384]{1,0:T(8,128)(2,1)S(1)}, u32[]{:S(2)}, u32[]{:S(2)}) collective-permute-start(bf16[128,384]{1,0:T(8,128)(2,1)S(1)} %get-tuple-element.14), channel_id=1, source_target_pairs={{0,8},{1,16},{2,10},{3,18},{4,12},{5,20},{6,14},{7,22},{8,0},{9,24... | collective-permute-start | bytes 294920 | tf_op jit(solution)/shard_map/ppermute | solution.py:34
  129.2 8.9 %collective-permute-start.11 = (bf16[128,384]{1,0:T(8,128)(2,1)S(1)}, bf16[128,384]{1,0:T(8,128)(2,1)S(1)}, u32[]{:S(2)}, u32[]{:S(2)}) collective-permute-start(bf16[128,384]{1,0:T(8,128)(2,1)S(1)} %get-tuple-element.15), channel_id=1, source_target_pairs={{0,16},{1,8},{2,18},{3,10},{4,20},{5,12},{6,22},{7,14},{8,24},{9,0... | collective-permute-start | bytes 294920 | tf_op jit(solution)/shard_map/ppermute | solution.py:34
  132.2 6.6 %collective-permute-start.12 = (bf16[128,384]{1,0:T(8,128)(2,1)S(1)}, bf16[128,384]{1,0:T(8,128)(2,1)S(1)}, u32[]{:S(2)}, u32[]{:S(2)}) collective-permute-start(bf16[128,384]{1,0:T(8,128)(2,1)S(1)} %get-tuple-element.16), channel_id=1, source_target_pairs={{0,24},{1,0},{2,26},{3,2},{4,28},{5,4},{6,30},{7,6},{8,16},{9,8},{... | collective-permute-start | bytes 294920 | tf_op jit(solution)/shard_map/ppermute | solution.py:34
  134.2 7.1 %collective-permute-start.9 = (bf16[128,384]{1,0:T(8,128)(2,1)S(1)}, bf16[128,384]{1,0:T(8,128)(2,1)S(1)}, u32[]{:S(2)}, u32[]{:S(2)}) collective-permute-start(bf16[128,384]{1,0:T(8,128)(2,1)S(1)} %get-tuple-element.13), channel_id=1, source_target_pairs={{0,0},{1,24},{2,2},{3,26},{4,4},{5,28},{6,6},{7,30},{8,8},{9,16},{... | collective-permute-start | bytes 294920 | tf_op jit(solution)/shard_map/ppermute | solution.py:34
Sparse Core Ops, SparseCore 0:
  21.1 92.2 all-gather.2

commit v7 on v6

--- a/solution.py
+++ b/solution.py
@@ -17,7 +17,7 @@
 AXES = ("z", "x", "y", "c")
 SLICE = D // (NZ * NX)
 PART = 2 * SLICE
-CHUNK = D // 4
+CHUNK = D // 2
 SHIFTS = (0, 1, 3, 2)
 TOKENS = FRAMES * 8
 
@@ -57,7 +57,11 @@
     weight_copies = []
     for i in range(D // PART):
         rows = pl.ds(i * PART, PART)
-        weight_copies.append(pltpu.make_async_copy(gathered.at[i], weights.at[:, rows], w_sems.at[i]))
+        for j in range(3):
+            lanes = pl.ds(j * GROUP, GROUP)
+            weight_copies.append(
+                pltpu.make_async_copy(gathered.at[i, j], weights.at[rows, lanes], w_sems.at[i, j])
+            )
     for copy in token_copies + weight_copies:
         copy.start()
 
@@ -75,46 +79,51 @@
 
     for copy in token_copies:
         copy.wait()
-    per_chunk = CHUNK // PART
+    per_chunk = 3 * CHUNK // PART
     for chunk in range(D // CHUNK):
         for copy in weight_copies[chunk * per_chunk : (chunk + 1) * per_chunk]:
             copy.wait()
         features = pl.ds(chunk * CHUNK, CHUNK)
-        for j in range(3):
-            product = jnp.dot(
-                tokens[:, features], weights[j, features, :], preferred_element_type=jnp.float32
-            )
-            if chunk:
-                product = sums[j] + product
-            if chunk < D // CHUNK - 1:
-                sums[j] = product
-            else:
-                qkv[j] = product.astype(jnp.bfloat16)
+        product = jnp.dot(
+            tokens[:, features], weights[features, :], preferred_element_type=jnp.float32
+        )
+        if chunk:
+            product = sums[...] + product
+        if chunk < D // CHUNK - 1:
+            sums[...] = product
+        else:
+            qkv[...] = product.astype(jnp.bfloat16)
 
     scale = 1.0 / jnp.sqrt(jnp.float32(HD))
-    for h in range(GROUP // HD):
-        lanes = pl.ds(h * HD, HD)
-        for i in range(4):
-            rows = pl.ds(i * 128, 128)
-            width = (i + 1) * 128
-            scores = lax.dot_general(
-                qkv[0, rows, lanes],
-                qkv[1, pl.ds(0, width), lanes],
+    heads = range(GROUP // HD)
+    for i in range(4):
+        rows = pl.ds(i * 128, 128)
+        keys = pl.ds(0, (i + 1) * 128)
+        scores = [
+            lax.dot_general(
+                qkv[rows, pl.ds(h * HD, HD)],
+                qkv[keys, pl.ds(GROUP + h * HD, HD)],
                 (((1,), (1,)), ((), ())),
                 preferred_element_type=jnp.float32,
             )
-            scores = scores * scale + bias[rows, pl.ds(0, width)]
-            shares = jnp.exp(scores - jnp.max(scores, axis=-1, keepdims=True))
-            total = jnp.sum(shares, axis=-1, keepdims=True)
-            summed = jnp.dot(
-                shares.astype(jnp.bfloat16),
-                qkv[2, pl.ds(0, width), lanes],
+            for h in heads
+        ]
+        scores = [s * scale + bias[rows, keys] for s in scores]
+        shares = [jnp.exp(s - jnp.max(s, axis=-1, keepdims=True)) for s in scores]
+        totals = [jnp.sum(s, axis=-1, keepdims=True) for s in shares]
+        summed = [
+            jnp.dot(
+                s.astype(jnp.bfloat16),
+                qkv[keys, pl.ds(2 * GROUP + h * HD, HD)],
                 preferred_element_type=jnp.float32,
             )
-            attended = (summed / total).reshape(4, NX, 8, HD)
+            for h, s in zip(heads, shares)
+        ]
+        for h in heads:
+            attended = (summed[h] / totals[h]).reshape(4, NX, 8, HD)
             for to_x in range(NX):
                 part = attended[:, to_x].reshape(32, HD)
-                result[to_x, pl.ds(i * 32, 32), lanes] = part.astype(jnp.bfloat16)
+                result[to_x, pl.ds(i * 32, 32), pl.ds(h * HD, HD)] = part.astype(jnp.bfloat16)
     for k, out in enumerate(outs):
         out[...] = result[place_x ^ k]
 
@@ -128,13 +137,13 @@
         + [pl.BlockSpec(memory_space=pl.ANY)] * len(arrays),
         out_specs=[pl.BlockSpec(memory_space=pltpu.VMEM)] * NX,
         scratch_shapes=[
-            pltpu.VMEM((3, D, GROUP), jnp.bfloat16),
+            pltpu.VMEM((D, 3 * GROUP), jnp.bfloat16),
             pltpu.VMEM((TOKENS, D), jnp.bfloat16),
-            pltpu.VMEM((3, TOKENS, GROUP), jnp.float32),
-            pltpu.VMEM((3, TOKENS, GROUP), jnp.bfloat16),
+            pltpu.VMEM((TOKENS, 3 * GROUP), jnp.float32),
+            pltpu.VMEM((TOKENS, 3 * GROUP), jnp.bfloat16),
             pltpu.VMEM((TOKENS, TOKENS), jnp.float32),
             pltpu.VMEM((NX, TOKENS // NX, GROUP), jnp.bfloat16),
-            pltpu.SemaphoreType.DMA((D // PART,)),
+            pltpu.SemaphoreType.DMA((D // PART, 3)),
             pltpu.SemaphoreType.DMA((8,)),
         ],
         compiler_params=pltpu.CompilerParams(vmem_limit_bytes=44 * 1024 * 1024),

time: 175 us -> 175 us (level)
  no operation moved by 1% of the time
where the time goes in v7:
time: 175 us
  blocking collectives  70.9 us (41%)
  starting transfers between devices  46.3 us (26%)
  waiting for transfers between devices  30.2 us (17%)
  between operations  13.6 us (8%)
  Pallas kernels  10.6 us (6%)
  local copies, waits for them, and re-layouts  1.83 us (1%)
    ppermute x13, starting transfers between devices, permute(): return lax.ppermute(array, AXES, pairs)  46.3 us
    all_to_all x1, blocking collectives, per_device(): lax.all_to_all(packed, ('z', 'x'), split_axis=0, concat_axis=0, tiled=True)  45.1 us
    ppermute x13, waiting for transfers between devices, permute(): return lax.ppermute(array, AXES, pairs)  28.7 us
    all_to_all x1, blocking collectives, per_device(): lax.all_to_all(output, 'z', split_axis=0, concat_axis=0, tiled=True)  25.8 us
    pallas_call x1, Pallas kernels, project_and_attend(): pl.pallas_call(attend_kernel, out_shape=[jax.ShapeDtypeStruct((TOKENS //...  10.6 us
  transfers between devices with their start and end apart: 14, of which 8 were waited for; matrix products, arithmetic and copies ran while one was open for 1% of the time, Pallas kernels for 0%

profile of v7, /device:TPU:1, one launch (start us, length us, event | category | flops | bytes accessed | tf_op | source)
XLA Modules:
  0.0 174.6 jit_solution(13696082577467241402)
XLA Ops:
  6.5 5.9 %collective-permute-start = (bf16[3,48,384]{2,1,0:T(8,128)(2,1)}, bf16[3,48,384]{2,1,0:T(8,128)(2,1)S(1)}, u32[]{:S(2)}, u32[]{:S(2)}) collective-permute-start(bf16[3,48,384]{2,1,0:T(8,128)(2,1)} %bitcast.34), channel_id=1, source_target_pairs={{0,0},{1,24},{2,2},{3,26},{4,4},{5,28},{6,6},{7,30},{8,8},{9,16},{... | collective-permute-start | bytes 331784 | tf_op jit(solution)/shard_map/ppermute | solution.py:34
  12.4 2.2 %collective-permute-start.1 = (bf16[3,48,384]{2,1,0:T(8,128)(2,1)}, bf16[3,48,384]{2,1,0:T(8,128)(2,1)S(1)}, u32[]{:S(2)}, u32[]{:S(2)}) collective-permute-start(bf16[3,48,384]{2,1,0:T(8,128)(2,1)} %bitcast.35), channel_id=1, source_target_pairs={{0,8},{1,16},{2,10},{3,18},{4,12},{5,20},{6,14},{7,22},{8,0},{9,24... | collective-permute-start | bytes 331784 | tf_op jit(solution)/shard_map/ppermute | solution.py:34
  14.7 1.1 constant_dynamic-slice_fusion
  15.8 0.1 reverse_select_fusion
  16.0 4.3 %collective-permute-done.1 = bf16[3,48,384]{2,1,0:T(8,128)(2,1)S(1)} collective-permute-done((bf16[3,48,384]{2,1,0:T(8,128)(2,1)}, bf16[3,48,384]{2,1,0:T(8,128)(2,1)S(1)}, u32[]{:S(2)}, u32[]{:S(2)}) %collective-permute-start.1) | collective-permute-done | bytes 110624 | tf_op jit(solution)/shard_map/ppermute | solution.py:34
  20.2 0.7 maximum_select_fusion
  21.0 0.0 all-gather.3.cloned.1.call-update
  21.0 45.1 %all_to_all.10 = bf16[64,8,384]{2,1,0:T(8,128)(2,1)S(1)} all-to-all(bf16[64,8,384]{2,1,0:T(8,128)(2,1)S(1)} %bitcast.31), channel_id=1, replica_groups=mesh['z'=16,'x'=4,'y'=4,'c'=2] {'z','x'}, dimensions={0} | all-to-all | bytes 786432 | tf_op jit(solution)/shard_map/all_to_all | solution.py:176
  66.1 5.2 %collective-permute-start.2 = (bf16[512,384]{1,0:T(8,128)(2,1)S(1)}, bf16[512,384]{1,0:T(8,128)(2,1)S(1)}, u32[]{:S(2)}, u32[]{:S(2)}) collective-permute-start(bf16[512,384]{1,0:T(8,128)(2,1)S(1)} %bitcast.25), channel_id=1, source_target_pairs={{0,24},{1,25},{2,26},{3,27},{4,28},{5,29},{6,30},{7,31},{8,16},{9,... | collective-permute-start | bytes 1179656 | tf_op jit(solution)/shard_map/ppermute | solution.py:34
  71.3 4.6 %collective-permute-start.3 = (bf16[512,384]{1,0:T(8,128)(2,1)S(1)}, bf16[512,384]{1,0:T(8,128)(2,1)S(1)}, u32[]{:S(2)}, u32[]{:S(2)}) collective-permute-start(bf16[512,384]{1,0:T(8,128)(2,1)S(1)} %bitcast.26), channel_id=1, source_target_pairs={{0,6},{1,7},{2,0},{3,1},{4,2},{5,3},{6,4},{7,5},{8,14},{9,15},{10,... | collective-permute-start | bytes 1179656 | tf_op jit(solution)/shard_map/ppermute | solution.py:34
  76.0 1.9 %collective-permute-start.5 = (bf16[512,384]{1,0:T(8,128)(2,1)S(1)}, bf16[512,384]{1,0:T(8,128)(2,1)S(1)}, u32[]{:S(2)}, u32[]{:S(2)}) collective-permute-start(bf16[512,384]{1,0:T(8,128)(2,1)S(1)} %bitcast.27), channel_id=1, source_target_pairs={{0,2},{1,3},{2,4},{3,5},{4,6},{5,7},{6,0},{7,1},{8,10},{9,11},{10,... | collective-permute-start | bytes 1179656 | tf_op jit(solution)/shard_map/ppermute | solution.py:34
  77.9 3.6 %collective-permute-start.7 = (bf16[512,384]{1,0:T(8,128)(2,1)S(1)}, bf16[512,384]{1,0:T(8,128)(2,1)S(1)}, u32[]{:S(2)}, u32[]{:S(2)}) collective-permute-start(bf16[512,384]{1,0:T(8,128)(2,1)S(1)} %bitcast.28), channel_id=1, source_target_pairs={{0,4},{1,5},{2,6},{3,7},{4,0},{5,1},{6,2},{7,3},{8,12},{9,13},{10,... | collective-permute-start | bytes 1179656 | tf_op jit(solution)/shard_map/ppermute | solution.py:34
  81.5 2.9 %collective-permute-start.4 = (bf16[512,384]{1,0:T(8,128)(2,1)S(1)}, bf16[512,384]{1,0:T(8,128)(2,1)S(1)}, u32[]{:S(2)}, u32[]{:S(2)}) collective-permute-start(bf16[512,384]{1,0:T(8,128)(2,1)S(1)} %collective-permute-done.2.refs_1_), channel_id=1, source_target_pairs={{0,6},{1,7},{2,0},{3,1},{4,2},{5,3},{6,4},{7,5},{8,14},{9,15},{10,... | collective-permute-start | bytes 1179656 | tf_op jit(solution)/shard_map/ppermute | solution.py:34
  84.4 2.5 %collective-permute-start.6 = (bf16[512,384]{1,0:T(8,128)(2,1)S(1)}, bf16[512,384]{1,0:T(8,128)(2,1)S(1)}, u32[]{:S(2)}, u32[]{:S(2)}) collective-permute-start(bf16[512,384]{1,0:T(8,128)(2,1)S(1)} %collective-permute-done.2.refs_1_), channel_id=1, source_target_pairs={{0,2},{1,3},{2,4},{3,5},{4,6},{5,7},{6,0},{7,1},{8,10},{9,11},{10,... | collective-permute-start | bytes 1179656 | tf_op jit(solution)/shard_map/ppermute | solution.py:34
  86.9 3.7 %collective-permute-start.8 = (bf16[512,384]{1,0:T(8,128)(2,1)S(1)}, bf16[512,384]{1,0:T(8,128)(2,1)S(1)}, u32[]{:S(2)}, u32[]{:S(2)}) collective-permute-start(bf16[512,384]{1,0:T(8,128)(2,1)S(1)} %collective-permute-done.2.refs_1_), channel_id=1, source_target_pairs={{0,4},{1,5},{2,6},{3,7},{4,0},{5,1},{6,2},{7,3},{8,12},{9,13},{10,... | collective-permute-start | bytes 1179656 | tf_op jit(solution)/shard_map/ppermute | solution.py:34
  90.6 0.1 pad_add_fusion.place
  90.7 4.3 %collective-permute-done.7.refs_6_ = bf16[512,384]{1,0:T(8,128)(2,1)S(1)} collective-permute-done((bf16[512,384]{1,0:T(8,128)(2,1)S(1)}, bf16[512,384]{1,0:T(8,128)(2,1)S(1)}, u32[]{:S(2)}, u32[]{:S(2)}) %collective-permute-start.7) | collective-permute-done | bytes 393248 | tf_op jit(solution)/shard_map/ppermute | solution.py:34
  95.0 7.8 %collective-permute-done.4.refs_3_ = bf16[512,384]{1,0:T(8,128)(2,1)S(1)} collective-permute-done((bf16[512,384]{1,0:T(8,128)(2,1)S(1)}, bf16[512,384]{1,0:T(8,128)(2,1)S(1)}, u32[]{:S(2)}, u32[]{:S(2)}) %collective-permute-start.4) | collective-permute-done | bytes 393248 | tf_op jit(solution)/shard_map/ppermute | solution.py:34
  102.8 4.4 %collective-permute-done.6.refs_5_ = bf16[512,384]{1,0:T(8,128)(2,1)S(1)} collective-permute-done((bf16[512,384]{1,0:T(8,128)(2,1)S(1)}, bf16[512,384]{1,0:T(8,128)(2,1)S(1)}, u32[]{:S(2)}, u32[]{:S(2)}) %collective-permute-start.6) | collective-permute-done | bytes 393248 | tf_op jit(solution)/shard_map/ppermute | solution.py:34
  107.1 4.8 %collective-permute-done.8.refs_7_ = bf16[512,384]{1,0:T(8,128)(2,1)S(1)} collective-permute-done((bf16[512,384]{1,0:T(8,128)(2,1)S(1)}, bf16[512,384]{1,0:T(8,128)(2,1)S(1)}, u32[]{:S(2)}, u32[]{:S(2)}) %collective-permute-start.8) | collective-permute-done | bytes 393248 | tf_op jit(solution)/shard_map/ppermute | solution.py:34
  111.9 1.5 all-gather.3.cloned.1.call-done
  113.4 10.6 %shard_map.37 = (bf16[128,384]{1,0:T(8,128)(2,1)S(1)}, bf16[128,384]{1,0:T(8,128)(2,1)S(1)}, bf16[128,384]{1,0:T(8,128)(2,1)S(1)}, bf16[128,384]{1,0:T(8,128)(2,1)S(1)}) custom-call(s32[3]{0:T(128)S(1)} %pad_add_fusion.place, s32[8,8]{1,0:T(8,128)S(1)} %copy-done, bf16[32,3,96,384]{3,2,1,0:T(8,128)(2,1)} %bitcast.30, bf16[512,384]{1,0:T(8,128)(2,1)S(1)} %bitcast.29, ...), custom_call_target="tpu_custom_call" | custom-call | tf_op jit(solution)/shard_map/pallas_call | solution.py:133
  124.0 4.9 %collective-permute-start.10 = (bf16[128,384]{1,0:T(8,128)(2,1)S(1)}, bf16[128,384]{1,0:T(8,128)(2,1)S(1)}, u32[]{:S(2)}, u32[]{:S(2)}) collective-permute-start(bf16[128,384]{1,0:T(8,128)(2,1)S(1)} %get-tuple-element.14), channel_id=1, source_target_pairs={{0,8},{1,16},{2,10},{3,18},{4,12},{5,20},{6,14},{7,22},{8,0},{9,24... | collective-permute-start | bytes 294920 | tf_op jit(solution)/shard_map/ppermute | solution.py:34
  128.8 3.1 %collective-permute-start.11 = (bf16[128,384]{1,0:T(8,128)(2,1)S(1)}, bf16[128,384]{1,0:T(8,128)(2,1)S(1)}, u32[]{:S(2)}, u32[]{:S(2)}) collective-permute-start(bf16[128,384]{1,0:T(8,128)(2,1)S(1)} %get-tuple-element.15), channel_id=1, source_target_pairs={{0,16},{1,8},{2,18},{3,10},{4,20},{5,12},{6,22},{7,14},{8,24},{9,0... | collective-permute-start | bytes 294920 | tf_op jit(solution)/shard_map/ppermute | solution.py:34
  131.9 1.9 %collective-permute-start.12 = (bf16[128,384]{1,0:T(8,128)(2,1)S(1)}, bf16[128,384]{1,0:T(8,128)(2,1)S(1)}, u32[]{:S(2)}, u32[]{:S(2)}) collective-permute-start(bf16[128,384]{1,0:T(8,128)(2,1)S(1)} %get-tuple-element.16), channel_id=1, source_target_pairs={{0,24},{1,0},{2,26},{3,2},{4,28},{5,4},{6,30},{7,6},{8,16},{9,8},{... | collective-permute-start | bytes 294920 | tf_op jit(solution)/shard_map/ppermute | solution.py:34
  133.8 3.9 %collective-permute-start.9 = (bf16[128,384]{1,0:T(8,128)(2,1)S(1)}, bf16[128,384]{1,0:T(8,128)(2,1)S(1)}, u32[]{:S(2)}, u32[]{:S(2)}) collective-permute-start(bf16[128,384]{1,0:T(8,128)(2,1)S(1)} %get-tuple-element.13), channel_id=1, source_target_pairs={{0,0},{1,24},{2,2},{3,26},{4,4},{5,28},{6,6},{7,30},{8,8},{9,16},{... | collective-permute-start | bytes 294920 | tf_op jit(solution)/shard_map/ppermute | solution.py:34
  137.8 0.7 collective-permute-done.12
  138.5 2.5 %collective-permute-done.9 = bf16[128,384]{1,0:T(8,128)(2,1)S(1)} collective-permute-done((bf16[128,384]{1,0:T(8,128)(2,1)S(1)}, bf16[128,384]{1,0:T(8,128)(2,1)S(1)}, u32[]{:S(2)}, u32[]{:S(2)}) %collective-permute-start.9) | collective-permute-done | bytes 98336 | tf_op jit(solution)/shard_map/ppermute | solution.py:34
  141.0 0.1 select_bitcast_fusion.3
  141.1 0.1 pad_maximum_fusion.1
  141.1 25.8 %all_to_all.11 = bf16[16,4,8,384]{3,2,1,0:T(8,128)(2,1)S(1)} all-to-all(bf16[16,4,8,384]{3,2,1,0:T(8,128)(2,1)S(1)} %pad_maximum_fusion.1), channel_id=1, replica_groups=mesh['z'=16,'x'=4,'y'=4,'c'=2] {'z'}, dimensions={0} | all-to-all | bytes 786432 | tf_op jit(solution)/shard_map/all_to_all | solution.py:189
  167.0 0.7 copy.10
  (10 shorter events, 0.1 us)
Async XLA Ops:
  6.5 106.9 %copy-start = (s32[8,8]{1,0:T(8,128)S(1)}, s32[8,8]{1,0:T(8,128)}, u32[]{:S(2)}) copy-start(s32[8,8]{1,0:T(8,128)} %mask.1) | copy-start | bytes 772
  6.5 106.8 %all-gather.3.cloned.1.call-start = ((), (), s32[]{:S(2)}) async-start(), calls=%async_computation.2 | async-start | bytes 7299072 | tf_op jit(solution)/shard_map/all_gather | solution.py:175
  6.5 9.4 %collective-permute-start = (bf16[3,48,384]{2,1,0:T(8,128)(2,1)}, bf16[3,48,384]{2,1,0:T(8,128)(2,1)S(1)}, u32[]{:S(2)}, u32[]{:S(2)}) collective-permute-start(bf16[3,48,384]{2,1,0:T(8,128)(2,1)} %bitcast.34), channel_id=1, source_target_pairs={{0,0},{1,24},{2,2},{3,26},{4,4},{5,28},{6,6},{7,30},{8,8},{9,16},{... | collective-permute-start | bytes 331784 | tf_op jit(solution)/shard_map/ppermute | solution.py:34
  12.4 7.8 %collective-permute-start.1 = (bf16[3,48,384]{2,1,0:T(8,128)(2,1)}, bf16[3,48,384]{2,1,0:T(8,128)(2,1)S(1)}, u32[]{:S(2)}, u32[]{:S(2)}) collective-permute-start(bf16[3,48,384]{2,1,0:T(8,128)(2,1)} %bitcast.35), channel_id=1, source_target_pairs={{0,8},{1,16},{2,10},{3,18},{4,12},{5,20},{6,14},{7,22},{8,0},{9,24... | collective-permute-start | bytes 331784 | tf_op jit(solution)/shard_map/ppermute | solution.py:34
  66.1 15.4 %collective-permute-start.2 = (bf16[512,384]{1,0:T(8,128)(2,1)S(1)}, bf16[512,384]{1,0:T(8,128)(2,1)S(1)}, u32[]{:S(2)}, u32[]{:S(2)}) collective-permute-start(bf16[512,384]{1,0:T(8,128)(2,1)S(1)} %bitcast.25), channel_id=1, source_target_pairs={{0,24},{1,25},{2,26},{3,27},{4,28},{5,29},{6,30},{7,31},{8,16},{9,... | collective-permute-start | bytes 1179656 | tf_op jit(solution)/shard_map/ppermute | solution.py:34
  71.3 15.6 %collective-permute-start.3 = (bf16[512,384]{1,0:T(8,128)(2,1)S(1)}, bf16[512,384]{1,0:T(8,128)(2,1)S(1)}, u32[]{:S(2)}, u32[]{:S(2)}) collective-permute-start(bf16[512,384]{1,0:T(8,128)(2,1)S(1)} %bitcast.26), channel_id=1, source_target_pairs={{0,6},{1,7},{2,0},{3,1},{4,2},{5,3},{6,4},{7,5},{8,14},{9,15},{10,... | collective-permute-start | bytes 1179656 | tf_op jit(solution)/shard_map/ppermute | solution.py:34
  76.0 14.7 %collective-permute-start.5 = (bf16[512,384]{1,0:T(8,128)(2,1)S(1)}, bf16[512,384]{1,0:T(8,128)(2,1)S(1)}, u32[]{:S(2)}, u32[]{:S(2)}) collective-permute-start(bf16[512,384]{1,0:T(8,128)(2,1)S(1)} %bitcast.27), channel_id=1, source_target_pairs={{0,2},{1,3},{2,4},{3,5},{4,6},{5,7},{6,0},{7,1},{8,10},{9,11},{10,... | collective-permute-start | bytes 1179656 | tf_op jit(solution)/shard_map/ppermute | solution.py:34
  77.9 17.1 %collective-permute-start.7 = (bf16[512,384]{1,0:T(8,128)(2,1)S(1)}, bf16[512,384]{1,0:T(8,128)(2,1)S(1)}, u32[]{:S(2)}, u32[]{:S(2)}) collective-permute-start(bf16[512,384]{1,0:T(8,128)(2,1)S(1)} %bitcast.28), channel_id=1, source_target_pairs={{0,4},{1,5},{2,6},{3,7},{4,0},{5,1},{6,2},{7,3},{8,12},{9,13},{10,... | collective-permute-start | bytes 1179656 | tf_op jit(solution)/shard_map/ppermute | solution.py:34
  81.5 21.3 %collective-permute-start.4 = (bf16[512,384]{1,0:T(8,128)(2,1)S(1)}, bf16[512,384]{1,0:T(8,128)(2,1)S(1)}, u32[]{:S(2)}, u32[]{:S(2)}) collective-permute-start(bf16[512,384]{1,0:T(8,128)(2,1)S(1)} %collective-permute-done.2.refs_1_), channel_id=1, source_target_pairs={{0,6},{1,7},{2,0},{3,1},{4,2},{5,3},{6,4},{7,5},{8,14},{9,15},{10,... | collective-permute-start | bytes 1179656 | tf_op jit(solution)/shard_map/ppermute | solution.py:34
  84.4 22.7 %collective-permute-start.6 = (bf16[512,384]{1,0:T(8,128)(2,1)S(1)}, bf16[512,384]{1,0:T(8,128)(2,1)S(1)}, u32[]{:S(2)}, u32[]{:S(2)}) collective-permute-start(bf16[512,384]{1,0:T(8,128)(2,1)S(1)} %collective-permute-done.2.refs_1_), channel_id=1, source_target_pairs={{0,2},{1,3},{2,4},{3,5},{4,6},{5,7},{6,0},{7,1},{8,10},{9,11},{10,... | collective-permute-start | bytes 1179656 | tf_op jit(solution)/shard_map/ppermute | solution.py:34
  86.9 25.0 %collective-permute-start.8 = (bf16[512,384]{1,0:T(8,128)(2,1)S(1)}, bf16[512,384]{1,0:T(8,128)(2,1)S(1)}, u32[]{:S(2)}, u32[]{:S(2)}) collective-permute-start(bf16[512,384]{1,0:T(8,128)(2,1)S(1)} %collective-permute-done.2.refs_1_), channel_id=1, source_target_pairs={{0,4},{1,5},{2,6},{3,7},{4,0},{5,1},{6,2},{7,3},{8,12},{9,13},{10,... | collective-permute-start | bytes 1179656 | tf_op jit(solution)/shard_map/ppermute | solution.py:34
  124.0 13.8 %collective-permute-start.10 = (bf16[128,384]{1,0:T(8,128)(2,1)S(1)}, bf16[128,384]{1,0:T(8,128)(2,1)S(1)}, u32[]{:S(2)}, u32[]{:S(2)}) collective-permute-start(bf16[128,384]{1,0:T(8,128)(2,1)S(1)} %get-tuple-element.14), channel_id=1, source_target_pairs={{0,8},{1,16},{2,10},{3,18},{4,12},{5,20},{6,14},{7,22},{8,0},{9,24... | collective-permute-start | bytes 294920 | tf_op jit(solution)/shard_map/ppermute | solution.py:34
  128.8 8.9 %collective-permute-start.11 = (bf16[128,384]{1,0:T(8,128)(2,1)S(1)}, bf16[128,384]{1,0:T(8,128)(2,1)S(1)}, u32[]{:S(2)}, u32[]{:S(2)}) collective-permute-start(bf16[128,384]{1,0:T(8,128)(2,1)S(1)} %get-tuple-element.15), channel_id=1, source_target_pairs={{0,16},{1,8},{2,18},{3,10},{4,20},{5,12},{6,22},{7,14},{8,24},{9,0... | collective-permute-start | bytes 294920 | tf_op jit(solution)/shard_map/ppermute | solution.py:34
  131.9 6.6 %collective-permute-start.12 = (bf16[128,384]{1,0:T(8,128)(2,1)S(1)}, bf16[128,384]{1,0:T(8,128)(2,1)S(1)}, u32[]{:S(2)}, u32[]{:S(2)}) collective-permute-start(bf16[128,384]{1,0:T(8,128)(2,1)S(1)} %get-tuple-element.16), channel_id=1, source_target_pairs={{0,24},{1,0},{2,26},{3,2},{4,28},{5,4},{6,30},{7,6},{8,16},{9,8},{... | collective-permute-start | bytes 294920 | tf_op jit(solution)/shard_map/ppermute | solution.py:34
  133.8 7.1 %collective-permute-start.9 = (bf16[128,384]{1,0:T(8,128)(2,1)S(1)}, bf16[128,384]{1,0:T(8,128)(2,1)S(1)}, u32[]{:S(2)}, u32[]{:S(2)}) collective-permute-start(bf16[128,384]{1,0:T(8,128)(2,1)S(1)} %get-tuple-element.13), channel_id=1, source_target_pairs={{0,0},{1,24},{2,2},{3,26},{4,4},{5,28},{6,6},{7,30},{8,8},{9,16},{... | collective-permute-start | bytes 294920 | tf_op jit(solution)/shard_map/ppermute | solution.py:34
Sparse Core Ops, SparseCore 0:
  21.1 92.2 all-gather.2

commit v8 on v7

--- a/solution.py
+++ b/solution.py
@@ -17,7 +17,7 @@
 AXES = ("z", "x", "y", "c")
 SLICE = D // (NZ * NX)
 PART = 2 * SLICE
-CHUNK = D // 2
+CHUNK = D // 4
 SHIFTS = (0, 1, 3, 2)
 TOKENS = FRAMES * 8
 
@@ -55,12 +55,14 @@
         at = pl.multiple_of((2 * source + half) * GROUP, GROUP)
         token_copies.append(pltpu.make_async_copy(piece, tokens.at[:, pl.ds(at, GROUP)], x_sems.at[i]))
     weight_copies = []
-    for i in range(D // PART):
-        rows = pl.ds(i * PART, PART)
+    for chunk in range(D // CHUNK):
+        parts = pl.ds(chunk * (CHUNK // PART), CHUNK // PART)
         for j in range(3):
             lanes = pl.ds(j * GROUP, GROUP)
             weight_copies.append(
-                pltpu.make_async_copy(gathered.at[i, j], weights.at[rows, lanes], w_sems.at[i, j])
+                pltpu.make_async_copy(
+                    gathered.at[parts, j], weights.at[parts, :, lanes], w_sems.at[chunk, j]
+                )
             )
     for copy in token_copies + weight_copies:
         copy.start()
@@ -79,13 +81,15 @@
 
     for copy in token_copies:
         copy.wait()
-    per_chunk = 3 * CHUNK // PART
     for chunk in range(D // CHUNK):
-        for copy in weight_copies[chunk * per_chunk : (chunk + 1) * per_chunk]:
+        for copy in weight_copies[3 * chunk : 3 * chunk + 3]:
             copy.wait()
         features = pl.ds(chunk * CHUNK, CHUNK)
+        parts = pl.ds(chunk * (CHUNK // PART), CHUNK // PART)
         product = jnp.dot(
-            tokens[:, features], weights[features, :], preferred_element_type=jnp.float32
+            tokens[:, features],
+            weights[parts].reshape(CHUNK, 3 * GROUP),
+            preferred_element_type=jnp.float32,
         )
         if chunk:
             product = sums[...] + product
@@ -137,13 +141,13 @@
         + [pl.BlockSpec(memory_space=pl.ANY)] * len(arrays),
         out_specs=[pl.BlockSpec(memory_space=pltpu.VMEM)] * NX,
         scratch_shapes=[
-            pltpu.VMEM((D, 3 * GROUP), jnp.bfloat16),
+            pltpu.VMEM((D // PART, PART, 3 * GROUP), jnp.bfloat16),
             pltpu.VMEM((TOKENS, D), jnp.bfloat16),
             pltpu.VMEM((TOKENS, 3 * GROUP), jnp.float32),
             pltpu.VMEM((TOKENS, 3 * GROUP), jnp.bfloat16),
             pltpu.VMEM((TOKENS, TOKENS), jnp.float32),
             pltpu.VMEM((NX, TOKENS // NX, GROUP), jnp.bfloat16),
-            pltpu.SemaphoreType.DMA((D // PART, 3)),
+            pltpu.SemaphoreType.DMA((D // CHUNK, 3)),
             pltpu.SemaphoreType.DMA((8,)),
         ],
         compiler_params=pltpu.CompilerParams(vmem_limit_bytes=44 * 1024 * 1024),

time: 175 us -> 174 us (level)
  no operation moved by 1% of the time
where the time goes in v8:
time: 174 us; the launch traced here: 173 us
  blocking collectives  70.9 us (41%)
  starting transfers between devices  46.3 us (27%)
  waiting for transfers between devices  30.2 us (17%)
  between operations  13.6 us (8%)
  Pallas kernels  9.32 us (5%)
  local copies, waits for them, and re-layouts  1.83 us (1%)
    ppermute x13, starting transfers between devices, permute(): return lax.ppermute(array, AXES, pairs)  46.3 us
    all_to_all x1, blocking collectives, per_device(): lax.all_to_all(packed, ('z', 'x'), split_axis=0, concat_axis=0, tiled=True)  45.1 us
    ppermute x13, waiting for transfers between devices, permute(): return lax.ppermute(array, AXES, pairs)  28.7 us
    all_to_all x1, blocking collectives, per_device(): lax.all_to_all(output, 'z', split_axis=0, concat_axis=0, tiled=True)  25.8 us
    pallas_call x1, Pallas kernels, project_and_attend(): pl.pallas_call(attend_kernel, out_shape=[jax.ShapeDtypeStruct((TOKENS //...  9.32 us
  transfers between devices with their start and end apart: 14, of which 8 were waited for; matrix products, arithmetic and copies ran while one was open for 1% of the time, Pallas kernels for 0%

profile of v8, /device:TPU:1, one launch (start us, length us, event | category | flops | bytes accessed | tf_op | source)
XLA Modules:
  0.0 173.3 jit_solution(3145415309911544996)
XLA Ops:
  6.5 5.9 %collective-permute-start = (bf16[3,48,384]{2,1,0:T(8,128)(2,1)}, bf16[3,48,384]{2,1,0:T(8,128)(2,1)S(1)}, u32[]{:S(2)}, u32[]{:S(2)}) collective-permute-start(bf16[3,48,384]{2,1,0:T(8,128)(2,1)} %bitcast.34), channel_id=1, source_target_pairs={{0,0},{1,24},{2,2},{3,26},{4,4},{5,28},{6,6},{7,30},{8,8},{9,16},{... | collective-permute-start | bytes 331784 | tf_op jit(solution)/shard_map/ppermute | solution.py:34
  12.4 2.2 %collective-permute-start.1 = (bf16[3,48,384]{2,1,0:T(8,128)(2,1)}, bf16[3,48,384]{2,1,0:T(8,128)(2,1)S(1)}, u32[]{:S(2)}, u32[]{:S(2)}) collective-permute-start(bf16[3,48,384]{2,1,0:T(8,128)(2,1)} %bitcast.35), channel_id=1, source_target_pairs={{0,8},{1,16},{2,10},{3,18},{4,12},{5,20},{6,14},{7,22},{8,0},{9,24... | collective-permute-start | bytes 331784 | tf_op jit(solution)/shard_map/ppermute | solution.py:34
  14.7 1.1 constant_dynamic-slice_fusion
  15.8 0.1 reverse_select_fusion
  16.0 4.3 %collective-permute-done.1 = bf16[3,48,384]{2,1,0:T(8,128)(2,1)S(1)} collective-permute-done((bf16[3,48,384]{2,1,0:T(8,128)(2,1)}, bf16[3,48,384]{2,1,0:T(8,128)(2,1)S(1)}, u32[]{:S(2)}, u32[]{:S(2)}) %collective-permute-start.1) | collective-permute-done | bytes 110624 | tf_op jit(solution)/shard_map/ppermute | solution.py:34
  20.2 0.7 maximum_select_fusion
  21.0 0.0 all-gather.3.cloned.1.call-update
  21.0 45.1 %all_to_all.10 = bf16[64,8,384]{2,1,0:T(8,128)(2,1)S(1)} all-to-all(bf16[64,8,384]{2,1,0:T(8,128)(2,1)S(1)} %bitcast.31), channel_id=1, replica_groups=mesh['z'=16,'x'=4,'y'=4,'c'=2] {'z','x'}, dimensions={0} | all-to-all | bytes 786432 | tf_op jit(solution)/shard_map/all_to_all | solution.py:180
  66.1 5.2 %collective-permute-start.2 = (bf16[512,384]{1,0:T(8,128)(2,1)S(1)}, bf16[512,384]{1,0:T(8,128)(2,1)S(1)}, u32[]{:S(2)}, u32[]{:S(2)}) collective-permute-start(bf16[512,384]{1,0:T(8,128)(2,1)S(1)} %bitcast.25), channel_id=1, source_target_pairs={{0,24},{1,25},{2,26},{3,27},{4,28},{5,29},{6,30},{7,31},{8,16},{9,... | collective-permute-start | bytes 1179656 | tf_op jit(solution)/shard_map/ppermute | solution.py:34
  71.3 4.6 %collective-permute-start.3 = (bf16[512,384]{1,0:T(8,128)(2,1)S(1)}, bf16[512,384]{1,0:T(8,128)(2,1)S(1)}, u32[]{:S(2)}, u32[]{:S(2)}) collective-permute-start(bf16[512,384]{1,0:T(8,128)(2,1)S(1)} %bitcast.26), channel_id=1, source_target_pairs={{0,6},{1,7},{2,0},{3,1},{4,2},{5,3},{6,4},{7,5},{8,14},{9,15},{10,... | collective-permute-start | bytes 1179656 | tf_op jit(solution)/shard_map/ppermute | solution.py:34
  76.0 1.9 %collective-permute-start.5 = (bf16[512,384]{1,0:T(8,128)(2,1)S(1)}, bf16[512,384]{1,0:T(8,128)(2,1)S(1)}, u32[]{:S(2)}, u32[]{:S(2)}) collective-permute-start(bf16[512,384]{1,0:T(8,128)(2,1)S(1)} %bitcast.27), channel_id=1, source_target_pairs={{0,2},{1,3},{2,4},{3,5},{4,6},{5,7},{6,0},{7,1},{8,10},{9,11},{10,... | collective-permute-start | bytes 1179656 | tf_op jit(solution)/shard_map/ppermute | solution.py:34
  77.9 3.6 %collective-permute-start.7 = (bf16[512,384]{1,0:T(8,128)(2,1)S(1)}, bf16[512,384]{1,0:T(8,128)(2,1)S(1)}, u32[]{:S(2)}, u32[]{:S(2)}) collective-permute-start(bf16[512,384]{1,0:T(8,128)(2,1)S(1)} %bitcast.28), channel_id=1, source_target_pairs={{0,4},{1,5},{2,6},{3,7},{4,0},{5,1},{6,2},{7,3},{8,12},{9,13},{10,... | collective-permute-start | bytes 1179656 | tf_op jit(solution)/shard_map/ppermute | solution.py:34
  81.5 2.9 %collective-permute-start.4 = (bf16[512,384]{1,0:T(8,128)(2,1)S(1)}, bf16[512,384]{1,0:T(8,128)(2,1)S(1)}, u32[]{:S(2)}, u32[]{:S(2)}) collective-permute-start(bf16[512,384]{1,0:T(8,128)(2,1)S(1)} %collective-permute-done.2.refs_1_), channel_id=1, source_target_pairs={{0,6},{1,7},{2,0},{3,1},{4,2},{5,3},{6,4},{7,5},{8,14},{9,15},{10,... | collective-permute-start | bytes 1179656 | tf_op jit(solution)/shard_map/ppermute | solution.py:34
  84.4 2.5 %collective-permute-start.6 = (bf16[512,384]{1,0:T(8,128)(2,1)S(1)}, bf16[512,384]{1,0:T(8,128)(2,1)S(1)}, u32[]{:S(2)}, u32[]{:S(2)}) collective-permute-start(bf16[512,384]{1,0:T(8,128)(2,1)S(1)} %collective-permute-done.2.refs_1_), channel_id=1, source_target_pairs={{0,2},{1,3},{2,4},{3,5},{4,6},{5,7},{6,0},{7,1},{8,10},{9,11},{10,... | collective-permute-start | bytes 1179656 | tf_op jit(solution)/shard_map/ppermute | solution.py:34
  86.9 3.7 %collective-permute-start.8 = (bf16[512,384]{1,0:T(8,128)(2,1)S(1)}, bf16[512,384]{1,0:T(8,128)(2,1)S(1)}, u32[]{:S(2)}, u32[]{:S(2)}) collective-permute-start(bf16[512,384]{1,0:T(8,128)(2,1)S(1)} %collective-permute-done.2.refs_1_), channel_id=1, source_target_pairs={{0,4},{1,5},{2,6},{3,7},{4,0},{5,1},{6,2},{7,3},{8,12},{9,13},{10,... | collective-permute-start | bytes 1179656 | tf_op jit(solution)/shard_map/ppermute | solution.py:34
  90.6 0.1 pad_add_fusion.place
  90.7 4.3 %collective-permute-done.7.refs_6_ = bf16[512,384]{1,0:T(8,128)(2,1)S(1)} collective-permute-done((bf16[512,384]{1,0:T(8,128)(2,1)S(1)}, bf16[512,384]{1,0:T(8,128)(2,1)S(1)}, u32[]{:S(2)}, u32[]{:S(2)}) %collective-permute-start.7) | collective-permute-done | bytes 393248 | tf_op jit(solution)/shard_map/ppermute | solution.py:34
  95.0 7.8 %collective-permute-done.4.refs_3_ = bf16[512,384]{1,0:T(8,128)(2,1)S(1)} collective-permute-done((bf16[512,384]{1,0:T(8,128)(2,1)S(1)}, bf16[512,384]{1,0:T(8,128)(2,1)S(1)}, u32[]{:S(2)}, u32[]{:S(2)}) %collective-permute-start.4) | collective-permute-done | bytes 393248 | tf_op jit(solution)/shard_map/ppermute | solution.py:34
  102.8 4.4 %collective-permute-done.6.refs_5_ = bf16[512,384]{1,0:T(8,128)(2,1)S(1)} collective-permute-done((bf16[512,384]{1,0:T(8,128)(2,1)S(1)}, bf16[512,384]{1,0:T(8,128)(2,1)S(1)}, u32[]{:S(2)}, u32[]{:S(2)}) %collective-permute-start.6) | collective-permute-done | bytes 393248 | tf_op jit(solution)/shard_map/ppermute | solution.py:34
  107.1 4.8 %collective-permute-done.8.refs_7_ = bf16[512,384]{1,0:T(8,128)(2,1)S(1)} collective-permute-done((bf16[512,384]{1,0:T(8,128)(2,1)S(1)}, bf16[512,384]{1,0:T(8,128)(2,1)S(1)}, u32[]{:S(2)}, u32[]{:S(2)}) %collective-permute-start.8) | collective-permute-done | bytes 393248 | tf_op jit(solution)/shard_map/ppermute | solution.py:34
  111.9 1.5 all-gather.3.cloned.1.call-done
  113.4 9.3 %shard_map.37 = (bf16[128,384]{1,0:T(8,128)(2,1)S(1)}, bf16[128,384]{1,0:T(8,128)(2,1)S(1)}, bf16[128,384]{1,0:T(8,128)(2,1)S(1)}, bf16[128,384]{1,0:T(8,128)(2,1)S(1)}) custom-call(s32[3]{0:T(128)S(1)} %pad_add_fusion.place, s32[8,8]{1,0:T(8,128)S(1)} %copy-done, bf16[32,3,96,384]{3,2,1,0:T(8,128)(2,1)} %bitcast.30, bf16[512,384]{1,0:T(8,128)(2,1)S(1)} %bitcast.29, ...), custom_call_target="tpu_custom_call" | custom-call | tf_op jit(solution)/shard_map/pallas_call | solution.py:137
  122.7 4.9 %collective-permute-start.10 = (bf16[128,384]{1,0:T(8,128)(2,1)S(1)}, bf16[128,384]{1,0:T(8,128)(2,1)S(1)}, u32[]{:S(2)}, u32[]{:S(2)}) collective-permute-start(bf16[128,384]{1,0:T(8,128)(2,1)S(1)} %get-tuple-element.14), channel_id=1, source_target_pairs={{0,8},{1,16},{2,10},{3,18},{4,12},{5,20},{6,14},{7,22},{8,0},{9,24... | collective-permute-start | bytes 294920 | tf_op jit(solution)/shard_map/ppermute | solution.py:34
  127.6 3.1 %collective-permute-start.11 = (bf16[128,384]{1,0:T(8,128)(2,1)S(1)}, bf16[128,384]{1,0:T(8,128)(2,1)S(1)}, u32[]{:S(2)}, u32[]{:S(2)}) collective-permute-start(bf16[128,384]{1,0:T(8,128)(2,1)S(1)} %get-tuple-element.15), channel_id=1, source_target_pairs={{0,16},{1,8},{2,18},{3,10},{4,20},{5,12},{6,22},{7,14},{8,24},{9,0... | collective-permute-start | bytes 294920 | tf_op jit(solution)/shard_map/ppermute | solution.py:34
  130.7 1.9 %collective-permute-start.12 = (bf16[128,384]{1,0:T(8,128)(2,1)S(1)}, bf16[128,384]{1,0:T(8,128)(2,1)S(1)}, u32[]{:S(2)}, u32[]{:S(2)}) collective-permute-start(bf16[128,384]{1,0:T(8,128)(2,1)S(1)} %get-tuple-element.16), channel_id=1, source_target_pairs={{0,24},{1,0},{2,26},{3,2},{4,28},{5,4},{6,30},{7,6},{8,16},{9,8},{... | collective-permute-start | bytes 294920 | tf_op jit(solution)/shard_map/ppermute | solution.py:34
  132.6 3.9 %collective-permute-start.9 = (bf16[128,384]{1,0:T(8,128)(2,1)S(1)}, bf16[128,384]{1,0:T(8,128)(2,1)S(1)}, u32[]{:S(2)}, u32[]{:S(2)}) collective-permute-start(bf16[128,384]{1,0:T(8,128)(2,1)S(1)} %get-tuple-element.13), channel_id=1, source_target_pairs={{0,0},{1,24},{2,2},{3,26},{4,4},{5,28},{6,6},{7,30},{8,8},{9,16},{... | collective-permute-start | bytes 294920 | tf_op jit(solution)/shard_map/ppermute | solution.py:34
  136.5 0.7 collective-permute-done.12
  137.2 2.5 %collective-permute-done.9 = bf16[128,384]{1,0:T(8,128)(2,1)S(1)} collective-permute-done((bf16[128,384]{1,0:T(8,128)(2,1)S(1)}, bf16[128,384]{1,0:T(8,128)(2,1)S(1)}, u32[]{:S(2)}, u32[]{:S(2)}) %collective-permute-start.9) | collective-permute-done | bytes 98336 | tf_op jit(solution)/shard_map/ppermute | solution.py:34
  139.8 0.1 select_bitcast_fusion.3
  139.8 0.1 pad_maximum_fusion.1
  139.9 25.8 %all_to_all.11 = bf16[16,4,8,384]{3,2,1,0:T(8,128)(2,1)S(1)} all-to-all(bf16[16,4,8,384]{3,2,1,0:T(8,128)(2,1)S(1)} %pad_maximum_fusion.1), channel_id=1, replica_groups=mesh['z'=16,'x'=4,'y'=4,'c'=2] {'z'}, dimensions={0} | all-to-all | bytes 786432 | tf_op jit(solution)/shard_map/all_to_all | solution.py:193
  165.7 0.7 copy.10
  (10 shorter events, 0.1 us)
Async XLA Ops:
  6.5 106.9 %copy-start = (s32[8,8]{1,0:T(8,128)S(1)}, s32[8,8]{1,0:T(8,128)}, u32[]{:S(2)}) copy-start(s32[8,8]{1,0:T(8,128)} %mask.1) | copy-start | bytes 772
  6.5 106.8 %all-gather.3.cloned.1.call-start = ((), (), s32[]{:S(2)}) async-start(), calls=%async_computation.2 | async-start | bytes 7299072 | tf_op jit(solution)/shard_map/all_gather | solution.py:179
  6.5 9.4 %collective-permute-start = (bf16[3,48,384]{2,1,0:T(8,128)(2,1)}, bf16[3,48,384]{2,1,0:T(8,128)(2,1)S(1)}, u32[]{:S(2)}, u32[]{:S(2)}) collective-permute-start(bf16[3,48,384]{2,1,0:T(8,128)(2,1)} %bitcast.34), channel_id=1, source_target_pairs={{0,0},{1,24},{2,2},{3,26},{4,4},{5,28},{6,6},{7,30},{8,8},{9,16},{... | collective-permute-start | bytes 331784 | tf_op jit(solution)/shard_map/ppermute | solution.py:34
  12.4 7.8 %collective-permute-start.1 = (bf16[3,48,384]{2,1,0:T(8,128)(2,1)}, bf16[3,48,384]{2,1,0:T(8,128)(2,1)S(1)}, u32[]{:S(2)}, u32[]{:S(2)}) collective-permute-start(bf16[3,48,384]{2,1,0:T(8,128)(2,1)} %bitcast.35), channel_id=1, source_target_pairs={{0,8},{1,16},{2,10},{3,18},{4,12},{5,20},{6,14},{7,22},{8,0},{9,24... | collective-permute-start | bytes 331784 | tf_op jit(solution)/shard_map/ppermute | solution.py:34
  66.1 15.4 %collective-permute-start.2 = (bf16[512,384]{1,0:T(8,128)(2,1)S(1)}, bf16[512,384]{1,0:T(8,128)(2,1)S(1)}, u32[]{:S(2)}, u32[]{:S(2)}) collective-permute-start(bf16[512,384]{1,0:T(8,128)(2,1)S(1)} %bitcast.25), channel_id=1, source_target_pairs={{0,24},{1,25},{2,26},{3,27},{4,28},{5,29},{6,30},{7,31},{8,16},{9,... | collective-permute-start | bytes 1179656 | tf_op jit(solution)/shard_map/ppermute | solution.py:34
  71.3 15.6 %collective-permute-start.3 = (bf16[512,384]{1,0:T(8,128)(2,1)S(1)}, bf16[512,384]{1,0:T(8,128)(2,1)S(1)}, u32[]{:S(2)}, u32[]{:S(2)}) collective-permute-start(bf16[512,384]{1,0:T(8,128)(2,1)S(1)} %bitcast.26), channel_id=1, source_target_pairs={{0,6},{1,7},{2,0},{3,1},{4,2},{5,3},{6,4},{7,5},{8,14},{9,15},{10,... | collective-permute-start | bytes 1179656 | tf_op jit(solution)/shard_map/ppermute | solution.py:34
  76.0 14.7 %collective-permute-start.5 = (bf16[512,384]{1,0:T(8,128)(2,1)S(1)}, bf16[512,384]{1,0:T(8,128)(2,1)S(1)}, u32[]{:S(2)}, u32[]{:S(2)}) collective-permute-start(bf16[512,384]{1,0:T(8,128)(2,1)S(1)} %bitcast.27), channel_id=1, source_target_pairs={{0,2},{1,3},{2,4},{3,5},{4,6},{5,7},{6,0},{7,1},{8,10},{9,11},{10,... | collective-permute-start | bytes 1179656 | tf_op jit(solution)/shard_map/ppermute | solution.py:34
  77.9 17.1 %collective-permute-start.7 = (bf16[512,384]{1,0:T(8,128)(2,1)S(1)}, bf16[512,384]{1,0:T(8,128)(2,1)S(1)}, u32[]{:S(2)}, u32[]{:S(2)}) collective-permute-start(bf16[512,384]{1,0:T(8,128)(2,1)S(1)} %bitcast.28), channel_id=1, source_target_pairs={{0,4},{1,5},{2,6},{3,7},{4,0},{5,1},{6,2},{7,3},{8,12},{9,13},{10,... | collective-permute-start | bytes 1179656 | tf_op jit(solution)/shard_map/ppermute | solution.py:34
  81.5 21.3 %collective-permute-start.4 = (bf16[512,384]{1,0:T(8,128)(2,1)S(1)}, bf16[512,384]{1,0:T(8,128)(2,1)S(1)}, u32[]{:S(2)}, u32[]{:S(2)}) collective-permute-start(bf16[512,384]{1,0:T(8,128)(2,1)S(1)} %collective-permute-done.2.refs_1_), channel_id=1, source_target_pairs={{0,6},{1,7},{2,0},{3,1},{4,2},{5,3},{6,4},{7,5},{8,14},{9,15},{10,... | collective-permute-start | bytes 1179656 | tf_op jit(solution)/shard_map/ppermute | solution.py:34
  84.4 22.7 %collective-permute-start.6 = (bf16[512,384]{1,0:T(8,128)(2,1)S(1)}, bf16[512,384]{1,0:T(8,128)(2,1)S(1)}, u32[]{:S(2)}, u32[]{:S(2)}) collective-permute-start(bf16[512,384]{1,0:T(8,128)(2,1)S(1)} %collective-permute-done.2.refs_1_), channel_id=1, source_target_pairs={{0,2},{1,3},{2,4},{3,5},{4,6},{5,7},{6,0},{7,1},{8,10},{9,11},{10,... | collective-permute-start | bytes 1179656 | tf_op jit(solution)/shard_map/ppermute | solution.py:34
  86.9 25.0 %collective-permute-start.8 = (bf16[512,384]{1,0:T(8,128)(2,1)S(1)}, bf16[512,384]{1,0:T(8,128)(2,1)S(1)}, u32[]{:S(2)}, u32[]{:S(2)}) collective-permute-start(bf16[512,384]{1,0:T(8,128)(2,1)S(1)} %collective-permute-done.2.refs_1_), channel_id=1, source_target_pairs={{0,4},{1,5},{2,6},{3,7},{4,0},{5,1},{6,2},{7,3},{8,12},{9,13},{10,... | collective-permute-start | bytes 1179656 | tf_op jit(solution)/shard_map/ppermute | solution.py:34
  122.7 13.8 %collective-permute-start.10 = (bf16[128,384]{1,0:T(8,128)(2,1)S(1)}, bf16[128,384]{1,0:T(8,128)(2,1)S(1)}, u32[]{:S(2)}, u32[]{:S(2)}) collective-permute-start(bf16[128,384]{1,0:T(8,128)(2,1)S(1)} %get-tuple-element.14), channel_id=1, source_target_pairs={{0,8},{1,16},{2,10},{3,18},{4,12},{5,20},{6,14},{7,22},{8,0},{9,24... | collective-permute-start | bytes 294920 | tf_op jit(solution)/shard_map/ppermute | solution.py:34
  127.6 8.9 %collective-permute-start.11 = (bf16[128,384]{1,0:T(8,128)(2,1)S(1)}, bf16[128,384]{1,0:T(8,128)(2,1)S(1)}, u32[]{:S(2)}, u32[]{:S(2)}) collective-permute-start(bf16[128,384]{1,0:T(8,128)(2,1)S(1)} %get-tuple-element.15), channel_id=1, source_target_pairs={{0,16},{1,8},{2,18},{3,10},{4,20},{5,12},{6,22},{7,14},{8,24},{9,0... | collective-permute-start | bytes 294920 | tf_op jit(solution)/shard_map/ppermute | solution.py:34
  130.7 6.6 %collective-permute-start.12 = (bf16[128,384]{1,0:T(8,128)(2,1)S(1)}, bf16[128,384]{1,0:T(8,128)(2,1)S(1)}, u32[]{:S(2)}, u32[]{:S(2)}) collective-permute-start(bf16[128,384]{1,0:T(8,128)(2,1)S(1)} %get-tuple-element.16), channel_id=1, source_target_pairs={{0,24},{1,0},{2,26},{3,2},{4,28},{5,4},{6,30},{7,6},{8,16},{9,8},{... | collective-permute-start | bytes 294920 | tf_op jit(solution)/shard_map/ppermute | solution.py:34
  132.6 7.1 %collective-permute-start.9 = (bf16[128,384]{1,0:T(8,128)(2,1)S(1)}, bf16[128,384]{1,0:T(8,128)(2,1)S(1)}, u32[]{:S(2)}, u32[]{:S(2)}) collective-permute-start(bf16[128,384]{1,0:T(8,128)(2,1)S(1)} %get-tuple-element.13), channel_id=1, source_target_pairs={{0,0},{1,24},{2,2},{3,26},{4,4},{5,28},{6,6},{7,30},{8,8},{9,16},{... | collective-permute-start | bytes 294920 | tf_op jit(solution)/shard_map/ppermute | solution.py:34
Sparse Core Ops, SparseCore 0:
  21.1 92.2 all-gather.2

commit v9 on v8

--- a/solution.py
+++ b/solution.py
@@ -1,5 +1,3 @@
-import functools
-
 import jax
 import jax.numpy as jnp
 from jax import lax
@@ -34,8 +32,8 @@
     return lax.ppermute(array, AXES, pairs)
 
 
-def home(z, x, y, c, k=0):
-    return (z, (x if c == x // 2 else 3 - x) ^ k, y, x // 2)
+def home(z, x, y, c):
+    return (z, x if c == x // 2 else 3 - x, y, x // 2)
 
 
 def second(z, x, y, c):
@@ -44,9 +42,9 @@
 
 
 def attend_kernel(place, mask, gathered, *refs):
-    pieces, outs = refs[:8], refs[8:12]
-    weights, tokens, sums, qkv, bias, result, w_sems, x_sems = refs[12:]
-    y, group, place_x = place[0], place[1], place[2]
+    pieces, out = refs[:8], refs[8]
+    weights, tokens, sums, qkv, bias, w_sems, x_sems = refs[9:]
+    y, group = place[0], place[1]
 
     token_copies = []
     for i, piece in enumerate(pieces):
@@ -126,27 +124,25 @@
         for h in heads:
             attended = (summed[h] / totals[h]).reshape(4, NX, 8, HD)
             for to_x in range(NX):
-                part = attended[:, to_x].reshape(32, HD)
-                result[to_x, pl.ds(i * 32, 32), pl.ds(h * HD, HD)] = part.astype(jnp.bfloat16)
-    for k, out in enumerate(outs):
-        out[...] = result[place_x ^ k]
+                part = attended[:, to_x].reshape(32, HD).astype(jnp.bfloat16)
+                for core in range(NC):
+                    out[NC * to_x + core, pl.ds(i * 32, 32), pl.ds(h * HD, HD)] = part
 
 
 def project_and_attend(place, span_mask, gathered, pieces):
     arrays = [gathered, *pieces]
     return pl.pallas_call(
         attend_kernel,
-        out_shape=[jax.ShapeDtypeStruct((TOKENS // NX, GROUP), jnp.bfloat16)] * NX,
+        out_shape=jax.ShapeDtypeStruct((NX * NC, TOKENS // NX, GROUP), jnp.bfloat16),
         in_specs=[pl.BlockSpec(memory_space=pltpu.SMEM)] * 2
         + [pl.BlockSpec(memory_space=pl.ANY)] * len(arrays),
-        out_specs=[pl.BlockSpec(memory_space=pltpu.VMEM)] * NX,
+        out_specs=pl.BlockSpec(memory_space=pltpu.VMEM),
         scratch_shapes=[
             pltpu.VMEM((D // PART, PART, 3 * GROUP), jnp.bfloat16),
             pltpu.VMEM((TOKENS, D), jnp.bfloat16),
             pltpu.VMEM((TOKENS, 3 * GROUP), jnp.float32),
             pltpu.VMEM((TOKENS, 3 * GROUP), jnp.bfloat16),
             pltpu.VMEM((TOKENS, TOKENS), jnp.float32),
-            pltpu.VMEM((NX, TOKENS // NX, GROUP), jnp.bfloat16),
             pltpu.SemaphoreType.DMA((D // CHUNK, 3)),
             pltpu.SemaphoreType.DMA((8,)),
         ],
@@ -185,10 +181,11 @@
         for block in (spread, partner):
             pieces.append(permute(block, lambda z, x, y, c, k=shift: (z, x, y - k, c)))
 
-    place = jnp.stack([y, group, slot]).astype(jnp.int32)
-    parts = project_and_attend(place, span_mask, gathered, pieces)
-    parts = [permute(part, functools.partial(home, k=k)) for k, part in enumerate(parts)]
-    parts = [lax.select_n(x, *[parts[k ^ at] for k in range(NX)]) for at in range(NX)]
+    place = jnp.stack([y, group]).astype(jnp.int32)
+    output = project_and_attend(place, span_mask, gathered, pieces)
+    output = lax.all_to_all(output, ("x", "c"), split_axis=0, concat_axis=0, tiled=True)
+    order = ((0, 6), (2, 4), (3, 5), (1, 7))
+    parts = [jnp.where(c == 0, output[low], output[high]) for low, high in order]
     output = jnp.stack([part.reshape(NZ, 8, GROUP) for part in parts], axis=1)
     output = lax.all_to_all(output, "z", split_axis=0, concat_axis=0, tiled=True)
     return output.reshape(1, NZ * NX * 8, GROUP)

time: 174 us -> 177 us (1.017)
  the two profiles are of different devices: /device:TPU:1 before, /device:TPU:16 now
where the time goes in v9:
time: 177 us; the launch traced here: 176 us
  blocking collectives  99.4 us (56%)
  starting transfers between devices  29.9 us (17%)
  waiting for transfers between devices  21.1 us (12%)
  between operations  13.5 us (8%)
  Pallas kernels  9.3 us (5%)
  local copies, waits for them, and re-layouts  1.82 us (1%)
    all_to_all x1, blocking collectives, per_device(): lax.all_to_all(packed, ('z', 'x'), split_axis=0, concat_axis=0, tiled=True)  52.5 us
    all_to_all x1, blocking collectives, per_device(): lax.all_to_all(output, 'z', split_axis=0, concat_axis=0, tiled=True)  30.5 us
    ppermute x9, starting transfers between devices, permute(): return lax.ppermute(array, AXES, pairs)  29.9 us
    ppermute x9, waiting for transfers between devices, permute(): return lax.ppermute(array, AXES, pairs)  18.4 us
    all_to_all x1, blocking collectives, per_device(): lax.all_to_all(output, ('x', 'c'), split_axis=0, concat_axis=0, tiled=True)  16.4 us
    pallas_call x1, Pallas kernels, project_and_attend(): pl.pallas_call(attend_kernel, out_shape=jax.ShapeDtypeStruct((NX * NC, TO...  9.3 us
  transfers between devices with their start and end apart: 10, of which 6 were waited for; matrix products, arithmetic and copies ran while one was open for 1% of the time, Pallas kernels for 0%

profile of v9, /device:TPU:16, one launch (start us, length us, event | category | flops | bytes accessed | tf_op | source)
XLA Modules:
  0.0 176.1 jit_solution(15091077809777304535)
XLA Ops:
  6.5 0.0 all-gather.3.cloned.1.call-start
  6.5 3.5 %collective-permute-start.1 = (bf16[3,48,384]{2,1,0:T(8,128)(2,1)}, bf16[3,48,384]{2,1,0:T(8,128)(2,1)S(1)}, u32[]{:S(2)}, u32[]{:S(2)}) collective-permute-start(bf16[3,48,384]{2,1,0:T(8,128)(2,1)} %bitcast.33), channel_id=1, source_target_pairs={{0,8},{1,16},{2,10},{3,18},{4,12},{5,20},{6,14},{7,22},{8,0},{9,24... | collective-permute-start | bytes 331784 | tf_op jit(solution)/shard_map/ppermute | solution.py:32
  10.1 1.6 collective-permute-start
  11.6 1.1 constant_dynamic-slice_fusion
  12.7 0.1 reverse_select_fusion
  12.9 0.8 collective-permute-done.1
  13.7 0.0 collective-permute-done
  13.7 0.7 maximum_select_fusion
  14.4 0.0 all-gather.3.cloned.1.call-update
  14.4 52.5 %all_to_all.15 = bf16[64,8,384]{2,1,0:T(8,128)(2,1)S(1)} all-to-all(bf16[64,8,384]{2,1,0:T(8,128)(2,1)S(1)} %bitcast.30), channel_id=1, replica_groups=mesh['z'=16,'x'=4,'y'=4,'c'=2] {'z','x'}, dimensions={0} | all-to-all | bytes 786432 | tf_op jit(solution)/shard_map/all_to_all | solution.py:176
  66.9 4.6 %collective-permute-start.2 = (bf16[512,384]{1,0:T(8,128)(2,1)S(1)}, bf16[512,384]{1,0:T(8,128)(2,1)S(1)}, u32[]{:S(2)}, u32[]{:S(2)}) collective-permute-start(bf16[512,384]{1,0:T(8,128)(2,1)S(1)} %bitcast.24), channel_id=1, source_target_pairs={{0,24},{1,25},{2,26},{3,27},{4,28},{5,29},{6,30},{7,31},{8,16},{9,... | collective-permute-start | bytes 1179656 | tf_op jit(solution)/shard_map/ppermute | solution.py:32
  71.5 2.2 %collective-permute-start.7 = (bf16[512,384]{1,0:T(8,128)(2,1)S(1)}, bf16[512,384]{1,0:T(8,128)(2,1)S(1)}, u32[]{:S(2)}, u32[]{:S(2)}) collective-permute-start(bf16[512,384]{1,0:T(8,128)(2,1)S(1)} %bitcast.25), channel_id=1, source_target_pairs={{0,4},{1,5},{2,6},{3,7},{4,0},{5,1},{6,2},{7,3},{8,12},{9,13},{10,... | collective-permute-start | bytes 1179656 | tf_op jit(solution)/shard_map/ppermute | solution.py:32
  73.7 4.1 %collective-permute-start.5 = (bf16[512,384]{1,0:T(8,128)(2,1)S(1)}, bf16[512,384]{1,0:T(8,128)(2,1)S(1)}, u32[]{:S(2)}, u32[]{:S(2)}) collective-permute-start(bf16[512,384]{1,0:T(8,128)(2,1)S(1)} %bitcast.26), channel_id=1, source_target_pairs={{0,2},{1,3},{2,4},{3,5},{4,6},{5,7},{6,0},{7,1},{8,10},{9,11},{10,... | collective-permute-start | bytes 1179656 | tf_op jit(solution)/shard_map/ppermute | solution.py:32
  77.8 2.3 %collective-permute-start.3 = (bf16[512,384]{1,0:T(8,128)(2,1)S(1)}, bf16[512,384]{1,0:T(8,128)(2,1)S(1)}, u32[]{:S(2)}, u32[]{:S(2)}) collective-permute-start(bf16[512,384]{1,0:T(8,128)(2,1)S(1)} %bitcast.27), channel_id=1, source_target_pairs={{0,6},{1,7},{2,0},{3,1},{4,2},{5,3},{6,4},{7,5},{8,14},{9,15},{10,... | collective-permute-start | bytes 1179656 | tf_op jit(solution)/shard_map/ppermute | solution.py:32
  80.0 0.0 collective-permute-done.2.refs_1_
  80.0 5.9 %collective-permute-start.8 = (bf16[512,384]{1,0:T(8,128)(2,1)S(1)}, bf16[512,384]{1,0:T(8,128)(2,1)S(1)}, u32[]{:S(2)}, u32[]{:S(2)}) collective-permute-start(bf16[512,384]{1,0:T(8,128)(2,1)S(1)} %collective-permute-done.2.refs_1_), channel_id=1, source_target_pairs={{0,4},{1,5},{2,6},{3,7},{4,0},{5,1},{6,2},{7,3},{8,12},{9,13},{10,... | collective-permute-start | bytes 1179656 | tf_op jit(solution)/shard_map/ppermute | solution.py:32
  85.9 2.0 %collective-permute-start.6 = (bf16[512,384]{1,0:T(8,128)(2,1)S(1)}, bf16[512,384]{1,0:T(8,128)(2,1)S(1)}, u32[]{:S(2)}, u32[]{:S(2)}) collective-permute-start(bf16[512,384]{1,0:T(8,128)(2,1)S(1)} %collective-permute-done.2.refs_1_), channel_id=1, source_target_pairs={{0,2},{1,3},{2,4},{3,5},{4,6},{5,7},{6,0},{7,1},{8,10},{9,11},{10,... | collective-permute-start | bytes 1179656 | tf_op jit(solution)/shard_map/ppermute | solution.py:32
  88.0 0.0 collective-permute-done.7.refs_6_
  88.0 3.8 %collective-permute-start.4 = (bf16[512,384]{1,0:T(8,128)(2,1)S(1)}, bf16[512,384]{1,0:T(8,128)(2,1)S(1)}, u32[]{:S(2)}, u32[]{:S(2)}) collective-permute-start(bf16[512,384]{1,0:T(8,128)(2,1)S(1)} %collective-permute-done.2.refs_1_), channel_id=1, source_target_pairs={{0,6},{1,7},{2,0},{3,1},{4,2},{5,3},{6,4},{7,5},{8,14},{9,15},{10,... | collective-permute-start | bytes 1179656 | tf_op jit(solution)/shard_map/ppermute | solution.py:32
  91.8 0.1 pad_add_fusion.place
  91.9 3.6 %collective-permute-done.5.refs_4_ = bf16[512,384]{1,0:T(8,128)(2,1)S(1)} collective-permute-done((bf16[512,384]{1,0:T(8,128)(2,1)S(1)}, bf16[512,384]{1,0:T(8,128)(2,1)S(1)}, u32[]{:S(2)}, u32[]{:S(2)}) %collective-permute-start.5) | collective-permute-done | bytes 393248 | tf_op jit(solution)/shard_map/ppermute | solution.py:32
  95.5 2.1 %collective-permute-done.3.refs_2_ = bf16[512,384]{1,0:T(8,128)(2,1)S(1)} collective-permute-done((bf16[512,384]{1,0:T(8,128)(2,1)S(1)}, bf16[512,384]{1,0:T(8,128)(2,1)S(1)}, u32[]{:S(2)}, u32[]{:S(2)}) %collective-permute-start.3) | collective-permute-done | bytes 393248 | tf_op jit(solution)/shard_map/ppermute | solution.py:32
  97.5 6.3 %collective-permute-done.8.refs_7_ = bf16[512,384]{1,0:T(8,128)(2,1)S(1)} collective-permute-done((bf16[512,384]{1,0:T(8,128)(2,1)S(1)}, bf16[512,384]{1,0:T(8,128)(2,1)S(1)}, u32[]{:S(2)}, u32[]{:S(2)}) %collective-permute-start.8) | collective-permute-done | bytes 393248 | tf_op jit(solution)/shard_map/ppermute | solution.py:32
  103.9 5.6 %collective-permute-done.6.refs_5_ = bf16[512,384]{1,0:T(8,128)(2,1)S(1)} collective-permute-done((bf16[512,384]{1,0:T(8,128)(2,1)S(1)}, bf16[512,384]{1,0:T(8,128)(2,1)S(1)}, u32[]{:S(2)}, u32[]{:S(2)}) %collective-permute-start.6) | collective-permute-done | bytes 393248 | tf_op jit(solution)/shard_map/ppermute | solution.py:32
  109.5 0.0 collective-permute-done.4.refs_3_
  109.5 2.6 %all-gather.3.cloned.1.call-done = bf16[96,96,384]{2,1,0:T(8,128)(2,1)} async-done(((bf16[3,96,384]{2,1,0:T(8,128)(2,1)}), bf16[96,96,384]{2,1,0:T(8,128)(2,1)}) %all-gather.3.cloned.1.call-update) | async-done | bytes 7077904 | tf_op jit(solution)/shard_map/all_gather | solution.py:175
  112.1 0.0 copy-done
  112.1 9.3 %shard_map.37 = bf16[8,128,384]{2,1,0:T(8,128)(2,1)S(1)} custom-call(s32[2]{0:T(128)S(1)} %pad_add_fusion.place, s32[8,8]{1,0:T(8,128)S(1)} %copy-done, bf16[32,3,96,384]{3,2,1,0:T(8,128)(2,1)} %bitcast.29, bf16[512,384]{1,0:T(8,128)(2,1)S(1)} %bitcast.28, bf16[512,384]{1,0:T(8,128)(2,1)S(1)} %collective-permute-done.2.refs_1_, ...), custom_call_target="tpu_custom_call" | custom-call | tf_op jit(solution)/shard_map/pallas_call | solution.py:134
  121.4 16.4 %all_to_all.16 = bf16[8,128,384]{2,1,0:T(8,128)(2,1)S(1)} all-to-all(bf16[8,128,384]{2,1,0:T(8,128)(2,1)S(1)} %shard_map.37), channel_id=1, replica_groups=mesh['z'=16,'x'=4,'y'=4,'c'=2] {'x','c'}, dimensions={0} | all-to-all | bytes 1572864 | tf_op jit(solution)/shard_map/all_to_all | solution.py:186
  137.9 0.1 pad_maximum_fusion.1
  138.0 30.5 %all_to_all.17 = bf16[16,4,8,384]{3,2,1,0:T(8,128)(2,1)S(1)} all-to-all(bf16[16,4,8,384]{3,2,1,0:T(8,128)(2,1)S(1)} %pad_maximum_fusion.1), channel_id=1, replica_groups=mesh['z'=16,'x'=4,'y'=4,'c'=2] {'z'}, dimensions={0} | all-to-all | bytes 786432 | tf_op jit(solution)/shard_map/all_to_all | solution.py:190
  168.5 0.7 copy.10
  (3 shorter events, 0.1 us)
Async XLA Ops:
  6.5 105.6 %copy-start = (s32[8,8]{1,0:T(8,128)S(1)}, s32[8,8]{1,0:T(8,128)}, u32[]{:S(2)}) copy-start(s32[8,8]{1,0:T(8,128)} %mask.1) | copy-start | bytes 772
  6.5 105.6 %all-gather.3.cloned.1.call-start = ((), (), s32[]{:S(2)}) async-start(), calls=%async_computation.3 | async-start | bytes 7299072 | tf_op jit(solution)/shard_map/all_gather | solution.py:175
  6.5 7.1 %collective-permute-start.1 = (bf16[3,48,384]{2,1,0:T(8,128)(2,1)}, bf16[3,48,384]{2,1,0:T(8,128)(2,1)S(1)}, u32[]{:S(2)}, u32[]{:S(2)}) collective-permute-start(bf16[3,48,384]{2,1,0:T(8,128)(2,1)} %bitcast.33), channel_id=1, source_target_pairs={{0,8},{1,16},{2,10},{3,18},{4,12},{5,20},{6,14},{7,22},{8,0},{9,24... | collective-permute-start | bytes 331784 | tf_op jit(solution)/shard_map/ppermute | solution.py:32
  10.1 3.6 %collective-permute-start = (bf16[3,48,384]{2,1,0:T(8,128)(2,1)}, bf16[3,48,384]{2,1,0:T(8,128)(2,1)S(1)}, u32[]{:S(2)}, u32[]{:S(2)}) collective-permute-start(bf16[3,48,384]{2,1,0:T(8,128)(2,1)} %bitcast.34), channel_id=1, source_target_pairs={{0,0},{1,24},{2,2},{3,26},{4,4},{5,28},{6,6},{7,30},{8,8},{9,16},{... | collective-permute-start | bytes 331784 | tf_op jit(solution)/shard_map/ppermute | solution.py:32
  66.9 13.1 %collective-permute-start.2 = (bf16[512,384]{1,0:T(8,128)(2,1)S(1)}, bf16[512,384]{1,0:T(8,128)(2,1)S(1)}, u32[]{:S(2)}, u32[]{:S(2)}) collective-permute-start(bf16[512,384]{1,0:T(8,128)(2,1)S(1)} %bitcast.24), channel_id=1, source_target_pairs={{0,24},{1,25},{2,26},{3,27},{4,28},{5,29},{6,30},{7,31},{8,16},{9,... | collective-permute-start | bytes 1179656 | tf_op jit(solution)/shard_map/ppermute | solution.py:32
  71.5 16.5 %collective-permute-start.7 = (bf16[512,384]{1,0:T(8,128)(2,1)S(1)}, bf16[512,384]{1,0:T(8,128)(2,1)S(1)}, u32[]{:S(2)}, u32[]{:S(2)}) collective-permute-start(bf16[512,384]{1,0:T(8,128)(2,1)S(1)} %bitcast.25), channel_id=1, source_target_pairs={{0,4},{1,5},{2,6},{3,7},{4,0},{5,1},{6,2},{7,3},{8,12},{9,13},{10,... | collective-permute-start | bytes 1179656 | tf_op jit(solution)/shard_map/ppermute | solution.py:32
  73.7 21.8 %collective-permute-start.5 = (bf16[512,384]{1,0:T(8,128)(2,1)S(1)}, bf16[512,384]{1,0:T(8,128)(2,1)S(1)}, u32[]{:S(2)}, u32[]{:S(2)}) collective-permute-start(bf16[512,384]{1,0:T(8,128)(2,1)S(1)} %bitcast.26), channel_id=1, source_target_pairs={{0,2},{1,3},{2,4},{3,5},{4,6},{5,7},{6,0},{7,1},{8,10},{9,11},{10,... | collective-permute-start | bytes 1179656 | tf_op jit(solution)/shard_map/ppermute | solution.py:32
  77.8 19.8 %collective-permute-start.3 = (bf16[512,384]{1,0:T(8,128)(2,1)S(1)}, bf16[512,384]{1,0:T(8,128)(2,1)S(1)}, u32[]{:S(2)}, u32[]{:S(2)}) collective-permute-start(bf16[512,384]{1,0:T(8,128)(2,1)S(1)} %bitcast.27), channel_id=1, source_target_pairs={{0,6},{1,7},{2,0},{3,1},{4,2},{5,3},{6,4},{7,5},{8,14},{9,15},{10,... | collective-permute-start | bytes 1179656 | tf_op jit(solution)/shard_map/ppermute | solution.py:32
  80.0 23.8 %collective-permute-start.8 = (bf16[512,384]{1,0:T(8,128)(2,1)S(1)}, bf16[512,384]{1,0:T(8,128)(2,1)S(1)}, u32[]{:S(2)}, u32[]{:S(2)}) collective-permute-start(bf16[512,384]{1,0:T(8,128)(2,1)S(1)} %collective-permute-done.2.refs_1_), channel_id=1, source_target_pairs={{0,4},{1,5},{2,6},{3,7},{4,0},{5,1},{6,2},{7,3},{8,12},{9,13},{10,... | collective-permute-start | bytes 1179656 | tf_op jit(solution)/shard_map/ppermute | solution.py:32
  85.9 23.6 %collective-permute-start.6 = (bf16[512,384]{1,0:T(8,128)(2,1)S(1)}, bf16[512,384]{1,0:T(8,128)(2,1)S(1)}, u32[]{:S(2)}, u32[]{:S(2)}) collective-permute-start(bf16[512,384]{1,0:T(8,128)(2,1)S(1)} %collective-permute-done.2.refs_1_), channel_id=1, source_target_pairs={{0,2},{1,3},{2,4},{3,5},{4,6},{5,7},{6,0},{7,1},{8,10},{9,11},{10,... | collective-permute-start | bytes 1179656 | tf_op jit(solution)/shard_map/ppermute | solution.py:32
  88.0 21.5 %collective-permute-start.4 = (bf16[512,384]{1,0:T(8,128)(2,1)S(1)}, bf16[512,384]{1,0:T(8,128)(2,1)S(1)}, u32[]{:S(2)}, u32[]{:S(2)}) collective-permute-start(bf16[512,384]{1,0:T(8,128)(2,1)S(1)} %collective-permute-done.2.refs_1_), channel_id=1, source_target_pairs={{0,6},{1,7},{2,0},{3,1},{4,2},{5,3},{6,4},{7,5},{8,14},{9,15},{10,... | collective-permute-start | bytes 1179656 | tf_op jit(solution)/shard_map/ppermute | solution.py:32
Sparse Core Ops, SparseCore 0:
  14.6 97.5 all-gather.2

commit v10 on v9

--- a/solution.py
+++ b/solution.py
@@ -1,3 +1,5 @@
+import functools
+
 import jax
 import jax.numpy as jnp
 from jax import lax
@@ -32,8 +34,8 @@
     return lax.ppermute(array, AXES, pairs)
 
 
-def home(z, x, y, c):
-    return (z, x if c == x // 2 else 3 - x, y, x // 2)
+def home(z, x, y, c, k=0):
+    return (z, (x if c == x // 2 else 3 - x) ^ k, y, x // 2)
 
 
 def second(z, x, y, c):
@@ -122,18 +124,14 @@
             for h, s in zip(heads, shares)
         ]
         for h in heads:
-            attended = (summed[h] / totals[h]).reshape(4, NX, 8, HD)
-            for to_x in range(NX):
-                part = attended[:, to_x].reshape(32, HD).astype(jnp.bfloat16)
-                for core in range(NC):
-                    out[NC * to_x + core, pl.ds(i * 32, 32), pl.ds(h * HD, HD)] = part
+            out[rows, pl.ds(h * HD, HD)] = (summed[h] / totals[h]).astype(jnp.bfloat16)
 
 
 def project_and_attend(place, span_mask, gathered, pieces):
     arrays = [gathered, *pieces]
     return pl.pallas_call(
         attend_kernel,
-        out_shape=jax.ShapeDtypeStruct((NX * NC, TOKENS // NX, GROUP), jnp.bfloat16),
+        out_shape=jax.ShapeDtypeStruct((TOKENS, GROUP), jnp.bfloat16),
         in_specs=[pl.BlockSpec(memory_space=pltpu.SMEM)] * 2
         + [pl.BlockSpec(memory_space=pl.ANY)] * len(arrays),
         out_specs=pl.BlockSpec(memory_space=pltpu.VMEM),
@@ -183,12 +181,14 @@
 
     place = jnp.stack([y, group]).astype(jnp.int32)
     output = project_and_attend(place, span_mask, gathered, pieces)
-    output = lax.all_to_all(output, ("x", "c"), split_axis=0, concat_axis=0, tiled=True)
-    order = ((0, 6), (2, 4), (3, 5), (1, 7))
-    parts = [jnp.where(c == 0, output[low], output[high]) for low, high in order]
-    output = jnp.stack([part.reshape(NZ, 8, GROUP) for part in parts], axis=1)
+    output = output.reshape(NZ, NX, 8, GROUP)
     output = lax.all_to_all(output, "z", split_axis=0, concat_axis=0, tiled=True)
-    return output.reshape(1, NZ * NX * 8, GROUP)
+    parts = []
+    for k in range(NX):
+        part = lax.dynamic_index_in_dim(output, slot ^ k, axis=1, keepdims=False)
+        parts.append(permute(part, functools.partial(home, k=k)))
+    parts = [lax.select_n(x, *[parts[k ^ at] for k in range(NX)]) for at in range(NX)]
+    return jnp.stack(parts, axis=1).reshape(1, NZ * NX * 8, GROUP)
 
 
 def solution(mesh):

time: 177 us -> 179 us (1.011)
  the two profiles are of different devices: /device:TPU:16 before, /device:TPU:1 now
where the time goes in v10:
time: 179 us
  starting transfers between devices  60.1 us (34%)
  waiting for transfers between devices  46.9 us (26%)
  blocking collectives  45.1 us (25%)
  between operations  13.6 us (8%)
  Pallas kernels  10 us (6%)
  other arithmetic  1.89 us (1%)
    ppermute x13, starting transfers between devices, permute(): return lax.ppermute(array, AXES, pairs)  53.5 us
    all_to_all x1, blocking collectives, per_device(): lax.all_to_all(packed, ('z', 'x'), split_axis=0, concat_axis=0, tiled=True)  45.1 us
    ppermute x13, waiting for transfers between devices, permute(): return lax.ppermute(array, AXES, pairs)  28 us
    all_to_all x1, waiting for transfers between devices, per_device(): lax.all_to_all(output, 'z', split_axis=0, concat_axis=0, tiled=True)  17.3 us
    pallas_call x1, Pallas kernels, project_and_attend(): pl.pallas_call(attend_kernel, out_shape=jax.ShapeDtypeStruct((TOKENS, GRO...  10 us
    all_to_all x1, starting transfers between devices, per_device(): lax.all_to_all(output, 'z', split_axis=0, concat_axis=0, tiled=True)  6.6 us
  transfers between devices with their start and end apart: 15, of which 8 were waited for; matrix products, arithmetic and copies ran while one was open for 1% of the time, Pallas kernels for 0%

profile of v10, /device:TPU:1, one launch (start us, length us, event | category | flops | bytes accessed | tf_op | source)
XLA Modules:
  0.0 178.8 jit_solution(12234929396565492563)
XLA Ops:
  6.5 5.9 %collective-permute-start = (bf16[3,48,384]{2,1,0:T(8,128)(2,1)}, bf16[3,48,384]{2,1,0:T(8,128)(2,1)S(1)}, u32[]{:S(2)}, u32[]{:S(2)}) collective-permute-start(bf16[3,48,384]{2,1,0:T(8,128)(2,1)} %bitcast.39), channel_id=1, source_target_pairs={{0,0},{1,24},{2,2},{3,26},{4,4},{5,28},{6,6},{7,30},{8,8},{9,16},{... | collective-permute-start | bytes 331784 | tf_op jit(solution)/shard_map/ppermute | solution.py:34
  12.4 2.2 %collective-permute-start.1 = (bf16[3,48,384]{2,1,0:T(8,128)(2,1)}, bf16[3,48,384]{2,1,0:T(8,128)(2,1)S(1)}, u32[]{:S(2)}, u32[]{:S(2)}) collective-permute-start(bf16[3,48,384]{2,1,0:T(8,128)(2,1)} %bitcast.40), channel_id=1, source_target_pairs={{0,8},{1,16},{2,10},{3,18},{4,12},{5,20},{6,14},{7,22},{8,0},{9,24... | collective-permute-start | bytes 331784 | tf_op jit(solution)/shard_map/ppermute | solution.py:34
  14.7 1.1 constant_dynamic-slice_fusion
  15.8 0.1 reverse_select_fusion
  15.9 0.0 collective-permute-done
  16.0 4.3 %collective-permute-done.1 = bf16[3,48,384]{2,1,0:T(8,128)(2,1)S(1)} collective-permute-done((bf16[3,48,384]{2,1,0:T(8,128)(2,1)}, bf16[3,48,384]{2,1,0:T(8,128)(2,1)S(1)}, u32[]{:S(2)}, u32[]{:S(2)}) %collective-permute-start.1) | collective-permute-done | bytes 110624 | tf_op jit(solution)/shard_map/ppermute | solution.py:34
  20.2 0.7 maximum_select_fusion
  21.0 0.0 all-gather.3.cloned.1.call-update
  21.0 45.1 %all_to_all.10 = bf16[64,8,384]{2,1,0:T(8,128)(2,1)S(1)} all-to-all(bf16[64,8,384]{2,1,0:T(8,128)(2,1)S(1)} %bitcast.37), channel_id=1, replica_groups=mesh['z'=16,'x'=4,'y'=4,'c'=2] {'z','x'}, dimensions={0} | all-to-all | bytes 786432 | tf_op jit(solution)/shard_map/all_to_all | solution.py:174
  66.1 5.2 %collective-permute-start.2 = (bf16[512,384]{1,0:T(8,128)(2,1)S(1)}, bf16[512,384]{1,0:T(8,128)(2,1)S(1)}, u32[]{:S(2)}, u32[]{:S(2)}) collective-permute-start(bf16[512,384]{1,0:T(8,128)(2,1)S(1)} %bitcast.31), channel_id=1, source_target_pairs={{0,24},{1,25},{2,26},{3,27},{4,28},{5,29},{6,30},{7,31},{8,16},{9,... | collective-permute-start | bytes 1179656 | tf_op jit(solution)/shard_map/ppermute | solution.py:34
  71.3 4.6 %collective-permute-start.3 = (bf16[512,384]{1,0:T(8,128)(2,1)S(1)}, bf16[512,384]{1,0:T(8,128)(2,1)S(1)}, u32[]{:S(2)}, u32[]{:S(2)}) collective-permute-start(bf16[512,384]{1,0:T(8,128)(2,1)S(1)} %bitcast.32), channel_id=1, source_target_pairs={{0,6},{1,7},{2,0},{3,1},{4,2},{5,3},{6,4},{7,5},{8,14},{9,15},{10,... | collective-permute-start | bytes 1179656 | tf_op jit(solution)/shard_map/ppermute | solution.py:34
  76.0 1.9 %collective-permute-start.5 = (bf16[512,384]{1,0:T(8,128)(2,1)S(1)}, bf16[512,384]{1,0:T(8,128)(2,1)S(1)}, u32[]{:S(2)}, u32[]{:S(2)}) collective-permute-start(bf16[512,384]{1,0:T(8,128)(2,1)S(1)} %bitcast.33), channel_id=1, source_target_pairs={{0,2},{1,3},{2,4},{3,5},{4,6},{5,7},{6,0},{7,1},{8,10},{9,11},{10,... | collective-permute-start | bytes 1179656 | tf_op jit(solution)/shard_map/ppermute | solution.py:34
  77.9 3.6 %collective-permute-start.7 = (bf16[512,384]{1,0:T(8,128)(2,1)S(1)}, bf16[512,384]{1,0:T(8,128)(2,1)S(1)}, u32[]{:S(2)}, u32[]{:S(2)}) collective-permute-start(bf16[512,384]{1,0:T(8,128)(2,1)S(1)} %bitcast.34), channel_id=1, source_target_pairs={{0,4},{1,5},{2,6},{3,7},{4,0},{5,1},{6,2},{7,3},{8,12},{9,13},{10,... | collective-permute-start | bytes 1179656 | tf_op jit(solution)/shard_map/ppermute | solution.py:34
  81.5 2.9 %collective-permute-start.4 = (bf16[512,384]{1,0:T(8,128)(2,1)S(1)}, bf16[512,384]{1,0:T(8,128)(2,1)S(1)}, u32[]{:S(2)}, u32[]{:S(2)}) collective-permute-start(bf16[512,384]{1,0:T(8,128)(2,1)S(1)} %collective-permute-done.2.refs_1_), channel_id=1, source_target_pairs={{0,6},{1,7},{2,0},{3,1},{4,2},{5,3},{6,4},{7,5},{8,14},{9,15},{10,... | collective-permute-start | bytes 1179656 | tf_op jit(solution)/shard_map/ppermute | solution.py:34
  84.4 2.5 %collective-permute-start.6 = (bf16[512,384]{1,0:T(8,128)(2,1)S(1)}, bf16[512,384]{1,0:T(8,128)(2,1)S(1)}, u32[]{:S(2)}, u32[]{:S(2)}) collective-permute-start(bf16[512,384]{1,0:T(8,128)(2,1)S(1)} %collective-permute-done.2.refs_1_), channel_id=1, source_target_pairs={{0,2},{1,3},{2,4},{3,5},{4,6},{5,7},{6,0},{7,1},{8,10},{9,11},{10,... | collective-permute-start | bytes 1179656 | tf_op jit(solution)/shard_map/ppermute | solution.py:34
  86.9 3.7 %collective-permute-start.8 = (bf16[512,384]{1,0:T(8,128)(2,1)S(1)}, bf16[512,384]{1,0:T(8,128)(2,1)S(1)}, u32[]{:S(2)}, u32[]{:S(2)}) collective-permute-start(bf16[512,384]{1,0:T(8,128)(2,1)S(1)} %collective-permute-done.2.refs_1_), channel_id=1, source_target_pairs={{0,4},{1,5},{2,6},{3,7},{4,0},{5,1},{6,2},{7,3},{8,12},{9,13},{10,... | collective-permute-start | bytes 1179656 | tf_op jit(solution)/shard_map/ppermute | solution.py:34
  90.6 0.1 pad_add_fusion.place
  90.7 4.3 %collective-permute-done.7.refs_6_ = bf16[512,384]{1,0:T(8,128)(2,1)S(1)} collective-permute-done((bf16[512,384]{1,0:T(8,128)(2,1)S(1)}, bf16[512,384]{1,0:T(8,128)(2,1)S(1)}, u32[]{:S(2)}, u32[]{:S(2)}) %collective-permute-start.7) | collective-permute-done | bytes 393248 | tf_op jit(solution)/shard_map/ppermute | solution.py:34
  95.0 7.8 %collective-permute-done.4.refs_3_ = bf16[512,384]{1,0:T(8,128)(2,1)S(1)} collective-permute-done((bf16[512,384]{1,0:T(8,128)(2,1)S(1)}, bf16[512,384]{1,0:T(8,128)(2,1)S(1)}, u32[]{:S(2)}, u32[]{:S(2)}) %collective-permute-start.4) | collective-permute-done | bytes 393248 | tf_op jit(solution)/shard_map/ppermute | solution.py:34
  102.8 4.4 %collective-permute-done.6.refs_5_ = bf16[512,384]{1,0:T(8,128)(2,1)S(1)} collective-permute-done((bf16[512,384]{1,0:T(8,128)(2,1)S(1)}, bf16[512,384]{1,0:T(8,128)(2,1)S(1)}, u32[]{:S(2)}, u32[]{:S(2)}) %collective-permute-start.6) | collective-permute-done | bytes 393248 | tf_op jit(solution)/shard_map/ppermute | solution.py:34
  107.1 4.8 %collective-permute-done.8.refs_7_ = bf16[512,384]{1,0:T(8,128)(2,1)S(1)} collective-permute-done((bf16[512,384]{1,0:T(8,128)(2,1)S(1)}, bf16[512,384]{1,0:T(8,128)(2,1)S(1)}, u32[]{:S(2)}, u32[]{:S(2)}) %collective-permute-start.8) | collective-permute-done | bytes 393248 | tf_op jit(solution)/shard_map/ppermute | solution.py:34
  111.9 1.5 all-gather.3.cloned.1.call-done
  113.4 10.0 %shard_map.37 = bf16[512,384]{1,0:T(8,128)(2,1)} custom-call(s32[2]{0:T(128)S(1)} %pad_add_fusion.place, s32[8,8]{1,0:T(8,128)S(1)} %copy-done, bf16[32,3,96,384]{3,2,1,0:T(8,128)(2,1)} %bitcast.36, bf16[512,384]{1,0:T(8,128)(2,1)S(1)} %bitcast.35, bf16[512,384]{1,0:T(8,128)(2,1)S(1)} %collective-permute-done.2.refs_1_, ...), custom_call_target="tpu_custom_call" | custom-call | tf_op jit(solution)/shard_map/pallas_call | solution.py:132
  123.4 6.6 %all-to-all-start.1 = ((bf16[16,4,8,384]{3,2,1,0:T(8,128)(2,1)}), bf16[16,4,8,384]{3,2,1,0:T(8,128)(2,1)S(1)}, u32[]{:S(2)}, u32[]{:S(2)}) async-start(bf16[16,4,8,384]{3,2,1,0:T(8,128)(2,1)} %bitcast.7), calls=%async_computation.1 | async-start | bytes 786432 | tf_op jit(solution)/shard_map/all_to_all | solution.py:185
  130.0 17.3 %all-to-all-done.1 = bf16[16,4,8,384]{3,2,1,0:T(8,128)(2,1)S(1)} async-done(((bf16[16,4,8,384]{3,2,1,0:T(8,128)(2,1)}), bf16[16,4,8,384]{3,2,1,0:T(8,128)(2,1)S(1)}, u32[]{:S(2)}, u32[]{:S(2)}) %all-to-all-start.1) | async-done | bytes 393248 | tf_op jit(solution)/shard_map/all_to_all | solution.py:185
  147.4 12.2 %collective-permute-start.10 = (bf16[16,8,384]{2,1,0:T(8,128)(2,1)S(1)}, bf16[16,8,384]{2,1,0:T(8,128)(2,1)S(1)}, u32[]{:S(2)}, u32[]{:S(2)}) collective-permute-start(bf16[16,8,384]{2,1,0:T(8,128)(2,1)S(1)} %get-tuple-element.17), channel_id=1, source_target_pairs={{0,8},{1,16},{2,10},{3,18},{4,12},{5,20},{6,14},{7,22},{8,0},{9,24... | collective-permute-start | bytes 294920 | tf_op jit(solution)/shard_map/ppermute | solution.py:34
  159.6 1.9 %collective-permute-start.11 = (bf16[16,8,384]{2,1,0:T(8,128)(2,1)S(1)}, bf16[16,8,384]{2,1,0:T(8,128)(2,1)S(1)}, u32[]{:S(2)}, u32[]{:S(2)}) collective-permute-start(bf16[16,8,384]{2,1,0:T(8,128)(2,1)S(1)} %get-tuple-element.15), channel_id=1, source_target_pairs={{0,16},{1,8},{2,18},{3,10},{4,20},{5,12},{6,22},{7,14},{8,24},{9,0... | collective-permute-start | bytes 294920 | tf_op jit(solution)/shard_map/ppermute | solution.py:34
  161.6 2.3 %collective-permute-start.12 = (bf16[16,8,384]{2,1,0:T(8,128)(2,1)S(1)}, bf16[16,8,384]{2,1,0:T(8,128)(2,1)S(1)}, u32[]{:S(2)}, u32[]{:S(2)}) collective-permute-start(bf16[16,8,384]{2,1,0:T(8,128)(2,1)S(1)} %get-tuple-element.16), channel_id=1, source_target_pairs={{0,24},{1,0},{2,26},{3,2},{4,28},{5,4},{6,30},{7,6},{8,16},{9,8},{... | collective-permute-start | bytes 294920 | tf_op jit(solution)/shard_map/ppermute | solution.py:34
  163.9 4.6 %collective-permute-start.9 = (bf16[16,8,384]{2,1,0:T(8,128)(2,1)S(1)}, bf16[16,8,384]{2,1,0:T(8,128)(2,1)S(1)}, u32[]{:S(2)}, u32[]{:S(2)}) collective-permute-start(bf16[16,8,384]{2,1,0:T(8,128)(2,1)S(1)} %get-tuple-element.18), channel_id=1, source_target_pairs={{0,0},{1,24},{2,2},{3,26},{4,4},{5,28},{6,6},{7,30},{8,8},{9,16},{... | collective-permute-start | bytes 294920 | tf_op jit(solution)/shard_map/ppermute | solution.py:34
  168.5 2.5 %collective-permute-done.9 = bf16[16,8,384]{2,1,0:T(8,128)(2,1)S(1)} collective-permute-done((bf16[16,8,384]{2,1,0:T(8,128)(2,1)S(1)}, bf16[16,8,384]{2,1,0:T(8,128)(2,1)S(1)}, u32[]{:S(2)}, u32[]{:S(2)}) %collective-permute-start.9) | collective-permute-done | bytes 98336 | tf_op jit(solution)/shard_map/ppermute | solution.py:34
  171.0 0.1 select_bitcast_fusion.3
  171.1 0.8 pad_maximum_fusion.1
  (11 shorter events, 0.1 us)
Async XLA Ops:
  6.5 106.9 %copy-start = (s32[8,8]{1,0:T(8,128)S(1)}, s32[8,8]{1,0:T(8,128)}, u32[]{:S(2)}) copy-start(s32[8,8]{1,0:T(8,128)} %mask.1) | copy-start | bytes 772
  6.5 106.8 %all-gather.3.cloned.1.call-start = ((), (), s32[]{:S(2)}) async-start(), calls=%async_computation.2 | async-start | bytes 7299072 | tf_op jit(solution)/shard_map/all_gather | solution.py:173
  6.5 9.4 %collective-permute-start = (bf16[3,48,384]{2,1,0:T(8,128)(2,1)}, bf16[3,48,384]{2,1,0:T(8,128)(2,1)S(1)}, u32[]{:S(2)}, u32[]{:S(2)}) collective-permute-start(bf16[3,48,384]{2,1,0:T(8,128)(2,1)} %bitcast.39), channel_id=1, source_target_pairs={{0,0},{1,24},{2,2},{3,26},{4,4},{5,28},{6,6},{7,30},{8,8},{9,16},{... | collective-permute-start | bytes 331784 | tf_op jit(solution)/shard_map/ppermute | solution.py:34
  12.4 7.8 %collective-permute-start.1 = (bf16[3,48,384]{2,1,0:T(8,128)(2,1)}, bf16[3,48,384]{2,1,0:T(8,128)(2,1)S(1)}, u32[]{:S(2)}, u32[]{:S(2)}) collective-permute-start(bf16[3,48,384]{2,1,0:T(8,128)(2,1)} %bitcast.40), channel_id=1, source_target_pairs={{0,8},{1,16},{2,10},{3,18},{4,12},{5,20},{6,14},{7,22},{8,0},{9,24... | collective-permute-start | bytes 331784 | tf_op jit(solution)/shard_map/ppermute | solution.py:34
  66.1 15.4 %collective-permute-start.2 = (bf16[512,384]{1,0:T(8,128)(2,1)S(1)}, bf16[512,384]{1,0:T(8,128)(2,1)S(1)}, u32[]{:S(2)}, u32[]{:S(2)}) collective-permute-start(bf16[512,384]{1,0:T(8,128)(2,1)S(1)} %bitcast.31), channel_id=1, source_target_pairs={{0,24},{1,25},{2,26},{3,27},{4,28},{5,29},{6,30},{7,31},{8,16},{9,... | collective-permute-start | bytes 1179656 | tf_op jit(solution)/shard_map/ppermute | solution.py:34
  71.3 15.6 %collective-permute-start.3 = (bf16[512,384]{1,0:T(8,128)(2,1)S(1)}, bf16[512,384]{1,0:T(8,128)(2,1)S(1)}, u32[]{:S(2)}, u32[]{:S(2)}) collective-permute-start(bf16[512,384]{1,0:T(8,128)(2,1)S(1)} %bitcast.32), channel_id=1, source_target_pairs={{0,6},{1,7},{2,0},{3,1},{4,2},{5,3},{6,4},{7,5},{8,14},{9,15},{10,... | collective-permute-start | bytes 1179656 | tf_op jit(solution)/shard_map/ppermute | solution.py:34
  76.0 14.7 %collective-permute-start.5 = (bf16[512,384]{1,0:T(8,128)(2,1)S(1)}, bf16[512,384]{1,0:T(8,128)(2,1)S(1)}, u32[]{:S(2)}, u32[]{:S(2)}) collective-permute-start(bf16[512,384]{1,0:T(8,128)(2,1)S(1)} %bitcast.33), channel_id=1, source_target_pairs={{0,2},{1,3},{2,4},{3,5},{4,6},{5,7},{6,0},{7,1},{8,10},{9,11},{10,... | collective-permute-start | bytes 1179656 | tf_op jit(solution)/shard_map/ppermute | solution.py:34
  77.9 17.1 %collective-permute-start.7 = (bf16[512,384]{1,0:T(8,128)(2,1)S(1)}, bf16[512,384]{1,0:T(8,128)(2,1)S(1)}, u32[]{:S(2)}, u32[]{:S(2)}) collective-permute-start(bf16[512,384]{1,0:T(8,128)(2,1)S(1)} %bitcast.34), channel_id=1, source_target_pairs={{0,4},{1,5},{2,6},{3,7},{4,0},{5,1},{6,2},{7,3},{8,12},{9,13},{10,... | collective-permute-start | bytes 1179656 | tf_op jit(solution)/shard_map/ppermute | solution.py:34
  81.5 21.3 %collective-permute-start.4 = (bf16[512,384]{1,0:T(8,128)(2,1)S(1)}, bf16[512,384]{1,0:T(8,128)(2,1)S(1)}, u32[]{:S(2)}, u32[]{:S(2)}) collective-permute-start(bf16[512,384]{1,0:T(8,128)(2,1)S(1)} %collective-permute-done.2.refs_1_), channel_id=1, source_target_pairs={{0,6},{1,7},{2,0},{3,1},{4,2},{5,3},{6,4},{7,5},{8,14},{9,15},{10,... | collective-permute-start | bytes 1179656 | tf_op jit(solution)/shard_map/ppermute | solution.py:34
  84.4 22.7 %collective-permute-start.6 = (bf16[512,384]{1,0:T(8,128)(2,1)S(1)}, bf16[512,384]{1,0:T(8,128)(2,1)S(1)}, u32[]{:S(2)}, u32[]{:S(2)}) collective-permute-start(bf16[512,384]{1,0:T(8,128)(2,1)S(1)} %collective-permute-done.2.refs_1_), channel_id=1, source_target_pairs={{0,2},{1,3},{2,4},{3,5},{4,6},{5,7},{6,0},{7,1},{8,10},{9,11},{10,... | collective-permute-start | bytes 1179656 | tf_op jit(solution)/shard_map/ppermute | solution.py:34
  86.9 25.0 %collective-permute-start.8 = (bf16[512,384]{1,0:T(8,128)(2,1)S(1)}, bf16[512,384]{1,0:T(8,128)(2,1)S(1)}, u32[]{:S(2)}, u32[]{:S(2)}) collective-permute-start(bf16[512,384]{1,0:T(8,128)(2,1)S(1)} %collective-permute-done.2.refs_1_), channel_id=1, source_target_pairs={{0,4},{1,5},{2,6},{3,7},{4,0},{5,1},{6,2},{7,3},{8,12},{9,13},{10,... | collective-permute-start | bytes 1179656 | tf_op jit(solution)/shard_map/ppermute | solution.py:34
  123.4 24.0 %all-to-all-start.1 = ((bf16[16,4,8,384]{3,2,1,0:T(8,128)(2,1)}), bf16[16,4,8,384]{3,2,1,0:T(8,128)(2,1)S(1)}, u32[]{:S(2)}, u32[]{:S(2)}) async-start(bf16[16,4,8,384]{3,2,1,0:T(8,128)(2,1)} %bitcast.7), calls=%async_computation.1 | async-start | bytes 786432 | tf_op jit(solution)/shard_map/all_to_all | solution.py:185
  147.4 21.0 %collective-permute-start.10 = (bf16[16,8,384]{2,1,0:T(8,128)(2,1)S(1)}, bf16[16,8,384]{2,1,0:T(8,128)(2,1)S(1)}, u32[]{:S(2)}, u32[]{:S(2)}) collective-permute-start(bf16[16,8,384]{2,1,0:T(8,128)(2,1)S(1)} %get-tuple-element.17), channel_id=1, source_target_pairs={{0,8},{1,16},{2,10},{3,18},{4,12},{5,20},{6,14},{7,22},{8,0},{9,24... | collective-permute-start | bytes 294920 | tf_op jit(solution)/shard_map/ppermute | solution.py:34
  159.6 8.8 %collective-permute-start.11 = (bf16[16,8,384]{2,1,0:T(8,128)(2,1)S(1)}, bf16[16,8,384]{2,1,0:T(8,128)(2,1)S(1)}, u32[]{:S(2)}, u32[]{:S(2)}) collective-permute-start(bf16[16,8,384]{2,1,0:T(8,128)(2,1)S(1)} %get-tuple-element.15), channel_id=1, source_target_pairs={{0,16},{1,8},{2,18},{3,10},{4,20},{5,12},{6,22},{7,14},{8,24},{9,0... | collective-permute-start | bytes 294920 | tf_op jit(solution)/shard_map/ppermute | solution.py:34
  161.6 6.9 %collective-permute-start.12 = (bf16[16,8,384]{2,1,0:T(8,128)(2,1)S(1)}, bf16[16,8,384]{2,1,0:T(8,128)(2,1)S(1)}, u32[]{:S(2)}, u32[]{:S(2)}) collective-permute-start(bf16[16,8,384]{2,1,0:T(8,128)(2,1)S(1)} %get-tuple-element.16), channel_id=1, source_target_pairs={{0,24},{1,0},{2,26},{3,2},{4,28},{5,4},{6,30},{7,6},{8,16},{9,8},{... | collective-permute-start | bytes 294920 | tf_op jit(solution)/shard_map/ppermute | solution.py:34
  163.9 7.1 %collective-permute-start.9 = (bf16[16,8,384]{2,1,0:T(8,128)(2,1)S(1)}, bf16[16,8,384]{2,1,0:T(8,128)(2,1)S(1)}, u32[]{:S(2)}, u32[]{:S(2)}) collective-permute-start(bf16[16,8,384]{2,1,0:T(8,128)(2,1)S(1)} %get-tuple-element.18), channel_id=1, source_target_pairs={{0,0},{1,24},{2,2},{3,26},{4,4},{5,28},{6,6},{7,30},{8,8},{9,16},{... | collective-permute-start | bytes 294920 | tf_op jit(solution)/shard_map/ppermute | solution.py:34
Sparse Core Ops, SparseCore 0:
  21.1 92.2 all-gather.2

commit v11 on v8

--- a/solution.py
+++ b/solution.py
@@ -18,6 +18,7 @@
 SLICE = D // (NZ * NX)
 PART = 2 * SLICE
 CHUNK = D // 4
+BLOCK = GROUP // PART
 SHIFTS = (0, 1, 3, 2)
 TOKENS = FRAMES * 8
 
@@ -45,26 +46,23 @@
 
 def attend_kernel(place, mask, gathered, *refs):
     pieces, outs = refs[:8], refs[8:12]
-    weights, tokens, sums, qkv, bias, result, w_sems, x_sems = refs[12:]
+    weights, sums, qkv, bias, result, w_sems = refs[12:]
     y, group, place_x = place[0], place[1], place[2]
 
-    token_copies = []
-    for i, piece in enumerate(pieces):
-        source = lax.rem(y + SHIFTS[i // 2], NY)
+    weight_copies = []
+    for i in range(8):
         half = group if i % 2 == 0 else 1 - group
-        at = pl.multiple_of((2 * source + half) * GROUP, GROUP)
-        token_copies.append(pltpu.make_async_copy(piece, tokens.at[:, pl.ds(at, GROUP)], x_sems.at[i]))
-    weight_copies = []
-    for chunk in range(D // CHUNK):
-        parts = pl.ds(chunk * (CHUNK // PART), CHUNK // PART)
+        source = (2 * lax.rem(y + SHIFTS[i // 2], NY) + half) * BLOCK
         for j in range(3):
             lanes = pl.ds(j * GROUP, GROUP)
             weight_copies.append(
                 pltpu.make_async_copy(
-                    gathered.at[parts, j], weights.at[parts, :, lanes], w_sems.at[chunk, j]
+                    gathered.at[pl.ds(source, BLOCK), j],
+                    weights.at[pl.ds(i * BLOCK, BLOCK), :, lanes],
+                    w_sems.at[i, j],
                 )
             )
-    for copy in token_copies + weight_copies:
+    for copy in weight_copies:
         copy.start()
 
     span_rows = TOKENS // SPANS
@@ -79,15 +77,12 @@
         ok = same & (jnp.broadcast_to(row, (span_rows, TOKENS)) > 0)
         bias[pl.ds(i * span_rows, span_rows), :] = jnp.where(ok, 0.0, -1e30)
 
-    for copy in token_copies:
-        copy.wait()
     for chunk in range(D // CHUNK):
-        for copy in weight_copies[3 * chunk : 3 * chunk + 3]:
+        for copy in weight_copies[6 * chunk : 6 * chunk + 6]:
             copy.wait()
-        features = pl.ds(chunk * CHUNK, CHUNK)
         parts = pl.ds(chunk * (CHUNK // PART), CHUNK // PART)
         product = jnp.dot(
-            tokens[:, features],
+            jnp.concatenate([pieces[2 * chunk][...], pieces[2 * chunk + 1][...]], axis=1),
             weights[parts].reshape(CHUNK, 3 * GROUP),
             preferred_element_type=jnp.float32,
         )
@@ -138,19 +133,18 @@
         attend_kernel,
         out_shape=[jax.ShapeDtypeStruct((TOKENS // NX, GROUP), jnp.bfloat16)] * NX,
         in_specs=[pl.BlockSpec(memory_space=pltpu.SMEM)] * 2
-        + [pl.BlockSpec(memory_space=pl.ANY)] * len(arrays),
+        + [pl.BlockSpec(memory_space=pl.ANY)]
+        + [pl.BlockSpec(memory_space=pltpu.VMEM)] * len(pieces),
         out_specs=[pl.BlockSpec(memory_space=pltpu.VMEM)] * NX,
         scratch_shapes=[
             pltpu.VMEM((D // PART, PART, 3 * GROUP), jnp.bfloat16),
-            pltpu.VMEM((TOKENS, D), jnp.bfloat16),
             pltpu.VMEM((TOKENS, 3 * GROUP), jnp.float32),
             pltpu.VMEM((TOKENS, 3 * GROUP), jnp.bfloat16),
             pltpu.VMEM((TOKENS, TOKENS), jnp.float32),
             pltpu.VMEM((NX, TOKENS // NX, GROUP), jnp.bfloat16),
-            pltpu.SemaphoreType.DMA((D // CHUNK, 3)),
-            pltpu.SemaphoreType.DMA((8,)),
+            pltpu.SemaphoreType.DMA((8, 3)),
         ],
-        compiler_params=pltpu.CompilerParams(vmem_limit_bytes=44 * 1024 * 1024),
+        compiler_params=pltpu.CompilerParams(vmem_limit_bytes=40 * 1024 * 1024),
     )(place, span_mask, *arrays)
 
 

time: 174 us -> 176 us (1.011)
  local copies, waits for them, and re-layouts: 1.83 us -> 4.84 us
    unnamed x3 -> x5, local copies, waits for them, and re-layouts: 0.75 us -> 3.76 us
where the time goes in v11:
time: 176 us; the launch traced here: 175 us
  blocking collectives  70.9 us (40%)
  starting transfers between devices  46.3 us (26%)
  waiting for transfers between devices  30.2 us (17%)
  between operations  13.6 us (8%)
  Pallas kernels  8.26 us (5%)
  local copies, waits for them, and re-layouts  4.84 us (3%)
    ppermute x13, starting transfers between devices, permute(): return lax.ppermute(array, AXES, pairs)  46.3 us
    all_to_all x1, blocking collectives, per_device(): lax.all_to_all(packed, ('z', 'x'), split_axis=0, concat_axis=0, tiled=True)  45.1 us
    ppermute x13, waiting for transfers between devices, permute(): return lax.ppermute(array, AXES, pairs)  28.7 us
    all_to_all x1, blocking collectives, per_device(): lax.all_to_all(output, 'z', split_axis=0, concat_axis=0, tiled=True)  25.8 us
    pallas_call x1, Pallas kernels, project_and_attend(): pl.pallas_call(attend_kernel, out_shape=[jax.ShapeDtypeStruct((TOKENS //...  8.26 us
    unnamed x5, local copies, waits for them, and re-layouts  3.76 us
  transfers between devices with their start and end apart: 14, of which 8 were waited for; matrix products, arithmetic and copies ran while one was open for 1% of the time, Pallas kernels for 0%

profile of v11, /device:TPU:1, one launch (start us, length us, event | category | flops | bytes accessed | tf_op | source)
XLA Modules:
  0.0 175.3 jit_solution(6493005478278840603)
XLA Ops:
  6.5 5.9 %collective-permute-start = (bf16[3,48,384]{2,1,0:T(8,128)(2,1)}, bf16[3,48,384]{2,1,0:T(8,128)(2,1)S(1)}, u32[]{:S(2)}, u32[]{:S(2)}) collective-permute-start(bf16[3,48,384]{2,1,0:T(8,128)(2,1)} %bitcast.34), channel_id=1, source_target_pairs={{0,0},{1,24},{2,2},{3,26},{4,4},{5,28},{6,6},{7,30},{8,8},{9,16},{... | collective-permute-start | bytes 331784 | tf_op jit(solution)/shard_map/ppermute | solution.py:35
  12.4 2.2 %collective-permute-start.1 = (bf16[3,48,384]{2,1,0:T(8,128)(2,1)}, bf16[3,48,384]{2,1,0:T(8,128)(2,1)S(1)}, u32[]{:S(2)}, u32[]{:S(2)}) collective-permute-start(bf16[3,48,384]{2,1,0:T(8,128)(2,1)} %bitcast.35), channel_id=1, source_target_pairs={{0,8},{1,16},{2,10},{3,18},{4,12},{5,20},{6,14},{7,22},{8,0},{9,24... | collective-permute-start | bytes 331784 | tf_op jit(solution)/shard_map/ppermute | solution.py:35
  14.7 1.1 constant_dynamic-slice_fusion
  15.8 0.1 reverse_select_fusion
  16.0 4.3 %collective-permute-done.1 = bf16[3,48,384]{2,1,0:T(8,128)(2,1)S(1)} collective-permute-done((bf16[3,48,384]{2,1,0:T(8,128)(2,1)}, bf16[3,48,384]{2,1,0:T(8,128)(2,1)S(1)}, u32[]{:S(2)}, u32[]{:S(2)}) %collective-permute-start.1) | collective-permute-done | bytes 110624 | tf_op jit(solution)/shard_map/ppermute | solution.py:35
  20.2 0.7 maximum_select_fusion
  21.0 45.1 %all_to_all.10 = bf16[64,8,384]{2,1,0:T(8,128)(2,1)S(1)} all-to-all(bf16[64,8,384]{2,1,0:T(8,128)(2,1)S(1)} %bitcast.31), channel_id=1, replica_groups=mesh['z'=16,'x'=4,'y'=4,'c'=2] {'z','x'}, dimensions={0} | all-to-all | bytes 786432 | tf_op jit(solution)/shard_map/all_to_all | solution.py:174
  66.1 5.2 %collective-permute-start.2 = (bf16[512,384]{1,0:T(8,128)(2,1)S(1)}, bf16[512,384]{1,0:T(8,128)(2,1)S(1)}, u32[]{:S(2)}, u32[]{:S(2)}) collective-permute-start(bf16[512,384]{1,0:T(8,128)(2,1)S(1)} %bitcast.26), channel_id=1, source_target_pairs={{0,24},{1,25},{2,26},{3,27},{4,28},{5,29},{6,30},{7,31},{8,16},{9,... | collective-permute-start | bytes 1179656 | tf_op jit(solution)/shard_map/ppermute | solution.py:35
  71.3 4.6 %collective-permute-start.3 = (bf16[512,384]{1,0:T(8,128)(2,1)S(1)}, bf16[512,384]{1,0:T(8,128)(2,1)S(1)}, u32[]{:S(2)}, u32[]{:S(2)}) collective-permute-start(bf16[512,384]{1,0:T(8,128)(2,1)S(1)} %bitcast.27), channel_id=1, source_target_pairs={{0,6},{1,7},{2,0},{3,1},{4,2},{5,3},{6,4},{7,5},{8,14},{9,15},{10,... | collective-permute-start | bytes 1179656 | tf_op jit(solution)/shard_map/ppermute | solution.py:35
  76.0 1.9 %collective-permute-start.5 = (bf16[512,384]{1,0:T(8,128)(2,1)S(1)}, bf16[512,384]{1,0:T(8,128)(2,1)S(1)}, u32[]{:S(2)}, u32[]{:S(2)}) collective-permute-start(bf16[512,384]{1,0:T(8,128)(2,1)S(1)} %bitcast.28), channel_id=1, source_target_pairs={{0,2},{1,3},{2,4},{3,5},{4,6},{5,7},{6,0},{7,1},{8,10},{9,11},{10,... | collective-permute-start | bytes 1179656 | tf_op jit(solution)/shard_map/ppermute | solution.py:35
  77.9 3.6 %collective-permute-start.7 = (bf16[512,384]{1,0:T(8,128)(2,1)S(1)}, bf16[512,384]{1,0:T(8,128)(2,1)S(1)}, u32[]{:S(2)}, u32[]{:S(2)}) collective-permute-start(bf16[512,384]{1,0:T(8,128)(2,1)S(1)} %bitcast.29), channel_id=1, source_target_pairs={{0,4},{1,5},{2,6},{3,7},{4,0},{5,1},{6,2},{7,3},{8,12},{9,13},{10,... | collective-permute-start | bytes 1179656 | tf_op jit(solution)/shard_map/ppermute | solution.py:35
  81.5 2.9 %collective-permute-start.4 = (bf16[512,384]{1,0:T(8,128)(2,1)S(1)}, bf16[512,384]{1,0:T(8,128)(2,1)S(1)}, u32[]{:S(2)}, u32[]{:S(2)}) collective-permute-start(bf16[512,384]{1,0:T(8,128)(2,1)S(1)} %collective-permute-done.2.refs_1_), channel_id=1, source_target_pairs={{0,6},{1,7},{2,0},{3,1},{4,2},{5,3},{6,4},{7,5},{8,14},{9,15},{10,... | collective-permute-start | bytes 1179656 | tf_op jit(solution)/shard_map/ppermute | solution.py:35
  84.4 2.5 %collective-permute-start.6 = (bf16[512,384]{1,0:T(8,128)(2,1)S(1)}, bf16[512,384]{1,0:T(8,128)(2,1)S(1)}, u32[]{:S(2)}, u32[]{:S(2)}) collective-permute-start(bf16[512,384]{1,0:T(8,128)(2,1)S(1)} %collective-permute-done.2.refs_1_), channel_id=1, source_target_pairs={{0,2},{1,3},{2,4},{3,5},{4,6},{5,7},{6,0},{7,1},{8,10},{9,11},{10,... | collective-permute-start | bytes 1179656 | tf_op jit(solution)/shard_map/ppermute | solution.py:35
  86.9 3.7 %collective-permute-start.8 = (bf16[512,384]{1,0:T(8,128)(2,1)S(1)}, bf16[512,384]{1,0:T(8,128)(2,1)S(1)}, u32[]{:S(2)}, u32[]{:S(2)}) collective-permute-start(bf16[512,384]{1,0:T(8,128)(2,1)S(1)} %collective-permute-done.2.refs_1_), channel_id=1, source_target_pairs={{0,4},{1,5},{2,6},{3,7},{4,0},{5,1},{6,2},{7,3},{8,12},{9,13},{10,... | collective-permute-start | bytes 1179656 | tf_op jit(solution)/shard_map/ppermute | solution.py:35
  90.6 0.1 pad_add_fusion.place
  90.7 4.3 %collective-permute-done.7.refs_6_ = bf16[512,384]{1,0:T(8,128)(2,1)S(1)} collective-permute-done((bf16[512,384]{1,0:T(8,128)(2,1)S(1)}, bf16[512,384]{1,0:T(8,128)(2,1)S(1)}, u32[]{:S(2)}, u32[]{:S(2)}) %collective-permute-start.7) | collective-permute-done | bytes 393248 | tf_op jit(solution)/shard_map/ppermute | solution.py:35
  95.0 7.8 %collective-permute-done.4.refs_3_ = bf16[512,384]{1,0:T(8,128)(2,1)S(1)} collective-permute-done((bf16[512,384]{1,0:T(8,128)(2,1)S(1)}, bf16[512,384]{1,0:T(8,128)(2,1)S(1)}, u32[]{:S(2)}, u32[]{:S(2)}) %collective-permute-start.4) | collective-permute-done | bytes 393248 | tf_op jit(solution)/shard_map/ppermute | solution.py:35
  102.8 4.4 %collective-permute-done.6.refs_5_ = bf16[512,384]{1,0:T(8,128)(2,1)S(1)} collective-permute-done((bf16[512,384]{1,0:T(8,128)(2,1)S(1)}, bf16[512,384]{1,0:T(8,128)(2,1)S(1)}, u32[]{:S(2)}, u32[]{:S(2)}) %collective-permute-start.6) | collective-permute-done | bytes 393248 | tf_op jit(solution)/shard_map/ppermute | solution.py:35
  107.1 4.8 %collective-permute-done.8.refs_7_ = bf16[512,384]{1,0:T(8,128)(2,1)S(1)} collective-permute-done((bf16[512,384]{1,0:T(8,128)(2,1)S(1)}, bf16[512,384]{1,0:T(8,128)(2,1)S(1)}, u32[]{:S(2)}, u32[]{:S(2)}) %collective-permute-start.8) | collective-permute-done | bytes 393248 | tf_op jit(solution)/shard_map/ppermute | solution.py:35
  111.9 1.5 all-gather.3.cloned.1.call-done
  113.4 3.0 %copy-done = bf16[96,96,384]{2,1,0:T(8,128)(2,1)S(1)} copy-done((bf16[96,96,384]{2,1,0:T(8,128)(2,1)S(1)}, bf16[96,96,384]{2,1,0:T(8,128)(2,1)}, u32[]{:S(2)}) %copy-start) | copy-done | bytes 7077912
  116.4 8.3 %shard_map.37 = (bf16[128,384]{1,0:T(8,128)(2,1)S(1)}, bf16[128,384]{1,0:T(8,128)(2,1)S(1)}, bf16[128,384]{1,0:T(8,128)(2,1)S(1)}, bf16[128,384]{1,0:T(8,128)(2,1)S(1)}) custom-call(s32[3]{0:T(128)S(1)} %pad_add_fusion.place, s32[8,8]{1,0:T(8,128)S(1)} %copy-done.1, bf16[32,3,96,384]{3,2,1,0:T(8,128)(2,1)S(1)} %bitcast.25, bf16[512,384]{1,0:T(8,128)(2,1)S(1)} %bitcast.30, ...), custom_call_target="tpu_custom_call" | custom-call | tf_op jit(solution)/shard_map/pallas_call | solution.py:132
  124.7 4.9 %collective-permute-start.10 = (bf16[128,384]{1,0:T(8,128)(2,1)S(1)}, bf16[128,384]{1,0:T(8,128)(2,1)S(1)}, u32[]{:S(2)}, u32[]{:S(2)}) collective-permute-start(bf16[128,384]{1,0:T(8,128)(2,1)S(1)} %get-tuple-element.14), channel_id=1, source_target_pairs={{0,8},{1,16},{2,10},{3,18},{4,12},{5,20},{6,14},{7,22},{8,0},{9,24... | collective-permute-start | bytes 294920 | tf_op jit(solution)/shard_map/ppermute | solution.py:35
  129.6 3.0 %collective-permute-start.11 = (bf16[128,384]{1,0:T(8,128)(2,1)S(1)}, bf16[128,384]{1,0:T(8,128)(2,1)S(1)}, u32[]{:S(2)}, u32[]{:S(2)}) collective-permute-start(bf16[128,384]{1,0:T(8,128)(2,1)S(1)} %get-tuple-element.15), channel_id=1, source_target_pairs={{0,16},{1,8},{2,18},{3,10},{4,20},{5,12},{6,22},{7,14},{8,24},{9,0... | collective-permute-start | bytes 294920 | tf_op jit(solution)/shard_map/ppermute | solution.py:35
  132.6 1.9 %collective-permute-start.12 = (bf16[128,384]{1,0:T(8,128)(2,1)S(1)}, bf16[128,384]{1,0:T(8,128)(2,1)S(1)}, u32[]{:S(2)}, u32[]{:S(2)}) collective-permute-start(bf16[128,384]{1,0:T(8,128)(2,1)S(1)} %get-tuple-element.16), channel_id=1, source_target_pairs={{0,24},{1,0},{2,26},{3,2},{4,28},{5,4},{6,30},{7,6},{8,16},{9,8},{... | collective-permute-start | bytes 294920 | tf_op jit(solution)/shard_map/ppermute | solution.py:35
  134.6 3.9 %collective-permute-start.9 = (bf16[128,384]{1,0:T(8,128)(2,1)S(1)}, bf16[128,384]{1,0:T(8,128)(2,1)S(1)}, u32[]{:S(2)}, u32[]{:S(2)}) collective-permute-start(bf16[128,384]{1,0:T(8,128)(2,1)S(1)} %get-tuple-element.13), channel_id=1, source_target_pairs={{0,0},{1,24},{2,2},{3,26},{4,4},{5,28},{6,6},{7,30},{8,8},{9,16},{... | collective-permute-start | bytes 294920 | tf_op jit(solution)/shard_map/ppermute | solution.py:35
  138.5 0.7 collective-permute-done.12
  139.2 2.5 %collective-permute-done.9 = bf16[128,384]{1,0:T(8,128)(2,1)S(1)} collective-permute-done((bf16[128,384]{1,0:T(8,128)(2,1)S(1)}, bf16[128,384]{1,0:T(8,128)(2,1)S(1)}, u32[]{:S(2)}, u32[]{:S(2)}) %collective-permute-start.9) | collective-permute-done | bytes 98336 | tf_op jit(solution)/shard_map/ppermute | solution.py:35
  141.7 0.1 select_bitcast_fusion.3
  141.8 0.1 pad_maximum_fusion.1
  141.9 25.8 %all_to_all.11 = bf16[16,4,8,384]{3,2,1,0:T(8,128)(2,1)S(1)} all-to-all(bf16[16,4,8,384]{3,2,1,0:T(8,128)(2,1)S(1)} %pad_maximum_fusion.1), channel_id=1, replica_groups=mesh['z'=16,'x'=4,'y'=4,'c'=2] {'z'}, dimensions={0} | all-to-all | bytes 786432 | tf_op jit(solution)/shard_map/all_to_all | solution.py:187
  167.7 0.7 copy.10
  (12 shorter events, 0.1 us)
Async XLA Ops:
  6.5 106.9 %copy-start.1 = (s32[8,8]{1,0:T(8,128)S(1)}, s32[8,8]{1,0:T(8,128)}, u32[]{:S(2)}) copy-start(s32[8,8]{1,0:T(8,128)} %mask.1) | copy-start | bytes 772
  6.5 106.8 %all-gather.3.cloned.1.call-start = ((), (), s32[]{:S(2)}) async-start(), calls=%async_computation.2 | async-start | bytes 7299072 | tf_op jit(solution)/shard_map/all_gather | solution.py:173
  6.5 9.4 %collective-permute-start = (bf16[3,48,384]{2,1,0:T(8,128)(2,1)}, bf16[3,48,384]{2,1,0:T(8,128)(2,1)S(1)}, u32[]{:S(2)}, u32[]{:S(2)}) collective-permute-start(bf16[3,48,384]{2,1,0:T(8,128)(2,1)} %bitcast.34), channel_id=1, source_target_pairs={{0,0},{1,24},{2,2},{3,26},{4,4},{5,28},{6,6},{7,30},{8,8},{9,16},{... | collective-permute-start | bytes 331784 | tf_op jit(solution)/shard_map/ppermute | solution.py:35
  12.4 7.8 %collective-permute-start.1 = (bf16[3,48,384]{2,1,0:T(8,128)(2,1)}, bf16[3,48,384]{2,1,0:T(8,128)(2,1)S(1)}, u32[]{:S(2)}, u32[]{:S(2)}) collective-permute-start(bf16[3,48,384]{2,1,0:T(8,128)(2,1)} %bitcast.35), channel_id=1, source_target_pairs={{0,8},{1,16},{2,10},{3,18},{4,12},{5,20},{6,14},{7,22},{8,0},{9,24... | collective-permute-start | bytes 331784 | tf_op jit(solution)/shard_map/ppermute | solution.py:35
  66.1 15.4 %collective-permute-start.2 = (bf16[512,384]{1,0:T(8,128)(2,1)S(1)}, bf16[512,384]{1,0:T(8,128)(2,1)S(1)}, u32[]{:S(2)}, u32[]{:S(2)}) collective-permute-start(bf16[512,384]{1,0:T(8,128)(2,1)S(1)} %bitcast.26), channel_id=1, source_target_pairs={{0,24},{1,25},{2,26},{3,27},{4,28},{5,29},{6,30},{7,31},{8,16},{9,... | collective-permute-start | bytes 1179656 | tf_op jit(solution)/shard_map/ppermute | solution.py:35
  71.3 15.6 %collective-permute-start.3 = (bf16[512,384]{1,0:T(8,128)(2,1)S(1)}, bf16[512,384]{1,0:T(8,128)(2,1)S(1)}, u32[]{:S(2)}, u32[]{:S(2)}) collective-permute-start(bf16[512,384]{1,0:T(8,128)(2,1)S(1)} %bitcast.27), channel_id=1, source_target_pairs={{0,6},{1,7},{2,0},{3,1},{4,2},{5,3},{6,4},{7,5},{8,14},{9,15},{10,... | collective-permute-start | bytes 1179656 | tf_op jit(solution)/shard_map/ppermute | solution.py:35
  76.0 14.7 %collective-permute-start.5 = (bf16[512,384]{1,0:T(8,128)(2,1)S(1)}, bf16[512,384]{1,0:T(8,128)(2,1)S(1)}, u32[]{:S(2)}, u32[]{:S(2)}) collective-permute-start(bf16[512,384]{1,0:T(8,128)(2,1)S(1)} %bitcast.28), channel_id=1, source_target_pairs={{0,2},{1,3},{2,4},{3,5},{4,6},{5,7},{6,0},{7,1},{8,10},{9,11},{10,... | collective-permute-start | bytes 1179656 | tf_op jit(solution)/shard_map/ppermute | solution.py:35
  77.9 17.1 %collective-permute-start.7 = (bf16[512,384]{1,0:T(8,128)(2,1)S(1)}, bf16[512,384]{1,0:T(8,128)(2,1)S(1)}, u32[]{:S(2)}, u32[]{:S(2)}) collective-permute-start(bf16[512,384]{1,0:T(8,128)(2,1)S(1)} %bitcast.29), channel_id=1, source_target_pairs={{0,4},{1,5},{2,6},{3,7},{4,0},{5,1},{6,2},{7,3},{8,12},{9,13},{10,... | collective-permute-start | bytes 1179656 | tf_op jit(solution)/shard_map/ppermute | solution.py:35
  81.5 21.3 %collective-permute-start.4 = (bf16[512,384]{1,0:T(8,128)(2,1)S(1)}, bf16[512,384]{1,0:T(8,128)(2,1)S(1)}, u32[]{:S(2)}, u32[]{:S(2)}) collective-permute-start(bf16[512,384]{1,0:T(8,128)(2,1)S(1)} %collective-permute-done.2.refs_1_), channel_id=1, source_target_pairs={{0,6},{1,7},{2,0},{3,1},{4,2},{5,3},{6,4},{7,5},{8,14},{9,15},{10,... | collective-permute-start | bytes 1179656 | tf_op jit(solution)/shard_map/ppermute | solution.py:35
  84.4 22.7 %collective-permute-start.6 = (bf16[512,384]{1,0:T(8,128)(2,1)S(1)}, bf16[512,384]{1,0:T(8,128)(2,1)S(1)}, u32[]{:S(2)}, u32[]{:S(2)}) collective-permute-start(bf16[512,384]{1,0:T(8,128)(2,1)S(1)} %collective-permute-done.2.refs_1_), channel_id=1, source_target_pairs={{0,2},{1,3},{2,4},{3,5},{4,6},{5,7},{6,0},{7,1},{8,10},{9,11},{10,... | collective-permute-start | bytes 1179656 | tf_op jit(solution)/shard_map/ppermute | solution.py:35
  86.9 25.0 %collective-permute-start.8 = (bf16[512,384]{1,0:T(8,128)(2,1)S(1)}, bf16[512,384]{1,0:T(8,128)(2,1)S(1)}, u32[]{:S(2)}, u32[]{:S(2)}) collective-permute-start(bf16[512,384]{1,0:T(8,128)(2,1)S(1)} %collective-permute-done.2.refs_1_), channel_id=1, source_target_pairs={{0,4},{1,5},{2,6},{3,7},{4,0},{5,1},{6,2},{7,3},{8,12},{9,13},{10,... | collective-permute-start | bytes 1179656 | tf_op jit(solution)/shard_map/ppermute | solution.py:35
  113.4 3.0 %copy-start = (bf16[96,96,384]{2,1,0:T(8,128)(2,1)S(1)}, bf16[96,96,384]{2,1,0:T(8,128)(2,1)}, u32[]{:S(2)}) copy-start(bf16[96,96,384]{2,1,0:T(8,128)(2,1)} %all-gather.3.cloned.1.call-done) | copy-start | bytes 21233668
  124.7 13.8 %collective-permute-start.10 = (bf16[128,384]{1,0:T(8,128)(2,1)S(1)}, bf16[128,384]{1,0:T(8,128)(2,1)S(1)}, u32[]{:S(2)}, u32[]{:S(2)}) collective-permute-start(bf16[128,384]{1,0:T(8,128)(2,1)S(1)} %get-tuple-element.14), channel_id=1, source_target_pairs={{0,8},{1,16},{2,10},{3,18},{4,12},{5,20},{6,14},{7,22},{8,0},{9,24... | collective-permute-start | bytes 294920 | tf_op jit(solution)/shard_map/ppermute | solution.py:35
  129.6 8.9 %collective-permute-start.11 = (bf16[128,384]{1,0:T(8,128)(2,1)S(1)}, bf16[128,384]{1,0:T(8,128)(2,1)S(1)}, u32[]{:S(2)}, u32[]{:S(2)}) collective-permute-start(bf16[128,384]{1,0:T(8,128)(2,1)S(1)} %get-tuple-element.15), channel_id=1, source_target_pairs={{0,16},{1,8},{2,18},{3,10},{4,20},{5,12},{6,22},{7,14},{8,24},{9,0... | collective-permute-start | bytes 294920 | tf_op jit(solution)/shard_map/ppermute | solution.py:35
  132.6 6.6 %collective-permute-start.12 = (bf16[128,384]{1,0:T(8,128)(2,1)S(1)}, bf16[128,384]{1,0:T(8,128)(2,1)S(1)}, u32[]{:S(2)}, u32[]{:S(2)}) collective-permute-start(bf16[128,384]{1,0:T(8,128)(2,1)S(1)} %get-tuple-element.16), channel_id=1, source_target_pairs={{0,24},{1,0},{2,26},{3,2},{4,28},{5,4},{6,30},{7,6},{8,16},{9,8},{... | collective-permute-start | bytes 294920 | tf_op jit(solution)/shard_map/ppermute | solution.py:35
  134.6 7.1 %collective-permute-start.9 = (bf16[128,384]{1,0:T(8,128)(2,1)S(1)}, bf16[128,384]{1,0:T(8,128)(2,1)S(1)}, u32[]{:S(2)}, u32[]{:S(2)}) collective-permute-start(bf16[128,384]{1,0:T(8,128)(2,1)S(1)} %get-tuple-element.13), channel_id=1, source_target_pairs={{0,0},{1,24},{2,2},{3,26},{4,4},{5,28},{6,6},{7,30},{8,8},{9,16},{... | collective-permute-start | bytes 294920 | tf_op jit(solution)/shard_map/ppermute | solution.py:35
Sparse Core Ops, SparseCore 0:
  21.1 92.2 all-gather.2

commit v12 on v11

--- a/solution.py
+++ b/solution.py
@@ -144,7 +144,7 @@
             pltpu.VMEM((NX, TOKENS // NX, GROUP), jnp.bfloat16),
             pltpu.SemaphoreType.DMA((8, 3)),
         ],
-        compiler_params=pltpu.CompilerParams(vmem_limit_bytes=40 * 1024 * 1024),
+        compiler_params=pltpu.CompilerParams(vmem_limit_bytes=54 * 1024 * 1024),
     )(place, span_mask, *arrays)
 
 

time: 176 us -> 176 us (level)
  local copies, waits for them, and re-layouts: 4.84 us -> 1.86 us
  Pallas kernels: 8.26 us -> 10.7 us
    unnamed x5 -> x17, local copies, waits for them, and re-layouts: 3.76 us -> 0.78 us
    pallas_call x1, Pallas kernels: 8.26 us -> 10.7 us  [project_and_attend(): pl.pallas_call(attend_kernel, out_shape=[jax.ShapeDtypeStruct((TOKENS //...]
where the time goes in v12:
time: 176 us; the launch traced here: 175 us
  blocking collectives  70.4 us (40%)
  starting transfers between devices  46.8 us (27%)
  waiting for transfers between devices  30.1 us (17%)
  between operations  13.7 us (8%)
  Pallas kernels  10.7 us (6%)
  local copies, waits for them, and re-layouts  1.86 us (1%)
    ppermute x13, starting transfers between devices, permute(): return lax.ppermute(array, AXES, pairs)  46.8 us
    all_to_all x1, blocking collectives, per_device(): lax.all_to_all(packed, ('z', 'x'), split_axis=0, concat_axis=0, tiled=True)  45.1 us
    ppermute x13, waiting for transfers between devices, permute(): return lax.ppermute(array, AXES, pairs)  28.8 us
    all_to_all x1, blocking collectives, per_device(): lax.all_to_all(output, 'z', split_axis=0, concat_axis=0, tiled=True)  25.4 us
    pallas_call x1, Pallas kernels, project_and_attend(): pl.pallas_call(attend_kernel, out_shape=[jax.ShapeDtypeStruct((TOKENS //...  10.7 us
  transfers between devices with their start and end apart: 14, of which 8 were waited for; matrix products, arithmetic and copies ran while one was open for 1% of the time, Pallas kernels for 0%

profile of v12, /device:TPU:1, one launch (start us, length us, event | category | flops | bytes accessed | tf_op | source)
XLA Modules:
  0.0 175.2 jit_solution(14692904741666940376)
XLA Ops:
  6.5 5.8 %collective-permute-start = (bf16[3,48,384]{2,1,0:T(8,128)(2,1)}, bf16[3,48,384]{2,1,0:T(8,128)(2,1)S(1)}, u32[]{:S(2)}, u32[]{:S(2)}) collective-permute-start(bf16[3,48,384]{2,1,0:T(8,128)(2,1)} %bitcast.34), channel_id=1, source_target_pairs={{0,0},{1,24},{2,2},{3,26},{4,4},{5,28},{6,6},{7,30},{8,8},{9,16},{... | collective-permute-start | bytes 331784 | tf_op jit(solution)/shard_map/ppermute | solution.py:35
  12.3 2.2 %collective-permute-start.1 = (bf16[3,48,384]{2,1,0:T(8,128)(2,1)}, bf16[3,48,384]{2,1,0:T(8,128)(2,1)S(1)}, u32[]{:S(2)}, u32[]{:S(2)}) collective-permute-start(bf16[3,48,384]{2,1,0:T(8,128)(2,1)} %bitcast.35), channel_id=1, source_target_pairs={{0,8},{1,16},{2,10},{3,18},{4,12},{5,20},{6,14},{7,22},{8,0},{9,24... | collective-permute-start | bytes 331784 | tf_op jit(solution)/shard_map/ppermute | solution.py:35
  14.5 1.1 constant_dynamic-slice_fusion
  15.6 0.1 reverse_select_fusion
  15.8 4.3 %collective-permute-done.1 = bf16[3,48,384]{2,1,0:T(8,128)(2,1)S(1)} collective-permute-done((bf16[3,48,384]{2,1,0:T(8,128)(2,1)}, bf16[3,48,384]{2,1,0:T(8,128)(2,1)S(1)}, u32[]{:S(2)}, u32[]{:S(2)}) %collective-permute-start.1) | collective-permute-done | bytes 110624 | tf_op jit(solution)/shard_map/ppermute | solution.py:35
  20.1 0.7 maximum_select_fusion
  20.8 0.0 all-gather.3.cloned.1.call-update
  20.9 45.1 %all_to_all.10 = bf16[64,8,384]{2,1,0:T(8,128)(2,1)S(1)} all-to-all(bf16[64,8,384]{2,1,0:T(8,128)(2,1)S(1)} %bitcast.31), channel_id=1, replica_groups=mesh['z'=16,'x'=4,'y'=4,'c'=2] {'z','x'}, dimensions={0} | all-to-all | bytes 786432 | tf_op jit(solution)/shard_map/all_to_all | solution.py:174
  65.9 5.2 %collective-permute-start.2 = (bf16[512,384]{1,0:T(8,128)(2,1)S(1)}, bf16[512,384]{1,0:T(8,128)(2,1)S(1)}, u32[]{:S(2)}, u32[]{:S(2)}) collective-permute-start(bf16[512,384]{1,0:T(8,128)(2,1)S(1)} %bitcast.26), channel_id=1, source_target_pairs={{0,24},{1,25},{2,26},{3,27},{4,28},{5,29},{6,30},{7,31},{8,16},{9,... | collective-permute-start | bytes 1179656 | tf_op jit(solution)/shard_map/ppermute | solution.py:35
  71.2 4.6 %collective-permute-start.3 = (bf16[512,384]{1,0:T(8,128)(2,1)S(1)}, bf16[512,384]{1,0:T(8,128)(2,1)S(1)}, u32[]{:S(2)}, u32[]{:S(2)}) collective-permute-start(bf16[512,384]{1,0:T(8,128)(2,1)S(1)} %bitcast.27), channel_id=1, source_target_pairs={{0,6},{1,7},{2,0},{3,1},{4,2},{5,3},{6,4},{7,5},{8,14},{9,15},{10,... | collective-permute-start | bytes 1179656 | tf_op jit(solution)/shard_map/ppermute | solution.py:35
  75.8 1.9 %collective-permute-start.5 = (bf16[512,384]{1,0:T(8,128)(2,1)S(1)}, bf16[512,384]{1,0:T(8,128)(2,1)S(1)}, u32[]{:S(2)}, u32[]{:S(2)}) collective-permute-start(bf16[512,384]{1,0:T(8,128)(2,1)S(1)} %bitcast.28), channel_id=1, source_target_pairs={{0,2},{1,3},{2,4},{3,5},{4,6},{5,7},{6,0},{7,1},{8,10},{9,11},{10,... | collective-permute-start | bytes 1179656 | tf_op jit(solution)/shard_map/ppermute | solution.py:35
  77.8 3.6 %collective-permute-start.7 = (bf16[512,384]{1,0:T(8,128)(2,1)S(1)}, bf16[512,384]{1,0:T(8,128)(2,1)S(1)}, u32[]{:S(2)}, u32[]{:S(2)}) collective-permute-start(bf16[512,384]{1,0:T(8,128)(2,1)S(1)} %bitcast.29), channel_id=1, source_target_pairs={{0,4},{1,5},{2,6},{3,7},{4,0},{5,1},{6,2},{7,3},{8,12},{9,13},{10,... | collective-permute-start | bytes 1179656 | tf_op jit(solution)/shard_map/ppermute | solution.py:35
  81.3 2.9 %collective-permute-start.4 = (bf16[512,384]{1,0:T(8,128)(2,1)S(1)}, bf16[512,384]{1,0:T(8,128)(2,1)S(1)}, u32[]{:S(2)}, u32[]{:S(2)}) collective-permute-start(bf16[512,384]{1,0:T(8,128)(2,1)S(1)} %collective-permute-done.2.refs_1_), channel_id=1, source_target_pairs={{0,6},{1,7},{2,0},{3,1},{4,2},{5,3},{6,4},{7,5},{8,14},{9,15},{10,... | collective-permute-start | bytes 1179656 | tf_op jit(solution)/shard_map/ppermute | solution.py:35
  84.3 2.5 %collective-permute-start.6 = (bf16[512,384]{1,0:T(8,128)(2,1)S(1)}, bf16[512,384]{1,0:T(8,128)(2,1)S(1)}, u32[]{:S(2)}, u32[]{:S(2)}) collective-permute-start(bf16[512,384]{1,0:T(8,128)(2,1)S(1)} %collective-permute-done.2.refs_1_), channel_id=1, source_target_pairs={{0,2},{1,3},{2,4},{3,5},{4,6},{5,7},{6,0},{7,1},{8,10},{9,11},{10,... | collective-permute-start | bytes 1179656 | tf_op jit(solution)/shard_map/ppermute | solution.py:35
  86.8 3.7 %collective-permute-start.8 = (bf16[512,384]{1,0:T(8,128)(2,1)S(1)}, bf16[512,384]{1,0:T(8,128)(2,1)S(1)}, u32[]{:S(2)}, u32[]{:S(2)}) collective-permute-start(bf16[512,384]{1,0:T(8,128)(2,1)S(1)} %collective-permute-done.2.refs_1_), channel_id=1, source_target_pairs={{0,4},{1,5},{2,6},{3,7},{4,0},{5,1},{6,2},{7,3},{8,12},{9,13},{10,... | collective-permute-start | bytes 1179656 | tf_op jit(solution)/shard_map/ppermute | solution.py:35
  90.5 0.6 pad_add_fusion.place
  91.1 3.8 %collective-permute-done.7.refs_6_ = bf16[512,384]{1,0:T(8,128)(2,1)S(1)} collective-permute-done((bf16[512,384]{1,0:T(8,128)(2,1)S(1)}, bf16[512,384]{1,0:T(8,128)(2,1)S(1)}, u32[]{:S(2)}, u32[]{:S(2)}) %collective-permute-start.7) | collective-permute-done | bytes 393248 | tf_op jit(solution)/shard_map/ppermute | solution.py:35
  94.9 7.8 %collective-permute-done.4.refs_3_ = bf16[512,384]{1,0:T(8,128)(2,1)S(1)} collective-permute-done((bf16[512,384]{1,0:T(8,128)(2,1)S(1)}, bf16[512,384]{1,0:T(8,128)(2,1)S(1)}, u32[]{:S(2)}, u32[]{:S(2)}) %collective-permute-start.4) | collective-permute-done | bytes 393248 | tf_op jit(solution)/shard_map/ppermute | solution.py:35
  102.7 4.4 %collective-permute-done.6.refs_5_ = bf16[512,384]{1,0:T(8,128)(2,1)S(1)} collective-permute-done((bf16[512,384]{1,0:T(8,128)(2,1)S(1)}, bf16[512,384]{1,0:T(8,128)(2,1)S(1)}, u32[]{:S(2)}, u32[]{:S(2)}) %collective-permute-start.6) | collective-permute-done | bytes 393248 | tf_op jit(solution)/shard_map/ppermute | solution.py:35
  107.0 4.8 %collective-permute-done.8.refs_7_ = bf16[512,384]{1,0:T(8,128)(2,1)S(1)} collective-permute-done((bf16[512,384]{1,0:T(8,128)(2,1)S(1)}, bf16[512,384]{1,0:T(8,128)(2,1)S(1)}, u32[]{:S(2)}, u32[]{:S(2)}) %collective-permute-start.8) | collective-permute-done | bytes 393248 | tf_op jit(solution)/shard_map/ppermute | solution.py:35
  111.8 1.3 all-gather.3.cloned.1.call-done
  113.2 10.7 %shard_map.37 = (bf16[128,384]{1,0:T(8,128)(2,1)}, bf16[128,384]{1,0:T(8,128)(2,1)}, bf16[128,384]{1,0:T(8,128)(2,1)}, bf16[128,384]{1,0:T(8,128)(2,1)}) custom-call(s32[3]{0:T(128)} %pad_add_fusion.place, s32[8,8]{1,0:T(8,128)} %mask.1, bf16[32,3,96,384]{3,2,1,0:T(8,128)(2,1)} %bitcast.25, bf16[512,384]{1,0:T(8,128)(2,1)} %bitcast.30, ...), custom_call_target="tpu_custom_call" | custom-call | tf_op jit(solution)/shard_map/pallas_call | solution.py:132
  123.9 5.4 %collective-permute-start.10 = (bf16[128,384]{1,0:T(8,128)(2,1)}, bf16[128,384]{1,0:T(8,128)(2,1)S(1)}, u32[]{:S(2)}, u32[]{:S(2)}) collective-permute-start(bf16[128,384]{1,0:T(8,128)(2,1)} %get-tuple-element.14), channel_id=1, source_target_pairs={{0,8},{1,16},{2,10},{3,18},{4,12},{5,20},{6,14},{7,22},{8,0},{9,24... | collective-permute-start | bytes 294920 | tf_op jit(solution)/shard_map/ppermute | solution.py:35
  129.3 3.5 %collective-permute-start.11 = (bf16[128,384]{1,0:T(8,128)(2,1)}, bf16[128,384]{1,0:T(8,128)(2,1)S(1)}, u32[]{:S(2)}, u32[]{:S(2)}) collective-permute-start(bf16[128,384]{1,0:T(8,128)(2,1)} %get-tuple-element.15), channel_id=1, source_target_pairs={{0,16},{1,8},{2,18},{3,10},{4,20},{5,12},{6,22},{7,14},{8,24},{9,0... | collective-permute-start | bytes 294920 | tf_op jit(solution)/shard_map/ppermute | solution.py:35
  132.8 1.9 %collective-permute-start.12 = (bf16[128,384]{1,0:T(8,128)(2,1)}, bf16[128,384]{1,0:T(8,128)(2,1)S(1)}, u32[]{:S(2)}, u32[]{:S(2)}) collective-permute-start(bf16[128,384]{1,0:T(8,128)(2,1)} %get-tuple-element.16), channel_id=1, source_target_pairs={{0,24},{1,0},{2,26},{3,2},{4,28},{5,4},{6,30},{7,6},{8,16},{9,8},{... | collective-permute-start | bytes 294920 | tf_op jit(solution)/shard_map/ppermute | solution.py:35
  134.7 3.5 %collective-permute-start.9 = (bf16[128,384]{1,0:T(8,128)(2,1)}, bf16[128,384]{1,0:T(8,128)(2,1)S(1)}, u32[]{:S(2)}, u32[]{:S(2)}) collective-permute-start(bf16[128,384]{1,0:T(8,128)(2,1)} %get-tuple-element.13), channel_id=1, source_target_pairs={{0,0},{1,24},{2,2},{3,26},{4,4},{5,28},{6,6},{7,30},{8,8},{9,16},{... | collective-permute-start | bytes 294920 | tf_op jit(solution)/shard_map/ppermute | solution.py:35
  138.3 1.3 collective-permute-done.12
  139.6 2.5 %collective-permute-done.9 = bf16[128,384]{1,0:T(8,128)(2,1)S(1)} collective-permute-done((bf16[128,384]{1,0:T(8,128)(2,1)}, bf16[128,384]{1,0:T(8,128)(2,1)S(1)}, u32[]{:S(2)}, u32[]{:S(2)}) %collective-permute-start.9) | collective-permute-done | bytes 98336 | tf_op jit(solution)/shard_map/ppermute | solution.py:35
  142.1 0.1 select_bitcast_fusion.3
  142.2 0.1 pad_maximum_fusion.1
  142.2 25.4 %all_to_all.11 = bf16[16,4,8,384]{3,2,1,0:T(8,128)(2,1)S(1)} all-to-all(bf16[16,4,8,384]{3,2,1,0:T(8,128)(2,1)S(1)} %pad_maximum_fusion.1), channel_id=1, replica_groups=mesh['z'=16,'x'=4,'y'=4,'c'=2] {'z'}, dimensions={0} | all-to-all | bytes 786432 | tf_op jit(solution)/shard_map/all_to_all | solution.py:187
  167.6 0.7 copy.10
  (24 shorter events, 0.1 us)
Async XLA Ops:
  6.5 106.6 %all-gather.3.cloned.1.call-start = ((), (), s32[]{:S(2)}) async-start(), calls=%async_computation.2 | async-start | bytes 7299072 | tf_op jit(solution)/shard_map/all_gather | solution.py:173
  6.5 9.3 %collective-permute-start = (bf16[3,48,384]{2,1,0:T(8,128)(2,1)}, bf16[3,48,384]{2,1,0:T(8,128)(2,1)S(1)}, u32[]{:S(2)}, u32[]{:S(2)}) collective-permute-start(bf16[3,48,384]{2,1,0:T(8,128)(2,1)} %bitcast.34), channel_id=1, source_target_pairs={{0,0},{1,24},{2,2},{3,26},{4,4},{5,28},{6,6},{7,30},{8,8},{9,16},{... | collective-permute-start | bytes 331784 | tf_op jit(solution)/shard_map/ppermute | solution.py:35
  12.3 7.8 %collective-permute-start.1 = (bf16[3,48,384]{2,1,0:T(8,128)(2,1)}, bf16[3,48,384]{2,1,0:T(8,128)(2,1)S(1)}, u32[]{:S(2)}, u32[]{:S(2)}) collective-permute-start(bf16[3,48,384]{2,1,0:T(8,128)(2,1)} %bitcast.35), channel_id=1, source_target_pairs={{0,8},{1,16},{2,10},{3,18},{4,12},{5,20},{6,14},{7,22},{8,0},{9,24... | collective-permute-start | bytes 331784 | tf_op jit(solution)/shard_map/ppermute | solution.py:35
  65.9 47.2 %copy-start = (bf16[64,8,384]{2,1,0:T(8,128)(2,1)}, bf16[64,8,384]{2,1,0:T(8,128)(2,1)S(1)}, u32[]{:S(2)}) copy-start(bf16[64,8,384]{2,1,0:T(8,128)(2,1)S(1)} %all_to_all.10) | copy-start | bytes 1179652
  65.9 15.4 %collective-permute-start.2 = (bf16[512,384]{1,0:T(8,128)(2,1)S(1)}, bf16[512,384]{1,0:T(8,128)(2,1)S(1)}, u32[]{:S(2)}, u32[]{:S(2)}) collective-permute-start(bf16[512,384]{1,0:T(8,128)(2,1)S(1)} %bitcast.26), channel_id=1, source_target_pairs={{0,24},{1,25},{2,26},{3,27},{4,28},{5,29},{6,30},{7,31},{8,16},{9,... | collective-permute-start | bytes 1179656 | tf_op jit(solution)/shard_map/ppermute | solution.py:35
  71.2 15.6 %collective-permute-start.3 = (bf16[512,384]{1,0:T(8,128)(2,1)S(1)}, bf16[512,384]{1,0:T(8,128)(2,1)S(1)}, u32[]{:S(2)}, u32[]{:S(2)}) collective-permute-start(bf16[512,384]{1,0:T(8,128)(2,1)S(1)} %bitcast.27), channel_id=1, source_target_pairs={{0,6},{1,7},{2,0},{3,1},{4,2},{5,3},{6,4},{7,5},{8,14},{9,15},{10,... | collective-permute-start | bytes 1179656 | tf_op jit(solution)/shard_map/ppermute | solution.py:35
  75.8 15.2 %collective-permute-start.5 = (bf16[512,384]{1,0:T(8,128)(2,1)S(1)}, bf16[512,384]{1,0:T(8,128)(2,1)S(1)}, u32[]{:S(2)}, u32[]{:S(2)}) collective-permute-start(bf16[512,384]{1,0:T(8,128)(2,1)S(1)} %bitcast.28), channel_id=1, source_target_pairs={{0,2},{1,3},{2,4},{3,5},{4,6},{5,7},{6,0},{7,1},{8,10},{9,11},{10,... | collective-permute-start | bytes 1179656 | tf_op jit(solution)/shard_map/ppermute | solution.py:35
  77.8 17.1 %collective-permute-start.7 = (bf16[512,384]{1,0:T(8,128)(2,1)S(1)}, bf16[512,384]{1,0:T(8,128)(2,1)S(1)}, u32[]{:S(2)}, u32[]{:S(2)}) collective-permute-start(bf16[512,384]{1,0:T(8,128)(2,1)S(1)} %bitcast.29), channel_id=1, source_target_pairs={{0,4},{1,5},{2,6},{3,7},{4,0},{5,1},{6,2},{7,3},{8,12},{9,13},{10,... | collective-permute-start | bytes 1179656 | tf_op jit(solution)/shard_map/ppermute | solution.py:35
  81.3 31.8 %copy-start.1 = (bf16[512,384]{1,0:T(8,128)(2,1)}, bf16[512,384]{1,0:T(8,128)(2,1)S(1)}, u32[]{:S(2)}) copy-start(bf16[512,384]{1,0:T(8,128)(2,1)S(1)} %collective-permute-done.2.refs_1_) | copy-start | bytes 1179652
  81.3 21.3 %collective-permute-start.4 = (bf16[512,384]{1,0:T(8,128)(2,1)S(1)}, bf16[512,384]{1,0:T(8,128)(2,1)S(1)}, u32[]{:S(2)}, u32[]{:S(2)}) collective-permute-start(bf16[512,384]{1,0:T(8,128)(2,1)S(1)} %collective-permute-done.2.refs_1_), channel_id=1, source_target_pairs={{0,6},{1,7},{2,0},{3,1},{4,2},{5,3},{6,4},{7,5},{8,14},{9,15},{10,... | collective-permute-start | bytes 1179656 | tf_op jit(solution)/shard_map/ppermute | solution.py:35
  84.3 22.7 %collective-permute-start.6 = (bf16[512,384]{1,0:T(8,128)(2,1)S(1)}, bf16[512,384]{1,0:T(8,128)(2,1)S(1)}, u32[]{:S(2)}, u32[]{:S(2)}) collective-permute-start(bf16[512,384]{1,0:T(8,128)(2,1)S(1)} %collective-permute-done.2.refs_1_), channel_id=1, source_target_pairs={{0,2},{1,3},{2,4},{3,5},{4,6},{5,7},{6,0},{7,1},{8,10},{9,11},{10,... | collective-permute-start | bytes 1179656 | tf_op jit(solution)/shard_map/ppermute | solution.py:35
  86.8 26.3 %copy-start.2 = (bf16[512,384]{1,0:T(8,128)(2,1)}, bf16[512,384]{1,0:T(8,128)(2,1)S(1)}, u32[]{:S(2)}) copy-start(bf16[512,384]{1,0:T(8,128)(2,1)S(1)} %collective-permute-done.3.refs_2_) | copy-start | bytes 1179652
  86.8 25.0 %collective-permute-start.8 = (bf16[512,384]{1,0:T(8,128)(2,1)S(1)}, bf16[512,384]{1,0:T(8,128)(2,1)S(1)}, u32[]{:S(2)}, u32[]{:S(2)}) collective-permute-start(bf16[512,384]{1,0:T(8,128)(2,1)S(1)} %collective-permute-done.2.refs_1_), channel_id=1, source_target_pairs={{0,4},{1,5},{2,6},{3,7},{4,0},{5,1},{6,2},{7,3},{8,12},{9,13},{10,... | collective-permute-start | bytes 1179656 | tf_op jit(solution)/shard_map/ppermute | solution.py:35
  91.1 22.1 %copy-start.3 = (bf16[512,384]{1,0:T(8,128)(2,1)}, bf16[512,384]{1,0:T(8,128)(2,1)S(1)}, u32[]{:S(2)}) copy-start(bf16[512,384]{1,0:T(8,128)(2,1)S(1)} %collective-permute-done.5.refs_4_) | copy-start | bytes 1179652
  94.9 18.3 %copy-start.4 = (bf16[512,384]{1,0:T(8,128)(2,1)}, bf16[512,384]{1,0:T(8,128)(2,1)S(1)}, u32[]{:S(2)}) copy-start(bf16[512,384]{1,0:T(8,128)(2,1)S(1)} %collective-permute-done.7.refs_6_) | copy-start | bytes 1179652
  102.7 10.5 %copy-start.5 = (bf16[512,384]{1,0:T(8,128)(2,1)}, bf16[512,384]{1,0:T(8,128)(2,1)S(1)}, u32[]{:S(2)}) copy-start(bf16[512,384]{1,0:T(8,128)(2,1)S(1)} %collective-permute-done.4.refs_3_) | copy-start | bytes 1179652
  107.0 6.1 %copy-start.6 = (bf16[512,384]{1,0:T(8,128)(2,1)}, bf16[512,384]{1,0:T(8,128)(2,1)S(1)}, u32[]{:S(2)}) copy-start(bf16[512,384]{1,0:T(8,128)(2,1)S(1)} %collective-permute-done.6.refs_5_) | copy-start | bytes 1179652
  111.8 1.4 copy-start.7
  123.9 14.4 %collective-permute-start.10 = (bf16[128,384]{1,0:T(8,128)(2,1)}, bf16[128,384]{1,0:T(8,128)(2,1)S(1)}, u32[]{:S(2)}, u32[]{:S(2)}) collective-permute-start(bf16[128,384]{1,0:T(8,128)(2,1)} %get-tuple-element.14), channel_id=1, source_target_pairs={{0,8},{1,16},{2,10},{3,18},{4,12},{5,20},{6,14},{7,22},{8,0},{9,24... | collective-permute-start | bytes 294920 | tf_op jit(solution)/shard_map/ppermute | solution.py:35
  129.3 9.0 %collective-permute-start.11 = (bf16[128,384]{1,0:T(8,128)(2,1)}, bf16[128,384]{1,0:T(8,128)(2,1)S(1)}, u32[]{:S(2)}, u32[]{:S(2)}) collective-permute-start(bf16[128,384]{1,0:T(8,128)(2,1)} %get-tuple-element.15), channel_id=1, source_target_pairs={{0,16},{1,8},{2,18},{3,10},{4,20},{5,12},{6,22},{7,14},{8,24},{9,0... | collective-permute-start | bytes 294920 | tf_op jit(solution)/shard_map/ppermute | solution.py:35
  132.8 6.8 %collective-permute-start.12 = (bf16[128,384]{1,0:T(8,128)(2,1)}, bf16[128,384]{1,0:T(8,128)(2,1)S(1)}, u32[]{:S(2)}, u32[]{:S(2)}) collective-permute-start(bf16[128,384]{1,0:T(8,128)(2,1)} %get-tuple-element.16), channel_id=1, source_target_pairs={{0,24},{1,0},{2,26},{3,2},{4,28},{5,4},{6,30},{7,6},{8,16},{9,8},{... | collective-permute-start | bytes 294920 | tf_op jit(solution)/shard_map/ppermute | solution.py:35
  134.7 7.4 %collective-permute-start.9 = (bf16[128,384]{1,0:T(8,128)(2,1)}, bf16[128,384]{1,0:T(8,128)(2,1)S(1)}, u32[]{:S(2)}, u32[]{:S(2)}) collective-permute-start(bf16[128,384]{1,0:T(8,128)(2,1)} %get-tuple-element.13), channel_id=1, source_target_pairs={{0,0},{1,24},{2,2},{3,26},{4,4},{5,28},{6,6},{7,30},{8,8},{9,16},{... | collective-permute-start | bytes 294920 | tf_op jit(solution)/shard_map/ppermute | solution.py:35
Sparse Core Ops, SparseCore 0:
  21.0 92.0 all-gather.2

commit v13 on v8

--- a/solution.py
+++ b/solution.py
@@ -48,24 +48,27 @@
     weights, tokens, sums, qkv, bias, result, w_sems, x_sems = refs[12:]
     y, group, place_x = place[0], place[1], place[2]
 
-    token_copies = []
+    token_copies, weight_copies = [], []
+    per_chunk = CHUNK // PART
     for i, piece in enumerate(pieces):
-        source = lax.rem(y + SHIFTS[i // 2], NY)
         half = group if i % 2 == 0 else 1 - group
-        at = pl.multiple_of((2 * source + half) * GROUP, GROUP)
+        at = pl.multiple_of(i // 2 * CHUNK + half * GROUP, GROUP)
         token_copies.append(pltpu.make_async_copy(piece, tokens.at[:, pl.ds(at, GROUP)], x_sems.at[i]))
-    weight_copies = []
     for chunk in range(D // CHUNK):
-        parts = pl.ds(chunk * (CHUNK // PART), CHUNK // PART)
+        source = lax.rem(y + SHIFTS[chunk], NY) * per_chunk
+        parts = pl.ds(chunk * per_chunk, per_chunk)
         for j in range(3):
             lanes = pl.ds(j * GROUP, GROUP)
             weight_copies.append(
                 pltpu.make_async_copy(
-                    gathered.at[parts, j], weights.at[parts, :, lanes], w_sems.at[chunk, j]
+                    gathered.at[pl.ds(source, per_chunk), j],
+                    weights.at[parts, :, lanes],
+                    w_sems.at[chunk, j],
                 )
             )
-    for copy in token_copies + weight_copies:
-        copy.start()
+    for chunk in range(D // CHUNK):
+        for copy in token_copies[2 * chunk : 2 * chunk + 2] + weight_copies[3 * chunk : 3 * chunk + 3]:
+            copy.start()
 
     span_rows = TOKENS // SPANS
     column = lax.broadcasted_iota(jnp.int32, (1, TOKENS), 1)
@@ -79,10 +82,8 @@
         ok = same & (jnp.broadcast_to(row, (span_rows, TOKENS)) > 0)
         bias[pl.ds(i * span_rows, span_rows), :] = jnp.where(ok, 0.0, -1e30)
 
-    for copy in token_copies:
-        copy.wait()
     for chunk in range(D // CHUNK):
-        for copy in weight_copies[3 * chunk : 3 * chunk + 3]:
+        for copy in token_copies[2 * chunk : 2 * chunk + 2] + weight_copies[3 * chunk : 3 * chunk + 3]:
             copy.wait()
         features = pl.ds(chunk * CHUNK, CHUNK)
         parts = pl.ds(chunk * (CHUNK // PART), CHUNK // PART)

time: 174 us -> 173 us (level)
  no operation moved by 1% of the time
where the time goes in v13:
time: 173 us
  blocking collectives  70.9 us (41%)
  starting transfers between devices  46.3 us (27%)
  waiting for transfers between devices  30.2 us (17%)
  between operations  13.6 us (8%)
  Pallas kernels  8.87 us (5%)
  local copies, waits for them, and re-layouts  1.83 us (1%)
    ppermute x13, starting transfers between devices, permute(): return lax.ppermute(array, AXES, pairs)  46.3 us
    all_to_all x1, blocking collectives, per_device(): lax.all_to_all(packed, ('z', 'x'), split_axis=0, concat_axis=0, tiled=True)  45.1 us
    ppermute x13, waiting for transfers between devices, permute(): return lax.ppermute(array, AXES, pairs)  28.7 us
    all_to_all x1, blocking collectives, per_device(): lax.all_to_all(output, 'z', split_axis=0, concat_axis=0, tiled=True)  25.8 us
    pallas_call x1, Pallas kernels, project_and_attend(): pl.pallas_call(attend_kernel, out_shape=[jax.ShapeDtypeStruct((TOKENS //...  8.87 us
  transfers between devices with their start and end apart: 14, of which 8 were waited for; matrix products, arithmetic and copies ran while one was open for 1% of the time, Pallas kernels for 0%

profile of v13, /device:TPU:1, one launch (start us, length us, event | category | flops | bytes accessed | tf_op | source)
XLA Modules:
  0.0 172.9 jit_solution(7081177666288208052)
XLA Ops:
  6.5 5.9 %collective-permute-start = (bf16[3,48,384]{2,1,0:T(8,128)(2,1)}, bf16[3,48,384]{2,1,0:T(8,128)(2,1)S(1)}, u32[]{:S(2)}, u32[]{:S(2)}) collective-permute-start(bf16[3,48,384]{2,1,0:T(8,128)(2,1)} %bitcast.34), channel_id=1, source_target_pairs={{0,0},{1,24},{2,2},{3,26},{4,4},{5,28},{6,6},{7,30},{8,8},{9,16},{... | collective-permute-start | bytes 331784 | tf_op jit(solution)/shard_map/ppermute | solution.py:34
  12.4 2.2 %collective-permute-start.1 = (bf16[3,48,384]{2,1,0:T(8,128)(2,1)}, bf16[3,48,384]{2,1,0:T(8,128)(2,1)S(1)}, u32[]{:S(2)}, u32[]{:S(2)}) collective-permute-start(bf16[3,48,384]{2,1,0:T(8,128)(2,1)} %bitcast.35), channel_id=1, source_target_pairs={{0,8},{1,16},{2,10},{3,18},{4,12},{5,20},{6,14},{7,22},{8,0},{9,24... | collective-permute-start | bytes 331784 | tf_op jit(solution)/shard_map/ppermute | solution.py:34
  14.7 1.1 constant_dynamic-slice_fusion
  15.8 0.1 reverse_select_fusion
  16.0 4.3 %collective-permute-done.1 = bf16[3,48,384]{2,1,0:T(8,128)(2,1)S(1)} collective-permute-done((bf16[3,48,384]{2,1,0:T(8,128)(2,1)}, bf16[3,48,384]{2,1,0:T(8,128)(2,1)S(1)}, u32[]{:S(2)}, u32[]{:S(2)}) %collective-permute-start.1) | collective-permute-done | bytes 110624 | tf_op jit(solution)/shard_map/ppermute | solution.py:34
  20.2 0.7 maximum_select_fusion
  21.0 0.0 all-gather.3.cloned.1.call-update
  21.0 45.1 %all_to_all.10 = bf16[64,8,384]{2,1,0:T(8,128)(2,1)S(1)} all-to-all(bf16[64,8,384]{2,1,0:T(8,128)(2,1)S(1)} %bitcast.31), channel_id=1, replica_groups=mesh['z'=16,'x'=4,'y'=4,'c'=2] {'z','x'}, dimensions={0} | all-to-all | bytes 786432 | tf_op jit(solution)/shard_map/all_to_all | solution.py:181
  66.1 5.2 %collective-permute-start.2 = (bf16[512,384]{1,0:T(8,128)(2,1)S(1)}, bf16[512,384]{1,0:T(8,128)(2,1)S(1)}, u32[]{:S(2)}, u32[]{:S(2)}) collective-permute-start(bf16[512,384]{1,0:T(8,128)(2,1)S(1)} %bitcast.25), channel_id=1, source_target_pairs={{0,24},{1,25},{2,26},{3,27},{4,28},{5,29},{6,30},{7,31},{8,16},{9,... | collective-permute-start | bytes 1179656 | tf_op jit(solution)/shard_map/ppermute | solution.py:34
  71.3 4.6 %collective-permute-start.3 = (bf16[512,384]{1,0:T(8,128)(2,1)S(1)}, bf16[512,384]{1,0:T(8,128)(2,1)S(1)}, u32[]{:S(2)}, u32[]{:S(2)}) collective-permute-start(bf16[512,384]{1,0:T(8,128)(2,1)S(1)} %bitcast.26), channel_id=1, source_target_pairs={{0,6},{1,7},{2,0},{3,1},{4,2},{5,3},{6,4},{7,5},{8,14},{9,15},{10,... | collective-permute-start | bytes 1179656 | tf_op jit(solution)/shard_map/ppermute | solution.py:34
  76.0 1.9 %collective-permute-start.5 = (bf16[512,384]{1,0:T(8,128)(2,1)S(1)}, bf16[512,384]{1,0:T(8,128)(2,1)S(1)}, u32[]{:S(2)}, u32[]{:S(2)}) collective-permute-start(bf16[512,384]{1,0:T(8,128)(2,1)S(1)} %bitcast.27), channel_id=1, source_target_pairs={{0,2},{1,3},{2,4},{3,5},{4,6},{5,7},{6,0},{7,1},{8,10},{9,11},{10,... | collective-permute-start | bytes 1179656 | tf_op jit(solution)/shard_map/ppermute | solution.py:34
  77.9 3.6 %collective-permute-start.7 = (bf16[512,384]{1,0:T(8,128)(2,1)S(1)}, bf16[512,384]{1,0:T(8,128)(2,1)S(1)}, u32[]{:S(2)}, u32[]{:S(2)}) collective-permute-start(bf16[512,384]{1,0:T(8,128)(2,1)S(1)} %bitcast.28), channel_id=1, source_target_pairs={{0,4},{1,5},{2,6},{3,7},{4,0},{5,1},{6,2},{7,3},{8,12},{9,13},{10,... | collective-permute-start | bytes 1179656 | tf_op jit(solution)/shard_map/ppermute | solution.py:34
  81.5 2.9 %collective-permute-start.4 = (bf16[512,384]{1,0:T(8,128)(2,1)S(1)}, bf16[512,384]{1,0:T(8,128)(2,1)S(1)}, u32[]{:S(2)}, u32[]{:S(2)}) collective-permute-start(bf16[512,384]{1,0:T(8,128)(2,1)S(1)} %collective-permute-done.2.refs_1_), channel_id=1, source_target_pairs={{0,6},{1,7},{2,0},{3,1},{4,2},{5,3},{6,4},{7,5},{8,14},{9,15},{10,... | collective-permute-start | bytes 1179656 | tf_op jit(solution)/shard_map/ppermute | solution.py:34
  84.4 2.5 %collective-permute-start.6 = (bf16[512,384]{1,0:T(8,128)(2,1)S(1)}, bf16[512,384]{1,0:T(8,128)(2,1)S(1)}, u32[]{:S(2)}, u32[]{:S(2)}) collective-permute-start(bf16[512,384]{1,0:T(8,128)(2,1)S(1)} %collective-permute-done.2.refs_1_), channel_id=1, source_target_pairs={{0,2},{1,3},{2,4},{3,5},{4,6},{5,7},{6,0},{7,1},{8,10},{9,11},{10,... | collective-permute-start | bytes 1179656 | tf_op jit(solution)/shard_map/ppermute | solution.py:34
  86.9 3.7 %collective-permute-start.8 = (bf16[512,384]{1,0:T(8,128)(2,1)S(1)}, bf16[512,384]{1,0:T(8,128)(2,1)S(1)}, u32[]{:S(2)}, u32[]{:S(2)}) collective-permute-start(bf16[512,384]{1,0:T(8,128)(2,1)S(1)} %collective-permute-done.2.refs_1_), channel_id=1, source_target_pairs={{0,4},{1,5},{2,6},{3,7},{4,0},{5,1},{6,2},{7,3},{8,12},{9,13},{10,... | collective-permute-start | bytes 1179656 | tf_op jit(solution)/shard_map/ppermute | solution.py:34
  90.6 0.1 pad_add_fusion.place
  90.7 4.3 %collective-permute-done.7.refs_6_ = bf16[512,384]{1,0:T(8,128)(2,1)S(1)} collective-permute-done((bf16[512,384]{1,0:T(8,128)(2,1)S(1)}, bf16[512,384]{1,0:T(8,128)(2,1)S(1)}, u32[]{:S(2)}, u32[]{:S(2)}) %collective-permute-start.7) | collective-permute-done | bytes 393248 | tf_op jit(solution)/shard_map/ppermute | solution.py:34
  95.0 7.8 %collective-permute-done.4.refs_3_ = bf16[512,384]{1,0:T(8,128)(2,1)S(1)} collective-permute-done((bf16[512,384]{1,0:T(8,128)(2,1)S(1)}, bf16[512,384]{1,0:T(8,128)(2,1)S(1)}, u32[]{:S(2)}, u32[]{:S(2)}) %collective-permute-start.4) | collective-permute-done | bytes 393248 | tf_op jit(solution)/shard_map/ppermute | solution.py:34
  102.8 4.4 %collective-permute-done.6.refs_5_ = bf16[512,384]{1,0:T(8,128)(2,1)S(1)} collective-permute-done((bf16[512,384]{1,0:T(8,128)(2,1)S(1)}, bf16[512,384]{1,0:T(8,128)(2,1)S(1)}, u32[]{:S(2)}, u32[]{:S(2)}) %collective-permute-start.6) | collective-permute-done | bytes 393248 | tf_op jit(solution)/shard_map/ppermute | solution.py:34
  107.1 4.8 %collective-permute-done.8.refs_7_ = bf16[512,384]{1,0:T(8,128)(2,1)S(1)} collective-permute-done((bf16[512,384]{1,0:T(8,128)(2,1)S(1)}, bf16[512,384]{1,0:T(8,128)(2,1)S(1)}, u32[]{:S(2)}, u32[]{:S(2)}) %collective-permute-start.8) | collective-permute-done | bytes 393248 | tf_op jit(solution)/shard_map/ppermute | solution.py:34
  111.9 1.5 all-gather.3.cloned.1.call-done
  113.4 8.9 %shard_map.37 = (bf16[128,384]{1,0:T(8,128)(2,1)S(1)}, bf16[128,384]{1,0:T(8,128)(2,1)S(1)}, bf16[128,384]{1,0:T(8,128)(2,1)S(1)}, bf16[128,384]{1,0:T(8,128)(2,1)S(1)}) custom-call(s32[3]{0:T(128)S(1)} %pad_add_fusion.place, s32[8,8]{1,0:T(8,128)S(1)} %copy-done, bf16[32,3,96,384]{3,2,1,0:T(8,128)(2,1)} %bitcast.30, bf16[512,384]{1,0:T(8,128)(2,1)S(1)} %bitcast.29, ...), custom_call_target="tpu_custom_call" | custom-call | tf_op jit(solution)/shard_map/pallas_call | solution.py:138
  122.3 4.9 %collective-permute-start.10 = (bf16[128,384]{1,0:T(8,128)(2,1)S(1)}, bf16[128,384]{1,0:T(8,128)(2,1)S(1)}, u32[]{:S(2)}, u32[]{:S(2)}) collective-permute-start(bf16[128,384]{1,0:T(8,128)(2,1)S(1)} %get-tuple-element.14), channel_id=1, source_target_pairs={{0,8},{1,16},{2,10},{3,18},{4,12},{5,20},{6,14},{7,22},{8,0},{9,24... | collective-permute-start | bytes 294920 | tf_op jit(solution)/shard_map/ppermute | solution.py:34
  127.2 3.1 %collective-permute-start.11 = (bf16[128,384]{1,0:T(8,128)(2,1)S(1)}, bf16[128,384]{1,0:T(8,128)(2,1)S(1)}, u32[]{:S(2)}, u32[]{:S(2)}) collective-permute-start(bf16[128,384]{1,0:T(8,128)(2,1)S(1)} %get-tuple-element.15), channel_id=1, source_target_pairs={{0,16},{1,8},{2,18},{3,10},{4,20},{5,12},{6,22},{7,14},{8,24},{9,0... | collective-permute-start | bytes 294920 | tf_op jit(solution)/shard_map/ppermute | solution.py:34
  130.2 1.9 %collective-permute-start.12 = (bf16[128,384]{1,0:T(8,128)(2,1)S(1)}, bf16[128,384]{1,0:T(8,128)(2,1)S(1)}, u32[]{:S(2)}, u32[]{:S(2)}) collective-permute-start(bf16[128,384]{1,0:T(8,128)(2,1)S(1)} %get-tuple-element.16), channel_id=1, source_target_pairs={{0,24},{1,0},{2,26},{3,2},{4,28},{5,4},{6,30},{7,6},{8,16},{9,8},{... | collective-permute-start | bytes 294920 | tf_op jit(solution)/shard_map/ppermute | solution.py:34
  132.2 3.9 %collective-permute-start.9 = (bf16[128,384]{1,0:T(8,128)(2,1)S(1)}, bf16[128,384]{1,0:T(8,128)(2,1)S(1)}, u32[]{:S(2)}, u32[]{:S(2)}) collective-permute-start(bf16[128,384]{1,0:T(8,128)(2,1)S(1)} %get-tuple-element.13), channel_id=1, source_target_pairs={{0,0},{1,24},{2,2},{3,26},{4,4},{5,28},{6,6},{7,30},{8,8},{9,16},{... | collective-permute-start | bytes 294920 | tf_op jit(solution)/shard_map/ppermute | solution.py:34
  136.1 0.7 collective-permute-done.12
  136.8 2.5 %collective-permute-done.9 = bf16[128,384]{1,0:T(8,128)(2,1)S(1)} collective-permute-done((bf16[128,384]{1,0:T(8,128)(2,1)S(1)}, bf16[128,384]{1,0:T(8,128)(2,1)S(1)}, u32[]{:S(2)}, u32[]{:S(2)}) %collective-permute-start.9) | collective-permute-done | bytes 98336 | tf_op jit(solution)/shard_map/ppermute | solution.py:34
  139.3 0.1 select_bitcast_fusion.3
  139.4 0.1 pad_maximum_fusion.1
  139.5 25.8 %all_to_all.11 = bf16[16,4,8,384]{3,2,1,0:T(8,128)(2,1)S(1)} all-to-all(bf16[16,4,8,384]{3,2,1,0:T(8,128)(2,1)S(1)} %pad_maximum_fusion.1), channel_id=1, replica_groups=mesh['z'=16,'x'=4,'y'=4,'c'=2] {'z'}, dimensions={0} | all-to-all | bytes 786432 | tf_op jit(solution)/shard_map/all_to_all | solution.py:194
  165.3 0.7 copy.10
  (10 shorter events, 0.1 us)
Async XLA Ops:
  6.5 106.9 %copy-start = (s32[8,8]{1,0:T(8,128)S(1)}, s32[8,8]{1,0:T(8,128)}, u32[]{:S(2)}) copy-start(s32[8,8]{1,0:T(8,128)} %mask.1) | copy-start | bytes 772
  6.5 106.8 %all-gather.3.cloned.1.call-start = ((), (), s32[]{:S(2)}) async-start(), calls=%async_computation.2 | async-start | bytes 7299072 | tf_op jit(solution)/shard_map/all_gather | solution.py:180
  6.5 9.4 %collective-permute-start = (bf16[3,48,384]{2,1,0:T(8,128)(2,1)}, bf16[3,48,384]{2,1,0:T(8,128)(2,1)S(1)}, u32[]{:S(2)}, u32[]{:S(2)}) collective-permute-start(bf16[3,48,384]{2,1,0:T(8,128)(2,1)} %bitcast.34), channel_id=1, source_target_pairs={{0,0},{1,24},{2,2},{3,26},{4,4},{5,28},{6,6},{7,30},{8,8},{9,16},{... | collective-permute-start | bytes 331784 | tf_op jit(solution)/shard_map/ppermute | solution.py:34
  12.4 7.8 %collective-permute-start.1 = (bf16[3,48,384]{2,1,0:T(8,128)(2,1)}, bf16[3,48,384]{2,1,0:T(8,128)(2,1)S(1)}, u32[]{:S(2)}, u32[]{:S(2)}) collective-permute-start(bf16[3,48,384]{2,1,0:T(8,128)(2,1)} %bitcast.35), channel_id=1, source_target_pairs={{0,8},{1,16},{2,10},{3,18},{4,12},{5,20},{6,14},{7,22},{8,0},{9,24... | collective-permute-start | bytes 331784 | tf_op jit(solution)/shard_map/ppermute | solution.py:34
  66.1 15.4 %collective-permute-start.2 = (bf16[512,384]{1,0:T(8,128)(2,1)S(1)}, bf16[512,384]{1,0:T(8,128)(2,1)S(1)}, u32[]{:S(2)}, u32[]{:S(2)}) collective-permute-start(bf16[512,384]{1,0:T(8,128)(2,1)S(1)} %bitcast.25), channel_id=1, source_target_pairs={{0,24},{1,25},{2,26},{3,27},{4,28},{5,29},{6,30},{7,31},{8,16},{9,... | collective-permute-start | bytes 1179656 | tf_op jit(solution)/shard_map/ppermute | solution.py:34
  71.3 15.6 %collective-permute-start.3 = (bf16[512,384]{1,0:T(8,128)(2,1)S(1)}, bf16[512,384]{1,0:T(8,128)(2,1)S(1)}, u32[]{:S(2)}, u32[]{:S(2)}) collective-permute-start(bf16[512,384]{1,0:T(8,128)(2,1)S(1)} %bitcast.26), channel_id=1, source_target_pairs={{0,6},{1,7},{2,0},{3,1},{4,2},{5,3},{6,4},{7,5},{8,14},{9,15},{10,... | collective-permute-start | bytes 1179656 | tf_op jit(solution)/shard_map/ppermute | solution.py:34
  76.0 14.7 %collective-permute-start.5 = (bf16[512,384]{1,0:T(8,128)(2,1)S(1)}, bf16[512,384]{1,0:T(8,128)(2,1)S(1)}, u32[]{:S(2)}, u32[]{:S(2)}) collective-permute-start(bf16[512,384]{1,0:T(8,128)(2,1)S(1)} %bitcast.27), channel_id=1, source_target_pairs={{0,2},{1,3},{2,4},{3,5},{4,6},{5,7},{6,0},{7,1},{8,10},{9,11},{10,... | collective-permute-start | bytes 1179656 | tf_op jit(solution)/shard_map/ppermute | solution.py:34
  77.9 17.1 %collective-permute-start.7 = (bf16[512,384]{1,0:T(8,128)(2,1)S(1)}, bf16[512,384]{1,0:T(8,128)(2,1)S(1)}, u32[]{:S(2)}, u32[]{:S(2)}) collective-permute-start(bf16[512,384]{1,0:T(8,128)(2,1)S(1)} %bitcast.28), channel_id=1, source_target_pairs={{0,4},{1,5},{2,6},{3,7},{4,0},{5,1},{6,2},{7,3},{8,12},{9,13},{10,... | collective-permute-start | bytes 1179656 | tf_op jit(solution)/shard_map/ppermute | solution.py:34
  81.5 21.3 %collective-permute-start.4 = (bf16[512,384]{1,0:T(8,128)(2,1)S(1)}, bf16[512,384]{1,0:T(8,128)(2,1)S(1)}, u32[]{:S(2)}, u32[]{:S(2)}) collective-permute-start(bf16[512,384]{1,0:T(8,128)(2,1)S(1)} %collective-permute-done.2.refs_1_), channel_id=1, source_target_pairs={{0,6},{1,7},{2,0},{3,1},{4,2},{5,3},{6,4},{7,5},{8,14},{9,15},{10,... | collective-permute-start | bytes 1179656 | tf_op jit(solution)/shard_map/ppermute | solution.py:34
  84.4 22.7 %collective-permute-start.6 = (bf16[512,384]{1,0:T(8,128)(2,1)S(1)}, bf16[512,384]{1,0:T(8,128)(2,1)S(1)}, u32[]{:S(2)}, u32[]{:S(2)}) collective-permute-start(bf16[512,384]{1,0:T(8,128)(2,1)S(1)} %collective-permute-done.2.refs_1_), channel_id=1, source_target_pairs={{0,2},{1,3},{2,4},{3,5},{4,6},{5,7},{6,0},{7,1},{8,10},{9,11},{10,... | collective-permute-start | bytes 1179656 | tf_op jit(solution)/shard_map/ppermute | solution.py:34
  86.9 25.0 %collective-permute-start.8 = (bf16[512,384]{1,0:T(8,128)(2,1)S(1)}, bf16[512,384]{1,0:T(8,128)(2,1)S(1)}, u32[]{:S(2)}, u32[]{:S(2)}) collective-permute-start(bf16[512,384]{1,0:T(8,128)(2,1)S(1)} %collective-permute-done.2.refs_1_), channel_id=1, source_target_pairs={{0,4},{1,5},{2,6},{3,7},{4,0},{5,1},{6,2},{7,3},{8,12},{9,13},{10,... | collective-permute-start | bytes 1179656 | tf_op jit(solution)/shard_map/ppermute | solution.py:34
  122.3 13.8 %collective-permute-start.10 = (bf16[128,384]{1,0:T(8,128)(2,1)S(1)}, bf16[128,384]{1,0:T(8,128)(2,1)S(1)}, u32[]{:S(2)}, u32[]{:S(2)}) collective-permute-start(bf16[128,384]{1,0:T(8,128)(2,1)S(1)} %get-tuple-element.14), channel_id=1, source_target_pairs={{0,8},{1,16},{2,10},{3,18},{4,12},{5,20},{6,14},{7,22},{8,0},{9,24... | collective-permute-start | bytes 294920 | tf_op jit(solution)/shard_map/ppermute | solution.py:34
  127.2 8.9 %collective-permute-start.11 = (bf16[128,384]{1,0:T(8,128)(2,1)S(1)}, bf16[128,384]{1,0:T(8,128)(2,1)S(1)}, u32[]{:S(2)}, u32[]{:S(2)}) collective-permute-start(bf16[128,384]{1,0:T(8,128)(2,1)S(1)} %get-tuple-element.15), channel_id=1, source_target_pairs={{0,16},{1,8},{2,18},{3,10},{4,20},{5,12},{6,22},{7,14},{8,24},{9,0... | collective-permute-start | bytes 294920 | tf_op jit(solution)/shard_map/ppermute | solution.py:34
  130.2 6.6 %collective-permute-start.12 = (bf16[128,384]{1,0:T(8,128)(2,1)S(1)}, bf16[128,384]{1,0:T(8,128)(2,1)S(1)}, u32[]{:S(2)}, u32[]{:S(2)}) collective-permute-start(bf16[128,384]{1,0:T(8,128)(2,1)S(1)} %get-tuple-element.16), channel_id=1, source_target_pairs={{0,24},{1,0},{2,26},{3,2},{4,28},{5,4},{6,30},{7,6},{8,16},{9,8},{... | collective-permute-start | bytes 294920 | tf_op jit(solution)/shard_map/ppermute | solution.py:34
  132.2 7.1 %collective-permute-start.9 = (bf16[128,384]{1,0:T(8,128)(2,1)S(1)}, bf16[128,384]{1,0:T(8,128)(2,1)S(1)}, u32[]{:S(2)}, u32[]{:S(2)}) collective-permute-start(bf16[128,384]{1,0:T(8,128)(2,1)S(1)} %get-tuple-element.13), channel_id=1, source_target_pairs={{0,0},{1,24},{2,2},{3,26},{4,4},{5,28},{6,6},{7,30},{8,8},{9,16},{... | collective-permute-start | bytes 294920 | tf_op jit(solution)/shard_map/ppermute | solution.py:34
Sparse Core Ops, SparseCore 0:
  21.1 92.2 all-gather.2

commit v14 on v13

--- a/solution.py
+++ b/solution.py
@@ -165,7 +165,7 @@
     low, high = places[..., :GROUP], places[..., GROUP:]
     low = jnp.where(c == 0, low, low[:, ::-1])
     high = jnp.where(c == 0, high[:, ::-1], high)
-    packed = jnp.concatenate([low, high], axis=1).reshape(NZ * NX, 8, GROUP)
+    packed = jnp.swapaxes(jnp.concatenate([low, high], axis=1), 0, 1).reshape(NZ * NX, 8, GROUP)
 
     piece = jnp.transpose(qkv_weight, (1, 0, 2))
     first = permute(piece, home)
@@ -178,8 +178,8 @@
     )
     half, packed = hold((half, packed))
     gathered = lax.all_gather(half[None], ("z", "c"), axis=0, tiled=True)
-    spread = lax.all_to_all(packed, ("z", "x"), split_axis=0, concat_axis=0, tiled=True)
-    spread = spread.reshape(TOKENS, GROUP)
+    spread = lax.all_to_all(packed, ("x", "z"), split_axis=0, concat_axis=0, tiled=True)
+    spread = jnp.swapaxes(spread.reshape(NX, NZ, 8, GROUP), 0, 1).reshape(TOKENS, GROUP)
     partner = permute(spread, lambda z, x, y, c: (z, 3 - x, y, c))
     pieces = [spread, partner]
     for shift in SHIFTS[1:]:

time: 173 us -> 174 us (level)
    all_gather x1, waiting for transfers between devices: 1.47 us -> 5.13 us  [per_device(): gathered = lax.all_gather(half[None], ('z', 'c'), axis=0, tiled=True)]
    ppermute x13, waiting for transfers between devices: 28.7 us -> 26.5 us  [permute(): return lax.ppermute(array, AXES, pairs)]
  transfers between devices with their start and end apart: 14 -> 14, of which waited for: 8 -> 7; matrix products, arithmetic and copies ran while one was open for 1% -> 1% of each run, Pallas kernels for 0% -> 0%
where the time goes in v14:
time: 174 us; the launch traced here: 173 us
  blocking collectives  70.1 us (40%)
  starting transfers between devices  45.8 us (26%)
  waiting for transfers between devices  31.6 us (18%)
  between operations  13.6 us (8%)
  Pallas kernels  8.87 us (5%)
  local copies, waits for them, and re-layouts  1.91 us (1%)
    ppermute x13, starting transfers between devices, permute(): return lax.ppermute(array, AXES, pairs)  45.8 us
    all_to_all x1, blocking collectives, per_device(): lax.all_to_all(packed, ('x', 'z'), split_axis=0, concat_axis=0, tiled=True)  43.7 us
    ppermute x13, waiting for transfers between devices, permute(): return lax.ppermute(array, AXES, pairs)  26.5 us
    all_to_all x1, blocking collectives, per_device(): lax.all_to_all(output, 'z', split_axis=0, concat_axis=0, tiled=True)  26.5 us
    pallas_call x1, Pallas kernels, project_and_attend(): pl.pallas_call(attend_kernel, out_shape=[jax.ShapeDtypeStruct((TOKENS //...  8.87 us
    all_gather x1, waiting for transfers between devices, per_device(): gathered = lax.all_gather(half[None], ('z', 'c'), axis=0, tiled=True)  5.13 us
  transfers between devices with their start and end apart: 14, of which 7 were waited for; matrix products, arithmetic and copies ran while one was open for 1% of the time, Pallas kernels for 0%

profile of v14, /device:TPU:1, one launch (start us, length us, event | category | flops | bytes accessed | tf_op | source)
XLA Modules:
  0.0 173.1 jit_solution(12058715924530492036)
XLA Ops:
  6.5 5.9 %collective-permute-start = (bf16[3,48,384]{2,1,0:T(8,128)(2,1)}, bf16[3,48,384]{2,1,0:T(8,128)(2,1)S(1)}, u32[]{:S(2)}, u32[]{:S(2)}) collective-permute-start(bf16[3,48,384]{2,1,0:T(8,128)(2,1)} %bitcast.40), channel_id=1, source_target_pairs={{0,0},{1,24},{2,2},{3,26},{4,4},{5,28},{6,6},{7,30},{8,8},{9,16},{... | collective-permute-start | bytes 331784 | tf_op jit(solution)/shard_map/ppermute | solution.py:34
  12.4 2.2 %collective-permute-start.1 = (bf16[3,48,384]{2,1,0:T(8,128)(2,1)}, bf16[3,48,384]{2,1,0:T(8,128)(2,1)S(1)}, u32[]{:S(2)}, u32[]{:S(2)}) collective-permute-start(bf16[3,48,384]{2,1,0:T(8,128)(2,1)} %bitcast.41), channel_id=1, source_target_pairs={{0,8},{1,16},{2,10},{3,18},{4,12},{5,20},{6,14},{7,22},{8,0},{9,24... | collective-permute-start | bytes 331784 | tf_op jit(solution)/shard_map/ppermute | solution.py:34
  14.7 1.1 constant_dynamic-slice_fusion
  15.8 0.1 reverse_select_fusion
  16.0 0.0 collective-permute-done
  16.0 4.2 %collective-permute-done.1 = bf16[3,48,384]{2,1,0:T(8,128)(2,1)S(1)} collective-permute-done((bf16[3,48,384]{2,1,0:T(8,128)(2,1)}, bf16[3,48,384]{2,1,0:T(8,128)(2,1)S(1)}, u32[]{:S(2)}, u32[]{:S(2)}) %collective-permute-start.1) | collective-permute-done | bytes 110624 | tf_op jit(solution)/shard_map/ppermute | solution.py:34
  20.2 0.7 maximum_select_fusion
  21.0 0.0 all-gather.3.cloned.1.call-update
  21.0 43.7 %all_to_all.10 = bf16[64,8,384]{2,1,0:T(8,128)(2,1)S(1)} all-to-all(bf16[64,8,384]{2,1,0:T(8,128)(2,1)S(1)} %bitcast.36), channel_id=1, replica_groups=mesh['z'=16,'x'=4,'y'=4,'c'=2] {'x','z'}, dimensions={0} | all-to-all | bytes 786432 | tf_op jit(solution)/shard_map/all_to_all | solution.py:181
  64.7 4.6 %collective-permute-start.2 = (bf16[512,384]{1,0:T(8,128)(2,1)S(1)}, bf16[512,384]{1,0:T(8,128)(2,1)S(1)}, u32[]{:S(2)}, u32[]{:S(2)}) collective-permute-start(bf16[512,384]{1,0:T(8,128)(2,1)S(1)} %bitcast.30), channel_id=1, source_target_pairs={{0,24},{1,25},{2,26},{3,27},{4,28},{5,29},{6,30},{7,31},{8,16},{9,... | collective-permute-start | bytes 1179656 | tf_op jit(solution)/shard_map/ppermute | solution.py:34
  69.3 4.8 %collective-permute-start.3 = (bf16[512,384]{1,0:T(8,128)(2,1)S(1)}, bf16[512,384]{1,0:T(8,128)(2,1)S(1)}, u32[]{:S(2)}, u32[]{:S(2)}) collective-permute-start(bf16[512,384]{1,0:T(8,128)(2,1)S(1)} %bitcast.31), channel_id=1, source_target_pairs={{0,6},{1,7},{2,0},{3,1},{4,2},{5,3},{6,4},{7,5},{8,14},{9,15},{10,... | collective-permute-start | bytes 1179656 | tf_op jit(solution)/shard_map/ppermute | solution.py:34
  74.1 1.9 %collective-permute-start.5 = (bf16[512,384]{1,0:T(8,128)(2,1)S(1)}, bf16[512,384]{1,0:T(8,128)(2,1)S(1)}, u32[]{:S(2)}, u32[]{:S(2)}) collective-permute-start(bf16[512,384]{1,0:T(8,128)(2,1)S(1)} %bitcast.32), channel_id=1, source_target_pairs={{0,2},{1,3},{2,4},{3,5},{4,6},{5,7},{6,0},{7,1},{8,10},{9,11},{10,... | collective-permute-start | bytes 1179656 | tf_op jit(solution)/shard_map/ppermute | solution.py:34
  76.0 3.5 %collective-permute-start.7 = (bf16[512,384]{1,0:T(8,128)(2,1)S(1)}, bf16[512,384]{1,0:T(8,128)(2,1)S(1)}, u32[]{:S(2)}, u32[]{:S(2)}) collective-permute-start(bf16[512,384]{1,0:T(8,128)(2,1)S(1)} %bitcast.33), channel_id=1, source_target_pairs={{0,4},{1,5},{2,6},{3,7},{4,0},{5,1},{6,2},{7,3},{8,12},{9,13},{10,... | collective-permute-start | bytes 1179656 | tf_op jit(solution)/shard_map/ppermute | solution.py:34
  79.5 3.0 %collective-permute-start.4 = (bf16[512,384]{1,0:T(8,128)(2,1)S(1)}, bf16[512,384]{1,0:T(8,128)(2,1)S(1)}, u32[]{:S(2)}, u32[]{:S(2)}) collective-permute-start(bf16[512,384]{1,0:T(8,128)(2,1)S(1)} %collective-permute-done.2.refs_1_), channel_id=1, source_target_pairs={{0,6},{1,7},{2,0},{3,1},{4,2},{5,3},{6,4},{7,5},{8,14},{9,15},{10,... | collective-permute-start | bytes 1179656 | tf_op jit(solution)/shard_map/ppermute | solution.py:34
  82.5 2.5 %collective-permute-start.6 = (bf16[512,384]{1,0:T(8,128)(2,1)S(1)}, bf16[512,384]{1,0:T(8,128)(2,1)S(1)}, u32[]{:S(2)}, u32[]{:S(2)}) collective-permute-start(bf16[512,384]{1,0:T(8,128)(2,1)S(1)} %collective-permute-done.2.refs_1_), channel_id=1, source_target_pairs={{0,2},{1,3},{2,4},{3,5},{4,6},{5,7},{6,0},{7,1},{8,10},{9,11},{10,... | collective-permute-start | bytes 1179656 | tf_op jit(solution)/shard_map/ppermute | solution.py:34
  85.0 3.7 %collective-permute-start.8 = (bf16[512,384]{1,0:T(8,128)(2,1)S(1)}, bf16[512,384]{1,0:T(8,128)(2,1)S(1)}, u32[]{:S(2)}, u32[]{:S(2)}) collective-permute-start(bf16[512,384]{1,0:T(8,128)(2,1)S(1)} %collective-permute-done.2.refs_1_), channel_id=1, source_target_pairs={{0,4},{1,5},{2,6},{3,7},{4,0},{5,1},{6,2},{7,3},{8,12},{9,13},{10,... | collective-permute-start | bytes 1179656 | tf_op jit(solution)/shard_map/ppermute | solution.py:34
  88.8 0.1 pad_add_fusion.place
  88.8 2.7 %collective-permute-done.7.refs_6_ = bf16[512,384]{1,0:T(8,128)(2,1)S(1)} collective-permute-done((bf16[512,384]{1,0:T(8,128)(2,1)S(1)}, bf16[512,384]{1,0:T(8,128)(2,1)S(1)}, u32[]{:S(2)}, u32[]{:S(2)}) %collective-permute-start.7) | collective-permute-done | bytes 393248 | tf_op jit(solution)/shard_map/ppermute | solution.py:34
  91.5 10.8 %collective-permute-done.4.refs_3_ = bf16[512,384]{1,0:T(8,128)(2,1)S(1)} collective-permute-done((bf16[512,384]{1,0:T(8,128)(2,1)S(1)}, bf16[512,384]{1,0:T(8,128)(2,1)S(1)}, u32[]{:S(2)}, u32[]{:S(2)}) %collective-permute-start.4) | collective-permute-done | bytes 393248 | tf_op jit(solution)/shard_map/ppermute | solution.py:34
  102.3 3.1 %collective-permute-done.6.refs_5_ = bf16[512,384]{1,0:T(8,128)(2,1)S(1)} collective-permute-done((bf16[512,384]{1,0:T(8,128)(2,1)S(1)}, bf16[512,384]{1,0:T(8,128)(2,1)S(1)}, u32[]{:S(2)}, u32[]{:S(2)}) %collective-permute-start.6) | collective-permute-done | bytes 393248 | tf_op jit(solution)/shard_map/ppermute | solution.py:34
  105.3 3.0 %collective-permute-done.8.refs_7_ = bf16[512,384]{1,0:T(8,128)(2,1)S(1)} collective-permute-done((bf16[512,384]{1,0:T(8,128)(2,1)S(1)}, bf16[512,384]{1,0:T(8,128)(2,1)S(1)}, u32[]{:S(2)}, u32[]{:S(2)}) %collective-permute-start.8) | collective-permute-done | bytes 393248 | tf_op jit(solution)/shard_map/ppermute | solution.py:34
  108.4 5.1 %all-gather.3.cloned.1.call-done = bf16[96,96,384]{2,1,0:T(8,128)(2,1)} async-done(((bf16[3,96,384]{2,1,0:T(8,128)(2,1)}), bf16[96,96,384]{2,1,0:T(8,128)(2,1)}) %all-gather.3.cloned.1.call-update) | async-done | bytes 7077904 | tf_op jit(solution)/shard_map/all_gather | solution.py:180
  113.5 8.9 %shard_map.37 = (bf16[128,384]{1,0:T(8,128)(2,1)S(1)}, bf16[128,384]{1,0:T(8,128)(2,1)S(1)}, bf16[128,384]{1,0:T(8,128)(2,1)S(1)}, bf16[128,384]{1,0:T(8,128)(2,1)S(1)}) custom-call(s32[3]{0:T(128)S(1)} %pad_add_fusion.place, s32[8,8]{1,0:T(8,128)S(1)} %copy-done, bf16[32,3,96,384]{3,2,1,0:T(8,128)(2,1)} %bitcast.35, bf16[512,384]{1,0:T(8,128)(2,1)S(1)} %bitcast.34, ...), custom_call_target="tpu_custom_call" | custom-call | tf_op jit(solution)/shard_map/pallas_call | solution.py:138
  122.4 4.9 %collective-permute-start.10 = (bf16[128,384]{1,0:T(8,128)(2,1)S(1)}, bf16[128,384]{1,0:T(8,128)(2,1)S(1)}, u32[]{:S(2)}, u32[]{:S(2)}) collective-permute-start(bf16[128,384]{1,0:T(8,128)(2,1)S(1)} %get-tuple-element.14), channel_id=1, source_target_pairs={{0,8},{1,16},{2,10},{3,18},{4,12},{5,20},{6,14},{7,22},{8,0},{9,24... | collective-permute-start | bytes 294920 | tf_op jit(solution)/shard_map/ppermute | solution.py:34
  127.3 1.9 %collective-permute-start.11 = (bf16[128,384]{1,0:T(8,128)(2,1)S(1)}, bf16[128,384]{1,0:T(8,128)(2,1)S(1)}, u32[]{:S(2)}, u32[]{:S(2)}) collective-permute-start(bf16[128,384]{1,0:T(8,128)(2,1)S(1)} %get-tuple-element.15), channel_id=1, source_target_pairs={{0,16},{1,8},{2,18},{3,10},{4,20},{5,12},{6,22},{7,14},{8,24},{9,0... | collective-permute-start | bytes 294920 | tf_op jit(solution)/shard_map/ppermute | solution.py:34
  129.3 2.5 %collective-permute-start.12 = (bf16[128,384]{1,0:T(8,128)(2,1)S(1)}, bf16[128,384]{1,0:T(8,128)(2,1)S(1)}, u32[]{:S(2)}, u32[]{:S(2)}) collective-permute-start(bf16[128,384]{1,0:T(8,128)(2,1)S(1)} %get-tuple-element.16), channel_id=1, source_target_pairs={{0,24},{1,0},{2,26},{3,2},{4,28},{5,4},{6,30},{7,6},{8,16},{9,8},{... | collective-permute-start | bytes 294920 | tf_op jit(solution)/shard_map/ppermute | solution.py:34
  131.8 4.4 %collective-permute-start.9 = (bf16[128,384]{1,0:T(8,128)(2,1)S(1)}, bf16[128,384]{1,0:T(8,128)(2,1)S(1)}, u32[]{:S(2)}, u32[]{:S(2)}) collective-permute-start(bf16[128,384]{1,0:T(8,128)(2,1)S(1)} %get-tuple-element.13), channel_id=1, source_target_pairs={{0,0},{1,24},{2,2},{3,26},{4,4},{5,28},{6,6},{7,30},{8,8},{9,16},{... | collective-permute-start | bytes 294920 | tf_op jit(solution)/shard_map/ppermute | solution.py:34
  136.2 2.7 %collective-permute-done.9 = bf16[128,384]{1,0:T(8,128)(2,1)S(1)} collective-permute-done((bf16[128,384]{1,0:T(8,128)(2,1)S(1)}, bf16[128,384]{1,0:T(8,128)(2,1)S(1)}, u32[]{:S(2)}, u32[]{:S(2)}) %collective-permute-start.9) | collective-permute-done | bytes 98336 | tf_op jit(solution)/shard_map/ppermute | solution.py:34
  138.9 0.1 select_bitcast_fusion.3
  139.0 0.1 pad_maximum_fusion
  139.1 26.5 %all_to_all.11 = bf16[16,4,8,384]{3,2,1,0:T(8,128)(2,1)S(1)} all-to-all(bf16[16,4,8,384]{3,2,1,0:T(8,128)(2,1)S(1)} %pad_maximum_fusion), channel_id=1, replica_groups=mesh['z'=16,'x'=4,'y'=4,'c'=2] {'z'}, dimensions={0} | all-to-all | bytes 786432 | tf_op jit(solution)/shard_map/all_to_all | solution.py:194
  165.5 0.7 copy.17
  (12 shorter events, 0.2 us)
Async XLA Ops:
  6.5 107.0 %copy-start = (s32[8,8]{1,0:T(8,128)S(1)}, s32[8,8]{1,0:T(8,128)}, u32[]{:S(2)}) copy-start(s32[8,8]{1,0:T(8,128)} %mask.1) | copy-start | bytes 772
  6.5 107.0 %all-gather.3.cloned.1.call-start = ((), (), s32[]{:S(2)}) async-start(), calls=%async_computation.2 | async-start | bytes 7299072 | tf_op jit(solution)/shard_map/all_gather | solution.py:180
  6.5 9.5 %collective-permute-start = (bf16[3,48,384]{2,1,0:T(8,128)(2,1)}, bf16[3,48,384]{2,1,0:T(8,128)(2,1)S(1)}, u32[]{:S(2)}, u32[]{:S(2)}) collective-permute-start(bf16[3,48,384]{2,1,0:T(8,128)(2,1)} %bitcast.40), channel_id=1, source_target_pairs={{0,0},{1,24},{2,2},{3,26},{4,4},{5,28},{6,6},{7,30},{8,8},{9,16},{... | collective-permute-start | bytes 331784 | tf_op jit(solution)/shard_map/ppermute | solution.py:34
  12.4 7.8 %collective-permute-start.1 = (bf16[3,48,384]{2,1,0:T(8,128)(2,1)}, bf16[3,48,384]{2,1,0:T(8,128)(2,1)S(1)}, u32[]{:S(2)}, u32[]{:S(2)}) collective-permute-start(bf16[3,48,384]{2,1,0:T(8,128)(2,1)} %bitcast.41), channel_id=1, source_target_pairs={{0,8},{1,16},{2,10},{3,18},{4,12},{5,20},{6,14},{7,22},{8,0},{9,24... | collective-permute-start | bytes 331784 | tf_op jit(solution)/shard_map/ppermute | solution.py:34
  64.7 14.8 %collective-permute-start.2 = (bf16[512,384]{1,0:T(8,128)(2,1)S(1)}, bf16[512,384]{1,0:T(8,128)(2,1)S(1)}, u32[]{:S(2)}, u32[]{:S(2)}) collective-permute-start(bf16[512,384]{1,0:T(8,128)(2,1)S(1)} %bitcast.30), channel_id=1, source_target_pairs={{0,24},{1,25},{2,26},{3,27},{4,28},{5,29},{6,30},{7,31},{8,16},{9,... | collective-permute-start | bytes 1179656 | tf_op jit(solution)/shard_map/ppermute | solution.py:34
  69.3 15.7 %collective-permute-start.3 = (bf16[512,384]{1,0:T(8,128)(2,1)S(1)}, bf16[512,384]{1,0:T(8,128)(2,1)S(1)}, u32[]{:S(2)}, u32[]{:S(2)}) collective-permute-start(bf16[512,384]{1,0:T(8,128)(2,1)S(1)} %bitcast.31), channel_id=1, source_target_pairs={{0,6},{1,7},{2,0},{3,1},{4,2},{5,3},{6,4},{7,5},{8,14},{9,15},{10,... | collective-permute-start | bytes 1179656 | tf_op jit(solution)/shard_map/ppermute | solution.py:34
  74.1 14.7 %collective-permute-start.5 = (bf16[512,384]{1,0:T(8,128)(2,1)S(1)}, bf16[512,384]{1,0:T(8,128)(2,1)S(1)}, u32[]{:S(2)}, u32[]{:S(2)}) collective-permute-start(bf16[512,384]{1,0:T(8,128)(2,1)S(1)} %bitcast.32), channel_id=1, source_target_pairs={{0,2},{1,3},{2,4},{3,5},{4,6},{5,7},{6,0},{7,1},{8,10},{9,11},{10,... | collective-permute-start | bytes 1179656 | tf_op jit(solution)/shard_map/ppermute | solution.py:34
  76.0 15.5 %collective-permute-start.7 = (bf16[512,384]{1,0:T(8,128)(2,1)S(1)}, bf16[512,384]{1,0:T(8,128)(2,1)S(1)}, u32[]{:S(2)}, u32[]{:S(2)}) collective-permute-start(bf16[512,384]{1,0:T(8,128)(2,1)S(1)} %bitcast.33), channel_id=1, source_target_pairs={{0,4},{1,5},{2,6},{3,7},{4,0},{5,1},{6,2},{7,3},{8,12},{9,13},{10,... | collective-permute-start | bytes 1179656 | tf_op jit(solution)/shard_map/ppermute | solution.py:34
  79.5 22.8 %collective-permute-start.4 = (bf16[512,384]{1,0:T(8,128)(2,1)S(1)}, bf16[512,384]{1,0:T(8,128)(2,1)S(1)}, u32[]{:S(2)}, u32[]{:S(2)}) collective-permute-start(bf16[512,384]{1,0:T(8,128)(2,1)S(1)} %collective-permute-done.2.refs_1_), channel_id=1, source_target_pairs={{0,6},{1,7},{2,0},{3,1},{4,2},{5,3},{6,4},{7,5},{8,14},{9,15},{10,... | collective-permute-start | bytes 1179656 | tf_op jit(solution)/shard_map/ppermute | solution.py:34
  82.5 22.8 %collective-permute-start.6 = (bf16[512,384]{1,0:T(8,128)(2,1)S(1)}, bf16[512,384]{1,0:T(8,128)(2,1)S(1)}, u32[]{:S(2)}, u32[]{:S(2)}) collective-permute-start(bf16[512,384]{1,0:T(8,128)(2,1)S(1)} %collective-permute-done.2.refs_1_), channel_id=1, source_target_pairs={{0,2},{1,3},{2,4},{3,5},{4,6},{5,7},{6,0},{7,1},{8,10},{9,11},{10,... | collective-permute-start | bytes 1179656 | tf_op jit(solution)/shard_map/ppermute | solution.py:34
  85.0 23.3 %collective-permute-start.8 = (bf16[512,384]{1,0:T(8,128)(2,1)S(1)}, bf16[512,384]{1,0:T(8,128)(2,1)S(1)}, u32[]{:S(2)}, u32[]{:S(2)}) collective-permute-start(bf16[512,384]{1,0:T(8,128)(2,1)S(1)} %collective-permute-done.2.refs_1_), channel_id=1, source_target_pairs={{0,4},{1,5},{2,6},{3,7},{4,0},{5,1},{6,2},{7,3},{8,12},{9,13},{10,... | collective-permute-start | bytes 1179656 | tf_op jit(solution)/shard_map/ppermute | solution.py:34
  122.4 13.8 %collective-permute-start.10 = (bf16[128,384]{1,0:T(8,128)(2,1)S(1)}, bf16[128,384]{1,0:T(8,128)(2,1)S(1)}, u32[]{:S(2)}, u32[]{:S(2)}) collective-permute-start(bf16[128,384]{1,0:T(8,128)(2,1)S(1)} %get-tuple-element.14), channel_id=1, source_target_pairs={{0,8},{1,16},{2,10},{3,18},{4,12},{5,20},{6,14},{7,22},{8,0},{9,24... | collective-permute-start | bytes 294920 | tf_op jit(solution)/shard_map/ppermute | solution.py:34
  127.3 8.8 %collective-permute-start.11 = (bf16[128,384]{1,0:T(8,128)(2,1)S(1)}, bf16[128,384]{1,0:T(8,128)(2,1)S(1)}, u32[]{:S(2)}, u32[]{:S(2)}) collective-permute-start(bf16[128,384]{1,0:T(8,128)(2,1)S(1)} %get-tuple-element.15), channel_id=1, source_target_pairs={{0,16},{1,8},{2,18},{3,10},{4,20},{5,12},{6,22},{7,14},{8,24},{9,0... | collective-permute-start | bytes 294920 | tf_op jit(solution)/shard_map/ppermute | solution.py:34
  129.3 6.9 %collective-permute-start.12 = (bf16[128,384]{1,0:T(8,128)(2,1)S(1)}, bf16[128,384]{1,0:T(8,128)(2,1)S(1)}, u32[]{:S(2)}, u32[]{:S(2)}) collective-permute-start(bf16[128,384]{1,0:T(8,128)(2,1)S(1)} %get-tuple-element.16), channel_id=1, source_target_pairs={{0,24},{1,0},{2,26},{3,2},{4,28},{5,4},{6,30},{7,6},{8,16},{9,8},{... | collective-permute-start | bytes 294920 | tf_op jit(solution)/shard_map/ppermute | solution.py:34
  131.8 7.1 %collective-permute-start.9 = (bf16[128,384]{1,0:T(8,128)(2,1)S(1)}, bf16[128,384]{1,0:T(8,128)(2,1)S(1)}, u32[]{:S(2)}, u32[]{:S(2)}) collective-permute-start(bf16[128,384]{1,0:T(8,128)(2,1)S(1)} %get-tuple-element.13), channel_id=1, source_target_pairs={{0,0},{1,24},{2,2},{3,26},{4,4},{5,28},{6,6},{7,30},{8,8},{9,16},{... | collective-permute-start | bytes 294920 | tf_op jit(solution)/shard_map/ppermute | solution.py:34
Sparse Core Ops, SparseCore 0:
  21.1 92.3 all-gather.2
